TPU v7x, 32 devices: a whole 2x2x4 slice. The times are simulated.
32 devices in a mesh: dp: 8 (over z, y), tensor: 4 (over x, core).
Axes of the slice: x: 2, y: 2, z: 4, core: 2. Of those that a mesh axis runs over, the one named last changes fastest.
Arguments:
- image: bfloat16 [8, 1024, 1536], P('dp', 'tensor'), may hold values from -8 to 8
- text: bfloat16 [8, 154, 1536], P('dp'), may hold values from -8 to 8
- cond: float32 [8, 1536], P('dp'), may hold values from -6 to 6
- w_ada: float32 [2, 1536, 6, 1536], P(None, 'dp', None, 'tensor'), may hold values from -0.15625 to 0.15625
- w_qkv: float32 [2, 1536, 3, 1536], P(None, 'dp', None, 'tensor'), may hold values from -0.15625 to 0.15625
- w_out: float32 [2, 1536, 1536], P(None, ('tensor', 'dp')), may hold values from -1.25 to 1.25
- w_up: float32 [2, 1536, 6144], P(None, 'dp', 'tensor'), may hold values from -0.15625 to 0.15625
- w_down: float32 [2, 6144, 1536], P(None, ('tensor', 'dp')), may hold values from -0.078125 to 0.078125
- grad_image: bfloat16 [8, 1024, 1536], P('dp', 'tensor'), may hold values from -6 to 6
- grad_text: bfloat16 [8, 154, 1536], P('dp'), may hold values from -6 to 6
Outputs:
- image_out: bfloat16 [8, 1024, 1536], P('dp', 'tensor')
- text_out: bfloat16 [8, 154, 1536], P('dp')
- image_grad: float32 [8, 1024, 1536], P('dp', 'tensor')
- text_grad: float32 [8, 154, 1536], P('dp')
- cond_grad: float32 [8, 1536], P('dp')
- shift_grad: float32 [8, 2, 1536], P('dp', None, 'tensor')
- w_ada_grad: float32 [2, 1536, 6, 1536], P(None, 'dp', None, 'tensor')
- w_qkv_grad: float32 [2, 1536, 3, 1536], P(None, 'dp', None, 'tensor')
- w_out_grad: float32 [2, 1536, 1536], P(None, ('tensor', 'dp'))
- w_up_grad: float32 [2, 1536, 6144], P(None, 'dp', 'tensor')
- w_down_grad: float32 [2, 6144, 1536], P(None, ('tensor', 'dp'))
All inputs are finite; a program needn't handle non-finite values.
Results may differ from a plain program's by a relative error of at most 0.022.
The roundings to bfloat16 on the way count: a program that leaves them out, or rounds other values in their place, can miss the bound.
Values may be sent and summed in bfloat16 or wider, within the bound.
A program may use at most 256 MiB of HBM per device.

v0:
```python
import jax
import jax.numpy as jnp
from jax import lax
from jax.sharding import PartitionSpec as P

HEAD_DIM = 64


EPS = 1e-06
LOW_TYPE = jnp.bfloat16
WIDE_TYPE = jnp.float32


def layer_norm(values):
    average = jnp.mean(values, axis=-1, keepdims=True)
    centred = values - average
    spread = jnp.mean(centred * centred, axis=-1, keepdims=True)
    return centred * lax.rsqrt(spread + EPS)


def gelu_tanh(values):
    return jax.nn.gelu(values, approximate=True)


def gather_rows(rows):
    return lax.all_gather(rows, "tensor", axis=1, tiled=True)


def scatter_rows(partial_rows):
    return lax.psum_scatter(
        partial_rows.astype(jnp.bfloat16), "tensor", scatter_dimension=1, tiled=True
    ).astype(jnp.float32)


def sum_text(partial_rows):
    return lax.psum(partial_rows.astype(jnp.bfloat16), "tensor").astype(jnp.float32)


def to_blocks(packed, num_heads):
    num_seqs, num_parts, num_rows, width_here = packed.shape
    reshaped = packed.reshape(num_seqs, num_parts, num_rows, num_heads, HEAD_DIM)
    return reshaped.transpose(0, 3, 1, 2, 4).reshape(
        num_seqs * num_heads, num_parts, num_rows, HEAD_DIM
    )


def from_blocks(blocks, num_seqs):
    num_blocks, num_parts, num_rows, head_size = blocks.shape
    num_heads = num_blocks // num_seqs
    reshaped = blocks.reshape(num_seqs, num_heads, num_parts, num_rows, head_size)
    return reshaped.transpose(0, 2, 3, 1, 4).reshape(
        num_seqs, num_parts, num_rows, num_heads * head_size
    )


def attend(block):
    queries, key_rows, value_rows = block
    scores = jnp.dot(queries, key_rows.T, preferred_element_type=WIDE_TYPE) * HEAD_DIM ** (-0.5)
    row_max = jnp.max(scores, axis=-1, keepdims=True)
    shifted = jnp.exp(scores - row_max)
    row_sum = jnp.sum(shifted, axis=-1, keepdims=True)
    attn_probs = (shifted / row_sum).astype(LOW_TYPE)
    output = jnp.dot(attn_probs, value_rows, preferred_element_type=WIDE_TYPE)
    return (output, row_max[:, 0] + jnp.log(row_sum[:, 0]))


def attend_back(block):
    queries, key_rows, value_rows, log_total, grad_output = block
    scaling = HEAD_DIM ** (-0.5)
    scores = jnp.dot(queries, key_rows.T, preferred_element_type=WIDE_TYPE) * scaling
    attn_probs = jnp.exp(scores - log_total[:, None])
    grad_probs = jnp.dot(grad_output, value_rows.T, preferred_element_type=WIDE_TYPE)
    row_dot = jnp.sum(grad_probs * attn_probs, axis=-1, keepdims=True)
    grad_scores = (attn_probs * (grad_probs - row_dot)).astype(LOW_TYPE)
    grad_queries = (
        jnp.dot(grad_scores, key_rows, preferred_element_type=WIDE_TYPE) * scaling
    ).astype(LOW_TYPE)
    grad_keys = (
        jnp.dot(grad_scores.T, queries, preferred_element_type=WIDE_TYPE) * scaling
    ).astype(LOW_TYPE)
    grad_values = jnp.dot(
        attn_probs.astype(LOW_TYPE).T, grad_output, preferred_element_type=WIDE_TYPE
    ).astype(LOW_TYPE)
    return (grad_queries, grad_keys, grad_values)


def local(image, text, cond, w_ada, w_qkv, w_out, w_up, w_down, grad_image, grad_text):
    ada_full, qkv_full, out_full, up_full, down_full = (
        lax.all_gather(w_ada.astype(LOW_TYPE), "dp", axis=1, tiled=True),
        lax.all_gather(w_qkv.astype(LOW_TYPE), "dp", axis=1, tiled=True),
        lax.all_gather(w_out.astype(LOW_TYPE), "dp", axis=1, tiled=True),
        lax.all_gather(w_up.astype(LOW_TYPE), "dp", axis=1, tiled=True),
        lax.all_gather(w_down.astype(LOW_TYPE), "dp", axis=1, tiled=True),
    )
    num_seqs = image.shape[0]
    heads_here = qkv_full.shape[-1] // HEAD_DIM
    cond_low = jax.nn.silu(cond).astype(LOW_TYPE)
    mod_part = jnp.einsum("nd,sdkf->nskf", cond_low, ada_full, preferred_element_type=WIDE_TYPE)
    modulation = lax.all_gather(mod_part, "tensor", axis=3, tiled=True)

    def mod_row(stream, index):
        return modulation[:, stream, index][:, None, :]

    streams = [image.astype(WIDE_TYPE), text.astype(WIDE_TYPE)]
    normed_in = [layer_norm(residual) for residual in streams]
    first_in = [
        (normed_in[stream] * (1.0 + mod_row(stream, 1)) + mod_row(stream, 0)).astype(LOW_TYPE)
        for stream in range(2)
    ]
    attn_rows = [gather_rows(first_in[0]), first_in[1]]
    joint = jnp.concatenate(
        [
            jnp.einsum(
                "ntd,dkf->nktf",
                attn_rows[stream],
                qkv_full[stream],
                preferred_element_type=WIDE_TYPE,
            )
            for stream in range(2)
        ],
        axis=2,
    ).astype(LOW_TYPE)
    blocks = to_blocks(joint, heads_here)
    attn_out, log_total = lax.map(attend, (blocks[:, 0], blocks[:, 1], blocks[:, 2]))
    mixed = from_blocks(attn_out[:, None], num_seqs)[:, 0].astype(LOW_TYPE)
    split_at = attn_rows[0].shape[1]
    mixed_rows = [mixed[:, :split_at], mixed[:, split_at:]]
    branch_parts = [
        jnp.einsum(
            "ntf,fd->ntd", mixed_rows[stream], out_full[stream], preferred_element_type=WIDE_TYPE
        )
        for stream in range(2)
    ]
    branches = [scatter_rows(branch_parts[0]), sum_text(branch_parts[1])]
    middle = [streams[stream] + mod_row(stream, 2) * branches[stream] for stream in range(2)]
    normed_mid = [layer_norm(residual) for residual in middle]
    second_in = [
        (normed_mid[stream] * (1.0 + mod_row(stream, 4)) + mod_row(stream, 3)).astype(LOW_TYPE)
        for stream in range(2)
    ]
    mlp_rows = [gather_rows(second_in[0]), second_in[1]]
    pre_act = [
        jnp.einsum(
            "ntd,df->ntf", mlp_rows[stream], up_full[stream], preferred_element_type=WIDE_TYPE
        )
        for stream in range(2)
    ]
    hidden = [gelu_tanh(pre_act[stream]).astype(LOW_TYPE) for stream in range(2)]
    ffn_parts = [
        jnp.einsum(
            "ntf,fd->ntd", hidden[stream], down_full[stream], preferred_element_type=WIDE_TYPE
        )
        for stream in range(2)
    ]
    ffn = [scatter_rows(ffn_parts[0]), sum_text(ffn_parts[1])]
    results = [
        (middle[stream] + mod_row(stream, 5) * ffn[stream]).astype(LOW_TYPE) for stream in range(2)
    ]
    cotangent = [grad_image.astype(WIDE_TYPE), grad_text.astype(WIDE_TYPE)]
    ffn_grad = [(mod_row(stream, 5) * cotangent[stream]).astype(LOW_TYPE) for stream in range(2)]
    ffn_rows = [gather_rows(ffn_grad[0]), ffn_grad[1]]
    down_grad = jnp.stack(
        [
            jnp.einsum(
                "ntf,ntd->fd", hidden[stream], ffn_rows[stream], preferred_element_type=WIDE_TYPE
            )
            for stream in range(2)
        ]
    )
    hidden_grad = [
        jnp.einsum(
            "ntd,fd->ntf", ffn_rows[stream], down_full[stream], preferred_element_type=WIDE_TYPE
        )
        for stream in range(2)
    ]
    pre_grad = [
        jax.vjp(gelu_tanh, pre_act[stream])[1](hidden_grad[stream])[0].astype(LOW_TYPE)
        for stream in range(2)
    ]
    up_grad = jnp.stack(
        [
            jnp.einsum(
                "ntd,ntf->df", mlp_rows[stream], pre_grad[stream], preferred_element_type=WIDE_TYPE
            )
            for stream in range(2)
        ]
    )
    second_parts = [
        jnp.einsum(
            "ntf,df->ntd", pre_grad[stream], up_full[stream], preferred_element_type=WIDE_TYPE
        )
        for stream in range(2)
    ]
    second_grad = [scatter_rows(second_parts[0]), sum_text(second_parts[1])]
    middle_grad = [
        cotangent[stream]
        + jax.vjp(layer_norm, middle[stream])[1](second_grad[stream] * (1.0 + mod_row(stream, 4)))[
            0
        ]
        for stream in range(2)
    ]
    branch_grad = [
        (mod_row(stream, 2) * middle_grad[stream]).astype(LOW_TYPE) for stream in range(2)
    ]
    branch_rows = [gather_rows(branch_grad[0]), branch_grad[1]]
    out_grad = jnp.stack(
        [
            jnp.einsum(
                "ntf,ntd->fd",
                mixed_rows[stream],
                branch_rows[stream],
                preferred_element_type=WIDE_TYPE,
            )
            for stream in range(2)
        ]
    )
    mixed_grad = jnp.concatenate(
        [
            jnp.einsum(
                "ntd,fd->ntf",
                branch_rows[stream],
                out_full[stream],
                preferred_element_type=WIDE_TYPE,
            )
            for stream in range(2)
        ],
        axis=1,
    ).astype(LOW_TYPE)
    grad_blocks = to_blocks(mixed_grad[:, None], heads_here)[:, 0]
    query_grad, key_grad, value_grad = lax.map(
        attend_back, (blocks[:, 0], blocks[:, 1], blocks[:, 2], log_total, grad_blocks)
    )
    joint_grad = from_blocks(jnp.stack([query_grad, key_grad, value_grad], axis=1), num_seqs)
    joint_rows = [joint_grad[:, :, :split_at], joint_grad[:, :, split_at:]]
    qkv_grad = jnp.stack(
        [
            jnp.einsum(
                "ntd,nktf->dkf",
                attn_rows[stream],
                joint_rows[stream],
                preferred_element_type=WIDE_TYPE,
            )
            for stream in range(2)
        ]
    )
    first_parts = [
        jnp.einsum(
            "nktf,dkf->ntd", joint_rows[stream], qkv_full[stream], preferred_element_type=WIDE_TYPE
        )
        for stream in range(2)
    ]
    first_grad = [scatter_rows(first_parts[0]), sum_text(first_parts[1])]
    input_grad = [
        middle_grad[stream]
        + jax.vjp(layer_norm, streams[stream])[1](first_grad[stream] * (1.0 + mod_row(stream, 1)))[
            0
        ]
        for stream in range(2)
    ]
    mod_terms = [
        jnp.stack(
            [
                jnp.sum(first_grad[stream], axis=1),
                jnp.sum(first_grad[stream] * normed_in[stream], axis=1),
                jnp.sum(middle_grad[stream] * branches[stream], axis=1),
                jnp.sum(second_grad[stream], axis=1),
                jnp.sum(second_grad[stream] * normed_mid[stream], axis=1),
                jnp.sum(cotangent[stream] * ffn[stream], axis=1),
            ],
            axis=1,
        )
        for stream in range(2)
    ]
    width_here = mod_part.shape[-1]
    image_mod = lax.psum_scatter(
        mod_terms[0].astype(jnp.bfloat16), "tensor", scatter_dimension=2, tiled=True
    ).astype(jnp.float32)
    text_mod = lax.dynamic_slice_in_dim(
        mod_terms[1], lax.axis_index("tensor") * width_here, width_here, 2
    )
    shift_grad = jnp.stack([image_mod[:, 3], text_mod[:, 3]], axis=1)
    mod_grad = jnp.stack([image_mod, text_mod], axis=1).astype(LOW_TYPE)
    ada_grad = jnp.einsum("nd,nskf->sdkf", cond_low, mod_grad, preferred_element_type=WIDE_TYPE)
    act_grad = lax.psum(
        jnp.einsum("nskf,sdkf->nd", mod_grad, ada_full, preferred_element_type=WIDE_TYPE), "tensor"
    )
    cond_grad = jax.vjp(jax.nn.silu, cond)[1](act_grad)[0]
    ada_sum, qkv_sum, out_sum, up_sum, down_sum = (
        lax.psum_scatter(
            ada_grad.astype(jnp.bfloat16), "dp", scatter_dimension=1, tiled=True
        ).astype(jnp.float32),
        lax.psum_scatter(
            qkv_grad.astype(jnp.bfloat16), "dp", scatter_dimension=1, tiled=True
        ).astype(jnp.float32),
        lax.psum_scatter(
            out_grad.astype(jnp.bfloat16), "dp", scatter_dimension=1, tiled=True
        ).astype(jnp.float32),
        lax.psum_scatter(
            up_grad.astype(jnp.bfloat16), "dp", scatter_dimension=1, tiled=True
        ).astype(jnp.float32),
        lax.psum_scatter(
            down_grad.astype(jnp.bfloat16), "dp", scatter_dimension=1, tiled=True
        ).astype(jnp.float32),
    )
    return (
        results[0],
        results[1],
        input_grad[0],
        input_grad[1],
        cond_grad,
        shift_grad,
        ada_sum,
        qkv_sum,
        out_sum,
        up_sum,
        down_sum,
    )


def solution(mesh):
    return jax.shard_map(
        local,
        mesh=mesh,
        in_specs=(
            P("dp", "tensor", None),
            P("dp", None, None),
            P("dp", None),
            P(None, "dp", None, "tensor"),
            P(None, "dp", None, "tensor"),
            P(None, ("tensor", "dp"), None),
            P(None, "dp", "tensor"),
            P(None, ("tensor", "dp"), None),
            P("dp", "tensor", None),
            P("dp", None, None),
        ),
        out_specs=(
            P("dp", "tensor", None),
            P("dp", None, None),
            P("dp", "tensor", None),
            P("dp", None, None),
            P("dp", None),
            P("dp", None, "tensor"),
            P(None, "dp", None, "tensor"),
            P(None, "dp", None, "tensor"),
            P(None, ("tensor", "dp"), None),
            P(None, "dp", "tensor"),
            P(None, ("tensor", "dp"), None),
        ),
        check_vma=False,
    )
```

profile of v0, /device:TPU:0, one launch (start us, length us, event | category | flops | bytes accessed | tf_op | source)
XLA Modules:
  0.0 1965.2 jit_solution(12619542089338196095)
XLA Ops:
  7.2 3.6 convert_element_type.248
  14.5 194.8 %all-gather.11.cloned.1.call-done = bf16[2,1536,6,384]{3,1,2,0:T(8,128)(2,1)} async-done(((bf16[2,192,6,384]{3,1,2,0:T(8,128)(2,1)}), bf16[2,1536,6,384]{3,1,2,0:T(8,128)(2,1)}) %all-gather.11.cloned.1.call-update) | async-done | bytes 14155792 | tf_op jit(solution)/shard_map/all_gather | solution.py:89
  209.3 7.0 fusion.199
  216.3 5.5 all-gather
  225.7 93.4 %all-gather.15.cloned.1.call-done = bf16[2,1536,3,384]{3,0,2,1:T(2,128)(2,1)} async-done(((bf16[2,192,3,384]{3,0,2,1:T(2,128)(2,1)}), bf16[2,1536,3,384]{3,0,2,1:T(2,128)(2,1)}) %all-gather.15.cloned.1.call-update) | async-done | bytes 7077904 | tf_op jit(solution)/shard_map/all_gather | solution.py:90
  319.1 15.4 fusion.218
  334.5 17.0 copy.67
  351.5 3.9 fusion.152
  356.1 8.4 fusion.117
  364.5 6.0 copy.47
  370.5 3.4 maximum_bitcast_fusion
  376.1 46.0 %while.26 = (s32[]{:T(128)}, bf16[6,1178,64]{1,2,0:T(8,128)(2,1)}, f32[6,1178]{1,0:T(8,128)}, bf16[6,1178,64]{2,1,0:T(8,128)(2,1)S(1)}, bf16[6,1178,64]{2,1,0:T(...) while((s32[]{:T(128)}, bf16[6,1178,64]{1,2,0:T(8,128)(2,1)}, f32[6,1178]{1,0:T(8,128)}, ...), condition=%wide.region_7.8_spmd, body=%wide.region_4.7_spmd.sunk | while | flops 364959712 | bytes 25703880 | solution.py:124
  422.1 5.7 fusion.85
  430.8 33.1 %reduce-scatter.13.cloned.1.call-done = bf16[1,256,1536]{2,1,0:T(8,128)(2,1)} async-done(((bf16[1,1024,1536]{2,1,0:T(8,128)(2,1)}), bf16[1,256,1536]{2,1,0:T(8,128)(2,1)}) %reduce-scatter.13.cloned.1.call-update) | async-done | bytes 786448 | tf_op jit(solution)/shard_map/reduce_scatter | solution.py:30
  468.5 2.9 convert_element_type.264
  472.6 2.7 fusion.107
  475.4 129.5 %all-gather.21.cloned.1.call-done = bf16[2,1536,1536]{2,1,0:T(8,128)(2,1)} async-done(((bf16[2,192,1536]{2,1,0:T(8,128)(2,1)}), bf16[2,1536,1536]{2,1,0:T(8,128)(2,1)}) %all-gather.21.cloned.1.call-update) | async-done | bytes 9437200 | tf_op jit(solution)/shard_map/all_gather | solution.py:92
  604.8 28.9 %all-gather.19.cloned.1.call-done = bf16[1,1024,1536]{2,1,0:T(8,128)(2,1)} async-done(((bf16[1,256,1536]{2,1,0:T(8,128)(2,1)}), bf16[1,1024,1536]{2,1,0:T(8,128)(2,1)}) %all-gather.19.cloned.1.call-update) | async-done | bytes 3145744 | tf_op jit(solution)/shard_map/all_gather | solution.py:26
  633.8 9.7 fusion.66
  643.4 131.4 %all-gather.23.cloned.1.call-done = bf16[2,1536,1536]{2,1,0:T(8,128)(2,1)} async-done(((bf16[2,192,1536]{2,1,0:T(8,128)(2,1)}), bf16[2,1536,1536]{2,1,0:T(8,128)(2,1)}) %all-gather.23.cloned.1.call-update) | async-done | bytes 9437200 | tf_op jit(solution)/shard_map/all_gather | solution.py:93
  774.9 29.0 %all-gather.25.cloned.1.call-done = bf16[1,1024,1536]{2,1,0:T(8,128)(2,1)} async-done(((bf16[1,256,1536]{2,1,0:T(8,128)(2,1)}), bf16[1,1024,1536]{2,1,0:T(8,128)(2,1)}) %all-gather.25.cloned.1.call-update) | async-done | bytes 3145744 | tf_op jit(solution)/shard_map/all_gather | solution.py:26
  803.8 11.6 fusion.64
  817.1 8.9 fusion.80
  826.0 10.1 fusion.81
  836.4 3.3 all-reduce.5.cloned.1.call-done
  842.4 3.6 fusion.70
  846.1 5.7 fusion.173
  855.1 25.2 %reduce-scatter.17.cloned.1.call-done = bf16[1,256,1536]{2,1,0:T(8,128)(2,1)} async-done(((bf16[1,1024,1536]{2,1,0:T(8,128)(2,1)}), bf16[1,256,1536]{2,1,0:T(8,128)(2,1)}) %reduce-scatter.17.cloned.1.call-update) | async-done | bytes 786448 | tf_op jit(solution)/shard_map/reduce_scatter | solution.py:30
  882.1 2.6 fusion.132
  884.8 36.1 %reduce-scatter.15.cloned.1.call-done = bf16[1,256,1536]{2,1,0:T(8,128)(2,1)} async-done(((bf16[1,1024,1536]{2,1,0:T(8,128)(2,1)}), bf16[1,256,1536]{2,1,0:T(8,128)(2,1)}) %reduce-scatter.15.cloned.1.call-update) | async-done | bytes 786448 | tf_op jit(solution)/shard_map/reduce_scatter | solution.py:30
  920.8 4.5 fusion.129
  927.9 3.3 fusion.219
  931.2 25.6 %all-reduce.7.cloned.1.call-done = bf16[1,154,1536]{2,1,0:T(8,128)(2,1)} async-done(((bf16[1,154,1536]{2,1,0:T(8,128)(2,1)}), bf16[1,154,1536]{2,1,0:T(8,128)(2,1)}) %all-reduce.7.cloned.1.call-update) | async-done | bytes 473104 | tf_op jit(solution)/shard_map/psum | solution.py:36
  964.2 23.4 %all-gather.27.cloned.1.call-done = bf16[1,1024,1536]{2,1,0:T(8,128)(2,1)} async-done(((bf16[1,256,1536]{2,1,0:T(8,128)(2,1)}), bf16[1,1024,1536]{2,1,0:T(8,128)(2,1)}) %all-gather.27.cloned.1.call-update) | async-done | bytes 3145744 | tf_op jit(solution)/shard_map/all_gather | solution.py:26
  987.5 3.7 fusion.146
  992.3 80.6 %while.27 = (s32[]{:T(128)}, bf16[6,1178,64]{1,2,0:T(8,128)(2,1)}, bf16[6,1178,64]{1,2,0:T(8,128)(2,1)}, bf16[6,1178,64]{1,2,0:T(8,128)(2,1)}, bf16[6,1178,64]{2...) while((s32[]{:T(128)}, bf16[6,1178,64]{1,2,0:T(8,128)(2,1)}, ...), condition=%wide.region_24.25_spmd, body=%wide.region_22.24_spmd.sunk | while | flops 899595008 | bytes 43994032 | solution.py:230
  1067.6 2.7 fusion.259
  1076.7 5.6 fusion.82
  1082.6 4.4 fusion.109
  1091.0 5.6 fusion.106
  1096.8 4.5 fusion.99
  1101.3 19.2 reduce-scatter.19.cloned.1.call-done
  1129.4 3.3 pad_maximum_fusion.4
  1132.8 3.7 fusion.54
  1136.5 6.9 fusion.56
  1143.5 8.3 pad_maximum_fusion
  1152.8 5.0 fusion.55
  1157.8 11.8 fusion.57
  1169.5 8.3 pad_maximum_fusion.1
  1181.2 7.5 fusion.78
  1188.6 3.7 pad_maximum_fusion.2
  1196.1 3.0 fusion.177
  1200.4 9.0 fusion.51
  1209.4 3.3 copy.54
  1212.8 44.7 %reduce-scatter.25.cloned.1.call-done = bf16[2,48,1536]{2,1,0:T(8,128)(2,1)} async-done(((bf16[2,384,1536]{2,1,0:T(8,128)(2,1)}), bf16[2,48,1536]{2,1,0:T(8,128)(2,1)}) %reduce-scatter.25.cloned.1.call-update) | async-done | bytes 294928 | tf_op jit(solution)/shard_map/reduce_scatter | solution.py:295
  1261.2 7.0 fusion.114
  1268.1 6.2 psum.39
  1275.5 148.5 %reduce-scatter.27.cloned.1.call-done = bf16[2,192,1536]{2,1,0:T(8,128)(2,1)} async-done(((bf16[2,1536,1536]{2,1,0:T(8,128)(2,1)}), bf16[2,192,1536]{2,1,0:T(8,128)(2,1)}) %reduce-scatter.27.cloned.1.call-update) | async-done | bytes 1179664 | tf_op jit(solution)/shard_map/reduce_scatter | solution.py:298
  1424.0 3.0 convert_element_type.303
  1426.9 163.4 %reduce-scatter.29.cloned.1.call-done = bf16[2,192,1536]{2,1,0:T(8,128)(2,1)} async-done(((bf16[2,1536,1536]{2,1,0:T(8,128)(2,1)}), bf16[2,192,1536]{2,1,0:T(8,128)(2,1)}) %reduce-scatter.29.cloned.1.call-update) | async-done | bytes 1179664 | tf_op jit(solution)/shard_map/reduce_scatter | solution.py:301
  1590.3 3.0 convert_element_type.304
  1593.3 129.3 %reduce-scatter.23.cloned.1.call-done = bf16[2,192,3,384]{3,1,2,0:T(8,128)(2,1)} async-done(((bf16[2,1536,3,384]{3,1,2,0:T(8,128)(2,1)}), bf16[2,192,3,384]{3,1,2,0:T(8,128)(2,1)}) %reduce-scatter.23.cloned.1.call-update) | async-done | bytes 884752 | tf_op jit(solution)/shard_map/reduce_scatter | solution.py:292
  1725.1 229.4 %reduce-scatter.21.cloned.1.call-done = bf16[2,192,6,384]{3,1,2,0:T(8,128)(2,1)} async-done(((bf16[2,1536,6,384]{3,1,2,0:T(8,128)(2,1)}), bf16[2,192,6,384]{3,1,2,0:T(8,128)(2,1)}) %reduce-scatter.21.cloned.1.call-update) | async-done | bytes 1769488 | tf_op jit(solution)/shard_map/reduce_scatter | solution.py:289
  1954.5 3.6 convert_element_type.300
  (412 shorter events, 197.1 us)
Async XLA Ops:
  7.2 202.1 %all-gather.11.cloned.1.call-start = ((), (), s32[]{:S(2)}) async-start(), calls=%async_computation.10 | async-start | bytes 15925248 | tf_op jit(solution)/shard_map/all_gather | solution.py:89
  10.8 308.3 %all-gather.15.cloned.1.call-start = ((), (), s32[]{:S(2)}) async-start(), calls=%async_computation.12 | async-start | bytes 7962624 | tf_op jit(solution)/shard_map/all_gather | solution.py:90
  13.2 342.9 %all-gather.13.cloned.1.call-start = ((), (), s32[]{:S(2)}) async-start(), calls=%async_computation.11 | async-start | bytes 3932160 | tf_op jit(solution)/shard_map/all_gather | solution.py:26
  13.4 209.1 %copy-start.40 = (f32[256]{0:T(256)}, f32[256]{0:T(256)S(1)}, u32[]{:S(2)}) copy-start(f32[256]{0:T(256)S(1)} %broadcast_multiply_fusion.3) | copy-start | bytes 3076
  13.8 202.5 %copy-start.69 = (f32[256]{0:T(256)}, f32[256]{0:T(256)S(1)}, u32[]{:S(2)}) copy-start(f32[256]{0:T(256)S(1)} %fusion.134) | copy-start | bytes 3076
  13.8 208.7 %copy-start.60 = (f32[256]{0:T(256)}, f32[256]{0:T(256)S(1)}, u32[]{:S(2)}) copy-start(f32[256]{0:T(256)S(1)} %fusion.202) | copy-start | bytes 3076
  14.5 194.8 %copy-start.36 = (f32[1,1536]{1,0:T(1,128)}, f32[1,1536]{1,0:T(1,128)S(1)}, u32[]{:S(2)}) copy-start(f32[1,1536]{1,0:T(1,128)S(1)} %get-tuple-element.213) | copy-start | bytes 18436
  209.3 14.6 copy-start.22
  216.3 8.9 copy-start.1
  222.5 112.0 %copy-start.23 = (f32[1536]{0:T(1024)}, f32[1536]{0:T(1024)S(1)}, u32[]{:S(2)}) copy-start(f32[1536]{0:T(1024)S(1)} %get-tuple-element.178) | copy-start | bytes 18436
  222.5 129.0 %copy-start.25 = (f32[1536]{0:T(1024)}, f32[1536]{0:T(1024)S(1)}, u32[]{:S(2)}) copy-start(f32[1536]{0:T(1024)S(1)} %get-tuple-element.176) | copy-start | bytes 18436
  222.5 129.0 %copy-start.52 = (f32[1536]{0:T(1024)}, f32[1536]{0:T(1024)S(1)}, u32[]{:S(2)}) copy-start(f32[1536]{0:T(1024)S(1)} %get-tuple-element.175) | copy-start | bytes 18436
  222.5 244.5 %copy-start.27 = (f32[1536]{0:T(1024)}, f32[1536]{0:T(1024)S(1)}, u32[]{:S(2)}) copy-start(f32[1536]{0:T(1024)S(1)} %get-tuple-element.173) | copy-start | bytes 18436
  222.5 248.9 %copy-start.32 = (f32[1536]{0:T(1024)}, f32[1536]{0:T(1024)S(1)}, u32[]{:S(2)}) copy-start(f32[1536]{0:T(1024)S(1)} %get-tuple-element.174) | copy-start | bytes 18436
  223.8 198.3 %all-gather.17.cloned.1.call-start = ((), (), s32[]{:S(2)}) async-start(), calls=%async_computation.13 | async-start | bytes 2654208 | tf_op jit(solution)/shard_map/all_gather | solution.py:91
  224.6 239.2 %reduce-scatter.13.cloned.1.call-start = ((), (), s32[]{:S(2)}) async-start(), calls=%async_computation.14 | async-start | bytes 3932160 | tf_op jit(solution)/shard_map/reduce_scatter | solution.py:30
  225.4 126.1 %copy-start.45 = (f32[154]{0:T(256)}, f32[154]{0:T(256)S(1)}, u32[]{:S(2)}) copy-start(f32[154]{0:T(256)S(1)} %broadcast_multiply_fusion.1) | copy-start | bytes 1852
  225.7 108.8 %copy-start.67 = (f32[154]{0:T(256)}, f32[154]{0:T(256)S(1)}, u32[]{:S(2)}) copy-start(f32[154]{0:T(256)S(1)} %fusion.174) | copy-start | bytes 1852
  225.7 125.8 %copy-start.65 = (f32[154]{0:T(256)}, f32[154]{0:T(256)S(1)}, u32[]{:S(2)}) copy-start(f32[154]{0:T(256)S(1)} %fusion.203) | copy-start | bytes 1852
  427.8 177.1 %all-gather.21.cloned.1.call-start = ((), (), s32[]{:S(2)}) async-start(), calls=%async_computation.16 | async-start | bytes 10616832 | tf_op jit(solution)/shard_map/all_gather | solution.py:92
  430.6 203.2 %all-gather.19.cloned.1.call-start = ((), (), s32[]{:S(2)}) async-start(), calls=%async_computation.15 | async-start | bytes 3932160 | tf_op jit(solution)/shard_map/all_gather | solution.py:26
  468.4 306.4 %all-gather.23.cloned.1.call-start = ((), (), s32[]{:S(2)}) async-start(), calls=%async_computation.17 | async-start | bytes 10616832 | tf_op jit(solution)/shard_map/all_gather | solution.py:93
  471.4 332.4 %all-gather.25.cloned.1.call-start = ((), (), s32[]{:S(2)}) async-start(), calls=%async_computation.20 | async-start | bytes 3932160 | tf_op jit(solution)/shard_map/all_gather | solution.py:26
  472.5 367.2 %all-reduce.5.cloned.1.call-start = ((), (), s32[]{:S(2)}) async-start(), calls=%async_computation.19 | async-start | bytes 983040 | tf_op jit(solution)/shard_map/psum | solution.py:36
  475.3 405.0 %reduce-scatter.17.cloned.1.call-start = ((), (), s32[]{:S(2)}) async-start(), calls=%async_computation.21 | async-start | bytes 3932160 | tf_op jit(solution)/shard_map/reduce_scatter | solution.py:30
  826.0 94.8 %reduce-scatter.15.cloned.1.call-start = ((), (), s32[]{:S(2)}) async-start(), calls=%async_computation.18 | async-start | bytes 3932160 | tf_op jit(solution)/shard_map/reduce_scatter | solution.py:30
  836.1 6.2 copy-start.77
  836.2 120.6 %all-reduce.7.cloned.1.call-start = ((), (), s32[]{:S(2)}) async-start(), calls=%async_computation.23 | async-start | bytes 983040 | tf_op jit(solution)/shard_map/psum | solution.py:36
  841.0 117.4 %copy-start.54 = (f32[154]{0:T(256)}, f32[154]{0:T(256)S(1)}, u32[]{:S(2)}) copy-start(f32[154]{0:T(256)S(1)} %broadcast_multiply_fusion) | copy-start | bytes 1852
  842.3 116.0 %copy-start.73 = (f32[154]{0:T(256)}, f32[154]{0:T(256)S(1)}, u32[]{:S(2)}) copy-start(f32[154]{0:T(256)S(1)} %fusion.205) | copy-start | bytes 1852
  842.4 10.2 slice-start
  842.4 10.1 slice-start.1
  846.1 6.5 slice-start.2
  852.6 27.8 %copy-start.28 = (f32[1536]{0:T(1024)S(1)}, f32[1536]{0:T(1024)}, u32[]{:S(2)}) copy-start(f32[1536]{0:T(1024)} %copy-done.27) | copy-start | bytes 18436
  852.6 27.7 %copy-start.44 = (f32[256]{0:T(256)S(1)}, f32[256]{0:T(256)}, u32[]{:S(2)}) copy-start(f32[256]{0:T(256)} %copy-done.43) | copy-start | bytes 3076
  852.6 29.5 %copy-start.72 = (f32[256]{0:T(256)S(1)}, f32[256]{0:T(256)}, u32[]{:S(2)}) copy-start(f32[256]{0:T(256)} %copy-done.71) | copy-start | bytes 3076
  852.6 29.5 %copy-start.64 = (f32[256]{0:T(256)S(1)}, f32[256]{0:T(256)}, u32[]{:S(2)}) copy-start(f32[256]{0:T(256)} %copy-done.63) | copy-start | bytes 3076
  855.1 65.8 %copy-start.33 = (f32[1536]{0:T(1024)S(1)}, f32[1536]{0:T(1024)}, u32[]{:S(2)}) copy-start(f32[1536]{0:T(1024)} %copy-done.32) | copy-start | bytes 18436
  855.1 132.5 %all-gather.27.cloned.1.call-start = ((), (), s32[]{:S(2)}) async-start(), calls=%async_computation.22 | async-start | bytes 3932160 | tf_op jit(solution)/shard_map/all_gather | solution.py:26
  880.3 40.5 %copy-start.9 = (bf16[1,256,1536]{2,1,0:T(8,128)(2,1)S(1)}, bf16[1,256,1536]{2,1,0:T(8,128)(2,1)}, u32[]{:S(2)}) copy-start(bf16[1,256,1536]{2,1,0:T(8,128)(2,1)} %reduce-scatter.17.cloned.1.call-done) | copy-start | bytes 2359300
  927.4 29.4 %copy-start.5 = (bf16[1,154,1536]{2,1,0:T(8,128)(2,1)S(1)}, bf16[1,154,1536]{2,1,0:T(8,128)(2,1)}, u32[]{:S(2)}) copy-start(bf16[1,154,1536]{2,1,0:T(8,128)(2,1)} %all-reduce.5.cloned.1.call-done) | copy-start | bytes 1419268
  927.5 193.0 %reduce-scatter.19.cloned.1.call-start = ((), (), s32[]{:S(2)}) async-start(), calls=%async_computation.24 | async-start | bytes 3932160 | tf_op jit(solution)/shard_map/reduce_scatter | solution.py:30
  927.9 32.7 %copy-start.30 = (f32[1536]{0:T(1024)S(1)}, f32[1536]{0:T(1024)}, u32[]{:S(2)}) copy-start(f32[1536]{0:T(1024)} %get-tuple-element.170) | copy-start | bytes 18436
  1082.4 7.2 copy-start.59
  1082.4 110.7 %all-reduce.9.cloned.1.call-start = ((), (), s32[]{:S(2)}) async-start(), calls=%async_computation.31 | async-start | bytes 1966080 | tf_op jit(solution)/shard_map/psum | solution.py:36
  1096.7 25.1 %copy-start.24 = (f32[1536]{0:T(1024)S(1)}, f32[1536]{0:T(1024)}, u32[]{:S(2)}) copy-start(f32[1536]{0:T(1024)} %copy-done.23) | copy-start | bytes 18436
  1096.7 25.1 %copy-start.41 = (f32[256]{0:T(256)S(1)}, f32[256]{0:T(256)}, u32[]{:S(2)}) copy-start(f32[256]{0:T(256)} %copy-done.40) | copy-start | bytes 3076
  1096.7 26.7 %copy-start.70 = (f32[256]{0:T(256)S(1)}, f32[256]{0:T(256)}, u32[]{:S(2)}) copy-start(f32[256]{0:T(256)} %copy-done.69) | copy-start | bytes 3076
  1096.7 26.7 %copy-start.61 = (f32[256]{0:T(256)S(1)}, f32[256]{0:T(256)}, u32[]{:S(2)}) copy-start(f32[256]{0:T(256)} %copy-done.60) | copy-start | bytes 3076
  1096.7 102.5 %reduce-scatter.31.cloned.1.call-start = ((), (), s32[]{:S(2)}) async-start(), calls=%async_computation.30 | async-start | bytes 491520
  1101.3 24.6 %copy-start.56 = (bf16[1,1,1536]{2,1,0:T(2,128)(2,1)S(1)}, bf16[1,1,1536]{2,1,0:T(2,128)(2,1)}, u32[]{:S(2)}) copy-start(bf16[1,1,1536]{2,1,0:T(2,128)(2,1)} %stack.116) | copy-start | bytes 9220
  1129.3 128.2 %reduce-scatter.25.cloned.1.call-start = ((), (), s32[]{:S(2)}) async-start(), calls=%async_computation.27 | async-start | bytes 2654208 | tf_op jit(solution)/shard_map/reduce_scatter | solution.py:295
  1132.7 291.3 %reduce-scatter.27.cloned.1.call-start = ((), (), s32[]{:S(2)}) async-start(), calls=%async_computation.28 | async-start | bytes 10616832 | tf_op jit(solution)/shard_map/reduce_scatter | solution.py:298
  1151.8 438.5 %reduce-scatter.29.cloned.1.call-start = ((), (), s32[]{:S(2)}) async-start(), calls=%async_computation.29 | async-start | bytes 10616832 | tf_op jit(solution)/shard_map/reduce_scatter | solution.py:301
  1177.9 544.7 %reduce-scatter.23.cloned.1.call-start = ((), (), s32[]{:S(2)}) async-start(), calls=%async_computation.26 | async-start | bytes 7962624 | tf_op jit(solution)/shard_map/reduce_scatter | solution.py:292
  1192.3 762.2 %reduce-scatter.21.cloned.1.call-start = ((), (), s32[]{:S(2)}) async-start(), calls=%async_computation.25 | async-start | bytes 15925248 | tf_op jit(solution)/shard_map/reduce_scatter | solution.py:289
  1209.4 50.0 %copy-start.79 = (f32[256]{0:T(256)S(1)}, f32[256]{0:T(256)}, u32[]{:S(2)}) copy-start(f32[256]{0:T(256)} %get-tuple-element.161) | copy-start | bytes 3076
  1209.4 50.0 %copy-start.42 = (f32[256]{0:T(256)S(1)}, f32[256]{0:T(256)}, u32[]{:S(2)}) copy-start(f32[256]{0:T(256)} %copy-done.40) | copy-start | bytes 3076
  1209.4 50.0 %copy-start.62 = (f32[256]{0:T(256)S(1)}, f32[256]{0:T(256)}, u32[]{:S(2)}) copy-start(f32[256]{0:T(256)} %copy-done.60) | copy-start | bytes 3076
  1209.4 50.0 %copy-start.76 = (f32[256]{0:T(256)S(1)}, f32[256]{0:T(256)}, u32[]{:S(2)}) copy-start(f32[256]{0:T(256)} %copy-done.75) | copy-start | bytes 3076
  1209.4 50.0 %copy-start.7 = (f32[1,256,1536]{2,1,0:T(8,128)S(1)}, f32[1,256,1536]{2,1,0:T(8,128)}, u32[]{:S(2)}) copy-start(f32[1,256,1536]{2,1,0:T(8,128)} %copy-done.6) | copy-start | bytes 4718596
  1209.4 50.0 %copy-start.8 = (bf16[1,256,1536]{2,1,0:T(8,128)(2,1)S(1)}, bf16[1,256,1536]{2,1,0:T(8,128)(2,1)}, u32[]{:S(2)}) copy-start(bf16[1,256,1536]{2,1,0:T(8,128)(2,1)} %reduce-scatter.19.cloned.1.call-done) | copy-start | bytes 2359300
  1261.1 13.7 copy-start.35
  1261.2 13.7 copy-start.37
  (58 other events, 147.6 us)
Sparse Core Ops, SparseCore 0:
  10.9 198.3 all-gather.10
  212.1 106.9 all-gather.14
  321.2 26.7 all-gather.12
  350.6 52.0 all-gather.16
  427.9 35.9 reduce-scatter.12
  466.7 138.0 all-gather.20
  607.0 26.6 all-gather.18
  636.8 138.0 all-gather.22
  777.1 26.6 all-gather.24
  806.7 32.9 all-reduce.4
  842.2 38.0 reduce-scatter.16
  882.9 37.9 reduce-scatter.14
  923.7 33.0 all-reduce.6
  958.9 28.6 all-gather.26
  1082.5 37.9 reduce-scatter.18
  1123.9 35.7 all-reduce.8
  1162.7 21.1 reduce-scatter.30
  1188.3 69.2 reduce-scatter.24
  1261.6 162.3 reduce-scatter.26
  1427.8 162.4 reduce-scatter.28
  1594.4 128.1 reduce-scatter.22
  1726.2 228.2 reduce-scatter.20
where the time goes:
time: 1970 us
  waiting for transfers between devices  1490 us (76%)
  matrix products  246 us (12%)
  other arithmetic  115 us (6%)
  local copies, waits for them, and re-layouts  85.7 us (4%)
    reduce_scatter x1, waiting for transfers between devices, local(): lax.psum_scatter(ada_grad.astype(jnp.bfloat16), 'dp', scatter_dimension=1...  229 us
    all_gather x1, waiting for transfers between devices, local(): lax.all_gather(w_ada.astype(LOW_TYPE), 'dp', axis=1, tiled=True)  195 us
    reduce_scatter x1, waiting for transfers between devices, local(): lax.psum_scatter(down_grad.astype(jnp.bfloat16), 'dp', scatter_dimension=...  163 us
    reduce_scatter x1, waiting for transfers between devices, local(): lax.psum_scatter(up_grad.astype(jnp.bfloat16), 'dp', scatter_dimension=1,...  148 us
    all_gather x1, waiting for transfers between devices, local(): lax.all_gather(w_down.astype(LOW_TYPE), 'dp', axis=1, tiled=True)  131 us
    all_gather x1, waiting for transfers between devices, local(): lax.all_gather(w_up.astype(LOW_TYPE), 'dp', axis=1, tiled=True)  129 us
    reduce_scatter x1, waiting for transfers between devices, local(): lax.psum_scatter(qkv_grad.astype(jnp.bfloat16), 'dp', scatter_dimension=1...  129 us
    reduce_scatter x4, waiting for transfers between devices, scatter_rows(): lax.psum_scatter(partial_rows.astype(jnp.bfloat16), 'tensor', scatter_dim...  113 us
  transfers between devices with their start and end apart: 22, of which 18 were waited for; matrix products, arithmetic and copies ran while one was open for 16% of the time, Pallas kernels for 0%

commit v1 on v0

v1 whole, which is shorter than its diff:
```python
import jax
import jax.numpy as jnp
from jax import lax
from jax.sharding import PartitionSpec as P

HEAD_DIM = 64
EPS = 1e-06
LOW = jnp.bfloat16
WIDE = jnp.float32
TEXT_TILE = 16


def dot(left, right, dims):
    return lax.dot_general(left, right, (dims, ((), ())), preferred_element_type=WIDE)


def layer_norm(values):
    average = jnp.mean(values, axis=-1, keepdims=True)
    centred = values - average
    spread = jnp.mean(centred * centred, axis=-1, keepdims=True)
    return centred * lax.rsqrt(spread + EPS)


def gelu_tanh(values):
    return jax.nn.gelu(values, approximate=True)


def ring_to_dp(place, size):
    return jnp.where(place < size // 2, 2 * place, 2 * (size - 1 - place) + 1)


def dp_to_ring(index, size):
    return jnp.where(index % 2 == 0, index // 2, size - 1 - index // 2)


def ring_pairs(size, step):
    order = list(range(0, size, 2)) + list(range(size - 1, 0, -2))
    return [(order[p], order[(p + step) % size]) for p in range(size)]


def gather_dp(block, size):
    rows = block.shape[0]
    if size != 8:
        return lax.all_gather(block, "dp", axis=0, tiled=True)
    place = dp_to_ring(lax.axis_index("dp"), size)
    full = jnp.zeros((size * rows,) + block.shape[1:], block.dtype)

    def put(full, piece, at, offset):
        start = ring_to_dp(at % size, size) * rows + offset
        return lax.dynamic_update_slice_in_dim(full, piece, start, 0)

    full = put(full, block, place, 0)
    up, down = block, block
    for step in range(1, size // 2):
        up = lax.ppermute(up, "dp", ring_pairs(size, 1))
        down = lax.ppermute(down, "dp", ring_pairs(size, -1))
        full = put(full, up, place - step + size, 0)
        full = put(full, down, place + step, 0)
    half = rows // 2
    up = lax.ppermute(up[:half], "dp", ring_pairs(size, 1))
    down = lax.ppermute(down[half:], "dp", ring_pairs(size, -1))
    full = put(full, up, place + size // 2, 0)
    full = put(full, down, place + size // 2, half)
    return full


def scatter_dp(grad, size):
    rows = grad.shape[0] // size
    if size != 8:
        return lax.psum_scatter(grad, "dp", scatter_dimension=0, tiled=True).astype(WIDE)
    place = dp_to_ring(lax.axis_index("dp"), size)
    half = rows // 2

    def own(at, offset):
        start = ring_to_dp(at % size, size) * rows + offset
        return lax.dynamic_slice_in_dim(grad, start, half, 0)

    parts = []
    for direction, offset in ((1, 0), (-1, half)):
        moving = own(place - direction + size, offset)
        for step in range(1, size):
            moving = lax.ppermute(moving, "dp", ring_pairs(size, direction))
            mine = own(place - direction * (step + 1) + 2 * size, offset)
            moving = moving.astype(WIDE) + mine.astype(WIDE)
            if step < size - 1:
                moving = moving.astype(LOW)
        parts.append(moving)
    return jnp.concatenate(parts, axis=0)


CORE = [(i, i ^ 1) for i in range(4)]
CHIP = [(i, i ^ 2) for i in range(4)]


def gather_rows(own):
    near = lax.ppermute(own, "tensor", CORE)
    far = lax.ppermute(own, "tensor", CHIP)
    last = lax.ppermute(far, "tensor", CORE)
    return [own, near, far, last]


def scatter_rows(parts):
    low = [part.astype(LOW) for part in parts]
    sent = lax.ppermute(jnp.concatenate([low[1], low[3]]), "tensor", CORE)
    rows = parts[0].shape[0]
    far = (low[2].astype(WIDE) + sent[rows:].astype(WIDE)).astype(LOW)
    far = lax.ppermute(far, "tensor", CHIP)
    return low[0].astype(WIDE) + sent[:rows].astype(WIDE) + far.astype(WIDE)


def gather_streams(own):
    split = own[0].shape[0]
    blocks = gather_rows(jnp.concatenate(own, axis=0))
    return [
        jnp.concatenate([block[:split] for block in blocks], axis=0),
        jnp.concatenate([block[split:] for block in blocks], axis=0),
    ]


def scatter_streams(partials):
    split = partials[0].shape[0] // 4
    text = partials[1].shape[0] // 4
    parts = [
        jnp.concatenate(
            [partials[0][b * split : (b + 1) * split], partials[1][b * text : (b + 1) * text]]
        )
        for b in range(4)
    ]
    own = scatter_rows(parts)
    return [own[:split], own[split:]]


def to_heads(rows, heads):
    return rows.reshape(rows.shape[0], heads, HEAD_DIM).transpose(1, 0, 2)


def from_heads(blocks):
    return blocks.transpose(1, 0, 2).reshape(blocks.shape[1], -1)


def attend(block, bias):
    queries, keys, values = block
    scores = dot(queries, keys, ((1,), (1,))) * HEAD_DIM ** (-0.5) + bias
    row_max = jnp.max(scores, axis=-1, keepdims=True)
    shifted = jnp.exp(scores - row_max)
    row_sum = jnp.sum(shifted, axis=-1, keepdims=True)
    output = dot((shifted / row_sum).astype(LOW), values, ((1,), (0,)))
    return output.astype(LOW), row_max[:, 0] + jnp.log(row_sum[:, 0])


def attend_back(block, bias):
    queries, keys, values, log_total, grad_output = block
    scaling = HEAD_DIM ** (-0.5)
    scores = dot(queries, keys, ((1,), (1,))) * scaling + bias
    probs = jnp.exp(scores - log_total[:, None])
    grad_probs = dot(grad_output, values, ((1,), (1,)))
    row_dot = jnp.sum(grad_probs * probs, axis=-1, keepdims=True)
    grad_scores = (probs * (grad_probs - row_dot)).astype(LOW)
    grad_queries = (dot(grad_scores, keys, ((1,), (0,))) * scaling).astype(LOW)
    grad_keys = (dot(grad_scores, queries, ((0,), (0,))) * scaling).astype(LOW)
    grad_values = dot(probs.astype(LOW), grad_output, ((0,), (0,))).astype(LOW)
    return grad_queries, grad_keys, grad_values


def local(size, image, text, cond, w_ada, w_qkv, w_out, w_up, w_down, grad_image, grad_text):
    index = lax.axis_index("tensor")
    dp_index = lax.axis_index("dp")
    seqs = size
    image_rows, width = image.shape[1], image.shape[2]
    text_tokens = text.shape[1]
    text_rows = -(-text_tokens // (4 * TEXT_TILE)) * TEXT_TILE
    text_pad = 4 * text_rows - text_tokens
    width_here = w_ada.shape[-1]
    ada_rows = w_ada.shape[1]
    heads_here = w_qkv.shape[-1] // HEAD_DIM
    rows_of = [image_rows, text_rows]

    def gathered(weight, stream):
        block = weight[stream].astype(LOW)
        return gather_dp(block.reshape(block.shape[0], -1), size)

    qkv_full = [gathered(w_qkv, stream) for stream in range(2)]
    out_full = [gathered(w_out, stream) for stream in range(2)]
    up_full, down_full = [None, None], [None, None]
    for stream in range(2):
        up_full[stream] = gathered(w_up, stream)
        down_full[stream] = gathered(w_down, stream)

    cond_low = jax.nn.silu(cond).astype(LOW)
    cond_rows = lax.all_to_all(
        cond_low.reshape(seqs, ada_rows), "dp", split_axis=0, concat_axis=0, tiled=True
    )
    ada_low = w_ada.astype(LOW)
    mod_parts = jnp.einsum("nd,sdkf->nskf", cond_rows, ada_low, preferred_element_type=WIDE)
    mod_parts = lax.all_to_all(mod_parts, "dp", split_axis=0, concat_axis=0, tiled=True)
    modulation = lax.all_gather(jnp.sum(mod_parts, axis=0), "tensor", axis=2, tiled=True)

    def mod_row(stream, which):
        return modulation[stream, which][None, :]

    def own_text(rows):
        padded = jnp.pad(rows, ((0, text_pad), (0, 0)))
        return lax.dynamic_slice_in_dim(padded, index * text_rows, text_rows, 0)

    streams = [image[0].astype(WIDE), own_text(text[0]).astype(WIDE)]
    cotangent = [grad_image[0].astype(WIDE), own_text(grad_text[0]).astype(WIDE)]
    normed_in = [layer_norm(residual) for residual in streams]
    first_in = [
        (normed_in[s] * (1.0 + mod_row(s, 1)) + mod_row(s, 0)).astype(LOW) for s in range(2)
    ]
    attn_rows = gather_streams(first_in)
    joint = jnp.concatenate(
        [dot(attn_rows[s], qkv_full[s], ((1,), (0,))).astype(LOW) for s in range(2)], axis=0
    )
    places = jnp.arange(4 * text_rows)
    token = ((places // text_rows) ^ index) * text_rows + places % text_rows
    bias = jnp.concatenate(
        [jnp.zeros((4 * image_rows,), WIDE), jnp.where(token < text_tokens, 0.0, -1e30)]
    )[None, :]
    queries, keys, values = [to_heads(part, heads_here) for part in jnp.split(joint, 3, axis=1)]
    attn_out, log_total = lax.map(lambda block: attend(block, bias), (queries, keys, values))
    mixed = from_heads(attn_out)
    split_at = 4 * image_rows
    mixed_rows = [mixed[:split_at], mixed[split_at:]]
    branches = scatter_streams([dot(mixed_rows[s], out_full[s], ((1,), (0,))) for s in range(2)])
    middle = [streams[s] + mod_row(s, 2) * branches[s] for s in range(2)]
    normed_mid = [layer_norm(residual) for residual in middle]
    second_in = [
        (normed_mid[s] * (1.0 + mod_row(s, 4)) + mod_row(s, 3)).astype(LOW) for s in range(2)
    ]
    ffn_grad = [(mod_row(s, 5) * cotangent[s]).astype(LOW) for s in range(2)]
    ffn_rows = gather_streams(ffn_grad)
    mlp_rows = gather_streams(second_in)
    ffn_parts, up_grad, down_grad, second_parts = [], [], [], []
    for s in range(2):
        pre_act = dot(mlp_rows[s], up_full[s], ((1,), (0,)))
        hidden = gelu_tanh(pre_act).astype(LOW)
        ffn_parts.append(dot(hidden, down_full[s], ((1,), (0,))))
        hidden_grad = dot(ffn_rows[s], down_full[s], ((1,), (1,)))
        pre_grad = jax.vjp(gelu_tanh, pre_act)[1](hidden_grad)[0].astype(LOW)
        second_parts.append(dot(pre_grad, up_full[s], ((1,), (1,))))
        down_grad.append(dot(hidden, ffn_rows[s], ((0,), (0,))).astype(LOW))
        up_grad.append(dot(mlp_rows[s], pre_grad, ((0,), (0,))).astype(LOW))
    down_sum, up_sum = [None, None], [None, None]
    for s in range(2):
        down_sum[s] = scatter_dp(down_grad[s], size)
        up_sum[s] = scatter_dp(up_grad[s], size)
    second_grad = scatter_streams(second_parts)
    ffn = scatter_streams(ffn_parts)
    results = [(middle[s] + mod_row(s, 5) * ffn[s]).astype(LOW) for s in range(2)]
    middle_grad = [
        cotangent[s]
        + jax.vjp(layer_norm, middle[s])[1](second_grad[s] * (1.0 + mod_row(s, 4)))[0]
        for s in range(2)
    ]
    branch_grad = [(mod_row(s, 2) * middle_grad[s]).astype(LOW) for s in range(2)]
    branch_rows = gather_streams(branch_grad)
    out_grad = [dot(mixed_rows[s], branch_rows[s], ((0,), (0,))).astype(LOW) for s in range(2)]
    out_sum = [scatter_dp(grad, size) for grad in out_grad]
    mixed_grad = jnp.concatenate(
        [dot(branch_rows[s], out_full[s], ((1,), (1,))).astype(LOW) for s in range(2)], axis=0
    )
    grads = lax.map(
        lambda block: attend_back(block, bias),
        (queries, keys, values, log_total, to_heads(mixed_grad, heads_here)),
    )
    joint_grad = jnp.concatenate([from_heads(grad) for grad in grads], axis=1)
    joint_rows = [joint_grad[:split_at], joint_grad[split_at:]]
    qkv_grad = [dot(attn_rows[s], joint_rows[s], ((0,), (0,))).astype(LOW) for s in range(2)]
    qkv_sum = [scatter_dp(grad, size) for grad in qkv_grad]
    first_grad = scatter_streams([dot(joint_rows[s], qkv_full[s], ((1,), (1,))) for s in range(2)])
    input_grad = [
        middle_grad[s]
        + jax.vjp(layer_norm, streams[s])[1](first_grad[s] * (1.0 + mod_row(s, 1)))[0]
        for s in range(2)
    ]
    mod_terms = jnp.stack(
        [
            jnp.stack(
                [
                    jnp.sum(first_grad[s], axis=0),
                    jnp.sum(first_grad[s] * normed_in[s], axis=0),
                    jnp.sum(middle_grad[s] * branches[s], axis=0),
                    jnp.sum(second_grad[s], axis=0),
                    jnp.sum(second_grad[s] * normed_mid[s], axis=0),
                    jnp.sum(cotangent[s] * ffn[s], axis=0),
                ]
            )
            for s in range(2)
        ]
    )
    mod_split = mod_terms.reshape(2, 6, 4, width_here).transpose(2, 0, 1, 3)
    mod_sum = jnp.sum(
        lax.all_to_all(mod_split, "tensor", split_axis=0, concat_axis=0, tiled=True), axis=0
    )
    shift_grad = mod_sum[:, 3]
    mod_grad = lax.all_gather(mod_sum.astype(LOW), "dp", axis=0, tiled=False)
    ada_grad = jnp.einsum("nd,nskf->sdkf", cond_rows, mod_grad, preferred_element_type=WIDE)
    act_parts = jnp.einsum("nskf,sdkf->nd", mod_grad, ada_low, preferred_element_type=WIDE)
    act_parts = lax.all_to_all(act_parts, "dp", split_axis=0, concat_axis=0, tiled=True)
    act_grad = lax.psum(act_parts.reshape(1, width), "tensor")
    cond_grad = jax.vjp(jax.nn.silu, cond)[1](act_grad)[0]

    def whole_text(rows):
        blocks = lax.all_gather(rows, "tensor", axis=0, tiled=True)
        return blocks[:text_tokens][None]

    def shard(sums, like):
        return jnp.stack(sums).reshape(like.shape)

    return (
        results[0][None],
        whole_text(results[1]),
        input_grad[0][None],
        whole_text(input_grad[1]),
        cond_grad,
        shift_grad[None],
        ada_grad,
        shard(qkv_sum, w_qkv),
        shard(out_sum, w_out),
        shard(up_sum, w_up),
        shard(down_sum, w_down),
    )


def solution(mesh):
    size = mesh.shape["dp"]

    def step(*args):
        return local(size, *args)

    return jax.shard_map(
        step,
        mesh=mesh,
        in_specs=(
            P("dp", "tensor", None),
            P("dp", None, None),
            P("dp", None),
            P(None, "dp", None, "tensor"),
            P(None, "dp", None, "tensor"),
            P(None, ("tensor", "dp"), None),
            P(None, "dp", "tensor"),
            P(None, ("tensor", "dp"), None),
            P("dp", "tensor", None),
            P("dp", None, None),
        ),
        out_specs=(
            P("dp", "tensor", None),
            P("dp", None, None),
            P("dp", "tensor", None),
            P("dp", None, None),
            P("dp", None),
            P("dp", None, "tensor"),
            P(None, "dp", None, "tensor"),
            P(None, "dp", None, "tensor"),
            P(None, ("tensor", "dp"), None),
            P(None, "dp", "tensor"),
            P(None, ("tensor", "dp"), None),
        ),
        check_vma=False,
    )
```

time: 1970 us -> 1170 us (0.59)
  waiting for transfers between devices: 1490 us -> 400 us
  starting transfers between devices: 2.87 us -> 241 us
  local copies, waits for them, and re-layouts: 85.7 us -> 173 us
  other arithmetic: 115 us -> 66 us
  blocking collectives: 11.6 us -> 49.2 us
  matrix products: 246 us -> 209 us
    reduce_scatter x9 -> x0, waiting for transfers between devices: 829 us -> none  [the longest x1 229 us: local(): lax.psum_scatter(ada_grad.astype(jnp.bfloat16), 'dp', scatter_dimension=1...]
    all_gather x9 -> x1, waiting for transfers between devices: 630 us -> 0.01 us  [whole_text(): blocks = lax.all_gather(rows, 'tensor', axis=0, tiled=True)]
    ppermute x0 -> x196, waiting for transfers between devices: none -> 395 us  [the longest x112 172 us: scatter_dp(): moving = lax.ppermute(moving, 'dp', ring_pairs(size, direction))]
    ppermute x0 -> x196, starting transfers between devices: none -> 224 us  [the longest x112 114 us: scatter_dp(): moving = lax.ppermute(moving, 'dp', ring_pairs(size, direction))]
    dynamic_update_slice x6 -> x78, local copies, waits for them, and re-layouts: 8.5 us -> 69.5 us  [the longest x72 60.9 us: put(): return lax.dynamic_update_slice_in_dim(full, piece, start, 0)]
    all_gather x1 -> x3, blocking collectives: 5.47 us -> 43.3 us  [the longest x1 30.5 us: local(): mod_grad = lax.all_gather(mod_sum.astype(LOW), 'dp', axis=0, tiled=False)]
    dot_general x68 -> x69, matrix products: 246 us -> 209 us  [the longest x66 203 us: dot(): lax.dot_general(left, right, (dims, ((), ())), preferred_element_type=WIDE)]
    another operation x15 -> x28, local copies, waits for them, and re-layouts: 2.1 us -> 32.3 us  [the longest x14 2.08 us: local(): jnp.stack([jnp.sum(first_grad[stream], axis=1), jnp.sum(first_grad[stream...]
  transfers between devices with their start and end apart: 22 -> 201, of which waited for: 18 -> 107; matrix products, arithmetic and copies ran while one was open for 16% -> 20% of each run, Pallas kernels for 0% -> 0%
where the time goes in v1:
time: 1170 us; the launch traced here: 1160 us
  waiting for transfers between devices  400 us (34%)
  starting transfers between devices  241 us (21%)
  matrix products  209 us (18%)
  local copies, waits for them, and re-layouts  173 us (15%)
  other arithmetic  66 us (6%)
  blocking collectives  49.2 us (4%)
  between operations  18 us (2%)
    dot_general x66, matrix products, dot(): lax.dot_general(left, right, (dims, ((), ())), preferred_element_type=WIDE)  203 us
    ppermute x112, waiting for transfers between devices, scatter_dp(): moving = lax.ppermute(moving, 'dp', ring_pairs(size, direction))  172 us
    ppermute x112, starting transfers between devices, scatter_dp(): moving = lax.ppermute(moving, 'dp', ring_pairs(size, direction))  114 us
    ppermute x24, waiting for transfers between devices, gather_dp(): up = lax.ppermute(up, 'dp', ring_pairs(size, 1))  67.2 us
    dynamic_update_slice x72, local copies, waits for them, and re-layouts, put(): return lax.dynamic_update_slice_in_dim(full, piece, start, 0)  60.9 us
    ppermute x24, waiting for transfers between devices, gather_dp(): down = lax.ppermute(down, 'dp', ring_pairs(size, -1))  50.7 us
    ppermute x4, waiting for transfers between devices, scatter_rows(): far = lax.ppermute(far, 'tensor', CHIP)  44.8 us
    ppermute x24, starting transfers between devices, gather_dp(): up = lax.ppermute(up, 'dp', ring_pairs(size, 1))  44.7 us
  transfers between devices with their start and end apart: 201, of which 107 were waited for; matrix products, arithmetic and copies ran while one was open for 20% of the time, Pallas kernels for 0%

profile of v1, /device:TPU:0, one launch (start us, length us, event | category | flops | bytes accessed | tf_op | source)
XLA Modules:
  0.0 1156.8 jit_solution(12941106298095090087)
XLA Ops:
  18.0 4.8 all-to-all-start
  69.1 4.2 collective-permute-done.28
  80.5 5.3 all_gather.13
  117.3 6.0 collective-permute-done.12
  125.6 7.2 collective-permute-done.4
  140.1 5.5 collective-permute-done.32
  181.6 4.6 collective-permute-done.48
  192.2 6.5 collective-permute-done.40
  210.4 7.2 collective-permute-done.5
  247.1 5.4 collective-permute-done.7
  254.2 11.4 collective-permute-done.8
  268.8 4.0 collective-permute-done.17
  281.2 5.0 collective-permute-done.18
  288.5 5.9 collective-permute-done.10
  300.3 8.8 convolution_convert_fusion.9
  320.7 39.6 %while.26 = (s32[]{:T(128)}, bf16[6,1216,64]{1,2,0:T(8,128)(2,1)S(1)}, f32[6,1216]{1,0:T(8,128)}, bf16[6,1216,64]{2,1,0:T(8,128)(2,1)}, bf16[6,1216,64]{2,1,0:T(...) while((s32[]{:T(128)}, ...), condition=%wide.region_8.9_spmd, body=%wide.region_5.8_spmd.sunk | while | flops 390441792 | bytes 19234676 | solution.py:221
  371.5 10.6 collective-permute-done.68
  384.1 10.6 collective-permute-done.60
  394.7 10.5 collective-permute-start.44
  426.8 16.7 %collective-permute-done.36 = bf16[304,1536]{1,0:T(8,128)(2,1)S(1)} collective-permute-done((bf16[304,1536]{1,0:T(8,128)(2,1)S(1)}, bf16[304,1536]{1,0:T(8,128)(2,1)S(1)}, u32[]{:S(2)}, u32[]{:S(2)}) %collective-permute-start.36) | collective-permute-done | bytes 933920 | tf_op jit(solution)/shard_map/ppermute | solution.py:107
  457.4 9.3 collective-permute-done.38
  468.7 7.5 collective-permute-done.47
  486.4 4.9 convolution_convert_fusion.14
  495.8 7.4 fusion.94
  505.9 7.2 convolution_convert_fusion.7
  513.0 13.3 %fusion.60 = bf16[1024,1536]{1,0:T(8,128)(2,1)} fusion(f32[1024,1536]{1,0:T(8,128)} %copy-done.129, bf16[1536,1536]{1,0:T(8,128)(2,1)S(1)} %constant_dynamic-update-slice_fusion.18, bf16[256,1536]{1,0:T(8,128)(2,1)S(1)} %slice.593, bf16[256,1536]{1,0:T(8,128)(2,1)S(1)} %copy-done.49, bf16[256,1536]{1,0:T(8,128)(2,1)S(1)} %copy-done.50, ...), kind=kOutput, calls=%fused_computation.72 | convolution fusion | flops 4875878400 | bytes 17301504 | tf_op jit(solution)/shard_map/dot_general | solution.py:14
  526.4 8.8 convolution_convert_fusion
  535.2 7.8 convolution_convert_fusion.6
  543.1 5.6 convolution_convert_fusion.1
  554.4 7.5 collective-permute-done.154
  564.0 4.1 collective-permute-done.140
  570.4 4.1 collective-permute-done.182
  576.7 4.1 collective-permute-done.168
  583.0 4.1 collective-permute-done.155
  589.3 4.1 collective-permute-done.141
  595.7 4.1 collective-permute-done.183
  602.0 4.1 collective-permute-done.169
  608.3 4.1 collective-permute-done.156
  614.6 4.1 collective-permute-done.142
  620.9 4.1 collective-permute-done.184
  627.3 4.1 collective-permute-done.170
  633.6 4.1 collective-permute-done.157
  639.9 4.1 collective-permute-done.143
  646.2 4.1 collective-permute-done.185
  652.5 4.1 collective-permute-done.171
  658.9 4.1 collective-permute-done.158
  665.2 4.1 collective-permute-done.144
  671.5 4.1 collective-permute-done.186
  677.8 4.1 collective-permute-done.172
  684.1 4.1 collective-permute-done.159
  690.4 4.1 collective-permute-done.145
  696.8 4.1 collective-permute-done.187
  703.3 3.9 collective-permute-done.173
  733.1 28.1 %collective-permute-done.78 = bf16[304,1536]{1,0:T(8,128)(2,1)S(1)} collective-permute-done((bf16[304,1536]{1,0:T(8,128)(2,1)S(1)}, bf16[304,1536]{1,0:T(8,128)(2,1)S(1)}, u32[]{:S(2)}, u32[]{:S(2)}) %collective-permute-start.78) | collective-permute-done | bytes 933920 | tf_op jit(solution)/shard_map/ppermute | solution.py:107
  768.6 13.5 %collective-permute-done.80 = bf16[304,1536]{1,0:T(8,128)(2,1)} collective-permute-done((bf16[304,1536]{1,0:T(8,128)(2,1)}, bf16[304,1536]{1,0:T(8,128)(2,1)}, u32[]{:S(2)}, u32[]{:S(2)}) %collective-permute-start.80) | collective-permute-done | bytes 933920 | tf_op jit(solution)/shard_map/ppermute | solution.py:97
  807.4 82.5 %while.27 = (s32[]{:T(128)}, bf16[6,1216,64]{1,2,0:T(8,128)(2,1)}, bf16[6,1216,64]{1,2,0:T(8,128)(2,1)}, bf16[6,1216,64]{1,2,0:T(8,128)(2,1)}, bf16[6,1216,64]{2...) while((s32[]{:T(128)}, bf16[6,1216,64]{1,2,0:T(8,128)(2,1)}, ...), condition=%wide.region_19.20_spmd, body=%wide.region_17.19_spmd.sunk | while | flops 960035648 | bytes 46779524 | solution.py:263
  897.1 6.7 convolution_convert_fusion.10
  903.9 4.7 convolution_convert_fusion.2
  916.9 4.7 collective-permute-done.126
  1055.2 7.5 all_gather.14
  1086.8 3.9 all-to-all-start.2
  1097.2 30.5 %all-gather = bf16[16,6,384]{2,1,0:T(8,128)(2,1)S(1)} all-gather(bf16[2,6,384]{2,1,0:T(8,128)(2,1)S(1)} %copy.131), channel_id=2, replica_groups=mesh['dp'=8,'tensor'=4] {'dp'}, dimensions={0}, use_global_device_ids=true | all-gather | bytes 82944 | tf_op jit(solution)/shard_map/all_gather | solution.py:297
  1129.0 4.5 all-to-all-start.3
  1140.1 5.8 psum.7
  (1073 shorter events, 714.6 us)
Async XLA Ops:
  10.2 161.7 %collective-permute-start.64 = (bf16[192,1536]{1,0:T(8,128)(2,1)}, bf16[192,1536]{1,0:T(8,128)(2,1)}, u32[]{:S(2)}, u32[]{:S(2)}) collective-permute-start(bf16[192,1536]{1,0:T(8,128)(2,1)} %get-tuple-element.488), channel_id=1, source_target_pairs={{0,8},{8,16},{16,24},{24,28},{28,20},{20,12},{12,4},{4,0},{1,9},{9... | collective-permute-start | bytes 1769480 | tf_op jit(solution)/shard_map/ppermute | solution.py:55
  13.2 161.1 %collective-permute-start.65 = (bf16[192,1536]{1,0:T(8,128)(2,1)}, bf16[192,1536]{1,0:T(8,128)(2,1)}, u32[]{:S(2)}, u32[]{:S(2)}) collective-permute-start(bf16[192,1536]{1,0:T(8,128)(2,1)} %get-tuple-element.488), channel_id=1, source_target_pairs={{0,4},{8,0},{16,8},{24,16},{28,24},{20,28},{12,20},{4,12},{1,5},{9... | collective-permute-start | bytes 1769480 | tf_op jit(solution)/shard_map/ppermute | solution.py:56
  14.7 96.8 %collective-permute-start.11 = (bf16[192,1152]{1,0:T(8,128)(2,1)}, bf16[192,1152]{1,0:T(8,128)(2,1)}, u32[]{:S(2)}, u32[]{:S(2)}) collective-permute-start(bf16[192,1152]{1,0:T(8,128)(2,1)} %bitcast.75), channel_id=1, source_target_pairs={{0,8},{8,16},{16,24},{24,28},{28,20},{20,12},{12,4},{4,0},{1,9},{9... | collective-permute-start | bytes 1327112 | tf_op jit(solution)/shard_map/ppermute | solution.py:55
  18.0 35.7 %all-to-all-start = ((bf16[8,1,192]{2,1,0:T(2,128)(2,1)}), bf16[8,1,192]{2,1,0:T(2,128)(2,1)S(1)}, u32[]{:S(2)}, u32[]{:S(2)}) async-start(bf16[8,1,192]{2,1,0:T(2,128)(2,1)} %all_to_all.27), calls=%async_computation | async-start | bytes 16384 | tf_op jit(solution)/shard_map/all_to_all | solution.py:190
  24.1 91.2 %collective-permute-start.3 = (bf16[192,1152]{1,0:T(8,128)(2,1)}, bf16[192,1152]{1,0:T(8,128)(2,1)}, u32[]{:S(2)}, u32[]{:S(2)}) collective-permute-start(bf16[192,1152]{1,0:T(8,128)(2,1)} %bitcast.72), channel_id=1, source_target_pairs={{0,8},{8,16},{16,24},{24,28},{28,20},{20,12},{12,4},{4,0},{1,9},{9... | collective-permute-start | bytes 1327112 | tf_op jit(solution)/shard_map/ppermute | solution.py:55
  26.8 33.8 %collective-permute-start.27 = (bf16[48,1536]{1,0:T(8,128)(2,1)}, bf16[48,1536]{1,0:T(8,128)(2,1)S(1)}, u32[]{:S(2)}, u32[]{:S(2)}) collective-permute-start(bf16[48,1536]{1,0:T(8,128)(2,1)} %get-tuple-element.509), channel_id=1, source_target_pairs={{0,8},{8,16},{16,24},{24,28},{28,20},{20,12},{12,4},{4,0},{1,9},{9... | collective-permute-start | bytes 442376 | tf_op jit(solution)/shard_map/ppermute | solution.py:55
  56.8 23.7 %all-to-all-start.1 = ((f32[8,2,6,384]{3,1,2,0:T(2,128)}), f32[8,2,6,384]{3,1,2,0:T(2,128)S(1)}, u32[]{:S(2)}, u32[]{:S(2)}) async-start(f32[8,2,6,384]{3,1,2,0:T(2,128)} %copy.117), calls=%async_computation.1 | async-start | bytes 294912 | tf_op jit(solution)/shard_map/all_to_all | solution.py:195
  60.6 1086.0 %all-gather.3.cloned.1.call-start = ((), (), s32[]{:S(2)}) async-start(), calls=%async_computation.4 | async-start | bytes 1474560 | tf_op jit(solution)/shard_map/all_gather | solution.py:305
  111.5 21.3 %collective-permute-start.4 = (bf16[192,1152]{1,0:T(8,128)(2,1)}, bf16[192,1152]{1,0:T(8,128)(2,1)S(1)}, u32[]{:S(2)}, u32[]{:S(2)}) collective-permute-start(bf16[192,1152]{1,0:T(8,128)(2,1)} %bitcast.72), channel_id=1, source_target_pairs={{0,4},{8,0},{16,8},{24,16},{28,24},{20,28},{12,20},{4,12},{1,5},{9... | collective-permute-start | bytes 1327112 | tf_op jit(solution)/shard_map/ppermute | solution.py:56
  115.3 62.5 %collective-permute-start.56 = (bf16[192,1536]{1,0:T(8,128)(2,1)S(1)}, bf16[192,1536]{1,0:T(8,128)(2,1)S(1)}, u32[]{:S(2)}, u32[]{:S(2)}) collective-permute-start(bf16[192,1536]{1,0:T(8,128)(2,1)S(1)} %copy-done.81), channel_id=1, source_target_pairs={{0,8},{8,16},{16,24},{24,28},{28,20},{20,12},{12,4},{4,0},{1,9},{9... | collective-permute-start | bytes 1769480 | tf_op jit(solution)/shard_map/ppermute | solution.py:55
  123.3 56.0 %collective-permute-start.57 = (bf16[192,1536]{1,0:T(8,128)(2,1)S(1)}, bf16[192,1536]{1,0:T(8,128)(2,1)S(1)}, u32[]{:S(2)}, u32[]{:S(2)}) collective-permute-start(bf16[192,1536]{1,0:T(8,128)(2,1)S(1)} %copy-done.81), channel_id=1, source_target_pairs={{0,4},{8,0},{16,8},{24,16},{28,24},{20,28},{12,20},{4,12},{1,5},{9... | collective-permute-start | bytes 1769480 | tf_op jit(solution)/shard_map/ppermute | solution.py:56
  169.8 16.4 %collective-permute-start.48 = (bf16[192,1536]{1,0:T(8,128)(2,1)S(1)}, bf16[192,1536]{1,0:T(8,128)(2,1)}, u32[]{:S(2)}, u32[]{:S(2)}) collective-permute-start(bf16[192,1536]{1,0:T(8,128)(2,1)S(1)} %copy-done.79), channel_id=1, source_target_pairs={{0,8},{8,16},{16,24},{24,28},{28,20},{20,12},{12,4},{4,0},{1,9},{9... | collective-permute-start | bytes 1769480 | tf_op jit(solution)/shard_map/ppermute | solution.py:55
  171.9 17.9 %collective-permute-start.49 = (bf16[192,1536]{1,0:T(8,128)(2,1)S(1)}, bf16[192,1536]{1,0:T(8,128)(2,1)}, u32[]{:S(2)}, u32[]{:S(2)}) collective-permute-start(bf16[192,1536]{1,0:T(8,128)(2,1)S(1)} %copy-done.79), channel_id=1, source_target_pairs={{0,4},{8,0},{16,8},{24,16},{28,24},{20,28},{12,20},{4,12},{1,5},{9... | collective-permute-start | bytes 1769480 | tf_op jit(solution)/shard_map/ppermute | solution.py:56
  174.4 24.4 %collective-permute-start.40 = (bf16[192,1536]{1,0:T(8,128)(2,1)S(1)}, bf16[192,1536]{1,0:T(8,128)(2,1)}, u32[]{:S(2)}, u32[]{:S(2)}) collective-permute-start(bf16[192,1536]{1,0:T(8,128)(2,1)S(1)} %copy-done.80), channel_id=1, source_target_pairs={{0,8},{8,16},{16,24},{24,28},{28,20},{20,12},{12,4},{4,0},{1,9},{9... | collective-permute-start | bytes 1769480 | tf_op jit(solution)/shard_map/ppermute | solution.py:55
  177.8 24.4 %collective-permute-start.41 = (bf16[192,1536]{1,0:T(8,128)(2,1)S(1)}, bf16[192,1536]{1,0:T(8,128)(2,1)}, u32[]{:S(2)}, u32[]{:S(2)}) collective-permute-start(bf16[192,1536]{1,0:T(8,128)(2,1)S(1)} %copy-done.80), channel_id=1, source_target_pairs={{0,4},{8,0},{16,8},{24,16},{28,24},{20,28},{12,20},{4,12},{1,5},{9... | collective-permute-start | bytes 1769480 | tf_op jit(solution)/shard_map/ppermute | solution.py:56
  179.2 61.9 %collective-permute-start.1 = (bf16[304,1536]{1,0:T(8,128)(2,1)S(1)}, bf16[304,1536]{1,0:T(8,128)(2,1)S(1)}, u32[]{:S(2)}, u32[]{:S(2)}) collective-permute-start(bf16[304,1536]{1,0:T(8,128)(2,1)S(1)} %pad_maximum_fusion.13), channel_id=1, source_target_pairs={{0,2},{1,3},{2,0},{3,1},{4,6},{5,7},{6,4},{7,5},{8,10},{9,11},{10,... | collective-permute-start | bytes 2801672 | tf_op jit(solution)/shard_map/ppermute | solution.py:97
  186.1 22.0 %collective-permute-start.13 = (bf16[192,1152]{1,0:T(8,128)(2,1)}, bf16[192,1152]{1,0:T(8,128)(2,1)S(1)}, u32[]{:S(2)}, u32[]{:S(2)}) collective-permute-start(bf16[192,1152]{1,0:T(8,128)(2,1)} %collective-permute-done.11), channel_id=1, source_target_pairs={{0,8},{8,16},{16,24},{24,28},{28,20},{20,12},{12,4},{4,0},{1,9},{9... | collective-permute-start | bytes 1327112 | tf_op jit(solution)/shard_map/ppermute | solution.py:55
  189.8 30.4 %collective-permute-start.14 = (bf16[192,1152]{1,0:T(8,128)(2,1)S(1)}, bf16[192,1152]{1,0:T(8,128)(2,1)S(1)}, u32[]{:S(2)}, u32[]{:S(2)}) collective-permute-start(bf16[192,1152]{1,0:T(8,128)(2,1)S(1)} %collective-permute-done.12), channel_id=1, source_target_pairs={{0,4},{8,0},{16,8},{24,16},{28,24},{20,28},{12,20},{4,12},{1,5},{9... | collective-permute-start | bytes 1327112 | tf_op jit(solution)/shard_map/ppermute | solution.py:56
  198.8 18.9 %collective-permute-start.5 = (bf16[192,1152]{1,0:T(8,128)(2,1)}, bf16[192,1152]{1,0:T(8,128)(2,1)S(1)}, u32[]{:S(2)}, u32[]{:S(2)}) collective-permute-start(bf16[192,1152]{1,0:T(8,128)(2,1)} %collective-permute-done.3), channel_id=1, source_target_pairs={{0,8},{8,16},{16,24},{24,28},{28,20},{20,12},{12,4},{4,0},{1,9},{9... | collective-permute-start | bytes 1327112 | tf_op jit(solution)/shard_map/ppermute | solution.py:55
  202.2 19.1 %collective-permute-start.6 = (bf16[192,1152]{1,0:T(8,128)(2,1)S(1)}, bf16[192,1152]{1,0:T(8,128)(2,1)S(1)}, u32[]{:S(2)}, u32[]{:S(2)}) collective-permute-start(bf16[192,1152]{1,0:T(8,128)(2,1)S(1)} %collective-permute-done.4), channel_id=1, source_target_pairs={{0,4},{8,0},{16,8},{24,16},{28,24},{20,28},{12,20},{4,12},{1,5},{9... | collective-permute-start | bytes 1327112 | tf_op jit(solution)/shard_map/ppermute | solution.py:56
  208.1 16.9 %collective-permute-start.66 = (bf16[192,1536]{1,0:T(8,128)(2,1)}, bf16[192,1536]{1,0:T(8,128)(2,1)S(1)}, u32[]{:S(2)}, u32[]{:S(2)}) collective-permute-start(bf16[192,1536]{1,0:T(8,128)(2,1)} %collective-permute-done.64), channel_id=1, source_target_pairs={{0,8},{8,16},{16,24},{24,28},{28,20},{20,12},{12,4},{4,0},{1,9},{9... | collective-permute-start | bytes 1769480 | tf_op jit(solution)/shard_map/ppermute | solution.py:55
  221.3 16.4 %collective-permute-start.59 = (bf16[192,1536]{1,0:T(8,128)(2,1)S(1)}, bf16[192,1536]{1,0:T(8,128)(2,1)S(1)}, u32[]{:S(2)}, u32[]{:S(2)}) collective-permute-start(bf16[192,1536]{1,0:T(8,128)(2,1)S(1)} %collective-permute-done.57), channel_id=1, source_target_pairs={{0,4},{8,0},{16,8},{24,16},{28,24},{20,28},{12,20},{4,12},{1,5},{9... | collective-permute-start | bytes 1769480 | tf_op jit(solution)/shard_map/ppermute | solution.py:56
  225.0 17.7 %collective-permute-start = (bf16[304,1536]{1,0:T(8,128)(2,1)S(1)}, bf16[304,1536]{1,0:T(8,128)(2,1)S(1)}, u32[]{:S(2)}, u32[]{:S(2)}) collective-permute-start(bf16[304,1536]{1,0:T(8,128)(2,1)S(1)} %pad_maximum_fusion.13), channel_id=1, source_target_pairs={{0,1},{1,0},{2,3},{3,2},{4,5},{5,4},{6,7},{7,6},{8,9},{9,8},{10,11... | collective-permute-start | bytes 2801672 | tf_op jit(solution)/shard_map/ppermute | solution.py:96
  227.7 16.4 %collective-permute-start.15 = (bf16[192,1152]{1,0:T(8,128)(2,1)S(1)}, bf16[192,1152]{1,0:T(8,128)(2,1)S(1)}, u32[]{:S(2)}, u32[]{:S(2)}) collective-permute-start(bf16[192,1152]{1,0:T(8,128)(2,1)S(1)} %collective-permute-done.13), channel_id=1, source_target_pairs={{0,8},{8,16},{16,24},{24,28},{28,20},{20,12},{12,4},{4,0},{1,9},{9... | collective-permute-start | bytes 1327112 | tf_op jit(solution)/shard_map/ppermute | solution.py:55
  241.1 128.0 %collective-permute-start.75 = (bf16[304,1536]{1,0:T(8,128)(2,1)}, bf16[304,1536]{1,0:T(8,128)(2,1)}, u32[]{:S(2)}, u32[]{:S(2)}) collective-permute-start(bf16[304,1536]{1,0:T(8,128)(2,1)} %pad_maximum_fusion.15), channel_id=1, source_target_pairs={{0,2},{1,3},{2,0},{3,1},{4,6},{5,7},{6,4},{7,5},{8,10},{9,11},{10,... | collective-permute-start | bytes 2801672 | tf_op jit(solution)/shard_map/ppermute | solution.py:97
  242.7 121.5 %collective-permute-start.50 = (bf16[192,1536]{1,0:T(8,128)(2,1)}, bf16[192,1536]{1,0:T(8,128)(2,1)}, u32[]{:S(2)}, u32[]{:S(2)}) collective-permute-start(bf16[192,1536]{1,0:T(8,128)(2,1)} %collective-permute-done.48), channel_id=1, source_target_pairs={{0,8},{8,16},{16,24},{24,28},{28,20},{20,12},{12,4},{4,0},{1,9},{9... | collective-permute-start | bytes 1769480 | tf_op jit(solution)/shard_map/ppermute | solution.py:55
  244.1 121.7 %collective-permute-start.51 = (bf16[192,1536]{1,0:T(8,128)(2,1)}, bf16[192,1536]{1,0:T(8,128)(2,1)}, u32[]{:S(2)}, u32[]{:S(2)}) collective-permute-start(bf16[192,1536]{1,0:T(8,128)(2,1)} %collective-permute-done.49), channel_id=1, source_target_pairs={{0,4},{8,0},{16,8},{24,16},{28,24},{20,28},{12,20},{4,12},{1,5},{9... | collective-permute-start | bytes 1769480 | tf_op jit(solution)/shard_map/ppermute | solution.py:56
  245.5 20.1 %collective-permute-start.8 = (bf16[192,1152]{1,0:T(8,128)(2,1)S(1)}, bf16[192,1152]{1,0:T(8,128)(2,1)S(1)}, u32[]{:S(2)}, u32[]{:S(2)}) collective-permute-start(bf16[192,1152]{1,0:T(8,128)(2,1)S(1)} %collective-permute-done.6), channel_id=1, source_target_pairs={{0,4},{8,0},{16,8},{24,16},{28,24},{20,28},{12,20},{4,12},{1,5},{9... | collective-permute-start | bytes 1327112 | tf_op jit(solution)/shard_map/ppermute | solution.py:56
  252.6 43.7 %collective-permute-start.2 = (bf16[304,1536]{1,0:T(8,128)(2,1)S(1)}, bf16[304,1536]{1,0:T(8,128)(2,1)S(1)}, u32[]{:S(2)}, u32[]{:S(2)}) collective-permute-start(bf16[304,1536]{1,0:T(8,128)(2,1)S(1)} %collective-permute-done.1), channel_id=1, source_target_pairs={{0,1},{1,0},{2,3},{3,2},{4,5},{5,4},{6,7},{7,6},{8,9},{9,8},{10,11... | collective-permute-start | bytes 2801672 | tf_op jit(solution)/shard_map/ppermute | solution.py:98
  294.4 72.6 %collective-permute-start.42 = (bf16[192,1536]{1,0:T(8,128)(2,1)}, bf16[192,1536]{1,0:T(8,128)(2,1)}, u32[]{:S(2)}, u32[]{:S(2)}) collective-permute-start(bf16[192,1536]{1,0:T(8,128)(2,1)} %collective-permute-done.40), channel_id=1, source_target_pairs={{0,8},{8,16},{16,24},{24,28},{28,20},{20,12},{12,4},{4,0},{1,9},{9... | collective-permute-start | bytes 1769480 | tf_op jit(solution)/shard_map/ppermute | solution.py:55
  296.3 71.6 %collective-permute-start.43 = (bf16[192,1536]{1,0:T(8,128)(2,1)}, bf16[192,1536]{1,0:T(8,128)(2,1)}, u32[]{:S(2)}, u32[]{:S(2)}) collective-permute-start(bf16[192,1536]{1,0:T(8,128)(2,1)} %collective-permute-done.41), channel_id=1, source_target_pairs={{0,4},{8,0},{16,8},{24,16},{28,24},{20,28},{12,20},{4,12},{1,5},{9... | collective-permute-start | bytes 1769480 | tf_op jit(solution)/shard_map/ppermute | solution.py:56
  365.8 16.3 %collective-permute-start.68 = (bf16[192,1536]{1,0:T(8,128)(2,1)S(1)}, bf16[192,1536]{1,0:T(8,128)(2,1)S(1)}, u32[]{:S(2)}, u32[]{:S(2)}) collective-permute-start(bf16[192,1536]{1,0:T(8,128)(2,1)S(1)} %copy-done.70), channel_id=1, source_target_pairs={{0,8},{8,16},{16,24},{24,28},{28,20},{20,12},{12,4},{4,0},{1,9},{9... | collective-permute-start | bytes 1769480 | tf_op jit(solution)/shard_map/ppermute | solution.py:55
  367.0 16.3 %collective-permute-start.69 = (bf16[192,1536]{1,0:T(8,128)(2,1)S(1)}, bf16[192,1536]{1,0:T(8,128)(2,1)S(1)}, u32[]{:S(2)}, u32[]{:S(2)}) collective-permute-start(bf16[192,1536]{1,0:T(8,128)(2,1)S(1)} %copy-done.72), channel_id=1, source_target_pairs={{0,4},{8,0},{16,8},{24,16},{28,24},{20,28},{12,20},{4,12},{1,5},{9... | collective-permute-start | bytes 1769480 | tf_op jit(solution)/shard_map/ppermute | solution.py:56
  367.9 26.9 %collective-permute-start.60 = (bf16[192,1536]{1,0:T(8,128)(2,1)S(1)}, bf16[192,1536]{1,0:T(8,128)(2,1)S(1)}, u32[]{:S(2)}, u32[]{:S(2)}) collective-permute-start(bf16[192,1536]{1,0:T(8,128)(2,1)S(1)} %copy-done.74), channel_id=1, source_target_pairs={{0,8},{8,16},{16,24},{24,28},{28,20},{20,12},{12,4},{4,0},{1,9},{9... | collective-permute-start | bytes 1769480 | tf_op jit(solution)/shard_map/ppermute | solution.py:55
  369.1 36.2 %collective-permute-start.61 = (bf16[192,1536]{1,0:T(8,128)(2,1)S(1)}, bf16[192,1536]{1,0:T(8,128)(2,1)S(1)}, u32[]{:S(2)}, u32[]{:S(2)}) collective-permute-start(bf16[192,1536]{1,0:T(8,128)(2,1)S(1)} %copy-done.76), channel_id=1, source_target_pairs={{0,4},{8,0},{16,8},{24,16},{28,24},{20,28},{12,20},{4,12},{1,5},{9... | collective-permute-start | bytes 1769480 | tf_op jit(solution)/shard_map/ppermute | solution.py:56
  370.1 53.0 %collective-permute-start.35 = (bf16[608,1536]{1,0:T(8,128)(2,1)S(1)}, bf16[608,1536]{1,0:T(8,128)(2,1)S(1)}, u32[]{:S(2)}, u32[]{:S(2)}) collective-permute-start(bf16[608,1536]{1,0:T(8,128)(2,1)S(1)} %pad_maximum_fusion.8), channel_id=1, source_target_pairs={{0,1},{1,0},{2,3},{3,2},{4,5},{5,4},{6,7},{7,6},{8,9},{9,8},{10,11... | collective-permute-start | bytes 5603336 | tf_op jit(solution)/shard_map/ppermute | solution.py:104
  382.1 33.1 %collective-permute-start.52 = (bf16[192,1536]{1,0:T(8,128)(2,1)}, bf16[192,1536]{1,0:T(8,128)(2,1)S(1)}, u32[]{:S(2)}, u32[]{:S(2)}) collective-permute-start(bf16[192,1536]{1,0:T(8,128)(2,1)} %collective-permute-done.50), channel_id=1, source_target_pairs={{0,8},{8,16},{16,24},{24,28},{28,20},{20,12},{12,4},{4,0},{1,9},{9... | collective-permute-start | bytes 1769480 | tf_op jit(solution)/shard_map/ppermute | solution.py:55
  383.3 32.0 %collective-permute-start.53 = (bf16[192,1536]{1,0:T(8,128)(2,1)}, bf16[192,1536]{1,0:T(8,128)(2,1)S(1)}, u32[]{:S(2)}, u32[]{:S(2)}) collective-permute-start(bf16[192,1536]{1,0:T(8,128)(2,1)} %collective-permute-done.51), channel_id=1, source_target_pairs={{0,4},{8,0},{16,8},{24,16},{28,24},{20,28},{12,20},{4,12},{1,5},{9... | collective-permute-start | bytes 1769480 | tf_op jit(solution)/shard_map/ppermute | solution.py:56
  394.7 23.8 %collective-permute-start.44 = (bf16[192,1536]{1,0:T(8,128)(2,1)}, bf16[192,1536]{1,0:T(8,128)(2,1)S(1)}, u32[]{:S(2)}, u32[]{:S(2)}) collective-permute-start(bf16[192,1536]{1,0:T(8,128)(2,1)} %collective-permute-done.42), channel_id=1, source_target_pairs={{0,8},{8,16},{16,24},{24,28},{28,20},{20,12},{12,4},{4,0},{1,9},{9... | collective-permute-start | bytes 1769480 | tf_op jit(solution)/shard_map/ppermute | solution.py:55
  405.2 15.2 %collective-permute-start.45 = (bf16[192,1536]{1,0:T(8,128)(2,1)}, bf16[192,1536]{1,0:T(8,128)(2,1)S(1)}, u32[]{:S(2)}, u32[]{:S(2)}) collective-permute-start(bf16[192,1536]{1,0:T(8,128)(2,1)} %collective-permute-done.43), channel_id=1, source_target_pairs={{0,4},{8,0},{16,8},{24,16},{28,24},{20,28},{12,20},{4,12},{1,5},{9... | collective-permute-start | bytes 1769480 | tf_op jit(solution)/shard_map/ppermute | solution.py:56
  415.2 61.7 %collective-permute-start.76 = (bf16[304,1536]{1,0:T(8,128)(2,1)}, bf16[304,1536]{1,0:T(8,128)(2,1)S(1)}, u32[]{:S(2)}, u32[]{:S(2)}) collective-permute-start(bf16[304,1536]{1,0:T(8,128)(2,1)} %collective-permute-done.75), channel_id=1, source_target_pairs={{0,1},{1,0},{2,3},{3,2},{4,5},{5,4},{6,7},{7,6},{8,9},{9,8},{10,11... | collective-permute-start | bytes 2801672 | tf_op jit(solution)/shard_map/ppermute | solution.py:98
  415.3 32.1 %collective-permute-start.70 = (bf16[96,1536]{1,0:T(8,128)(2,1)S(1)}, bf16[96,1536]{1,0:T(8,128)(2,1)S(1)}, u32[]{:S(2)}, u32[]{:S(2)}) collective-permute-start(bf16[96,1536]{1,0:T(8,128)(2,1)S(1)} %slice.576), channel_id=1, source_target_pairs={{0,8},{8,16},{16,24},{24,28},{28,20},{20,12},{12,4},{4,0},{1,9},{9... | collective-permute-start | bytes 884744 | tf_op jit(solution)/shard_map/ppermute | solution.py:60
  418.5 30.4 %collective-permute-start.71 = (bf16[96,1536]{1,0:T(8,128)(2,1)S(1)}, bf16[96,1536]{1,0:T(8,128)(2,1)S(1)}, u32[]{:S(2)}, u32[]{:S(2)}) collective-permute-start(bf16[96,1536]{1,0:T(8,128)(2,1)S(1)} %slice.577), channel_id=1, source_target_pairs={{0,4},{8,0},{16,8},{24,16},{28,24},{20,28},{12,20},{4,12},{1,5},{9... | collective-permute-start | bytes 884744 | tf_op jit(solution)/shard_map/ppermute | solution.py:61
  420.5 29.0 %collective-permute-start.62 = (bf16[96,1536]{1,0:T(8,128)(2,1)S(1)}, bf16[96,1536]{1,0:T(8,128)(2,1)S(1)}, u32[]{:S(2)}, u32[]{:S(2)}) collective-permute-start(bf16[96,1536]{1,0:T(8,128)(2,1)S(1)} %slice.573), channel_id=1, source_target_pairs={{0,8},{8,16},{16,24},{24,28},{28,20},{20,12},{12,4},{4,0},{1,9},{9... | collective-permute-start | bytes 884744 | tf_op jit(solution)/shard_map/ppermute | solution.py:60
  423.3 20.2 %collective-permute-start.36 = (bf16[304,1536]{1,0:T(8,128)(2,1)S(1)}, bf16[304,1536]{1,0:T(8,128)(2,1)S(1)}, u32[]{:S(2)}, u32[]{:S(2)}) collective-permute-start(bf16[304,1536]{1,0:T(8,128)(2,1)S(1)} %add_convert_fusion.3), channel_id=1, source_target_pairs={{0,2},{1,3},{2,0},{3,1},{4,6},{5,7},{6,4},{7,5},{8,10},{9,11},{10,... | collective-permute-start | bytes 2801672 | tf_op jit(solution)/shard_map/ppermute | solution.py:107
  447.4 19.3 %collective-permute-start.38 = (bf16[304,1536]{1,0:T(8,128)(2,1)S(1)}, bf16[304,1536]{1,0:T(8,128)(2,1)S(1)}, u32[]{:S(2)}, u32[]{:S(2)}) collective-permute-start(bf16[304,1536]{1,0:T(8,128)(2,1)S(1)} %pad_maximum_fusion.14), channel_id=1, source_target_pairs={{0,2},{1,3},{2,0},{3,1},{4,6},{5,7},{6,4},{7,5},{8,10},{9,11},{10,... | collective-permute-start | bytes 2801672 | tf_op jit(solution)/shard_map/ppermute | solution.py:97
  449.5 17.1 %collective-permute-start.55 = (bf16[96,1536]{1,0:T(8,128)(2,1)S(1)}, bf16[96,1536]{1,0:T(8,128)(2,1)S(1)}, u32[]{:S(2)}, u32[]{:S(2)}) collective-permute-start(bf16[96,1536]{1,0:T(8,128)(2,1)S(1)} %slice.567), channel_id=1, source_target_pairs={{0,4},{8,0},{16,8},{24,16},{28,24},{20,28},{12,20},{4,12},{1,5},{9... | collective-permute-start | bytes 884744 | tf_op jit(solution)/shard_map/ppermute | solution.py:61
  452.5 15.5 %collective-permute-start.46 = (bf16[96,1536]{1,0:T(8,128)(2,1)S(1)}, bf16[96,1536]{1,0:T(8,128)(2,1)S(1)}, u32[]{:S(2)}, u32[]{:S(2)}) collective-permute-start(bf16[96,1536]{1,0:T(8,128)(2,1)S(1)} %slice.563), channel_id=1, source_target_pairs={{0,8},{8,16},{16,24},{24,28},{28,20},{20,12},{12,4},{4,0},{1,9},{9... | collective-permute-start | bytes 884744 | tf_op jit(solution)/shard_map/ppermute | solution.py:60
  457.4 19.7 %collective-permute-start.37 = (bf16[304,1536]{1,0:T(8,128)(2,1)S(1)}, bf16[304,1536]{1,0:T(8,128)(2,1)S(1)}, u32[]{:S(2)}, u32[]{:S(2)}) collective-permute-start(bf16[304,1536]{1,0:T(8,128)(2,1)S(1)} %pad_maximum_fusion.14), channel_id=1, source_target_pairs={{0,1},{1,0},{2,3},{3,2},{4,5},{5,4},{6,7},{7,6},{8,9},{9,8},{10,11... | collective-permute-start | bytes 2801672 | tf_op jit(solution)/shard_map/ppermute | solution.py:96
  550.1 159.3 %collective-permute-start.72 = (bf16[608,1536]{1,0:T(8,128)(2,1)S(1)}, bf16[608,1536]{1,0:T(8,128)(2,1)S(1)}, u32[]{:S(2)}, u32[]{:S(2)}) collective-permute-start(bf16[608,1536]{1,0:T(8,128)(2,1)S(1)} %pad_maximum_fusion.9), channel_id=1, source_target_pairs={{0,1},{1,0},{2,3},{3,2},{4,5},{5,4},{6,7},{7,6},{8,9},{9,8},{10,11... | collective-permute-start | bytes 5603336 | tf_op jit(solution)/shard_map/ppermute | solution.py:104
  554.1 157.7 %collective-permute-start.77 = (bf16[608,1536]{1,0:T(8,128)(2,1)S(1)}, bf16[608,1536]{1,0:T(8,128)(2,1)S(1)}, u32[]{:S(2)}, u32[]{:S(2)}) collective-permute-start(bf16[608,1536]{1,0:T(8,128)(2,1)S(1)} %pad_maximum_fusion.10), channel_id=1, source_target_pairs={{0,1},{1,0},{2,3},{3,2},{4,5},{5,4},{6,7},{7,6},{8,9},{9,8},{10,11... | collective-permute-start | bytes 5603336 | tf_op jit(solution)/shard_map/ppermute | solution.py:104
  713.5 16.2 %collective-permute-start.195 = (bf16[96,1536]{1,0:T(8,128)(2,1)S(1)}, bf16[96,1536]{1,0:T(8,128)(2,1)S(1)}, u32[]{:S(2)}, u32[]{:S(2)}) collective-permute-start(bf16[96,1536]{1,0:T(8,128)(2,1)S(1)} %get-tuple-element.354), channel_id=1, source_target_pairs={{0,4},{8,0},{16,8},{24,16},{28,24},{20,28},{12,20},{4,12},{1,5},{9... | collective-permute-start | bytes 884744 | tf_op jit(solution)/shard_map/ppermute | solution.py:82
  723.5 62.7 %collective-permute-start.73 = (bf16[304,1536]{1,0:T(8,128)(2,1)}, bf16[304,1536]{1,0:T(8,128)(2,1)}, u32[]{:S(2)}, u32[]{:S(2)}) collective-permute-start(bf16[304,1536]{1,0:T(8,128)(2,1)} %add_convert_fusion.2), channel_id=1, source_target_pairs={{0,2},{1,3},{2,0},{3,1},{4,6},{5,7},{6,4},{7,5},{8,10},{9,11},{10,... | collective-permute-start | bytes 2801672 | tf_op jit(solution)/shard_map/ppermute | solution.py:107
  726.2 35.0 %collective-permute-start.78 = (bf16[304,1536]{1,0:T(8,128)(2,1)S(1)}, bf16[304,1536]{1,0:T(8,128)(2,1)S(1)}, u32[]{:S(2)}, u32[]{:S(2)}) collective-permute-start(bf16[304,1536]{1,0:T(8,128)(2,1)S(1)} %add_convert_fusion.1), channel_id=1, source_target_pairs={{0,2},{1,3},{2,0},{3,1},{4,6},{5,7},{6,4},{7,5},{8,10},{9,11},{10,... | collective-permute-start | bytes 2801672 | tf_op jit(solution)/shard_map/ppermute | solution.py:107
  765.3 16.8 %collective-permute-start.80 = (bf16[304,1536]{1,0:T(8,128)(2,1)}, bf16[304,1536]{1,0:T(8,128)(2,1)}, u32[]{:S(2)}, u32[]{:S(2)}) collective-permute-start(bf16[304,1536]{1,0:T(8,128)(2,1)} %pad_maximum_fusion.16), channel_id=1, source_target_pairs={{0,2},{1,3},{2,0},{3,1},{4,6},{5,7},{6,4},{7,5},{8,10},{9,11},{10,... | collective-permute-start | bytes 2801672 | tf_op jit(solution)/shard_map/ppermute | solution.py:97
  768.6 23.1 %collective-permute-start.79 = (bf16[304,1536]{1,0:T(8,128)(2,1)}, bf16[304,1536]{1,0:T(8,128)(2,1)}, u32[]{:S(2)}, u32[]{:S(2)}) collective-permute-start(bf16[304,1536]{1,0:T(8,128)(2,1)} %pad_maximum_fusion.16), channel_id=1, source_target_pairs={{0,1},{1,0},{2,3},{3,2},{4,5},{5,4},{6,7},{7,6},{8,9},{9,8},{10,11... | collective-permute-start | bytes 2801672 | tf_op jit(solution)/shard_map/ppermute | solution.py:96
  912.1 116.1 %collective-permute-start.82 = (bf16[608,1536]{1,0:T(8,128)(2,1)S(1)}, bf16[608,1536]{1,0:T(8,128)(2,1)S(1)}, u32[]{:S(2)}, u32[]{:S(2)}) collective-permute-start(bf16[608,1536]{1,0:T(8,128)(2,1)S(1)} %pad_maximum_fusion.11), channel_id=1, source_target_pairs={{0,1},{1,0},{2,3},{3,2},{4,5},{5,4},{6,7},{7,6},{8,9},{9,8},{10,11... | collective-permute-start | bytes 5603336 | tf_op jit(solution)/shard_map/ppermute | solution.py:104
  912.7 25.4 %collective-permute-start.98 = (bf16[96,1152]{1,0:T(8,128)(2,1)S(1)}, bf16[96,1152]{1,0:T(8,128)(2,1)S(1)}, u32[]{:S(2)}, u32[]{:S(2)}) collective-permute-start(bf16[96,1152]{1,0:T(8,128)(2,1)S(1)} %get-tuple-element.429), channel_id=1, source_target_pairs={{0,8},{8,16},{16,24},{24,28},{28,20},{20,12},{12,4},{4,0},{1,9},{9... | collective-permute-start | bytes 663560 | tf_op jit(solution)/shard_map/ppermute | solution.py:82
  914.4 25.5 %collective-permute-start.105 = (bf16[96,1152]{1,0:T(8,128)(2,1)S(1)}, bf16[96,1152]{1,0:T(8,128)(2,1)S(1)}, u32[]{:S(2)}, u32[]{:S(2)}) collective-permute-start(bf16[96,1152]{1,0:T(8,128)(2,1)S(1)} %get-tuple-element.430), channel_id=1, source_target_pairs={{0,4},{8,0},{16,8},{24,16},{28,24},{20,28},{12,20},{4,12},{1,5},{9... | collective-permute-start | bytes 663560 | tf_op jit(solution)/shard_map/ppermute | solution.py:82
  946.0 24.3 %collective-permute-start.99 = (bf16[96,1152]{1,0:T(8,128)(2,1)S(1)}, bf16[96,1152]{1,0:T(8,128)(2,1)S(1)}, u32[]{:S(2)}, u32[]{:S(2)}) collective-permute-start(bf16[96,1152]{1,0:T(8,128)(2,1)S(1)} %get-tuple-element.427), channel_id=1, source_target_pairs={{0,8},{8,16},{16,24},{24,28},{28,20},{20,12},{12,4},{4,0},{1,9},{9... | collective-permute-start | bytes 663560 | tf_op jit(solution)/shard_map/ppermute | solution.py:82
  947.9 23.7 %collective-permute-start.106 = (bf16[96,1152]{1,0:T(8,128)(2,1)S(1)}, bf16[96,1152]{1,0:T(8,128)(2,1)S(1)}, u32[]{:S(2)}, u32[]{:S(2)}) collective-permute-start(bf16[96,1152]{1,0:T(8,128)(2,1)S(1)} %get-tuple-element.428), channel_id=1, source_target_pairs={{0,4},{8,0},{16,8},{24,16},{28,24},{20,28},{12,20},{4,12},{1,5},{9... | collective-permute-start | bytes 663560 | tf_op jit(solution)/shard_map/ppermute | solution.py:82
  967.9 15.8 %collective-permute-start.85 = (bf16[96,1152]{1,0:T(8,128)(2,1)S(1)}, bf16[96,1152]{1,0:T(8,128)(2,1)S(1)}, u32[]{:S(2)}, u32[]{:S(2)}) collective-permute-start(bf16[96,1152]{1,0:T(8,128)(2,1)S(1)} %get-tuple-element.411), channel_id=1, source_target_pairs={{0,8},{8,16},{16,24},{24,28},{28,20},{20,12},{12,4},{4,0},{1,9},{9... | collective-permute-start | bytes 663560 | tf_op jit(solution)/shard_map/ppermute | solution.py:82
  969.4 15.1 %collective-permute-start.92 = (bf16[96,1152]{1,0:T(8,128)(2,1)S(1)}, bf16[96,1152]{1,0:T(8,128)(2,1)S(1)}, u32[]{:S(2)}, u32[]{:S(2)}) collective-permute-start(bf16[96,1152]{1,0:T(8,128)(2,1)S(1)} %get-tuple-element.412), channel_id=1, source_target_pairs={{0,4},{8,0},{16,8},{24,16},{28,24},{20,28},{12,20},{4,12},{1,5},{9... | collective-permute-start | bytes 663560 | tf_op jit(solution)/shard_map/ppermute | solution.py:82
  1029.5 15.1 %collective-permute-start.83 = (bf16[304,1536]{1,0:T(8,128)(2,1)}, bf16[304,1536]{1,0:T(8,128)(2,1)}, u32[]{:S(2)}, u32[]{:S(2)}) collective-permute-start(bf16[304,1536]{1,0:T(8,128)(2,1)} %add_convert_fusion), channel_id=1, source_target_pairs={{0,2},{1,3},{2,0},{3,1},{4,6},{5,7},{6,4},{7,5},{8,10},{9,11},{10,... | collective-permute-start | bytes 2801672 | tf_op jit(solution)/shard_map/ppermute | solution.py:107
  (274 other events, 3321.0 us)
Sparse Core Ops, SparseCore 0:
  1062.8 16.5 all-gather.2

commit v2 on v1

v2 whole, which is shorter than its diff:
```python
import functools

import jax
import jax.numpy as jnp
from jax import lax
from jax.experimental import pallas as pl
from jax.experimental.pallas import tpu as pltpu
from jax.sharding import PartitionSpec as P

HEAD_DIM = 64
EPS = 1e-06
LOW = jnp.bfloat16
WIDE = jnp.float32
TEXT_TILE = 64
POOL_TILE = 8
LANES = 128
NT, NN, TN = ((1,), (1,)), ((1,), (0,)), ((0,), (0,))


def dot(left, right, dims):
    return lax.dot_general(left, right, (dims, ((), ())), preferred_element_type=WIDE)


def layer_norm(values):
    average = jnp.mean(values, axis=-1, keepdims=True)
    centred = values - average
    spread = jnp.mean(centred * centred, axis=-1, keepdims=True)
    return centred * lax.rsqrt(spread + EPS)


def gelu_tanh(values):
    return jax.nn.gelu(values, approximate=True)


MESH = pl.DeviceIdType.MESH
RING = 8


def ring_dp(place):
    place = place % RING
    return 2 * place + (place // (RING // 2)) * (2 * RING - 1 - 4 * place)


def ring_place():
    index = lax.axis_index("dp")
    return index // 2 + (index % 2) * (RING - 1 - 2 * (index // 2))


def ring_sides(place):
    tensor = lax.axis_index("tensor")
    return (ring_dp(place + 1), tensor), (ring_dp(place + RING - 1), tensor)


def meet(sides):
    barrier = pltpu.get_barrier_semaphore()
    for side in sides:
        pl.semaphore_signal(barrier, inc=1, device_id=side, device_id_type=MESH)
    pl.semaphore_wait(barrier, len(sides))


def half_of(rows, columns, way):
    if rows // 2 % 16 == 0:
        return way * (rows // 2), rows // 2, 0, columns
    return 0, rows, way * (columns // 2), columns // 2


class GatherRing:
    STEPS = RING // 2

    def __init__(self, blocks, fulls, sems):
        self.blocks, self.fulls = blocks, fulls
        self.own_sem, self.send_sem, self.recv_sem = sems
        self.place = ring_place()
        self.sides = ring_sides(self.place)

    @staticmethod
    def scratch(count):
        steps = RING // 2
        return [
            pltpu.SemaphoreType.DMA((count,)),
            pltpu.SemaphoreType.DMA((count, 2, steps)),
            pltpu.SemaphoreType.DMA((count, 2, steps)),
        ]

    def copy(self, i, way, step):
        rows, columns = self.blocks[i].shape
        at = self.place + (RING - step if way == 0 else step)
        top, high, left, wide = 0, rows, 0, columns
        if step == self.STEPS - 1:
            top, high, left, wide = half_of(rows, columns, way)
        there = self.fulls[i].at[pl.ds(ring_dp(at) * rows + top, high), pl.ds(left, wide)]
        here = there if step else self.blocks[i]
        return pltpu.make_async_remote_copy(
            src_ref=here,
            dst_ref=there,
            send_sem=self.send_sem.at[i, way, step],
            recv_sem=self.recv_sem.at[i, way, step],
            device_id=self.sides[way],
            device_id_type=MESH,
        )

    def own(self, i):
        rows = self.blocks[i].shape[0]
        start = ring_dp(self.place) * rows
        return pltpu.make_async_copy(
            self.blocks[i], self.fulls[i].at[pl.ds(start, rows)], self.own_sem.at[i]
        )

    def start(self):
        for i in range(len(self.blocks)):
            for way in range(2):
                self.copy(i, way, 0).start()
            self.own(i).start()

    def step(self, step):
        for i in range(len(self.blocks)):
            for way in range(2):
                self.copy(i, way, step - 1).wait_recv()
                if step < self.STEPS:
                    self.copy(i, way, step).start()

    def end(self):
        for i in range(len(self.blocks)):
            self.own(i).wait()
            for way in range(2):
                for step in range(self.STEPS):
                    self.copy(i, way, step).wait_send()


class ScatterRing:
    STEPS = RING - 1

    def __init__(self, grads, sums, scratch):
        self.grads, self.sums = grads, sums
        count = len(grads)
        self.mine, self.got = scratch[:count], scratch[count : 2 * count]
        self.mine_sem, self.send_sem, self.recv_sem = scratch[2 * count :]
        self.place = ring_place()
        self.sides = ring_sides(self.place)

    @staticmethod
    def scratch(shapes):
        sizes = [half_of(rows // RING, columns, 0) for rows, columns in shapes]
        halves = [(2, RING, high, wide) for _, high, _, wide in sizes]
        gots = [(2, RING - 1, high, wide) for _, high, _, wide in sizes]
        count = len(shapes)
        return [
            *[pltpu.VMEM(shape, LOW) for shape in halves],
            *[pltpu.VMEM(shape, LOW) for shape in gots],
            pltpu.SemaphoreType.DMA((count, 2, RING)),
            pltpu.SemaphoreType.DMA((count, 2, RING - 1)),
            pltpu.SemaphoreType.DMA((count, 2, RING - 1)),
        ]

    def load(self, i, way, step):
        rows, columns = self.grads[i].shape[0] // RING, self.grads[i].shape[1]
        at = self.place + (2 * RING - step - 1 if way == 0 else step + 1)
        top, high, left, wide = half_of(rows, columns, way)
        return pltpu.make_async_copy(
            self.grads[i].at[pl.ds(ring_dp(at) * rows + top, high), pl.ds(left, wide)],
            self.mine[i].at[way, step],
            self.mine_sem.at[i, way, step],
        )

    def copy(self, i, way, step):
        return pltpu.make_async_remote_copy(
            src_ref=self.mine[i].at[way, step],
            dst_ref=self.got[i].at[way, step],
            send_sem=self.send_sem.at[i, way, step],
            recv_sem=self.recv_sem.at[i, way, step],
            device_id=self.sides[way],
            device_id_type=MESH,
        )

    def load_all(self):
        for step in range(RING):
            for i in range(len(self.grads)):
                for way in range(2):
                    self.load(i, way, step).start()

    def start(self):
        for i in range(len(self.grads)):
            for way in range(2):
                self.load(i, way, 0).wait()
                self.copy(i, way, 0).start()

    def step(self, step):
        for i in range(len(self.grads)):
            rows, columns = self.grads[i].shape[0] // RING, self.grads[i].shape[1]
            for way in range(2):
                top, high, left, wide = half_of(rows, columns, way)
                self.load(i, way, step).wait()
                self.copy(i, way, step - 1).wait_recv()
                total = self.mine[i][way, step].astype(WIDE) + self.got[i][way, step - 1].astype(WIDE)
                if step < self.STEPS:
                    self.mine[i][way, step] = total.astype(LOW)
                    self.copy(i, way, step).start()
                else:
                    self.sums[i][pl.ds(top, high), pl.ds(left, wide)] = total

    def end(self):
        for i in range(len(self.grads)):
            for way in range(2):
                for step in range(self.STEPS):
                    self.copy(i, way, step).wait_send()


ANY = pl.BlockSpec(memory_space=pl.ANY)
WHOLE = pl.BlockSpec(memory_space=pltpu.VMEM)
VMEM_LIMIT = 56 << 20


def gather_kernel(count, *refs):
    ring = GatherRing(refs[:count], refs[count : 2 * count], refs[2 * count :])
    meet(ring.sides)
    ring.start()
    for step in range(1, ring.STEPS + 1):
        ring.step(step)
    ring.end()


def gather_ring(blocks, ident):
    count = len(blocks)
    return pl.pallas_call(
        functools.partial(gather_kernel, count),
        out_shape=[
            jax.ShapeDtypeStruct((RING * block.shape[0], block.shape[1]), block.dtype)
            for block in blocks
        ],
        in_specs=[ANY] * count,
        out_specs=[ANY] * count,
        scratch_shapes=GatherRing.scratch(count),
        compiler_params=pltpu.CompilerParams(
            collective_id=ident, has_side_effects=True, vmem_limit_bytes=VMEM_LIMIT
        ),
        name="gather_ring",
    )(*blocks)


def scatter_kernel(count, *refs):
    ring = ScatterRing(refs[:count], refs[count : 2 * count], refs[2 * count :])
    ring.load_all()
    meet(ring.sides)
    ring.start()
    for step in range(1, ring.STEPS + 1):
        ring.step(step)
    ring.end()


def scatter_ring(grads, ident):
    count = len(grads)
    return pl.pallas_call(
        functools.partial(scatter_kernel, count),
        out_shape=[
            jax.ShapeDtypeStruct((grad.shape[0] // RING, grad.shape[1]), WIDE) for grad in grads
        ],
        in_specs=[ANY] * count,
        out_specs=[WHOLE] * count,
        scratch_shapes=ScatterRing.scratch([grad.shape for grad in grads]),
        compiler_params=pltpu.CompilerParams(
            collective_id=ident, has_side_effects=True, vmem_limit_bytes=VMEM_LIMIT
        ),
        name="scatter_ring",
    )(*grads)


def gather_dp(blocks, size, ident):
    if size == RING:
        return gather_ring(blocks, ident)
    return [lax.all_gather(block, "dp", axis=0, tiled=True) for block in blocks]


def scatter_dp(grads, size, ident):
    if size == RING:
        return scatter_ring(grads, ident)
    return [
        lax.psum_scatter(grad, "dp", scatter_dimension=0, tiled=True).astype(WIDE)
        for grad in grads
    ]


def beside(ring, blocks, size, ident, before, after):
    blocks = lax.optimization_barrier(tuple(blocks) + tuple(before))[: len(blocks)]
    found = tuple(ring(list(blocks), size, ident))
    held = lax.optimization_barrier(found + tuple(after))
    return held[: len(found)], held[len(found) :]


CORE = [(i, i ^ 1) for i in range(4)]
CHIP = [(i, i ^ 2) for i in range(4)]


def gather_start(own):
    near = lax.ppermute(own, "tensor", CORE)
    far = lax.ppermute(own, "tensor", CHIP)
    return near, far


def gather_end(own, near, far):
    last = lax.ppermute(far, "tensor", CORE)
    return jnp.concatenate([own, near, far, last], axis=0)


def gather_rows(own):
    return gather_end(own, *gather_start(own))


def scatter_start(partial):
    rows = partial.shape[0] // 4
    low = partial.astype(LOW)
    part = [low[b * rows : (b + 1) * rows] for b in range(4)]
    sent = lax.ppermute(jnp.concatenate([part[1], part[3]]), "tensor", CORE)
    here = part[0].astype(WIDE) + sent[:rows].astype(WIDE)
    return here, (part[2].astype(WIDE) + sent[rows:].astype(WIDE)).astype(LOW)


def scatter_rows(partial):
    here, there = scatter_start(partial)
    return here + lax.ppermute(there, "tensor", CHIP).astype(WIDE)


def head_lanes(head):
    lane = lax.broadcasted_iota(jnp.int32, (1, LANES), 1)
    return (lane < HEAD_DIM) if head == 0 else (lane >= HEAD_DIM)


def attend_pair(split, bias_ref, q_ref, k_ref, v_ref, out_ref, lse_ref):
    scale = HEAD_DIM ** (-0.5)
    bias = bias_ref[...]
    outs, totals = [], []
    for head in range(2):
        mine = head_lanes(head)
        queries = jnp.where(mine, q_ref[...] * scale, 0).astype(LOW)
        image = dot(queries, k_ref[:split], NT)
        text = dot(queries, k_ref[split:], NT) + bias
        top = jnp.maximum(
            jnp.max(image, axis=1, keepdims=True), jnp.max(text, axis=1, keepdims=True)
        )
        image = jnp.exp(image - top).astype(LOW)
        text = jnp.exp(text - top).astype(LOW)
        values = jnp.where(mine, v_ref[...], 1).astype(LOW)
        both = dot(image, values[:split], NN) + dot(text, values[split:], NN)
        sums = pltpu.roll(both, HEAD_DIM, 1)
        outs.append(both / sums)
        totals.append(top + jnp.log(sums))
    first = head_lanes(0)
    out_ref[...] = jnp.where(first, outs[0], outs[1]).astype(out_ref.dtype)
    flipped = jnp.where(first, totals[0], totals[1]).T
    lse_ref[0] = jnp.concatenate([flipped[:4], flipped[HEAD_DIM : HEAD_DIM + 4]], axis=0)


def attend_kernel(split, count, waits, *refs):
    bias_ref, q_ref, k_ref, v_ref = refs[:4]
    blocks, (out_ref, lse_ref) = refs[4 : 4 + count], refs[4 + count : 6 + count]
    at = pl.program_id(0) * pl.num_programs(1) + pl.program_id(1)
    if count:
        ring = GatherRing(blocks, refs[6 + count : 6 + 2 * count], refs[6 + 2 * count :])

        @pl.when(at == 0)
        def _():
            meet(ring.sides)
            ring.start()

        for step, when in enumerate(waits):

            @pl.when(at == when)
            def _():
                ring.step(step + 1)

    attend_pair(split, bias_ref, q_ref, k_ref, v_ref, out_ref, lse_ref)
    if count:

        @pl.when(at == pl.num_programs(0) * pl.num_programs(1) - 1)
        def _():
            for step in range(len(waits) + 1, ring.STEPS + 1):
                ring.step(step)
            ring.end()


def attend(joint, bias, split, heads, blocks, ident, waits):
    rows, pairs, count, block = joint.shape[0], heads // 2, len(blocks), joint.shape[0] // 2
    whole = lambda part: pl.BlockSpec((rows, LANES), lambda h, i: (0, part * pairs + h))
    extra = dict(collective_id=ident, has_side_effects=True) if count else {}
    found = pl.pallas_call(
        functools.partial(attend_kernel, split, count, waits),
        grid=(pairs, 2),
        in_specs=[
            pl.BlockSpec((1, rows - split), lambda h, i: (0, 0)),
            pl.BlockSpec((block, LANES), lambda h, i: (i, h)),
            whole(1),
            whole(2),
            *[ANY] * count,
        ],
        out_specs=[
            pl.BlockSpec((block, LANES), lambda h, i: (i, h)),
            pl.BlockSpec((1, 8, block), lambda h, i: (h, 0, i)),
            *[ANY] * count,
        ],
        out_shape=[
            jax.ShapeDtypeStruct((rows, heads * HEAD_DIM), LOW),
            jax.ShapeDtypeStruct((pairs, 8, rows), WIDE),
            *[jax.ShapeDtypeStruct((RING * b.shape[0], b.shape[1]), b.dtype) for b in blocks],
        ],
        scratch_shapes=GatherRing.scratch(count) if count else [],
        compiler_params=pltpu.CompilerParams(vmem_limit_bytes=VMEM_LIMIT, **extra),
        name="attend",
    )(bias, joint, joint, joint, *blocks)
    return found[0], found[1], found[2:]


def attend_back_pair(split, refs):
    (bias_ref, q_ref, k_ref, v_ref, o_ref, g_ref, lse_ref, dq_ref, dk_ref, dv_ref, dk_acc, dv_acc) = refs
    step = pl.program_id(1)
    scale = HEAD_DIM ** (-0.5)

    @pl.when(step == 0)
    def _():
        dk_acc[...] = jnp.zeros_like(dk_acc)
        dv_acc[...] = jnp.zeros_like(dv_acc)

    product = (g_ref[...].astype(WIDE) * o_ref[...].astype(WIDE)).T
    bias = bias_ref[...]
    dq = None
    for head in range(2):
        mine = head_lanes(head)
        queries = jnp.where(mine, q_ref[...] * scale, 0).astype(LOW)
        grads = jnp.where(mine, g_ref[...], 0).astype(LOW)
        keys = jnp.where(mine, k_ref[...], 0).astype(LOW)
        own = product[head * HEAD_DIM : (head + 1) * HEAD_DIM]
        delta = jnp.sum(own, axis=0, keepdims=True)
        total = lse_ref[0][4 * head : 4 * head + 1]
        for low, high in ((0, split), (split, k_ref.shape[0])):
            scores = dot(k_ref[low:high], queries, NT)
            if low:
                scores = scores + bias
            probs = jnp.exp(scores - total)
            grad_probs = dot(v_ref[low:high], grads, NT)
            grad_scores = (probs * (grad_probs - delta)).astype(LOW)
            dv_acc[low:high] += dot(probs.astype(LOW), grads, NN)
            dk_acc[low:high] += dot(grad_scores, queries, NN)
            part = dot(grad_scores, keys[low:high], TN)
            dq = part if dq is None else dq + part
    dq_ref[...] = (dq * scale).astype(LOW)

    @pl.when(step == pl.num_programs(1) - 1)
    def _():
        dk_ref[...] = dk_acc[...].astype(LOW)
        dv_ref[...] = dv_acc[...].astype(LOW)


def attend_back_kernel(split, count, waits, *refs):
    ins, rest = refs[:7], refs[7:]
    grads, outs, rest = rest[:count], rest[count : count + 3], rest[count + 3 :]
    sums, accs, rest = rest[:count], rest[count : count + 2], rest[count + 2 :]
    at = pl.program_id(0) * pl.num_programs(1) + pl.program_id(1)
    if count:
        ring = ScatterRing(grads, sums, rest)

        @pl.when(at == 0)
        def _():
            ring.load_all()
            meet(ring.sides)
            ring.start()

        for step, when in enumerate(waits):

            @pl.when(at == when)
            def _():
                ring.step(step + 1)

    attend_back_pair(split, (*ins, *outs, *accs))
    if count:

        @pl.when(at == pl.num_programs(0) * pl.num_programs(1) - 1)
        def _():
            for step in range(len(waits) + 1, ring.STEPS + 1):
                ring.step(step)
            ring.end()


def attend_back(joint, bias, mixed, grad, lse, split, heads, grads, ident, waits):
    rows, pairs, count, block = joint.shape[0], heads // 2, len(grads), joint.shape[0] // 2
    whole = lambda part: pl.BlockSpec((rows, LANES), lambda h, i: (0, part * pairs + h))
    some = pl.BlockSpec((block, LANES), lambda h, i: (i, h))
    extra = dict(collective_id=ident, has_side_effects=True) if count else {}
    found = pl.pallas_call(
        functools.partial(attend_back_kernel, split, count, waits),
        grid=(pairs, 2),
        in_specs=[
            pl.BlockSpec((rows - split, 1), lambda h, i: (0, 0)),
            some,
            whole(1),
            whole(2),
            some,
            some,
            pl.BlockSpec((1, 8, block), lambda h, i: (h, 0, i)),
            *[ANY] * count,
        ],
        out_specs=[some, whole(0), whole(0), *[WHOLE] * count],
        out_shape=[
            *[jax.ShapeDtypeStruct((rows, heads * HEAD_DIM), LOW)] * 3,
            *[jax.ShapeDtypeStruct((g.shape[0] // RING, g.shape[1]), WIDE) for g in grads],
        ],
        scratch_shapes=[
            *[pltpu.VMEM((rows, LANES), WIDE)] * 2,
            *(ScatterRing.scratch([g.shape for g in grads]) if count else []),
        ],
        compiler_params=pltpu.CompilerParams(vmem_limit_bytes=VMEM_LIMIT, **extra),
        name="attend_back",
    )(bias.T, joint, joint, joint, mixed, grad, lse, *grads)
    return found[:3], found[3:]


def local(size, image, text, cond, w_ada, w_qkv, w_out, w_up, w_down, grad_image, grad_text):
    index = lax.axis_index("tensor")
    seqs = size
    image_rows, width = image.shape[1], image.shape[2]
    text_tokens = text.shape[1]
    text_own = -(-text_tokens // 4)
    text_rows = -(-text_own // TEXT_TILE) * TEXT_TILE
    pool_rows = -(-text_own // POOL_TILE) * POOL_TILE
    width_here = w_ada.shape[-1]
    ada_rows = w_ada.shape[1]
    heads_here = w_qkv.shape[-1] // HEAD_DIM

    def blocks_of(weight):
        return [weight[stream].astype(LOW).reshape(weight.shape[1], -1) for stream in range(2)]

    up_blocks, down_blocks = blocks_of(w_up), blocks_of(w_down)

    units = up_blocks[1].shape[1] // size
    text_up = lax.all_to_all(
        up_blocks[1].reshape(-1, size, units), "dp", split_axis=1, concat_axis=0, tiled=True
    ).reshape(width, units)
    text_down = down_blocks[1]

    def pool_start(rows):
        copies = jnp.broadcast_to(rows[None, :pool_rows], (size, pool_rows, width))
        rows = lax.all_to_all(copies, "dp", split_axis=0, concat_axis=0, tiled=True)
        return rows.reshape(-1, width)

    def unpool_end(part):
        part = part.astype(LOW).reshape(size, pool_rows, width)
        part = lax.all_to_all(part, "dp", split_axis=0, concat_axis=0, tiled=True)
        total = jnp.sum(part.astype(WIDE), axis=0)
        return jnp.pad(total, ((0, text_rows - pool_rows), (0, 0)))

    cond_low = jax.nn.silu(cond).astype(LOW)
    cond_rows = lax.all_to_all(
        cond_low.reshape(seqs, ada_rows), "dp", split_axis=0, concat_axis=0, tiled=True
    )
    ada_low = w_ada.astype(LOW)
    mod_parts = jnp.einsum("nd,sdkf->nskf", cond_rows, ada_low, preferred_element_type=WIDE)
    mod_parts = lax.all_to_all(mod_parts, "dp", split_axis=0, concat_axis=0, tiled=True)
    modulation = lax.all_gather(jnp.sum(mod_parts, axis=0), "tensor", axis=2, tiled=True)

    def mod_row(stream, which):
        return modulation[stream, which][None, :]

    def own_text(rows):
        padded = jnp.pad(rows, ((0, 4 * text_own - text_tokens), (0, 0)))
        own = lax.dynamic_slice_in_dim(padded, index * text_own, text_own, 0)
        return jnp.pad(own, ((0, text_rows - text_own), (0, 0)))

    split_at = 4 * image_rows
    places = jnp.arange(4 * text_rows)
    token = ((places // text_rows) ^ index) * text_own + places % text_rows
    is_key = (places % text_rows < text_own) & (token < text_tokens)
    bias = jnp.where(is_key, 0.0, -1e30).astype(WIDE)[None, :]

    streams = [image[0].astype(WIDE), own_text(text[0]).astype(WIDE)]
    cotangent = [grad_image[0].astype(WIDE), own_text(grad_text[0]).astype(WIDE)]
    normed_in = [layer_norm(residual) for residual in streams]
    first_in = [
        (normed_in[s] * (1.0 + mod_row(s, 1)) + mod_row(s, 0)).astype(LOW) for s in range(2)
    ]
    ffn_grad = [(mod_row(s, 5) * cotangent[s]).astype(LOW) for s in range(2)]
    moved = [gather_start(first_in[s]) for s in range(2)]
    pooled_grad = pool_start(ffn_grad[1])
    ring = functools.partial(beside, gather_dp)
    found, held = ring(
        blocks_of(w_qkv) + blocks_of(w_out),
        size,
        1,
        first_in + [ffn_grad[1]],
        [*moved[0], *moved[1], pooled_grad, ffn_grad[0]],
    )
    qkv_full, out_full = found[:2], found[2:]
    pooled_grad, image_ffn_grad = held[4:]
    attn_rows = [
        gather_end(first_in[0], held[0], held[1]),
        gather_end(first_in[1], held[2], held[3]),
    ]
    joint = jnp.concatenate(
        [dot(attn_rows[s], qkv_full[s], NN).astype(LOW) for s in range(2)], axis=0
    )
    ffn_moved = gather_start(image_ffn_grad)
    text_ffn_moved = gather_start(pooled_grad)
    if size == RING:
        mixed, log_total, (up_full,) = attend(
            joint, bias, split_at, heads_here, [up_blocks[0]], 2, (4,)
        )
    else:
        mixed, log_total, _ = attend(joint, bias, split_at, heads_here, [], 0, ())
        (up_full,) = gather_dp([up_blocks[0]], size, 2)
    mixed, *ffn_moved = lax.optimization_barrier((mixed, *ffn_moved, *text_ffn_moved))
    mixed_rows = [mixed[:split_at], mixed[split_at:]]
    ffn_rows = gather_end(image_ffn_grad, *ffn_moved[:2])
    text_ffn_rows = gather_end(pooled_grad, *ffn_moved[2:])
    branches = [None, None]
    here, there = scatter_start(dot(mixed_rows[0], out_full[0], NN))
    branches[1] = scatter_rows(dot(mixed_rows[1], out_full[1], NN))
    far = lax.ppermute(there, "tensor", CHIP)
    branches[0] = here + far.astype(WIDE)
    middle = [streams[s] + mod_row(s, 2) * branches[s] for s in range(2)]
    normed_mid = [layer_norm(residual) for residual in middle]
    second_in = [
        (normed_mid[s] * (1.0 + mod_row(s, 4)) + mod_row(s, 3)).astype(LOW) for s in range(2)
    ]
    moved = gather_start(second_in[0])
    pooled_in = pool_start(second_in[1])
    (down_full,), (*moved, pooled_in) = ring(
        [down_blocks[0]], size, 3, second_in, [*moved, pooled_in]
    )
    mlp_rows = gather_end(second_in[0], *moved)
    text_moved = gather_start(pooled_in)

    def gelu_back(pre_act, hidden_grad):
        return jax.vjp(gelu_tanh, pre_act)[1](hidden_grad)[0].astype(LOW)

    pre_act = dot(mlp_rows, up_full, NN)
    hidden = gelu_tanh(pre_act).astype(LOW)
    pre_grad = gelu_back(pre_act, dot(ffn_rows, down_full, NT))
    here, there = scatter_start(dot(pre_grad, up_full, NT))
    far = lax.ppermute(there, "tensor", CHIP)
    down_grad = dot(hidden, ffn_rows, TN).astype(LOW)
    far, there, down_grad, *text_moved = lax.optimization_barrier(
        (far, there, down_grad, *text_moved)
    )
    second_grad, ffn = [None, None], [None, None]
    middle_grad, branch_grad = [None, None], [None, None]

    def middle_back(s):
        wide = second_grad[s] * (1.0 + mod_row(s, 4))
        middle_grad[s] = cotangent[s] + jax.vjp(layer_norm, middle[s])[1](wide)[0]
        branch_grad[s] = (mod_row(s, 2) * middle_grad[s]).astype(LOW)

    second_grad[0] = here + far.astype(WIDE)
    middle_back(0)
    moved = gather_start(branch_grad[0])
    text_mlp_rows = gather_end(pooled_in, *text_moved)
    text_pre_act = dot(text_mlp_rows, text_up, NN)
    text_hidden = gelu_tanh(text_pre_act).astype(LOW)
    text_pre_grad = gelu_back(text_pre_act, dot(text_ffn_rows, text_down, NT))
    text_here, text_there = scatter_start(dot(text_pre_grad, text_up, NT))
    text_far = lax.ppermute(text_there, "tensor", CHIP)
    up_grad = dot(mlp_rows, pre_grad, TN).astype(LOW)
    up_grad, text_far = lax.optimization_barrier((up_grad, text_far))
    second_grad[1] = unpool_end(text_here + text_far.astype(WIDE))
    here, there = scatter_start(dot(hidden, down_full, NN))
    moved = lax.optimization_barrier((*moved, there))[:2]
    branch_rows = [gather_end(branch_grad[0], *moved), None]
    middle_back(1)
    branch_rows[1] = gather_rows(branch_grad[1])
    far = lax.ppermute(there, "tensor", CHIP)
    text_here, text_there = scatter_start(dot(text_hidden, text_down, NN))
    text_far = lax.ppermute(text_there, "tensor", CHIP)
    mixed_grad = jnp.concatenate(
        [dot(branch_rows[s], out_full[s], NT).astype(LOW) for s in range(2)], axis=0
    )
    if size == RING:
        grads, (down_sum, up_sum) = attend_back(
            joint, bias, mixed, mixed_grad, log_total, split_at, heads_here,
            [down_grad, up_grad], 4, (3, 5),
        )
    else:
        grads, _ = attend_back(
            joint, bias, mixed, mixed_grad, log_total, split_at, heads_here, [], 0, ()
        )
        down_sum, up_sum = scatter_dp([down_grad, up_grad], size, 4)
    joint_grad = jnp.concatenate(grads, axis=1)
    joint_grad, far, text_far = lax.optimization_barrier((joint_grad, far, text_far))
    ffn[0] = here + far.astype(WIDE)
    ffn[1] = unpool_end(text_here + text_far.astype(WIDE))
    joint_rows = [joint_grad[:split_at], joint_grad[split_at:]]
    here, there = scatter_start(dot(joint_rows[0], qkv_full[0], NT))
    text_first = scatter_rows(dot(joint_rows[1], qkv_full[1], NT))
    far = lax.ppermute(there, "tensor", CHIP)
    qkv_grad = [dot(attn_rows[s], joint_rows[s], TN).astype(LOW) for s in range(2)]
    out_grad = [dot(mixed_rows[s], branch_rows[s], TN).astype(LOW) for s in range(2)]
    rest_sum, (far, text_first, ffn[1]) = beside(
        scatter_dp,
        qkv_grad + out_grad, size, 5, [there], [far, text_first, ffn[1]]
    )
    first_grad = [here + far.astype(WIDE), text_first]
    text_down_grad = dot(text_hidden, text_ffn_rows, TN)
    text_up_grad = lax.all_to_all(
        dot(text_mlp_rows, text_pre_grad, TN).astype(LOW).reshape(size, -1, units),
        "dp", split_axis=0, concat_axis=2, tiled=True,
    ).reshape(-1, size * units).astype(WIDE)
    results = [(middle[s] + mod_row(s, 5) * ffn[s]).astype(LOW) for s in range(2)]
    input_grad = [
        middle_grad[s]
        + jax.vjp(layer_norm, streams[s])[1](first_grad[s] * (1.0 + mod_row(s, 1)))[0]
        for s in range(2)
    ]
    mod_terms = jnp.stack(
        [
            jnp.stack(
                [
                    jnp.sum(first_grad[s], axis=0),
                    jnp.sum(first_grad[s] * normed_in[s], axis=0),
                    jnp.sum(middle_grad[s] * branches[s], axis=0),
                    jnp.sum(second_grad[s], axis=0),
                    jnp.sum(second_grad[s] * normed_mid[s], axis=0),
                    jnp.sum(cotangent[s] * ffn[s], axis=0),
                ]
            )
            for s in range(2)
        ]
    )
    mod_split = mod_terms.reshape(2, 6, 4, width_here).transpose(2, 0, 1, 3)
    mod_sum = jnp.sum(
        lax.all_to_all(mod_split, "tensor", split_axis=0, concat_axis=0, tiled=True), axis=0
    )
    shift_grad = mod_sum[:, 3]
    mod_low = jnp.broadcast_to(mod_sum.astype(LOW)[None], (seqs,) + mod_sum.shape)
    mod_grad = lax.all_to_all(mod_low, "dp", split_axis=0, concat_axis=0, tiled=True)
    ada_grad = jnp.einsum("nd,nskf->sdkf", cond_rows, mod_grad, preferred_element_type=WIDE)
    act_parts = jnp.einsum("nskf,sdkf->nd", mod_grad, ada_low, preferred_element_type=WIDE)
    act_parts = lax.all_to_all(act_parts, "dp", split_axis=0, concat_axis=0, tiled=True)
    act_grad = lax.psum(act_parts.reshape(1, width), "tensor")
    cond_grad = jax.vjp(jax.nn.silu, cond)[1](act_grad)[0]
    text_out, text_grad = results[1], input_grad[1]

    def whole_text(rows):
        blocks = lax.all_gather(rows, "tensor", axis=0)
        return blocks[:, :text_own].reshape(4 * text_own, width)[:text_tokens][None]

    down_sum = jnp.stack([down_sum, text_down_grad])
    up_sum = jnp.stack([up_sum, text_up_grad])
    qkv_sum, out_sum = jnp.stack(rest_sum[:2]), jnp.stack(rest_sum[2:])

    return (
        results[0][None],
        whole_text(text_out),
        input_grad[0][None],
        whole_text(text_grad),
        cond_grad,
        shift_grad[None],
        ada_grad,
        qkv_sum.reshape(w_qkv.shape),
        out_sum.reshape(w_out.shape),
        up_sum,
        down_sum,
    )


def solution(mesh):
    size = mesh.shape["dp"]

    def step(*args):
        return local(size, *args)

    return jax.shard_map(
        step,
        mesh=mesh,
        in_specs=(
            P("dp", "tensor", None),
            P("dp", None, None),
            P("dp", None),
            P(None, "dp", None, "tensor"),
            P(None, "dp", None, "tensor"),
            P(None, ("tensor", "dp"), None),
            P(None, "dp", "tensor"),
            P(None, ("tensor", "dp"), None),
            P("dp", "tensor", None),
            P("dp", None, None),
        ),
        out_specs=(
            P("dp", "tensor", None),
            P("dp", None, None),
            P("dp", "tensor", None),
            P("dp", None, None),
            P("dp", None),
            P("dp", None, "tensor"),
            P(None, "dp", None, "tensor"),
            P(None, "dp", None, "tensor"),
            P(None, ("tensor", "dp"), None),
            P(None, "dp", "tensor"),
            P(None, ("tensor", "dp"), None),
        ),
        check_vma=False,
    )
```

time: 1170 us -> 899 us (0.77)
  Pallas kernels: 0 us -> 404 us
  waiting for transfers between devices: 400 us -> 88.2 us
  starting transfers between devices: 241 us -> 79.9 us
  local copies, waits for them, and re-layouts: 173 us -> 72.6 us
  matrix products: 209 us -> 119 us
  blocking collectives: 49.2 us -> 25 us
  other arithmetic: 66 us -> 85.7 us
    pallas_call x0 -> x5, Pallas kernels: none -> 404 us  [the longest x2 153 us: gather_ring(): pl.pallas_call(functools.partial(gather_kernel, count), out_shape=[jax.Sh...]
    ppermute x196 -> x40, waiting for transfers between devices: 395 us -> 55.6 us  [the longest x2 23 us: local(): text_far = lax.ppermute(text_there, 'tensor', CHIP)]
    ppermute x196 -> x40, starting transfers between devices: 224 us -> 23.2 us  [the longest x8 9.22 us: gather_start(): far = lax.ppermute(own, 'tensor', CHIP)]
    dot_general x66 -> x24, matrix products: 203 us -> 114 us  [dot(): lax.dot_general(left, right, (dims, ((), ())), preferred_element_type=WIDE)]
    dynamic_update_slice x78 -> x0, local copies, waits for them, and re-layouts: 69.5 us -> none  [the longest x72 60.9 us: put(): return lax.dynamic_update_slice_in_dim(full, piece, start, 0)]
    all_to_all x0 -> x7, starting transfers between devices: none -> 36 us  [the longest x1 8.68 us: local(): lax.all_to_all(up_blocks[1].reshape(-1, size, units), 'dp', split_axis=1,...]
    all_to_all x0 -> x7, waiting for transfers between devices: none -> 24.5 us  [the longest x1 12.4 us: local(): lax.all_to_all(dot(text_mlp_rows, text_pre_grad, TN).astype(LOW).reshape(...]
    all_gather x2 -> x1, blocking collectives: 38.1 us -> 14 us  [whole_text(): blocks = lax.all_gather(rows, 'tensor', axis=0)]
  transfers between devices with their start and end apart: 201 -> 52, of which waited for: 107 -> 12; matrix products, arithmetic and copies ran while one was open for 20% -> 28% of each run, Pallas kernels for 0% -> 45%
where the time goes in v2:
time: 899 us; the launch traced here: 891 us
  Pallas kernels  404 us (45%)
  matrix products  119 us (13%)
  waiting for transfers between devices  88.2 us (10%)
  other arithmetic  85.7 us (10%)
  starting transfers between devices  79.9 us (9%)
  local copies, waits for them, and re-layouts  72.6 us (8%)
  blocking collectives  25 us (3%)
  between operations  16.5 us (2%)
    pallas_call x2, Pallas kernels, gather_ring(): pl.pallas_call(functools.partial(gather_kernel, count), out_shape=[jax.Sh...  153 us
    dot_general x24, matrix products, dot(): lax.dot_general(left, right, (dims, ((), ())), preferred_element_type=WIDE)  114 us
    pallas_call x1, Pallas kernels, scatter_ring(): pl.pallas_call(functools.partial(scatter_kernel, count), out_shape=[jax.S...  98.4 us
    pallas_call x1, Pallas kernels, attend_back(): pl.pallas_call(functools.partial(attend_back_kernel, split, count, waits)...  98.4 us
    pallas_call x1, Pallas kernels, attend(): pl.pallas_call(functools.partial(attend_kernel, split, count, waits), gri...  54.8 us
    unnamed x287, local copies, waits for them, and re-layouts  26.7 us
    ppermute x2, waiting for transfers between devices, local(): text_far = lax.ppermute(text_there, 'tensor', CHIP)  23 us
    ppermute x4, waiting for transfers between devices, local(): far = lax.ppermute(there, 'tensor', CHIP)  19.6 us
  transfers between devices with their start and end apart: 52, of which 12 were waited for; matrix products, arithmetic and copies ran while one was open for 28% of the time, Pallas kernels for 45%

profile of v2, /device:TPU:0, one launch (start us, length us, event | category | flops | bytes accessed | tf_op | source)
XLA Modules:
  0.0 891.4 jit_solution(15319272121028986525)
XLA Ops:
  9.3 7.3 all-to-all-start
  24.4 6.0 all-to-all-start.1
  32.9 4.9 all-to-all-done.1
  37.9 5.3 all_gather.15
  45.0 3.6 all-to-all-start.2
  56.8 100.9 %gather_ring.2 = (bf16[1536,1152]{1,0:T(8,128)(2,1)}, bf16[1536,1152]{1,0:T(8,128)(2,1)}, bf16[384,1536]{1,0:T(8,128)(2,1)}, bf16[384,1536]{1,0:T(8,128)(2,1)}) custom-call(bf16[192,1152]{1,0:T(8,128)(2,1)} %bitcast.161, bf16[192,1152]{1,0:T(8,128)(2,1)} %bitcast.160, bf16[48,1536]{1,0:T(8,128)(2,1)} %get-tuple-element.75.refs_2_, ...), custom_call_target="tpu_custom_call" | custom-call | tf_op jit(solution)/shard_map/gather_ring/pallas_call | solution.py:224
  162.7 8.7 all-to-all-start.4
  179.5 5.6 convolution_convert_fusion.9
  186.9 54.8 %attend.1 = (bf16[1280,384]{1,0:T(8,128)(2,1)}, f32[3,8,1280]{2,1,0:T(8,128)}, bf16[1536,1536]{1,0:T(8,128)(2,1)}) custom-call(f32[1,256]{1,0:T(1,128)} %and_select_fusion.refs_0_, bf16[1280,1152]{1,0:T(8,128)(2,1)} %pad_maximum_fusion.3.refs_1_.refs_2_.refs_3_, bf16[1280,1152]{1,0:T(8,128)(2,1)} %pad_maximum_fusion.3.refs_1_.refs_2_.refs_3_, ...), custom_call_target="tpu_custom_call" | custom-call | tf_op jit(solution)/shard_map/attend/pallas_call | solution.py:384
  249.2 2.4 copy.102
  251.6 2.4 reshape.411
  256.7 4.4 collective-permute-done.13
  265.8 4.4 all-to-all-start.3
  270.2 11.4 %collective-permute-done.11 = bf16[256,1536]{1,0:T(8,128)(2,1)S(1)} collective-permute-done((bf16[256,1536]{1,0:T(8,128)(2,1)S(1)}, bf16[256,1536]{1,0:T(8,128)(2,1)S(1)}, u32[]{:S(2)}, u32[]{:S(2)}) %collective-permute-start.11) | collective-permute-done | bytes 786464 | tf_op jit(solution)/shard_map/ppermute | solution.py:613
  291.6 2.2 constant_dynamic-update-slice_fusion.5
  293.8 52.0 %gather_ring.3 = bf16[1536,1536]{1,0:T(8,128)(2,1)} custom-call(bf16[192,1536]{1,0:T(8,128)(2,1)} %slice_bitcast_fusion.2.refs_0_), custom_call_target="tpu_custom_call" | custom-call | tf_op jit(solution)/shard_map/gather_ring/pallas_call | solution.py:224
  353.3 10.9 %fusion.43 = f32[1024,1536]{1,0:T(8,128)} fusion(bf16[1536,1536]{1,0:T(8,128)(2,1)} %get-tuple-element.96, bf16[256,1536]{1,0:T(8,128)(2,1)S(1)} %collective-permute-done.16, bf16[256,1536]{1,0:T(8,128)(2,1)} %collective-permute-done.15, bf16[256,1536]{1,0:T(8,128)(2,1)} %collective-permute-done.14, bf16[256,1536]{1,0:T(8,128)(2,1)} %add_convert_fusion.8), kind=kOutput, calls=%fused_computation.128 | convolution fusion | flops 4844421120 | bytes 14155776 | tf_op jit(solution)/shard_map/dot_general | solution.py:21
  364.1 11.4 %fusion.6 = bf16[1024,1536]{1,0:T(8,128)(2,1)S(1)} fusion(f32[1024,1536]{1,0:T(8,128)} %fusion.43, bf16[1024,1536]{1,0:T(8,128)(2,1)} %constant_dynamic-update-slice_fusion, bf16[1536,1536]{1,0:T(8,128)(2,1)S(1)} %bitcast.150), kind=kOutput, calls=%fused_computation.14 | convolution fusion | flops 4863295488 | bytes 17301504 | tf_op jit(solution)/shard_map/dot_general | solution.py:21
  375.5 5.3 convolution_convert_fusion.6
  381.4 7.5 convolution_convert_fusion.7
  391.2 10.0 %convolution_convert_fusion.2.refs_7_ = bf16[1536,1536]{1,0:T(8,128)(2,1)} fusion(bf16[1024,1536]{1,0:T(8,128)(2,1)} %constant_dynamic-update-slice_fusion, f32[1024,1536]{1,0:T(8,128)} %fusion.43), kind=kOutput, calls=%fused_computation.4 | convolution fusion | flops 4848353280 | bytes 14155776 | tf_op jit(solution)/shard_map/dot_general | solution.py:21
  401.2 8.3 collective-permute-done.20
  415.7 4.1 fusion.35
  427.4 8.9 convolution_convert_fusion.1.refs_8_
  440.1 6.4 collective-permute-done.24
  446.5 2.7 add_convert_fusion.3
  450.7 3.9 convolution_convert_fusion.16
  456.7 2.6 convolution_convert_fusion.4
  460.8 23.0 %collective-permute-done.29 = bf16[320,1536]{1,0:T(8,128)(2,1)} collective-permute-done((bf16[320,1536]{1,0:T(8,128)(2,1)}, bf16[320,1536]{1,0:T(8,128)(2,1)}, u32[]{:S(2)}, u32[]{:S(2)}) %collective-permute-start.29) | collective-permute-done | bytes 983072 | tf_op jit(solution)/shard_map/ppermute | solution.py:656
  483.8 3.1 add_convert_fusion.2
  486.9 4.3 all-to-all-start.5
  491.2 3.0 pad_maximum_fusion.9
  494.2 4.2 convolution_bitcast_fusion
  498.4 4.6 convolution_convert_fusion.17
  503.1 4.3 convolution_convert_fusion.12.refs_2_
  507.3 8.2 all-to-all-done.5
  515.6 4.4 all-to-all-start.10
  527.4 12.4 %all-to-all-done.10 = bf16[8,192,192]{2,1,0:T(8,128)(2,1)} async-done(((bf16[8,192,192]{2,1,0:T(8,128)(2,1)}), bf16[8,192,192]{2,1,0:T(8,128)(2,1)}, u32[]{:S(2)}, u32[]{:S(2)}) %all-to-all-start.10) | async-done | bytes 589856 | tf_op jit(solution)/shard_map/all_to_all | solution.py:697
  543.2 2.7 reshape.419
  546.4 2.7 add_convert_fusion.1
  551.8 2.3 convolution_convert_fusion.18
  555.1 98.4 %attend_back.1 = (bf16[1280,384]{1,0:T(8,128)(2,1)}, bf16[1280,384]{1,0:T(8,128)(2,1)}, bf16[1280,384]{1,0:T(8,128)(2,1)}, f32[192,1536]{1,0:T(8,128)}, f32[192,1536]{1,0:T(8,128)}) custom-call(f32[256,1]{1,0:T(8,128)} %fusion.73.refs_0_, bf16[1280,1152]{1,0:T(8,128)(2,1)} %pad_maximum_fusion.3.refs_1_.refs_2_.refs_3_, ...), custom_call_target="tpu_custom_call" | custom-call | tf_op jit(solution)/shard_map/attend_back/pallas_call | solution.py:486
  659.0 4.5 convolution_convert_fusion.10
  669.6 7.5 convolution_convert_fusion.refs_0_
  677.1 3.3 add_convert_fusion
  680.4 4.0 fusion.25
  686.0 4.3 all-to-all-start.6
  690.6 4.2 convolution_convert_fusion.3.refs_1_
  696.4 2.4 add_convert_fusion.4
  700.3 2.8 convolution_convert_fusion.11.refs_3_
  704.7 98.4 %scatter_ring.1 = (f32[192,1152]{1,0:T(8,128)}, f32[192,1152]{1,0:T(8,128)}, f32[48,1536]{1,0:T(8,128)}, f32[48,1536]{1,0:T(8,128)}) custom-call(bf16[1536,1152]{1,0:T(8,128)(2,1)} %convolution_convert_fusion.refs_0_, bf16[1536,1152]{1,0:T(8,128)(2,1)} %convolution_convert_fusion.3.refs_1_, bf16[384,1536]{1,0:T(8,128)(2,1)} %convolution_convert_fusion.12.refs_2_, ...), custom_call_target="tpu_custom_call" | custom-call | tf_op jit(solution)/shard_map/scatter_ring/pallas_call | solution.py:252
  808.3 2.5 fusion.59
  810.9 2.6 fusion.21
  814.5 3.9 all-to-all-start.7
  818.4 14.0 %all-gather = bf16[256,1536]{1,0:T(8,128)(2,1)S(1)} all-gather(bf16[64,1536]{1,0:T(8,128)(2,1)S(1)} %copy-done.53), channel_id=2, replica_groups=mesh['dp'=8,'tensor'=4] {'tensor'}, dimensions={0}, use_global_device_ids=true | all-gather | bytes 983040 | tf_op jit(solution)/shard_map/all_gather | solution.py:737
  835.2 2.3 stack.96
  837.6 2.3 stack.97
  839.9 3.8 add_bitcast_fusion
  848.9 6.4 all-to-all-start.8
  858.5 3.9 all-to-all-done.8
  864.4 3.3 all-to-all-start.9
  867.8 3.3 convolution_bitcast_fusion.1
  871.1 3.1 all-to-all-done.9
  874.3 5.7 psum.7
  (508 shorter events, 150.9 us)
Async XLA Ops:
  9.3 13.9 %all-to-all-start = ((bf16[8,1,192]{2,1,0:T(2,128)(2,1)}), bf16[8,1,192]{2,1,0:T(2,128)(2,1)S(1)}, u32[]{:S(2)}, u32[]{:S(2)}) async-start(bf16[8,1,192]{2,1,0:T(2,128)(2,1)} %all_to_all.69), calls=%async_computation | async-start | bytes 16384 | tf_op jit(solution)/shard_map/all_to_all | solution.py:549
  24.4 13.5 %all-to-all-start.1 = ((f32[8,2,6,384]{3,1,2,0:T(2,128)}), f32[8,2,6,384]{3,1,2,0:T(2,128)S(1)}, u32[]{:S(2)}, u32[]{:S(2)}) async-start(f32[8,2,6,384]{3,1,2,0:T(2,128)} %copy.98), calls=%async_computation.1 | async-start | bytes 294912 | tf_op jit(solution)/shard_map/all_to_all | solution.py:554
  30.4 24.4 %copy-start.103 = (f32[64]{0:T(128)}, f32[64]{0:T(128)S(1)}, u32[]{:S(2)}) copy-start(f32[64]{0:T(128)S(1)} %fusion.92) | copy-start | bytes 772
  44.0 217.1 %copy-start.62 = (f32[1536]{0:T(1024)}, f32[1536]{0:T(1024)S(1)}, u32[]{:S(2)}) copy-start(f32[1536]{0:T(1024)S(1)} %get-tuple-element.219) | copy-start | bytes 18436
  45.0 114.3 %all-to-all-start.2 = ((bf16[8,40,1536]{2,1,0:T(8,128)(2,1)}), bf16[8,40,1536]{2,1,0:T(8,128)(2,1)S(1)}, u32[]{:S(2)}, u32[]{:S(2)}) async-start(bf16[8,40,1536]{2,1,0:T(8,128)(2,1)} %broadcast_in_dim.44), calls=%async_computation.2 | async-start | bytes 1966080 | tf_op jit(solution)/shard_map/all_to_all | solution.py:539
  52.8 107.6 %copy-start.85 = (f32[256]{0:T(256)}, f32[256]{0:T(256)S(1)}, u32[]{:S(2)}) copy-start(f32[256]{0:T(256)S(1)} %fusion.90) | copy-start | bytes 3076
  53.2 104.5 %copy-start.46 = (bf16[256,1536]{1,0:T(8,128)(2,1)}, bf16[256,1536]{1,0:T(8,128)(2,1)S(1)}, u32[]{:S(2)}) copy-start(bf16[256,1536]{1,0:T(8,128)(2,1)S(1)} %fusion.20) | copy-start | bytes 2359300
  53.2 104.5 %collective-permute-start.1 = (bf16[256,1536]{1,0:T(8,128)(2,1)S(1)}, bf16[256,1536]{1,0:T(8,128)(2,1)S(1)}, u32[]{:S(2)}, u32[]{:S(2)}) collective-permute-start(bf16[256,1536]{1,0:T(8,128)(2,1)S(1)} %fusion.20), channel_id=1, source_target_pairs={{0,2},{1,3},{2,0},{3,1},{4,6},{5,7},{6,4},{7,5},{8,10},{9,11},{10,... | collective-permute-start | bytes 2359304 | tf_op jit(solution)/shard_map/ppermute | solution.py:295
  54.8 104.5 %collective-permute-start = (bf16[256,1536]{1,0:T(8,128)(2,1)S(1)}, bf16[256,1536]{1,0:T(8,128)(2,1)}, u32[]{:S(2)}, u32[]{:S(2)}) collective-permute-start(bf16[256,1536]{1,0:T(8,128)(2,1)S(1)} %fusion.20), channel_id=1, source_target_pairs={{0,1},{1,0},{2,3},{3,2},{4,5},{5,4},{6,7},{7,6},{8,9},{9,8},{10,11... | collective-permute-start | bytes 2359304 | tf_op jit(solution)/shard_map/ppermute | solution.py:294
  55.0 102.8 %copy-start.59 = (bf16[64,1536]{1,0:T(8,128)(2,1)}, bf16[64,1536]{1,0:T(8,128)(2,1)S(1)}, u32[]{:S(2)}) copy-start(bf16[64,1536]{1,0:T(8,128)(2,1)S(1)} %fusion.53) | copy-start | bytes 589828
  55.0 102.7 %collective-permute-start.3 = (bf16[64,1536]{1,0:T(8,128)(2,1)S(1)}, bf16[64,1536]{1,0:T(8,128)(2,1)S(1)}, u32[]{:S(2)}, u32[]{:S(2)}) collective-permute-start(bf16[64,1536]{1,0:T(8,128)(2,1)S(1)} %fusion.53), channel_id=1, source_target_pairs={{0,2},{1,3},{2,0},{3,1},{4,6},{5,7},{6,4},{7,5},{8,10},{9,11},{10,... | collective-permute-start | bytes 589832 | tf_op jit(solution)/shard_map/ppermute | solution.py:295
  55.6 102.1 %collective-permute-start.2 = (bf16[64,1536]{1,0:T(8,128)(2,1)S(1)}, bf16[64,1536]{1,0:T(8,128)(2,1)S(1)}, u32[]{:S(2)}, u32[]{:S(2)}) collective-permute-start(bf16[64,1536]{1,0:T(8,128)(2,1)S(1)} %fusion.53), channel_id=1, source_target_pairs={{0,1},{1,0},{2,3},{3,2},{4,5},{5,4},{6,7},{7,6},{8,9},{9,8},{10,11... | collective-permute-start | bytes 589832 | tf_op jit(solution)/shard_map/ppermute | solution.py:294
  159.3 20.2 %collective-permute-start.4 = (bf16[256,1536]{1,0:T(8,128)(2,1)}, bf16[256,1536]{1,0:T(8,128)(2,1)}, u32[]{:S(2)}, u32[]{:S(2)}) collective-permute-start(bf16[256,1536]{1,0:T(8,128)(2,1)} %copy-done.116), channel_id=1, source_target_pairs={{0,1},{1,0},{2,3},{3,2},{4,5},{5,4},{6,7},{7,6},{8,9},{9,8},{10,11... | collective-permute-start | bytes 2359304 | tf_op jit(solution)/shard_map/ppermute | solution.py:300
  162.7 86.5 %all-to-all-start.4 = ((bf16[192,8,192]{0,2,1:T(8,128)(2,1)}), bf16[192,8,192]{0,2,1:T(8,128)(2,1)}, u32[]{:S(2)}, u32[]{:S(2)}) async-start(bf16[192,8,192]{0,2,1:T(8,128)(2,1)} %bitcast.155), calls=%async_computation.4 | async-start | bytes 1572864 | tf_op jit(solution)/shard_map/all_to_all | solution.py:532
  173.3 75.0 %copy-start.26 = (bf16[2,192,1536]{2,1,0:T(8,128)(2,1)}, bf16[2,192,1536]{2,1,0:T(8,128)(2,1)S(1)}, u32[]{:S(2)}) copy-start(bf16[2,192,1536]{2,1,0:T(8,128)(2,1)S(1)} %convert.23) | copy-start | bytes 3538948
  173.3 3.7 collective-permute-start.5
  174.9 66.8 %collective-permute-start.7 = (bf16[256,1536]{1,0:T(8,128)(2,1)S(1)}, bf16[256,1536]{1,0:T(8,128)(2,1)}, u32[]{:S(2)}, u32[]{:S(2)}) collective-permute-start(bf16[256,1536]{1,0:T(8,128)(2,1)S(1)} %copy-done.21), channel_id=1, source_target_pairs={{0,2},{1,3},{2,0},{3,1},{4,6},{5,7},{6,4},{7,5},{8,10},{9,11},{10,... | collective-permute-start | bytes 2359304 | tf_op jit(solution)/shard_map/ppermute | solution.py:295
  176.5 65.3 %collective-permute-start.6 = (bf16[256,1536]{1,0:T(8,128)(2,1)S(1)}, bf16[256,1536]{1,0:T(8,128)(2,1)}, u32[]{:S(2)}, u32[]{:S(2)}) collective-permute-start(bf16[256,1536]{1,0:T(8,128)(2,1)S(1)} %copy-done.21), channel_id=1, source_target_pairs={{0,1},{1,0},{2,3},{3,2},{4,5},{5,4},{6,7},{7,6},{8,9},{9,8},{10,11... | collective-permute-start | bytes 2359304 | tf_op jit(solution)/shard_map/ppermute | solution.py:294
  176.5 65.3 %collective-permute-start.9 = (bf16[320,1536]{1,0:T(8,128)(2,1)S(1)}, bf16[320,1536]{1,0:T(8,128)(2,1)}, u32[]{:S(2)}, u32[]{:S(2)}) collective-permute-start(bf16[320,1536]{1,0:T(8,128)(2,1)S(1)} %bitcast.151), channel_id=1, source_target_pairs={{0,2},{1,3},{2,0},{3,1},{4,6},{5,7},{6,4},{7,5},{8,10},{9,11},{10,... | collective-permute-start | bytes 2949128 | tf_op jit(solution)/shard_map/ppermute | solution.py:295
  177.1 64.7 %collective-permute-start.8 = (bf16[320,1536]{1,0:T(8,128)(2,1)S(1)}, bf16[320,1536]{1,0:T(8,128)(2,1)S(1)}, u32[]{:S(2)}, u32[]{:S(2)}) collective-permute-start(bf16[320,1536]{1,0:T(8,128)(2,1)S(1)} %bitcast.152), channel_id=1, source_target_pairs={{0,1},{1,0},{2,3},{3,2},{4,5},{5,4},{6,7},{7,6},{8,9},{9,8},{10,11... | collective-permute-start | bytes 2949128 | tf_op jit(solution)/shard_map/ppermute | solution.py:294
  186.9 54.9 %copy-start.39 = (bf16[384,1536]{1,0:T(8,128)(2,1)S(1)}, bf16[384,1536]{1,0:T(8,128)(2,1)}, u32[]{:S(2)}) copy-start(bf16[384,1536]{1,0:T(8,128)(2,1)} %get-tuple-element.92) | copy-start | bytes 3538948
  243.8 10.3 %collective-permute-start.12 = (bf16[128,1536]{1,0:T(8,128)(2,1)S(1)}, bf16[128,1536]{1,0:T(8,128)(2,1)S(1)}, u32[]{:S(2)}, u32[]{:S(2)}) collective-permute-start(bf16[128,1536]{1,0:T(8,128)(2,1)S(1)} %pad_maximum_fusion.24), channel_id=1, source_target_pairs={{0,1},{1,0},{2,3},{3,2},{4,5},{5,4},{6,7},{7,6},{8,9},{9,8},{10,11... | collective-permute-start | bytes 1179656 | tf_op jit(solution)/shard_map/ppermute | solution.py:312
  247.9 13.4 %collective-permute-start.10 = (bf16[512,1536]{1,0:T(8,128)(2,1)}, bf16[512,1536]{1,0:T(8,128)(2,1)}, u32[]{:S(2)}, u32[]{:S(2)}) collective-permute-start(bf16[512,1536]{1,0:T(8,128)(2,1)} %pad_maximum_fusion.10), channel_id=1, source_target_pairs={{0,1},{1,0},{2,3},{3,2},{4,5},{5,4},{6,7},{7,6},{8,9},{9,8},{10,11... | collective-permute-start | bytes 4718600 | tf_op jit(solution)/shard_map/ppermute | solution.py:312
  254.1 6.9 collective-permute-start.13
  262.9 18.7 %collective-permute-start.11 = (bf16[256,1536]{1,0:T(8,128)(2,1)S(1)}, bf16[256,1536]{1,0:T(8,128)(2,1)S(1)}, u32[]{:S(2)}, u32[]{:S(2)}) collective-permute-start(bf16[256,1536]{1,0:T(8,128)(2,1)S(1)} %add_convert_fusion.9), channel_id=1, source_target_pairs={{0,2},{1,3},{2,0},{3,1},{4,6},{5,7},{6,4},{7,5},{8,10},{9,11},{10,... | collective-permute-start | bytes 2359304 | tf_op jit(solution)/shard_map/ppermute | solution.py:613
  265.8 80.0 %all-to-all-start.3 = ((bf16[8,40,1536]{2,1,0:T(8,128)(2,1)}), bf16[8,40,1536]{2,1,0:T(8,128)(2,1)}, u32[]{:S(2)}, u32[]{:S(2)}) async-start(bf16[8,40,1536]{2,1,0:T(8,128)(2,1)} %broadcast_in_dim.86), calls=%async_computation.3 | async-start | bytes 1966080 | tf_op jit(solution)/shard_map/all_to_all | solution.py:539
  285.4 60.3 %collective-permute-start.15 = (bf16[256,1536]{1,0:T(8,128)(2,1)}, bf16[256,1536]{1,0:T(8,128)(2,1)}, u32[]{:S(2)}, u32[]{:S(2)}) collective-permute-start(bf16[256,1536]{1,0:T(8,128)(2,1)} %add_convert_fusion.8), channel_id=1, source_target_pairs={{0,2},{1,3},{2,0},{3,1},{4,6},{5,7},{6,4},{7,5},{8,10},{9,11},{10,... | collective-permute-start | bytes 2359304 | tf_op jit(solution)/shard_map/ppermute | solution.py:295
  286.9 58.9 %collective-permute-start.14 = (bf16[256,1536]{1,0:T(8,128)(2,1)}, bf16[256,1536]{1,0:T(8,128)(2,1)}, u32[]{:S(2)}, u32[]{:S(2)}) collective-permute-start(bf16[256,1536]{1,0:T(8,128)(2,1)} %add_convert_fusion.8), channel_id=1, source_target_pairs={{0,1},{1,0},{2,3},{3,2},{4,5},{5,4},{6,7},{7,6},{8,9},{9,8},{10,11... | collective-permute-start | bytes 2359304 | tf_op jit(solution)/shard_map/ppermute | solution.py:294
  287.8 60.1 %collective-permute-start.18 = (bf16[256,1536]{1,0:T(8,128)(2,1)}, bf16[256,1536]{1,0:T(8,128)(2,1)}, u32[]{:S(2)}, u32[]{:S(2)}) collective-permute-start(bf16[256,1536]{1,0:T(8,128)(2,1)} %collective-permute-done.7), channel_id=1, source_target_pairs={{0,1},{1,0},{2,3},{3,2},{4,5},{5,4},{6,7},{7,6},{8,9},{9,8},{10,11... | collective-permute-start | bytes 2359304 | tf_op jit(solution)/shard_map/ppermute | solution.py:300
  288.4 61.6 %collective-permute-start.26 = (bf16[320,1536]{1,0:T(8,128)(2,1)}, bf16[320,1536]{1,0:T(8,128)(2,1)S(1)}, u32[]{:S(2)}, u32[]{:S(2)}) collective-permute-start(bf16[320,1536]{1,0:T(8,128)(2,1)} %collective-permute-done.9), channel_id=1, source_target_pairs={{0,1},{1,0},{2,3},{3,2},{4,5},{5,4},{6,7},{7,6},{8,9},{9,8},{10,11... | collective-permute-start | bytes 2949128 | tf_op jit(solution)/shard_map/ppermute | solution.py:300
  345.8 7.4 collective-permute-start.16
  351.1 50.1 %collective-permute-start.22 = (bf16[320,1536]{1,0:T(8,128)(2,1)}, bf16[320,1536]{1,0:T(8,128)(2,1)S(1)}, u32[]{:S(2)}, u32[]{:S(2)}) collective-permute-start(bf16[320,1536]{1,0:T(8,128)(2,1)} %bitcast.10), channel_id=1, source_target_pairs={{0,2},{1,3},{2,0},{3,1},{4,6},{5,7},{6,4},{7,5},{8,10},{9,11},{10,... | collective-permute-start | bytes 2949128 | tf_op jit(solution)/shard_map/ppermute | solution.py:295
  351.6 49.6 %collective-permute-start.21 = (bf16[320,1536]{1,0:T(8,128)(2,1)}, bf16[320,1536]{1,0:T(8,128)(2,1)S(1)}, u32[]{:S(2)}, u32[]{:S(2)}) collective-permute-start(bf16[320,1536]{1,0:T(8,128)(2,1)} %bitcast.10), channel_id=1, source_target_pairs={{0,1},{1,0},{2,3},{3,2},{4,5},{5,4},{6,7},{7,6},{8,9},{9,8},{10,11... | collective-permute-start | bytes 2949128 | tf_op jit(solution)/shard_map/ppermute | solution.py:294
  381.1 8.4 collective-permute-start.19
  388.9 47.4 %copy-start.20 = (bf16[1024,1536]{1,0:T(8,128)(2,1)}, bf16[1024,1536]{1,0:T(8,128)(2,1)S(1)}, u32[]{:S(2)}) copy-start(bf16[1024,1536]{1,0:T(8,128)(2,1)S(1)} %convolution_convert_fusion.7) | copy-start | bytes 9437188
  389.1 47.1 %collective-permute-start.17 = (bf16[512,1536]{1,0:T(8,128)(2,1)S(1)}, bf16[512,1536]{1,0:T(8,128)(2,1)S(1)}, u32[]{:S(2)}, u32[]{:S(2)}) collective-permute-start(bf16[512,1536]{1,0:T(8,128)(2,1)S(1)} %pad_maximum_fusion.11), channel_id=1, source_target_pairs={{0,1},{1,0},{2,3},{3,2},{4,5},{5,4},{6,7},{7,6},{8,9},{9,8},{10,11... | collective-permute-start | bytes 4718600 | tf_op jit(solution)/shard_map/ppermute | solution.py:312
  389.6 19.8 %collective-permute-start.20 = (bf16[256,1536]{1,0:T(8,128)(2,1)S(1)}, bf16[256,1536]{1,0:T(8,128)(2,1)S(1)}, u32[]{:S(2)}, u32[]{:S(2)}) collective-permute-start(bf16[256,1536]{1,0:T(8,128)(2,1)S(1)} %add_convert_fusion.7), channel_id=1, source_target_pairs={{0,2},{1,3},{2,0},{3,1},{4,6},{5,7},{6,4},{7,5},{8,10},{9,11},{10,... | collective-permute-start | bytes 2359304 | tf_op jit(solution)/shard_map/ppermute | solution.py:635
  410.8 2.6 collective-permute-start.27
  424.4 22.1 %collective-permute-start.28 = (bf16[640,1536]{1,0:T(8,128)(2,1)}, bf16[640,1536]{1,0:T(8,128)(2,1)}, u32[]{:S(2)}, u32[]{:S(2)}) collective-permute-start(bf16[640,1536]{1,0:T(8,128)(2,1)} %pad_maximum_fusion.8), channel_id=1, source_target_pairs={{0,1},{1,0},{2,3},{3,2},{4,5},{5,4},{6,7},{7,6},{8,9},{9,8},{10,11... | collective-permute-start | bytes 5898248 | tf_op jit(solution)/shard_map/ppermute | solution.py:312
  425.8 20.7 %collective-permute-start.24 = (bf16[256,1536]{1,0:T(8,128)(2,1)}, bf16[256,1536]{1,0:T(8,128)(2,1)}, u32[]{:S(2)}, u32[]{:S(2)}) collective-permute-start(bf16[256,1536]{1,0:T(8,128)(2,1)} %multiply_convert_fusion.1), channel_id=1, source_target_pairs={{0,2},{1,3},{2,0},{3,1},{4,6},{5,7},{6,4},{7,5},{8,10},{9,11},{10,... | collective-permute-start | bytes 2359304 | tf_op jit(solution)/shard_map/ppermute | solution.py:295
  427.3 19.2 %collective-permute-start.23 = (bf16[256,1536]{1,0:T(8,128)(2,1)}, bf16[256,1536]{1,0:T(8,128)(2,1)}, u32[]{:S(2)}, u32[]{:S(2)}) collective-permute-start(bf16[256,1536]{1,0:T(8,128)(2,1)} %multiply_convert_fusion.1), channel_id=1, source_target_pairs={{0,1},{1,0},{2,3},{3,2},{4,5},{5,4},{6,7},{7,6},{8,9},{9,8},{10,11... | collective-permute-start | bytes 2359304 | tf_op jit(solution)/shard_map/ppermute | solution.py:294
  437.7 218.1 %collective-permute-start.33 = (bf16[256,1536]{1,0:T(8,128)(2,1)}, bf16[256,1536]{1,0:T(8,128)(2,1)}, u32[]{:S(2)}, u32[]{:S(2)}) collective-permute-start(bf16[256,1536]{1,0:T(8,128)(2,1)} %add_convert_fusion.6), channel_id=1, source_target_pairs={{0,2},{1,3},{2,0},{3,1},{4,6},{5,7},{6,4},{7,5},{8,10},{9,11},{10,... | collective-permute-start | bytes 2359304 | tf_op jit(solution)/shard_map/ppermute | solution.py:665
  446.5 52.0 %collective-permute-start.25 = (bf16[256,1536]{1,0:T(8,128)(2,1)}, bf16[256,1536]{1,0:T(8,128)(2,1)}, u32[]{:S(2)}, u32[]{:S(2)}) collective-permute-start(bf16[256,1536]{1,0:T(8,128)(2,1)} %collective-permute-done.24), channel_id=1, source_target_pairs={{0,1},{1,0},{2,3},{3,2},{4,5},{5,4},{6,7},{7,6},{8,9},{9,8},{10,11... | collective-permute-start | bytes 2359304 | tf_op jit(solution)/shard_map/ppermute | solution.py:300
  449.2 34.7 %collective-permute-start.29 = (bf16[320,1536]{1,0:T(8,128)(2,1)}, bf16[320,1536]{1,0:T(8,128)(2,1)}, u32[]{:S(2)}, u32[]{:S(2)}) collective-permute-start(bf16[320,1536]{1,0:T(8,128)(2,1)} %add_convert_fusion.3), channel_id=1, source_target_pairs={{0,2},{1,3},{2,0},{3,1},{4,6},{5,7},{6,4},{7,5},{8,10},{9,11},{10,... | collective-permute-start | bytes 2949128 | tf_op jit(solution)/shard_map/ppermute | solution.py:656
  459.4 27.6 %copy-start.18 = (bf16[1280,1536]{1,0:T(8,128)(2,1)}, bf16[1280,1536]{1,0:T(8,128)(2,1)S(1)}, u32[]{:S(2)}) copy-start(bf16[1280,1536]{1,0:T(8,128)(2,1)S(1)} %convolution_convert_fusion.4) | copy-start | bytes 11796484
  486.9 28.6 %all-to-all-start.5 = ((bf16[8,40,1536]{2,1,0:T(8,128)(2,1)}), bf16[8,40,1536]{2,1,0:T(8,128)(2,1)}, u32[]{:S(2)}, u32[]{:S(2)}) async-start(bf16[8,40,1536]{2,1,0:T(8,128)(2,1)} %bitcast.154), calls=%async_computation.5 | async-start | bytes 1966080 | tf_op jit(solution)/shard_map/all_to_all | solution.py:544
  494.2 52.2 %collective-permute-start.34 = (bf16[640,1536]{1,0:T(8,128)(2,1)}, bf16[640,1536]{1,0:T(8,128)(2,1)}, u32[]{:S(2)}, u32[]{:S(2)}) collective-permute-start(bf16[640,1536]{1,0:T(8,128)(2,1)} %pad_maximum_fusion.9), channel_id=1, source_target_pairs={{0,1},{1,0},{2,3},{3,2},{4,5},{5,4},{6,7},{7,6},{8,9},{9,8},{10,11... | collective-permute-start | bytes 5898248 | tf_op jit(solution)/shard_map/ppermute | solution.py:312
  515.6 24.2 %all-to-all-start.10 = ((bf16[8,192,192]{2,1,0:T(8,128)(2,1)}), bf16[8,192,192]{2,1,0:T(8,128)(2,1)}, u32[]{:S(2)}, u32[]{:S(2)}) async-start(bf16[8,192,192]{2,1,0:T(8,128)(2,1)} %bitcast.156), calls=%async_computation.10 | async-start | bytes 1572864 | tf_op jit(solution)/shard_map/all_to_all | solution.py:697
  525.9 20.0 %collective-permute-start.31 = (bf16[64,1536]{1,0:T(8,128)(2,1)}, bf16[64,1536]{1,0:T(8,128)(2,1)}, u32[]{:S(2)}, u32[]{:S(2)}) collective-permute-start(bf16[64,1536]{1,0:T(8,128)(2,1)} %multiply_convert_fusion.3), channel_id=1, source_target_pairs={{0,2},{1,3},{2,0},{3,1},{4,6},{5,7},{6,4},{7,5},{8,10},{9,11},{10,... | collective-permute-start | bytes 589832 | tf_op jit(solution)/shard_map/ppermute | solution.py:295
  545.9 5.9 collective-permute-start.30
  545.9 5.9 collective-permute-start.32
  549.1 106.7 %collective-permute-start.35 = (bf16[320,1536]{1,0:T(8,128)(2,1)}, bf16[320,1536]{1,0:T(8,128)(2,1)}, u32[]{:S(2)}, u32[]{:S(2)}) collective-permute-start(bf16[320,1536]{1,0:T(8,128)(2,1)} %add_convert_fusion.1), channel_id=1, source_target_pairs={{0,2},{1,3},{2,0},{3,1},{4,6},{5,7},{6,4},{7,5},{8,10},{9,11},{10,... | collective-permute-start | bytes 2949128 | tf_op jit(solution)/shard_map/ppermute | solution.py:667
  664.4 30.4 %collective-permute-start.38 = (bf16[128,1536]{1,0:T(8,128)(2,1)}, bf16[128,1536]{1,0:T(8,128)(2,1)}, u32[]{:S(2)}, u32[]{:S(2)}) collective-permute-start(bf16[128,1536]{1,0:T(8,128)(2,1)} %pad_maximum_fusion.25), channel_id=1, source_target_pairs={{0,1},{1,0},{2,3},{3,2},{4,5},{5,4},{6,7},{7,6},{8,9},{9,8},{10,11... | collective-permute-start | bytes 1179656 | tf_op jit(solution)/shard_map/ppermute | solution.py:312
  666.5 29.9 %collective-permute-start.36 = (bf16[512,1536]{1,0:T(8,128)(2,1)}, bf16[512,1536]{1,0:T(8,128)(2,1)}, u32[]{:S(2)}, u32[]{:S(2)}) collective-permute-start(bf16[512,1536]{1,0:T(8,128)(2,1)} %pad_maximum_fusion.13), channel_id=1, source_target_pairs={{0,1},{1,0},{2,3},{3,2},{4,5},{5,4},{6,7},{7,6},{8,9},{9,8},{10,11... | collective-permute-start | bytes 4718600 | tf_op jit(solution)/shard_map/ppermute | solution.py:312
  686.0 117.1 %all-to-all-start.6 = ((bf16[8,40,1536]{2,1,0:T(8,128)(2,1)}), bf16[8,40,1536]{2,1,0:T(8,128)(2,1)}, u32[]{:S(2)}, u32[]{:S(2)}) async-start(bf16[8,40,1536]{2,1,0:T(8,128)(2,1)} %bitcast.18), calls=%async_computation.6 | async-start | bytes 1966080 | tf_op jit(solution)/shard_map/all_to_all | solution.py:544
  690.3 190.4 %all-gather.4.cloned.1.call-start = ((), (), s32[]{:S(2)}) async-start(), calls=%async_computation.11 | async-start | bytes 1966080 | tf_op jit(solution)/shard_map/all_gather | solution.py:737
  695.8 7.9 collective-permute-start.39
  698.8 106.6 %collective-permute-start.37 = (bf16[256,1536]{1,0:T(8,128)(2,1)}, bf16[256,1536]{1,0:T(8,128)(2,1)}, u32[]{:S(2)}, u32[]{:S(2)}) collective-permute-start(bf16[256,1536]{1,0:T(8,128)(2,1)} %add_convert_fusion.4), channel_id=1, source_target_pairs={{0,2},{1,3},{2,0},{3,1},{4,6},{5,7},{6,4},{7,5},{8,10},{9,11},{10,... | collective-permute-start | bytes 2359304 | tf_op jit(solution)/shard_map/ppermute | solution.py:688
  704.7 100.7 %copy-start.11 = (bf16[39,1536]{1,0:T(8,128)(2,1)S(1)}, bf16[39,1536]{1,0:T(8,128)(2,1)}, u32[]{:S(2)}) copy-start(bf16[39,1536]{1,0:T(8,128)(2,1)} %copy-done.9) | copy-start | bytes 359428
  704.7 100.7 %copy-start.56 = (f32[1536]{0:T(1024)S(1)}, f32[1536]{0:T(1024)}, u32[]{:S(2)}) copy-start(f32[1536]{0:T(1024)} %copy-done.55) | copy-start | bytes 18436
  704.7 100.7 %copy-start.94 = (f32[64]{0:T(128)S(1)}, f32[64]{0:T(128)}, u32[]{:S(2)}) copy-start(f32[64]{0:T(128)} %copy-done.92) | copy-start | bytes 772
  814.5 31.1 %all-to-all-start.7 = ((f32[4,2,6,384]{3,1,2,0:T(2,128)}), f32[4,2,6,384]{3,1,2,0:T(2,128)}, u32[]{:S(2)}, u32[]{:S(2)}) async-start(f32[4,2,6,384]{3,1,2,0:T(2,128)} %maximum_bitcast_fusion), calls=%async_computation.7 | async-start | bytes 147456 | tf_op jit(solution)/shard_map/all_to_all | solution.py:724
  848.9 13.5 %all-to-all-start.8 = ((bf16[8,2,6,384]{3,1,2,0:T(2,128)(2,1)}), bf16[8,2,6,384]{3,1,2,0:T(2,128)(2,1)}, u32[]{:S(2)}, u32[]{:S(2)}) async-start(bf16[8,2,6,384]{3,1,2,0:T(2,128)(2,1)} %broadcast_in_dim.101), calls=%async_computation.8 | async-start | bytes 147456 | tf_op jit(solution)/shard_map/all_to_all | solution.py:728
  864.4 9.8 %all-to-all-start.9 = ((f32[8,1,192]{2,1,0:T(1,128)}), f32[8,1,192]{2,1,0:T(1,128)S(1)}, u32[]{:S(2)}, u32[]{:S(2)}) async-start(f32[8,1,192]{2,1,0:T(1,128)} %copy.107), calls=%async_computation.9 | async-start | bytes 16384 | tf_op jit(solution)/shard_map/all_to_all | solution.py:731
  (119 other events, 775.7 us)
Sparse Core Ops, SparseCore 0:
  811.0 25.2 all-gather.3

commit v3 on v2

--- a/solution.py
+++ b/solution.py
@@ -286,6 +286,93 @@
     return held[: len(found)], held[len(found) :]
 
 
+def ring_to_dp(place, size):
+    return jnp.where(place < size // 2, 2 * place, 2 * (size - 1 - place) + 1)
+
+
+def dp_to_ring(index, size):
+    return jnp.where(index % 2 == 0, index // 2, size - 1 - index // 2)
+
+
+def ring_pairs(size, step):
+    order = list(range(0, size, 2)) + list(range(size - 1, 0, -2))
+    return [(order[p], order[(p + step) % size]) for p in range(size)]
+
+
+class GatherSteps:
+    def __init__(self, blocks, size):
+        self.size, self.step = size, 0
+        self.place = dp_to_ring(lax.axis_index("dp"), size)
+        if size != 8:
+            self.payload = ()
+            self.fulls = [lax.all_gather(block, "dp", axis=0, tiled=True) for block in blocks]
+            return
+        self.fulls = [
+            jnp.zeros((size * block.shape[0],) + block.shape[1:], block.dtype) for block in blocks
+        ]
+        self.payload = tuple(blocks) + tuple(blocks)
+        for i, block in enumerate(blocks):
+            self.put(i, block, self.place, 0)
+
+    def put(self, i, piece, at, offset):
+        rows = self.fulls[i].shape[0] // self.size
+        start = ring_to_dp(at % self.size, self.size) * rows + offset
+        self.fulls[i] = lax.dynamic_update_slice_in_dim(self.fulls[i], piece, start, 0)
+
+    def launch(self, payload):
+        self.step += 1
+        count = len(payload) // 2
+        if self.step == self.size // 2:
+            payload = [piece[: piece.shape[0] // 2] for piece in payload[:count]] + [
+                piece[piece.shape[0] // 2 :] for piece in payload[count:]
+            ]
+        return tuple(
+            lax.ppermute(piece, "dp", ring_pairs(self.size, 1 if i < count else -1))
+            for i, piece in enumerate(payload)
+        )
+
+    def land(self, got):
+        count = len(got) // 2
+        self.payload = got
+        for i, piece in enumerate(got):
+            direction = -1 if i < count else 1
+            half = self.step == self.size // 2 and i >= count
+            at = self.place + direction * self.step + self.size
+            self.put(i % count, piece, at, piece.shape[0] if half else 0)
+
+
+class Line:
+    def __init__(self):
+        self.jobs, self.flying, self.job = [], (), None
+
+    def add(self, job, steps):
+        if job.size == 8:
+            self.jobs += [job] * steps
+
+    def beat(self, *values):
+        count, flown = len(values), len(self.flying)
+        fresh = ()
+        if self.jobs and self.jobs[0] is not self.job:
+            fresh = tuple(self.jobs[0].payload)
+        held = tuple(values) + tuple(self.flying) + fresh
+        if held:
+            held = lax.optimization_barrier(held)
+        values = held[:count]
+        if flown:
+            self.job.land(held[count : count + flown])
+        self.flying = ()
+        if self.jobs:
+            job = self.jobs.pop(0)
+            self.flying = job.launch(job.payload if job is self.job else held[count + flown :])
+            self.job = job
+        return values[0] if count == 1 else values
+
+    def finish(self, job):
+        while job in self.jobs or (self.flying and self.job is job):
+            self.beat()
+        return job.fulls
+
+
 CORE = [(i, i ^ 1) for i in range(4)]
 CHIP = [(i, i ^ 2) for i in range(4)]
 
@@ -317,6 +404,135 @@
 def scatter_rows(partial):
     here, there = scatter_start(partial)
     return here + lax.ppermute(there, "tensor", CHIP).astype(WIDE)
+
+
+def tensor_peer(hop):
+    index = lax.axis_index("tensor")
+    if hop == 1:
+        return index + 1 - 2 * (index % 2)
+    return (index + 2) % 4 if hop == 2 else 3 - index
+
+
+def tail_kernel(columns, *refs):
+    here, there, text_first, scale, other, x_image, x_text, mid_image, mid_text = refs[:9]
+    grads, refs = refs[9:11], refs[11:]
+    image_grad, text_grad, mod_sum, mod_all, *sums = refs[:6]
+    far, terms, parts, low, slots, far_sem, part_sem, slot_sem = refs[6:14]
+    ring = ScatterRing(grads, sums, refs[14:])
+    me, index = lax.axis_index("dp"), lax.axis_index("tensor")
+    far_copy = pltpu.make_async_remote_copy(
+        src_ref=there, dst_ref=far, send_sem=far_sem.at[0], recv_sem=far_sem.at[1],
+        device_id=(me, tensor_peer(2)), device_id_type=MESH,
+    )
+
+    def part_copy(hop):
+        peer = tensor_peer(hop)
+        start = pl.multiple_of(peer * columns, LANES)
+        return pltpu.make_async_remote_copy(
+            src_ref=terms.at[:, pl.ds(start, columns)], dst_ref=parts.at[hop - 1],
+            send_sem=part_sem.at[0, hop - 1], recv_sem=part_sem.at[1, hop - 1],
+            device_id=(me, peer), device_id_type=MESH,
+        )
+
+    def slot_copy(hop):
+        return pltpu.make_async_remote_copy(
+            src_ref=low, dst_ref=slots.at[me],
+            send_sem=slot_sem.at[0, hop - 1], recv_sem=slot_sem.at[1, hop - 1],
+            device_id=((me + hop) % RING, index), device_id_type=MESH,
+        )
+
+    def rows_back(first, x, middle, gain):
+        x = x.astype(WIDE)
+        centred = x - jnp.mean(x, axis=-1, keepdims=True)
+        spread = lax.rsqrt(jnp.mean(centred * centred, axis=-1, keepdims=True) + EPS)
+        normed = centred * spread
+        wide = first * gain
+        inner = jnp.mean(wide, axis=-1, keepdims=True)
+        cross = jnp.mean(wide * normed, axis=-1, keepdims=True)
+        sums = jnp.sum(first, axis=0, keepdims=True), jnp.sum(first * normed, axis=0, keepdims=True)
+        return middle + (wide - inner - normed * cross) * spread, *sums
+
+    ring.load_all()
+    meet(
+        [(me, tensor_peer(hop)) for hop in (1, 2, 3)]
+        + [((me + hop) % RING, index) for hop in range(1, RING)]
+    )
+    far_copy.start()
+    ring.start()
+    ring.step(1)
+    far_copy.wait()
+    terms[...] = other[...]
+    chunk = 64
+
+    def image_chunk(at, totals):
+        rows = pl.ds(pl.multiple_of(at * chunk, chunk), chunk)
+        first = here[rows] + far[rows].astype(WIDE)
+        out, shift, gain = rows_back(first, x_image[rows], mid_image[rows], scale[0:1])
+        image_grad[rows] = out
+        return totals[0] + shift, totals[1] + gain
+
+    zero = jnp.zeros((1, here.shape[1]), WIDE)
+    shift, gain = lax.fori_loop(0, here.shape[0] // chunk, image_chunk, (zero, zero))
+    terms[0:1] = shift
+    terms[1:2] = gain
+    ring.step(2)
+    out, shift, gain = rows_back(text_first[...], x_text[...], mid_text[...], scale[1:2])
+    text_grad[...] = out
+    terms[6:7] = shift
+    terms[7:8] = gain
+    for hop in (1, 2, 3):
+        part_copy(hop).start()
+    ring.step(3)
+    for hop in (1, 2, 3):
+        part_copy(hop).wait()
+    own = terms[:, pl.ds(pl.multiple_of(index * columns, LANES), columns)]
+    total = own + parts[0] + parts[1] + parts[2]
+    mod_sum[...] = total
+    low[...] = total.astype(LOW)
+    slots[pl.ds(me, 1)] = total.astype(LOW)[None]
+    for hop in range(1, RING):
+        slot_copy(hop).start()
+    ring.step(4)
+    ring.step(5)
+    for hop in range(1, RING):
+        slot_copy(hop).wait()
+    mod_all[...] = slots[...]
+    ring.step(6)
+    ring.step(7)
+    ring.end()
+
+
+def tail_ring(here, there, text_first, scale, other, x, middle, grads, columns, ident):
+    width, shapes = here.shape[1], [grad.shape for grad in grads]
+    rows, text_rows = here.shape[0], text_first.shape[0]
+    found = pl.pallas_call(
+        functools.partial(tail_kernel, columns),
+        out_shape=[
+            jax.ShapeDtypeStruct((rows, width), WIDE),
+            jax.ShapeDtypeStruct((text_rows, width), WIDE),
+            jax.ShapeDtypeStruct((16, columns), WIDE),
+            jax.ShapeDtypeStruct((RING, 16, columns), LOW),
+            *[jax.ShapeDtypeStruct((r // RING, c), WIDE) for r, c in shapes],
+        ],
+        in_specs=[WHOLE] * 9 + [ANY] * len(grads),
+        out_specs=[WHOLE] * (4 + len(grads)),
+        scratch_shapes=[
+            pltpu.VMEM((rows, width), LOW),
+            pltpu.VMEM((16, width), WIDE),
+            pltpu.VMEM((3, 16, columns), WIDE),
+            pltpu.VMEM((16, columns), LOW),
+            pltpu.VMEM((RING, 16, columns), LOW),
+            pltpu.SemaphoreType.DMA((2,)),
+            pltpu.SemaphoreType.DMA((2, 3)),
+            pltpu.SemaphoreType.DMA((2, RING - 1)),
+            *ScatterRing.scratch(shapes),
+        ],
+        compiler_params=pltpu.CompilerParams(
+            collective_id=ident, has_side_effects=True, vmem_limit_bytes=VMEM_LIMIT
+        ),
+        name="tail_ring",
+    )(here, there, text_first, scale, other, *x, *middle, *grads)
+    return found
 
 
 def head_lanes(head):
@@ -347,6 +563,191 @@
     out_ref[...] = jnp.where(first, outs[0], outs[1]).astype(out_ref.dtype)
     flipped = jnp.where(first, totals[0], totals[1]).T
     lse_ref[0] = jnp.concatenate([flipped[:4], flipped[HEAD_DIM : HEAD_DIM + 4]], axis=0)
+
+
+def exchange_sums(part, sent, got, sems, me):
+    copy = pltpu.make_async_remote_copy(
+        src_ref=sent, dst_ref=got, send_sem=sems.at[0, 0], recv_sem=sems.at[1, 0],
+        device_id=(me, tensor_peer(1)), device_id_type=MESH,
+    )
+    sent[0] = part(1).astype(LOW)
+    sent[1] = part(3).astype(LOW)
+    copy.start()
+    return copy
+
+
+def middle_kernel(split, chunk, *refs):
+    bias_ref, q_ref, k_ref, v_ref, x_image, x_text, mods = refs[:7]
+    out_blocks, ffn_blocks, refs = refs[7:9], refs[9:11], refs[11:]
+    mixed, lse_ref, *wide_outs, text_in, image_in = refs[:8]
+    branch_image, branch_text, mid_image, mid_text = wide_outs
+    out_fulls, ffn_fulls, refs = refs[8:10], refs[10:12], refs[12:]
+    weights, sent, got, far_sent, far_got, here, mine = refs[:7]
+    sems, weight_sem, row_sem, own_sem = refs[7:11]
+    first = GatherRing(out_blocks, out_fulls, refs[11:14])
+    second = GatherRing(ffn_blocks, ffn_fulls, refs[14:17])
+    me = lax.axis_index("dp")
+    block = q_ref.shape[0]
+    pair, at = pl.program_id(0), pl.program_id(0) * 2 + pl.program_id(1)
+    rows = x_image.shape[0]
+
+    @pl.when(at == 0)
+    def _():
+        meet([*first.sides, *[(me, tensor_peer(hop)) for hop in (1, 2)]])
+        first.start()
+
+    for step in range(1, 5):
+
+        @pl.when(at == step)
+        def _():
+            first.step(step)
+
+    weight_copies = [
+        pltpu.make_async_copy(out_fulls[s], weights.at[s], weight_sem.at[s]) for s in range(2)
+    ]
+
+    @pl.when(at == 4)
+    def _():
+        first.end()
+        second.start()
+        for copy in weight_copies:
+            copy.start()
+
+    place = (
+        pl.ds(pl.multiple_of(pl.program_id(1) * block, block), block),
+        pl.ds(pl.multiple_of(pair * LANES, LANES), LANES),
+    )
+    attend_pair(split, bias_ref, q_ref, k_ref, v_ref, mixed.at[place], lse_ref)
+
+    @pl.when(at == 2 * pl.num_programs(0) - 1)
+    def _():
+        for copy in weight_copies:
+            copy.wait()
+        text_rows = x_text.shape[0]
+
+        def part(b):
+            image = dot(mixed[b * rows : (b + 1) * rows], weights[0], NN)
+            low = split + b * text_rows
+            text = dot(mixed[low : low + text_rows], weights[1], NN)
+            return jnp.concatenate([image, text], axis=0)
+
+        near = exchange_sums(part, sent, got, sems, me)
+        here[...] = part(0)
+        far_sent[...] = part(2).astype(LOW)
+        near.wait()
+        far_sent[...] = (far_sent[...].astype(WIDE) + got[1].astype(WIDE)).astype(LOW)
+        far = pltpu.make_async_remote_copy(
+            src_ref=far_sent, dst_ref=far_got, send_sem=sems.at[0, 1], recv_sem=sems.at[1, 1],
+            device_id=(me, tensor_peer(2)), device_id_type=MESH,
+        )
+        far.start()
+        here[...] += got[0].astype(WIDE)
+        second.step(1)
+        far.wait()
+
+        def norm_rows(x, branch, stream):
+            middle = x.astype(WIDE) + mods[3 * stream : 3 * stream + 1] * branch
+            centred = middle - jnp.mean(middle, axis=-1, keepdims=True)
+            spread = lax.rsqrt(jnp.mean(centred * centred, axis=-1, keepdims=True) + EPS)
+            gain, shift = mods[3 * stream + 1 : 3 * stream + 2], mods[3 * stream + 2 : 3 * stream + 3]
+            return middle, (centred * spread * gain + shift).astype(LOW)
+
+        def image_chunk(i, _):
+            some = pl.ds(pl.multiple_of(i * chunk, chunk), chunk)
+            branch = here[some] + far_got[some].astype(WIDE)
+            branch_image[some] = branch
+            middle, low = norm_rows(x_image[some], branch, 0)
+            mid_image[some] = middle
+            mine[some] = low
+            return 0
+
+        lax.fori_loop(0, rows // chunk, image_chunk, 0)
+
+        def row_copy(source, slot, hop, sem):
+            return pltpu.make_async_remote_copy(
+                src_ref=source, dst_ref=image_in.at[pl.ds(slot * rows, rows)],
+                send_sem=row_sem.at[0, sem], recv_sem=row_sem.at[1, sem],
+                device_id=(me, tensor_peer(hop)), device_id_type=MESH,
+            )
+
+        own = pltpu.make_async_copy(mine, image_in.at[pl.ds(0, rows)], own_sem.at[0])
+        to_far, to_near = row_copy(mine, 2, 2, 0), row_copy(mine, 1, 1, 1)
+        to_far.start()
+        to_near.start()
+        own.start()
+        branch = here[rows:] + far_got[rows:].astype(WIDE)
+        branch_text[...] = branch
+        middle, low = norm_rows(x_text[...], branch, 1)
+        mid_text[...] = middle
+        text_in[...] = low
+        second.step(2)
+        to_far.wait()
+        last = row_copy(image_in.at[pl.ds(2 * rows, rows)], 3, 1, 2)
+        last.start()
+        second.step(3)
+        own.wait()
+        to_near.wait()
+        last.wait()
+        second.step(4)
+        second.end()
+
+
+def middle_ring(joint, bias, x, mods, split, heads, out_blocks, ffn_blocks, ident):
+    rows, pairs, block = joint.shape[0], heads // 2, joint.shape[0] // 2
+    whole = lambda part: pl.BlockSpec((rows, LANES), lambda h, i: (0, part * pairs + h))
+    image_rows, width = x[0].shape
+    text_rows = x[1].shape[0]
+    both = image_rows + text_rows
+    depth = heads * HEAD_DIM
+    found = pl.pallas_call(
+        functools.partial(middle_kernel, split, 64),
+        grid=(pairs, 2),
+        in_specs=[
+            pl.BlockSpec((1, rows - split), lambda h, i: (0, 0)),
+            pl.BlockSpec((block, LANES), lambda h, i: (i, h)),
+            whole(1),
+            whole(2),
+            *[WHOLE] * 3,
+            *[ANY] * 4,
+        ],
+        out_specs=[
+            WHOLE,
+            pl.BlockSpec((1, 8, block), lambda h, i: (h, 0, i)),
+            *[WHOLE] * 5,
+            *[ANY] * 5,
+        ],
+        out_shape=[
+            jax.ShapeDtypeStruct((rows, depth), LOW),
+            jax.ShapeDtypeStruct((pairs, 8, rows), WIDE),
+            *[jax.ShapeDtypeStruct((n, width), WIDE) for n in (image_rows, text_rows) * 2],
+            jax.ShapeDtypeStruct((text_rows, width), LOW),
+            jax.ShapeDtypeStruct((4 * image_rows, width), LOW),
+            *[
+                jax.ShapeDtypeStruct((RING * b.shape[0], b.shape[1]), b.dtype)
+                for b in (*out_blocks, *ffn_blocks)
+            ],
+        ],
+        scratch_shapes=[
+            pltpu.VMEM((2, depth, width), LOW),
+            pltpu.VMEM((2, both, width), LOW),
+            pltpu.VMEM((2, both, width), LOW),
+            pltpu.VMEM((both, width), LOW),
+            pltpu.VMEM((both, width), LOW),
+            pltpu.VMEM((both, width), WIDE),
+            pltpu.VMEM((image_rows, width), LOW),
+            pltpu.SemaphoreType.DMA((2, 2)),
+            pltpu.SemaphoreType.DMA((2,)),
+            pltpu.SemaphoreType.DMA((2, 3)),
+            pltpu.SemaphoreType.DMA((1,)),
+            *GatherRing.scratch(2),
+            *GatherRing.scratch(2),
+        ],
+        compiler_params=pltpu.CompilerParams(
+            collective_id=ident, has_side_effects=True, vmem_limit_bytes=VMEM_LIMIT
+        ),
+        name="middle_ring",
+    )(bias, joint, joint, joint, *x, mods, *out_blocks, *ffn_blocks)
+    return found
 
 
 def attend_kernel(split, count, waits, *refs):
@@ -545,10 +946,16 @@
         total = jnp.sum(part.astype(WIDE), axis=0)
         return jnp.pad(total, ((0, text_rows - pool_rows), (0, 0)))
 
+    line = Line()
+    qkv_steps = GatherSteps(blocks_of(w_qkv), size)
+    line.add(qkv_steps, size // 2)
+    line.beat()
+
     cond_low = jax.nn.silu(cond).astype(LOW)
     cond_rows = lax.all_to_all(
         cond_low.reshape(seqs, ada_rows), "dp", split_axis=0, concat_axis=0, tiled=True
     )
+    cond_rows = line.beat(cond_rows)
     ada_low = w_ada.astype(LOW)
     mod_parts = jnp.einsum("nd,sdkf->nskf", cond_rows, ada_low, preferred_element_type=WIDE)
     mod_parts = lax.all_to_all(mod_parts, "dp", split_axis=0, concat_axis=0, tiled=True)
@@ -575,54 +982,55 @@
         (normed_in[s] * (1.0 + mod_row(s, 1)) + mod_row(s, 0)).astype(LOW) for s in range(2)
     ]
     ffn_grad = [(mod_row(s, 5) * cotangent[s]).astype(LOW) for s in range(2)]
+    first_in = line.beat(*first_in)
     moved = [gather_start(first_in[s]) for s in range(2)]
+    *image_moved, text_near, text_far = line.beat(*moved[0], *moved[1])
     pooled_grad = pool_start(ffn_grad[1])
-    ring = functools.partial(beside, gather_dp)
-    found, held = ring(
-        blocks_of(w_qkv) + blocks_of(w_out),
-        size,
-        1,
-        first_in + [ffn_grad[1]],
-        [*moved[0], *moved[1], pooled_grad, ffn_grad[0]],
-    )
-    qkv_full, out_full = found[:2], found[2:]
-    pooled_grad, image_ffn_grad = held[4:]
     attn_rows = [
-        gather_end(first_in[0], held[0], held[1]),
-        gather_end(first_in[1], held[2], held[3]),
+        gather_end(first_in[0], *image_moved),
+        gather_end(first_in[1], text_near, text_far),
     ]
+    qkv_full = line.finish(qkv_steps)
+    attn_rows = line.beat(*attn_rows)
     joint = jnp.concatenate(
         [dot(attn_rows[s], qkv_full[s], NN).astype(LOW) for s in range(2)], axis=0
     )
+    image_ffn_grad = ffn_grad[0]
     ffn_moved = gather_start(image_ffn_grad)
     text_ffn_moved = gather_start(pooled_grad)
+    ffn_blocks = [up_blocks[0], down_blocks[0]]
+    x_rows = [image[0], own_text(text[0])]
     if size == RING:
-        mixed, log_total, (up_full,) = attend(
-            joint, bias, split_at, heads_here, [up_blocks[0]], 2, (4,)
-        )
+        mods = jnp.concatenate(
+            [row for s in range(2) for row in (mod_row(s, 2), 1.0 + mod_row(s, 4), mod_row(s, 3))]
+            + [jnp.zeros((2, width), WIDE)],
+            axis=0,
+        )
+        found = middle_ring(
+            joint, bias, x_rows, mods, split_at, heads_here, blocks_of(w_out), ffn_blocks, 2
+        )
+        mixed, log_total, *found = found
+        branches, middle, text_in, mlp_rows = found[:2], found[2:4], found[4], found[5]
+        out_full, up_full, down_full = found[6:8], found[8], found[9]
     else:
         mixed, log_total, _ = attend(joint, bias, split_at, heads_here, [], 0, ())
-        (up_full,) = gather_dp([up_blocks[0]], size, 2)
+        *out_full, up_full, down_full = gather_dp(blocks_of(w_out) + ffn_blocks, size, 2)
+        branches = [
+            scatter_rows(dot(mixed[:split_at], out_full[0], NN)),
+            scatter_rows(dot(mixed[split_at:], out_full[1], NN)),
+        ]
+        middle = [streams[s] + mod_row(s, 2) * branches[s] for s in range(2)]
+        second_in = [
+            (layer_norm(middle[s]) * (1.0 + mod_row(s, 4)) + mod_row(s, 3)).astype(LOW)
+            for s in range(2)
+        ]
+        mlp_rows, text_in = gather_rows(second_in[0]), second_in[1]
     mixed, *ffn_moved = lax.optimization_barrier((mixed, *ffn_moved, *text_ffn_moved))
     mixed_rows = [mixed[:split_at], mixed[split_at:]]
     ffn_rows = gather_end(image_ffn_grad, *ffn_moved[:2])
     text_ffn_rows = gather_end(pooled_grad, *ffn_moved[2:])
-    branches = [None, None]
-    here, there = scatter_start(dot(mixed_rows[0], out_full[0], NN))
-    branches[1] = scatter_rows(dot(mixed_rows[1], out_full[1], NN))
-    far = lax.ppermute(there, "tensor", CHIP)
-    branches[0] = here + far.astype(WIDE)
-    middle = [streams[s] + mod_row(s, 2) * branches[s] for s in range(2)]
     normed_mid = [layer_norm(residual) for residual in middle]
-    second_in = [
-        (normed_mid[s] * (1.0 + mod_row(s, 4)) + mod_row(s, 3)).astype(LOW) for s in range(2)
-    ]
-    moved = gather_start(second_in[0])
-    pooled_in = pool_start(second_in[1])
-    (down_full,), (*moved, pooled_in) = ring(
-        [down_blocks[0]], size, 3, second_in, [*moved, pooled_in]
-    )
-    mlp_rows = gather_end(second_in[0], *moved)
+    pooled_in = pool_start(text_in)
     text_moved = gather_start(pooled_in)
 
     def gelu_back(pre_act, hidden_grad):
@@ -634,34 +1042,37 @@
     here, there = scatter_start(dot(pre_grad, up_full, NT))
     far = lax.ppermute(there, "tensor", CHIP)
     down_grad = dot(hidden, ffn_rows, TN).astype(LOW)
-    far, there, down_grad, *text_moved = lax.optimization_barrier(
-        (far, there, down_grad, *text_moved)
-    )
-    second_grad, ffn = [None, None], [None, None]
-    middle_grad, branch_grad = [None, None], [None, None]
-
-    def middle_back(s):
-        wide = second_grad[s] * (1.0 + mod_row(s, 4))
-        middle_grad[s] = cotangent[s] + jax.vjp(layer_norm, middle[s])[1](wide)[0]
-        branch_grad[s] = (mod_row(s, 2) * middle_grad[s]).astype(LOW)
-
-    second_grad[0] = here + far.astype(WIDE)
-    middle_back(0)
-    moved = gather_start(branch_grad[0])
+    there, down_grad, *text_moved = lax.optimization_barrier((there, down_grad, *text_moved))
     text_mlp_rows = gather_end(pooled_in, *text_moved)
     text_pre_act = dot(text_mlp_rows, text_up, NN)
     text_hidden = gelu_tanh(text_pre_act).astype(LOW)
     text_pre_grad = gelu_back(text_pre_act, dot(text_ffn_rows, text_down, NT))
     text_here, text_there = scatter_start(dot(text_pre_grad, text_up, NT))
     text_far = lax.ppermute(text_there, "tensor", CHIP)
+    (down_sum,), (far, text_far) = beside(
+        scatter_dp, [down_grad], size, 4, [there, text_there], [far, text_far]
+    )
+    second_grad, ffn = [None, None], [None, None]
+    middle_grad, branch_grad = [None, None], [None, None]
+
+    def middle_back(s):
+        wide = second_grad[s] * (1.0 + mod_row(s, 4))
+        middle_grad[s] = cotangent[s] + jax.vjp(layer_norm, middle[s])[1](wide)[0]
+        branch_grad[s] = (mod_row(s, 2) * middle_grad[s]).astype(LOW)
+
+    second_grad[1] = unpool_end(text_here + text_far.astype(WIDE))
+    second_grad[0] = here + far.astype(WIDE)
+    middle_back(0)
+    moved = gather_start(branch_grad[0])
     up_grad = dot(mlp_rows, pre_grad, TN).astype(LOW)
-    up_grad, text_far = lax.optimization_barrier((up_grad, text_far))
-    second_grad[1] = unpool_end(text_here + text_far.astype(WIDE))
     here, there = scatter_start(dot(hidden, down_full, NN))
-    moved = lax.optimization_barrier((*moved, there))[:2]
-    branch_rows = [gather_end(branch_grad[0], *moved), None]
+    up_grad, there, second_grad[1], *moved = lax.optimization_barrier(
+        (up_grad, there, second_grad[1], *moved)
+    )
     middle_back(1)
-    branch_rows[1] = gather_rows(branch_grad[1])
+    text_moved = gather_start(branch_grad[1])
+    branch_rows = [gather_end(branch_grad[0], *moved), gather_end(branch_grad[1], *text_moved)]
+    out_grad = [dot(mixed_rows[s], branch_rows[s], TN).astype(LOW) for s in range(2)]
     far = lax.ppermute(there, "tensor", CHIP)
     text_here, text_there = scatter_start(dot(text_hidden, text_down, NN))
     text_far = lax.ppermute(text_there, "tensor", CHIP)
@@ -669,63 +1080,68 @@
         [dot(branch_rows[s], out_full[s], NT).astype(LOW) for s in range(2)], axis=0
     )
     if size == RING:
-        grads, (down_sum, up_sum) = attend_back(
+        grads, (up_sum, *out_sum) = attend_back(
             joint, bias, mixed, mixed_grad, log_total, split_at, heads_here,
-            [down_grad, up_grad], 4, (3, 5),
+            [up_grad] + out_grad, 5, (2, 4),
         )
     else:
         grads, _ = attend_back(
             joint, bias, mixed, mixed_grad, log_total, split_at, heads_here, [], 0, ()
         )
-        down_sum, up_sum = scatter_dp([down_grad, up_grad], size, 4)
+        up_sum, *out_sum = scatter_dp([up_grad] + out_grad, size, 5)
     joint_grad = jnp.concatenate(grads, axis=1)
     joint_grad, far, text_far = lax.optimization_barrier((joint_grad, far, text_far))
     ffn[0] = here + far.astype(WIDE)
     ffn[1] = unpool_end(text_here + text_far.astype(WIDE))
     joint_rows = [joint_grad[:split_at], joint_grad[split_at:]]
+    qkv_grad = [dot(attn_rows[s], joint_rows[s], TN).astype(LOW) for s in range(2)]
     here, there = scatter_start(dot(joint_rows[0], qkv_full[0], NT))
     text_first = scatter_rows(dot(joint_rows[1], qkv_full[1], NT))
-    far = lax.ppermute(there, "tensor", CHIP)
-    qkv_grad = [dot(attn_rows[s], joint_rows[s], TN).astype(LOW) for s in range(2)]
-    out_grad = [dot(mixed_rows[s], branch_rows[s], TN).astype(LOW) for s in range(2)]
-    rest_sum, (far, text_first, ffn[1]) = beside(
-        scatter_dp,
-        qkv_grad + out_grad, size, 5, [there], [far, text_first, ffn[1]]
-    )
-    first_grad = [here + far.astype(WIDE), text_first]
+    results = [(middle[s] + mod_row(s, 5) * ffn[s]).astype(LOW) for s in range(2)]
     text_down_grad = dot(text_hidden, text_ffn_rows, TN)
     text_up_grad = lax.all_to_all(
         dot(text_mlp_rows, text_pre_grad, TN).astype(LOW).reshape(size, -1, units),
         "dp", split_axis=0, concat_axis=2, tiled=True,
-    ).reshape(-1, size * units).astype(WIDE)
-    results = [(middle[s] + mod_row(s, 5) * ffn[s]).astype(LOW) for s in range(2)]
-    input_grad = [
-        middle_grad[s]
-        + jax.vjp(layer_norm, streams[s])[1](first_grad[s] * (1.0 + mod_row(s, 1)))[0]
-        for s in range(2)
-    ]
-    mod_terms = jnp.stack(
-        [
-            jnp.stack(
-                [
-                    jnp.sum(first_grad[s], axis=0),
-                    jnp.sum(first_grad[s] * normed_in[s], axis=0),
-                    jnp.sum(middle_grad[s] * branches[s], axis=0),
-                    jnp.sum(second_grad[s], axis=0),
-                    jnp.sum(second_grad[s] * normed_mid[s], axis=0),
-                    jnp.sum(cotangent[s] * ffn[s], axis=0),
-                ]
-            )
-            for s in range(2)
+    )
+    other = []
+    for s in range(2):
+        other += [
+            jnp.zeros((2, width), WIDE),
+            jnp.sum(middle_grad[s] * branches[s], axis=0)[None],
+            jnp.sum(second_grad[s], axis=0)[None],
+            jnp.sum(second_grad[s] * normed_mid[s], axis=0)[None],
+            jnp.sum(cotangent[s] * ffn[s], axis=0)[None],
         ]
-    )
-    mod_split = mod_terms.reshape(2, 6, 4, width_here).transpose(2, 0, 1, 3)
-    mod_sum = jnp.sum(
-        lax.all_to_all(mod_split, "tensor", split_axis=0, concat_axis=0, tiled=True), axis=0
-    )
+    other = jnp.concatenate(other + [jnp.zeros((4, width), WIDE)], axis=0)
+    if size == RING:
+        scale = jnp.concatenate([1.0 + mod_row(s, 1) for s in range(2)], axis=0)
+        *input_grad, mod_sum, mod_grad, qkv_image, qkv_text = tail_ring(
+            here, there, text_first, scale, other, x_rows, middle_grad, qkv_grad, width_here, 6
+        )
+        qkv_sums = [qkv_image, qkv_text]
+        mod_sum = mod_sum[:12].reshape(2, 6, width_here)
+        mod_grad = mod_grad[:, :12].reshape(seqs, 2, 6, width_here)
+        mod_grad, text_up_grad = lax.optimization_barrier((mod_grad, text_up_grad))
+    else:
+        qkv_sums = scatter_dp(qkv_grad, size, 6)
+        far = lax.ppermute(there, "tensor", CHIP)
+        first_grad = [here + far.astype(WIDE), text_first]
+        input_grad, first_terms = [None, None], []
+        for s in range(2):
+            wide = first_grad[s] * (1.0 + mod_row(s, 1))
+            input_grad[s] = middle_grad[s] + jax.vjp(layer_norm, streams[s])[1](wide)[0]
+            shift = jnp.sum(first_grad[s], axis=0)
+            gain = jnp.sum(first_grad[s] * normed_in[s], axis=0)
+            first_terms.append(jnp.stack([shift, gain]))
+        mod_terms = other[:12].reshape(2, 6, width).at[:, :2].set(jnp.stack(first_terms))
+        mod_split = mod_terms.reshape(2, 6, 4, width_here).transpose(2, 0, 1, 3)
+        mod_sum = jnp.sum(
+            lax.all_to_all(mod_split, "tensor", split_axis=0, concat_axis=0, tiled=True), axis=0
+        )
+        mod_low = jnp.broadcast_to(mod_sum.astype(LOW)[None], (seqs,) + mod_sum.shape)
+        mod_grad = lax.all_to_all(mod_low, "dp", split_axis=0, concat_axis=0, tiled=True)
     shift_grad = mod_sum[:, 3]
-    mod_low = jnp.broadcast_to(mod_sum.astype(LOW)[None], (seqs,) + mod_sum.shape)
-    mod_grad = lax.all_to_all(mod_low, "dp", split_axis=0, concat_axis=0, tiled=True)
+    text_up_grad = text_up_grad.reshape(-1, size * units).astype(WIDE)
     ada_grad = jnp.einsum("nd,nskf->sdkf", cond_rows, mod_grad, preferred_element_type=WIDE)
     act_parts = jnp.einsum("nskf,sdkf->nd", mod_grad, ada_low, preferred_element_type=WIDE)
     act_parts = lax.all_to_all(act_parts, "dp", split_axis=0, concat_axis=0, tiled=True)
@@ -739,7 +1155,7 @@
 
     down_sum = jnp.stack([down_sum, text_down_grad])
     up_sum = jnp.stack([up_sum, text_up_grad])
-    qkv_sum, out_sum = jnp.stack(rest_sum[:2]), jnp.stack(rest_sum[2:])
+    qkv_sum, out_sum = jnp.stack(qkv_sums), jnp.stack(out_sum)
 
     return (
         results[0][None],

time: 899 us -> 795 us (0.88)
  Pallas kernels: 404 us -> 346 us
  waiting for transfers between devices: 88.2 us -> 46.2 us
  other arithmetic: 85.7 us -> 74.9 us
    pallas_call x1, Pallas kernels: 98.4 us -> 66.5 us  [scatter_ring(): pl.pallas_call(functools.partial(scatter_kernel, count), out_shape=[jax.S...]
    dynamic_update_slice x0 -> x17, local copies, waits for them, and re-layouts: none -> 24.8 us  [put(): lax.dynamic_update_slice_in_dim(self.fulls[i], piece, start, 0)]
    ppermute x2, waiting for transfers between devices: 23 us -> 0.01 us  [local(): text_far = lax.ppermute(text_there, 'tensor', CHIP)]
    ppermute x0 -> x16, starting transfers between devices: none -> 22.5 us  [launch(): lax.ppermute(piece, 'dp', ring_pairs(self.size, 1 if i < count else -1))]
    pallas_call x1, Pallas kernels: 98.4 us -> 76.6 us  [attend_back(): pl.pallas_call(functools.partial(attend_back_kernel, split, count, waits)...]
    ppermute x4 -> x2, waiting for transfers between devices: 19.6 us -> 0.01 us  [local(): far = lax.ppermute(there, 'tensor', CHIP)]
    unnamed x287 -> x211, local copies, waits for them, and re-layouts: 26.7 us -> 10.7 us
    ppermute x0 -> x16, waiting for transfers between devices: none -> 15.4 us  [launch(): lax.ppermute(piece, 'dp', ring_pairs(self.size, 1 if i < count else -1))]
  transfers between devices with their start and end apart: 52 -> 58, of which waited for: 12 -> 12; matrix products, arithmetic and copies ran while one was open for 28% -> 30% of each run, Pallas kernels for 45% -> 34%
where the time goes in v3:
time: 795 us; the launch traced here: 785 us
  Pallas kernels  346 us (44%)
  matrix products  114 us (14%)
  starting transfers between devices  86.3 us (11%)
  local copies, waits for them, and re-layouts  81.3 us (10%)
  other arithmetic  74.9 us (9%)
  waiting for transfers between devices  46.2 us (6%)
  blocking collectives  20.2 us (3%)
  between operations  16.1 us (2%)
    pallas_call x1, Pallas kernels, middle_ring(): pl.pallas_call(functools.partial(middle_kernel, split, 64), grid=(pairs,...  125 us
    dot_general x22, matrix products, dot(): lax.dot_general(left, right, (dims, ((), ())), preferred_element_type=WIDE)  109 us
    pallas_call x1, Pallas kernels, tail_ring(): pl.pallas_call(functools.partial(tail_kernel, columns), out_shape=[jax.Sh...  77.6 us
    pallas_call x1, Pallas kernels, attend_back(): pl.pallas_call(functools.partial(attend_back_kernel, split, count, waits)...  76.6 us
    pallas_call x1, Pallas kernels, scatter_ring(): pl.pallas_call(functools.partial(scatter_kernel, count), out_shape=[jax.S...  66.5 us
    dynamic_update_slice x17, local copies, waits for them, and re-layouts, put(): lax.dynamic_update_slice_in_dim(self.fulls[i], piece, start, 0)  24.8 us
    ppermute x16, starting transfers between devices, launch(): lax.ppermute(piece, 'dp', ring_pairs(self.size, 1 if i < count else -1))  22.5 us
  transfers between devices with their start and end apart: 58, of which 12 were waited for; matrix products, arithmetic and copies ran while one was open for 30% of the time, Pallas kernels for 34%

profile of v3, /device:TPU:0, one launch (start us, length us, event | category | flops | bytes accessed | tf_op | source)
XLA Modules:
  0.0 785.3 jit_solution(9688921035157880263)
XLA Ops:
  9.2 7.3 all-to-all-start
  19.1 2.1 collective-permute-start
  33.2 2.0 broadcast.449.clone
  36.0 2.1 broadcast.449.clone.1
  43.0 2.3 fusion.63
  46.1 4.5 all-to-all-start.1
  58.4 2.1 constant_dynamic-update-slice_fusion.6
  60.5 6.0 all-to-all-start.4
  66.6 5.3 all_gather.15
  79.6 2.2 collective-permute-start.12
  87.5 7.0 collective-permute-done.12
  94.4 4.5 collective-permute-start.15
  104.6 7.3 all-to-all-start.2
  118.3 3.0 collective-permute-start.21
  121.3 2.0 collective-permute-start.20
  132.7 4.7 collective-permute-done.20
  143.9 4.3 convolution_convert_fusion.12
  148.2 6.5 convolution_convert_fusion.8
  156.5 125.1 %middle_ring.1 = (bf16[1280,384]{1,0:T(8,128)(2,1)}, f32[3,8,1280]{2,1,0:T(8,128)}, f32[256,1536]{1,0:T(8,128)}, f32[64,1536]{1,0:T(8,128)}, f32[256,1536]{1,0:T...) custom-call(f32[1,256]{1,0:T(1,128)} %and_select_fusion.refs_0_, ...), custom_call_target="tpu_custom_call" | custom-call | tf_op jit(solution)/shard_map/middle_ring/pallas_call | solution.py:702
  283.6 4.5 all-to-all-start.3
  288.2 8.0 %fusion.99 = f32[1024,1536]{1,0:T(8,128)S(1)} fusion(bf16[1024,1536]{1,0:T(8,128)(2,1)} %get-tuple-element.116, bf16[1536,1536]{1,0:T(8,128)(2,1)} %get-tuple-element.117), kind=kOutput, calls=%fused_computation.250 | convolution fusion | flops 4831838208 | bytes 14155776 | tf_op jit(solution)/shard_map/dot_general | solution.py:21
  296.3 5.7 convolution_convert_fusion.7
  302.1 13.2 %fusion.6 = bf16[1024,1536]{1,0:T(8,128)(2,1)S(1)} fusion(f32[1024,1536]{1,0:T(8,128)} %copy-done.95, bf16[1536,1536]{1,0:T(8,128)(2,1)S(1)} %bitcast.159, bf16[256,1536]{1,0:T(8,128)(2,1)S(1)} %collective-permute-done.27, bf16[256,1536]{1,0:T(8,128)(2,1)} %collective-permute-done.24, bf16[256,1536]{1,0:T(8,128)(2,1)} %collective-permute-done.23, ...), kind=kOutput, calls=%fused_computation.14 | convolution fusion | flops 4875878400 | bytes 17301504 | tf_op jit(solution)/shard_map/dot_general | solution.py:21
  315.3 5.5 convolution_convert_fusion.6
  327.1 11.6 %convolution_convert_fusion.2.refs_0_ = bf16[1536,1536]{1,0:T(8,128)(2,1)} fusion(bf16[256,1536]{1,0:T(8,128)(2,1)} %copy-done.92, bf16[256,1536]{1,0:T(8,128)(2,1)} %collective-permute-done.24, bf16[256,1536]{1,0:T(8,128)(2,1)} %collective-permute-done.23, bf16[256,1536]{1,0:T(8,128)(2,1)} %fusion.17, f32[1024,1536]{1,0:T(8,128)} %copy-done.95), kind=kOutput, calls=%fused_computation.4 | convolution fusion | flops 4860936192 | bytes 14155776 | tf_op jit(solution)/shard_map/dot_general | solution.py:21
  338.7 2.5 add_convert_fusion.7
  341.2 8.6 %collective-permute-done.30 = bf16[320,1536]{1,0:T(8,128)(2,1)S(1)} collective-permute-done((bf16[320,1536]{1,0:T(8,128)(2,1)}, bf16[320,1536]{1,0:T(8,128)(2,1)S(1)}, u32[]{:S(2)}, u32[]{:S(2)}) %collective-permute-start.30) | collective-permute-done | bytes 983072 | tf_op jit(solution)/shard_map/ppermute | solution.py:382
  352.4 2.6 fusion.31
  356.4 3.6 fusion.28
  362.7 4.0 add_convert_fusion.6
  366.6 7.3 convolution_convert_fusion.1.refs_7_
  377.6 2.1 convolution_convert_fusion.14
  380.9 6.0 all-to-all-start.7
  386.9 2.6 convolution_convert_fusion.4
  392.8 66.5 %scatter_ring.1 = f32[192,1536]{1,0:T(8,128)} custom-call(bf16[1536,1536]{1,0:T(8,128)(2,1)} %convolution_convert_fusion.2.refs_0_), custom_call_target="tpu_custom_call" | custom-call | tf_op jit(solution)/shard_map/scatter_ring/pallas_call | solution.py:252
  459.3 2.7 multiply_reduce_fusion
  462.0 3.3 fusion.90
  465.9 2.8 add_convert_fusion.2
  468.7 4.4 all-to-all-start.5
  473.2 2.4 multiply_reduce_fusion.1
  479.6 3.8 convolution_bitcast_fusion
  484.8 2.5 all_to_all.67
  487.3 6.9 all-to-all-done.5
  499.9 2.4 add_convert_fusion.1
  512.7 3.4 convolution_convert_fusion.15
  516.1 4.0 convolution_convert_fusion.11.refs_8_
  521.2 76.6 %attend_back.1 = (bf16[1280,384]{1,0:T(8,128)(2,1)}, bf16[1280,384]{1,0:T(8,128)(2,1)}, bf16[1280,384]{1,0:T(8,128)(2,1)}, f32[192,1536]{1,0:T(8,128)}, f32[48,1536]{1,0:T(8,128)}, /*index=5*/f32[48,1536]{1,0:T(8,128)}) custom-call(f32[256,1]{1,0:T(8,128)} %fusion.58.refs_0_, bf16[1280,1152]{1,0:T(8,128)(2,1)} %pad_maximum_fusion.5.refs_1_.refs_2_.refs_3_, ...), custom_call_target="tpu_custom_call" | custom-call | tf_op jit(solution)/shard_map/attend_back/pallas_call | solution.py:887
  597.9 2.0 pad_maximum_fusion.6
  600.0 4.3 convolution_convert_fusion.13
  604.3 6.8 convolution_convert_fusion.9
  611.1 6.0 convolution_convert_fusion.refs_9_
  619.9 2.9 add_convert_fusion
  622.7 2.9 fusion.18
  626.2 3.7 all-to-all-start.6
  629.9 4.2 convolution_convert_fusion.3.refs_10_
  637.0 5.0 collective-permute-done.47
  643.7 3.2 add_convert_fusion.4
  647.0 7.5 all-to-all-done.6
  656.8 77.6 %tail_ring.1 = (f32[256,1536]{1,0:T(8,128)}, f32[64,1536]{1,0:T(8,128)}, f32[16,384]{1,0:T(8,128)}, bf16[8,16,384]{2,1,0:T(8,128)(2,1)}, f32[192,1152]{1,0:T(8,128)}, /*index=5*/f32[192,1152]{1,0:T(8,128)}) custom-call(f32[256,1536]{1,0:T(8,128)} %get-tuple-element.245.refs_0_, bf16[256,1536]{1,0:T(8,128)(2,1)} %get-tuple-element.244.refs_1_, ...), custom_call_target="tpu_custom_call" | custom-call | tf_op jit(solution)/shard_map/tail_ring/pallas_call | solution.py:508
  734.5 8.6 %all-gather = bf16[256,1536]{1,0:T(8,128)(2,1)S(1)} all-gather(bf16[64,1536]{1,0:T(8,128)(2,1)} %get-tuple-element.265), channel_id=2, replica_groups=mesh['dp'=8,'tensor'=4] {'tensor'}, dimensions={0}, use_global_device_ids=true | all-gather | bytes 983040 | tf_op jit(solution)/shard_map/all_gather | solution.py:1153
  749.3 3.5 all-to-all-start.8
  757.8 2.9 pad_maximum_fusion.8
  760.7 2.4 convolution_bitcast_fusion.1
  766.5 6.4 psum.7
  (447 shorter events, 149.2 us)
Async XLA Ops:
  9.2 32.3 %all-to-all-start = ((bf16[8,1,192]{2,1,0:T(2,128)(2,1)}), bf16[8,1,192]{2,1,0:T(2,128)(2,1)S(1)}, u32[]{:S(2)}, u32[]{:S(2)}) async-start(bf16[8,1,192]{2,1,0:T(2,128)(2,1)} %all_to_all.70), calls=%async_computation | async-start | bytes 16384 | tf_op jit(solution)/shard_map/all_to_all | solution.py:955
  19.1 22.4 %collective-permute-start = (bf16[192,1152]{1,0:T(8,128)(2,1)S(1)}, bf16[192,1152]{1,0:T(8,128)(2,1)}, u32[]{:S(2)}, u32[]{:S(2)}) collective-permute-start(bf16[192,1152]{1,0:T(8,128)(2,1)S(1)} %bitcast.140), channel_id=1, source_target_pairs={{0,8},{8,16},{16,24},{24,28},{28,20},{20,12},{12,4},{4,0},{1,9},{9... | collective-permute-start | bytes 1327112 | tf_op jit(solution)/shard_map/ppermute | solution.py:330
  21.2 20.3 %collective-permute-start.1 = (bf16[192,1152]{1,0:T(8,128)(2,1)S(1)}, bf16[192,1152]{1,0:T(8,128)(2,1)}, u32[]{:S(2)}, u32[]{:S(2)}) collective-permute-start(bf16[192,1152]{1,0:T(8,128)(2,1)S(1)} %bitcast.137), channel_id=1, source_target_pairs={{0,8},{8,16},{16,24},{24,28},{28,20},{20,12},{12,4},{4,0},{1,9},{9... | collective-permute-start | bytes 1327112 | tf_op jit(solution)/shard_map/ppermute | solution.py:330
  22.6 18.8 %collective-permute-start.2 = (bf16[192,1152]{1,0:T(8,128)(2,1)S(1)}, bf16[192,1152]{1,0:T(8,128)(2,1)}, u32[]{:S(2)}, u32[]{:S(2)}) collective-permute-start(bf16[192,1152]{1,0:T(8,128)(2,1)S(1)} %bitcast.141), channel_id=1, source_target_pairs={{0,4},{8,0},{16,8},{24,16},{28,24},{20,28},{12,20},{4,12},{1,5},{9... | collective-permute-start | bytes 1327112 | tf_op jit(solution)/shard_map/ppermute | solution.py:330
  23.2 19.8 %collective-permute-start.3 = (bf16[192,1152]{1,0:T(8,128)(2,1)S(1)}, bf16[192,1152]{1,0:T(8,128)(2,1)}, u32[]{:S(2)}, u32[]{:S(2)}) collective-permute-start(bf16[192,1152]{1,0:T(8,128)(2,1)S(1)} %bitcast.138), channel_id=1, source_target_pairs={{0,4},{8,0},{16,8},{24,16},{28,24},{20,28},{12,20},{4,12},{1,5},{9... | collective-permute-start | bytes 1327112 | tf_op jit(solution)/shard_map/ppermute | solution.py:330
  45.3 27.3 %copy-start.38 = (f32[64,1536]{1,0:T(8,128)S(1)}, f32[64,1536]{1,0:T(8,128)}, u32[]{:S(2)}) copy-start(f32[64,1536]{1,0:T(8,128)} %pad_convert_fusion) | copy-start | bytes 1179652
  46.1 27.2 %copy-start.6 = (bf16[1,256,1536]{2,1,0:T(8,128)(2,1)S(1)}, bf16[1,256,1536]{2,1,0:T(8,128)(2,1)}, u32[]{:S(2)}) copy-start(bf16[1,256,1536]{2,1,0:T(8,128)(2,1)} %param.18) | copy-start | bytes 2359300
  46.1 14.4 %all-to-all-start.1 = ((f32[8,2,6,384]{3,1,2,0:T(2,128)}), f32[8,2,6,384]{3,1,2,0:T(2,128)S(1)}, u32[]{:S(2)}, u32[]{:S(2)}) async-start(f32[8,2,6,384]{3,1,2,0:T(2,128)} %copy.85), calls=%async_computation.1 | async-start | bytes 294912 | tf_op jit(solution)/shard_map/all_to_all | solution.py:961
  50.6 26.1 %collective-permute-start.4 = (bf16[192,1152]{1,0:T(8,128)(2,1)}, bf16[192,1152]{1,0:T(8,128)(2,1)}, u32[]{:S(2)}, u32[]{:S(2)}) collective-permute-start(bf16[192,1152]{1,0:T(8,128)(2,1)} %collective-permute-done), channel_id=1, source_target_pairs={{0,8},{8,16},{16,24},{24,28},{28,20},{20,12},{12,4},{4,0},{1,9},{9... | collective-permute-start | bytes 1327112 | tf_op jit(solution)/shard_map/ppermute | solution.py:330
  52.6 24.1 %collective-permute-start.5 = (bf16[192,1152]{1,0:T(8,128)(2,1)}, bf16[192,1152]{1,0:T(8,128)(2,1)}, u32[]{:S(2)}, u32[]{:S(2)}) collective-permute-start(bf16[192,1152]{1,0:T(8,128)(2,1)} %collective-permute-done.1), channel_id=1, source_target_pairs={{0,8},{8,16},{16,24},{24,28},{28,20},{20,12},{12,4},{4,0},{1,9},{9... | collective-permute-start | bytes 1327112 | tf_op jit(solution)/shard_map/ppermute | solution.py:330
  54.1 22.6 %collective-permute-start.6 = (bf16[192,1152]{1,0:T(8,128)(2,1)}, bf16[192,1152]{1,0:T(8,128)(2,1)}, u32[]{:S(2)}, u32[]{:S(2)}) collective-permute-start(bf16[192,1152]{1,0:T(8,128)(2,1)} %collective-permute-done.2), channel_id=1, source_target_pairs={{0,4},{8,0},{16,8},{24,16},{28,24},{20,28},{12,20},{4,12},{1,5},{9... | collective-permute-start | bytes 1327112 | tf_op jit(solution)/shard_map/ppermute | solution.py:330
  54.7 22.6 %collective-permute-start.7 = (bf16[192,1152]{1,0:T(8,128)(2,1)}, bf16[192,1152]{1,0:T(8,128)(2,1)}, u32[]{:S(2)}, u32[]{:S(2)}) collective-permute-start(bf16[192,1152]{1,0:T(8,128)(2,1)} %collective-permute-done.3), channel_id=1, source_target_pairs={{0,4},{8,0},{16,8},{24,16},{28,24},{20,28},{12,20},{4,12},{1,5},{9... | collective-permute-start | bytes 1327112 | tf_op jit(solution)/shard_map/ppermute | solution.py:330
  60.5 42.2 %all-to-all-start.4 = ((bf16[192,8,192]{0,2,1:T(8,128)(2,1)}), bf16[192,8,192]{0,2,1:T(8,128)(2,1)S(1)}, u32[]{:S(2)}, u32[]{:S(2)}) async-start(bf16[192,8,192]{0,2,1:T(8,128)(2,1)} %bitcast.20), calls=%async_computation.4 | async-start | bytes 1572864 | tf_op jit(solution)/shard_map/all_to_all | solution.py:933
  76.0 28.5 %copy-start.55 = (f32[2,1536]{1,0:T(2,128)}, f32[2,1536]{1,0:T(2,128)S(1)}, u32[]{:S(2)}) copy-start(f32[2,1536]{1,0:T(2,128)S(1)} %broadcast.450) | copy-start | bytes 36868
  77.3 8.1 %collective-permute-start.11 = (bf16[64,1536]{1,0:T(8,128)(2,1)S(1)}, bf16[64,1536]{1,0:T(8,128)(2,1)S(1)}, u32[]{:S(2)}, u32[]{:S(2)}) collective-permute-start(bf16[64,1536]{1,0:T(8,128)(2,1)S(1)} %fusion.44), channel_id=1, source_target_pairs={{0,2},{1,3},{2,0},{3,1},{4,6},{5,7},{6,4},{7,5},{8,10},{9,11},{10,... | collective-permute-start | bytes 589832 | tf_op jit(solution)/shard_map/ppermute | solution.py:382
  78.8 8.5 %collective-permute-start.10 = (bf16[64,1536]{1,0:T(8,128)(2,1)S(1)}, bf16[64,1536]{1,0:T(8,128)(2,1)S(1)}, u32[]{:S(2)}, u32[]{:S(2)}) collective-permute-start(bf16[64,1536]{1,0:T(8,128)(2,1)S(1)} %fusion.44), channel_id=1, source_target_pairs={{0,1},{1,0},{2,3},{3,2},{4,5},{5,4},{6,7},{7,6},{8,9},{9,8},{10,11... | collective-permute-start | bytes 589832 | tf_op jit(solution)/shard_map/ppermute | solution.py:381
  78.8 36.6 %collective-permute-start.9 = (bf16[256,1536]{1,0:T(8,128)(2,1)S(1)}, bf16[256,1536]{1,0:T(8,128)(2,1)}, u32[]{:S(2)}, u32[]{:S(2)}) collective-permute-start(bf16[256,1536]{1,0:T(8,128)(2,1)S(1)} %fusion.16), channel_id=1, source_target_pairs={{0,2},{1,3},{2,0},{3,1},{4,6},{5,7},{6,4},{7,5},{8,10},{9,11},{10,... | collective-permute-start | bytes 2359304 | tf_op jit(solution)/shard_map/ppermute | solution.py:382
  79.3 36.0 %collective-permute-start.8 = (bf16[256,1536]{1,0:T(8,128)(2,1)S(1)}, bf16[256,1536]{1,0:T(8,128)(2,1)}, u32[]{:S(2)}, u32[]{:S(2)}) collective-permute-start(bf16[256,1536]{1,0:T(8,128)(2,1)S(1)} %fusion.16), channel_id=1, source_target_pairs={{0,1},{1,0},{2,3},{3,2},{4,5},{5,4},{6,7},{7,6},{8,9},{9,8},{10,11... | collective-permute-start | bytes 2359304 | tf_op jit(solution)/shard_map/ppermute | solution.py:381
  79.6 14.9 %collective-permute-start.12 = (bf16[192,1152]{1,0:T(8,128)(2,1)}, bf16[192,1152]{1,0:T(8,128)(2,1)S(1)}, u32[]{:S(2)}, u32[]{:S(2)}) collective-permute-start(bf16[192,1152]{1,0:T(8,128)(2,1)} %collective-permute-done.4), channel_id=1, source_target_pairs={{0,8},{8,16},{16,24},{24,28},{28,20},{20,12},{12,4},{4,0},{1,9},{9... | collective-permute-start | bytes 1327112 | tf_op jit(solution)/shard_map/ppermute | solution.py:330
  85.4 28.4 %collective-permute-start.13 = (bf16[192,1152]{1,0:T(8,128)(2,1)}, bf16[192,1152]{1,0:T(8,128)(2,1)}, u32[]{:S(2)}, u32[]{:S(2)}) collective-permute-start(bf16[192,1152]{1,0:T(8,128)(2,1)} %collective-permute-done.5), channel_id=1, source_target_pairs={{0,8},{8,16},{16,24},{24,28},{28,20},{20,12},{12,4},{4,0},{1,9},{9... | collective-permute-start | bytes 1327112 | tf_op jit(solution)/shard_map/ppermute | solution.py:330
  87.3 28.0 %collective-permute-start.14 = (bf16[192,1152]{1,0:T(8,128)(2,1)}, bf16[192,1152]{1,0:T(8,128)(2,1)}, u32[]{:S(2)}, u32[]{:S(2)}) collective-permute-start(bf16[192,1152]{1,0:T(8,128)(2,1)} %collective-permute-done.6), channel_id=1, source_target_pairs={{0,4},{8,0},{16,8},{24,16},{28,24},{20,28},{12,20},{4,12},{1,5},{9... | collective-permute-start | bytes 1327112 | tf_op jit(solution)/shard_map/ppermute | solution.py:330
  94.4 20.9 %collective-permute-start.15 = (bf16[192,1152]{1,0:T(8,128)(2,1)}, bf16[192,1152]{1,0:T(8,128)(2,1)}, u32[]{:S(2)}, u32[]{:S(2)}) collective-permute-start(bf16[192,1152]{1,0:T(8,128)(2,1)} %collective-permute-done.7), channel_id=1, source_target_pairs={{0,4},{8,0},{16,8},{24,16},{28,24},{20,28},{12,20},{4,12},{1,5},{9... | collective-permute-start | bytes 1327112 | tf_op jit(solution)/shard_map/ppermute | solution.py:330
  104.6 37.3 %all-to-all-start.2 = ((bf16[8,40,1536]{2,1,0:T(8,128)(2,1)}), bf16[8,40,1536]{2,1,0:T(8,128)(2,1)}, u32[]{:S(2)}, u32[]{:S(2)}) async-start(bf16[8,40,1536]{2,1,0:T(8,128)(2,1)} %broadcast_in_dim.92), calls=%async_computation.2 | async-start | bytes 1966080 | tf_op jit(solution)/shard_map/all_to_all | solution.py:940
  113.9 182.3 %collective-permute-start.24 = (bf16[256,1536]{1,0:T(8,128)(2,1)}, bf16[256,1536]{1,0:T(8,128)(2,1)}, u32[]{:S(2)}, u32[]{:S(2)}) collective-permute-start(bf16[256,1536]{1,0:T(8,128)(2,1)} %fusion.17), channel_id=1, source_target_pairs={{0,2},{1,3},{2,0},{3,1},{4,6},{5,7},{6,4},{7,5},{8,10},{9,11},{10,... | collective-permute-start | bytes 2359304 | tf_op jit(solution)/shard_map/ppermute | solution.py:382
  115.4 16.2 %collective-permute-start.17 = (bf16[64,1536]{1,0:T(8,128)(2,1)}, bf16[64,1536]{1,0:T(8,128)(2,1)S(1)}, u32[]{:S(2)}, u32[]{:S(2)}) collective-permute-start(bf16[64,1536]{1,0:T(8,128)(2,1)} %copy-done.51), channel_id=1, source_target_pairs={{0,1},{1,0},{2,3},{3,2},{4,5},{5,4},{6,7},{7,6},{8,9},{9,8},{10,11... | collective-permute-start | bytes 589832 | tf_op jit(solution)/shard_map/ppermute | solution.py:387
  118.3 13.8 %collective-permute-start.21 = (bf16[96,1152]{1,0:T(8,128)(2,1)S(1)}, bf16[96,1152]{1,0:T(8,128)(2,1)S(1)}, u32[]{:S(2)}, u32[]{:S(2)}) collective-permute-start(bf16[96,1152]{1,0:T(8,128)(2,1)S(1)} %slice.244), channel_id=1, source_target_pairs={{0,4},{8,0},{16,8},{24,16},{28,24},{20,28},{12,20},{4,12},{1,5},{9... | collective-permute-start | bytes 663560 | tf_op jit(solution)/shard_map/ppermute | solution.py:330
  121.3 10.9 %collective-permute-start.19 = (bf16[96,1152]{1,0:T(8,128)(2,1)S(1)}, bf16[96,1152]{1,0:T(8,128)(2,1)S(1)}, u32[]{:S(2)}, u32[]{:S(2)}) collective-permute-start(bf16[96,1152]{1,0:T(8,128)(2,1)S(1)} %slice.242), channel_id=1, source_target_pairs={{0,8},{8,16},{16,24},{24,28},{28,20},{20,12},{12,4},{4,0},{1,9},{9... | collective-permute-start | bytes 663560 | tf_op jit(solution)/shard_map/ppermute | solution.py:330
  121.3 16.1 %collective-permute-start.20 = (bf16[96,1152]{1,0:T(8,128)(2,1)S(1)}, bf16[96,1152]{1,0:T(8,128)(2,1)S(1)}, u32[]{:S(2)}, u32[]{:S(2)}) collective-permute-start(bf16[96,1152]{1,0:T(8,128)(2,1)S(1)} %slice.243), channel_id=1, source_target_pairs={{0,4},{8,0},{16,8},{24,16},{28,24},{20,28},{12,20},{4,12},{1,5},{9... | collective-permute-start | bytes 663560 | tf_op jit(solution)/shard_map/ppermute | solution.py:330
  131.6 7.4 collective-permute-start.18
  132.2 164.0 %collective-permute-start.23 = (bf16[256,1536]{1,0:T(8,128)(2,1)}, bf16[256,1536]{1,0:T(8,128)(2,1)}, u32[]{:S(2)}, u32[]{:S(2)}) collective-permute-start(bf16[256,1536]{1,0:T(8,128)(2,1)} %fusion.17), channel_id=1, source_target_pairs={{0,1},{1,0},{2,3},{3,2},{4,5},{5,4},{6,7},{7,6},{8,9},{9,8},{10,11... | collective-permute-start | bytes 2359304 | tf_op jit(solution)/shard_map/ppermute | solution.py:381
  132.2 10.1 %collective-permute-start.16 = (bf16[256,1536]{1,0:T(8,128)(2,1)}, bf16[256,1536]{1,0:T(8,128)(2,1)S(1)}, u32[]{:S(2)}, u32[]{:S(2)}) collective-permute-start(bf16[256,1536]{1,0:T(8,128)(2,1)} %collective-permute-done.9), channel_id=1, source_target_pairs={{0,1},{1,0},{2,3},{3,2},{4,5},{5,4},{6,7},{7,6},{8,9},{9,8},{10,11... | collective-permute-start | bytes 2359304 | tf_op jit(solution)/shard_map/ppermute | solution.py:387
  141.8 154.4 %collective-permute-start.26 = (bf16[320,1536]{1,0:T(8,128)(2,1)}, bf16[320,1536]{1,0:T(8,128)(2,1)}, u32[]{:S(2)}, u32[]{:S(2)}) collective-permute-start(bf16[320,1536]{1,0:T(8,128)(2,1)} %bitcast.16), channel_id=1, source_target_pairs={{0,2},{1,3},{2,0},{3,1},{4,6},{5,7},{6,4},{7,5},{8,10},{9,11},{10,... | collective-permute-start | bytes 2949128 | tf_op jit(solution)/shard_map/ppermute | solution.py:382
  142.4 153.8 %collective-permute-start.25 = (bf16[320,1536]{1,0:T(8,128)(2,1)}, bf16[320,1536]{1,0:T(8,128)(2,1)}, u32[]{:S(2)}, u32[]{:S(2)}) collective-permute-start(bf16[320,1536]{1,0:T(8,128)(2,1)} %bitcast.16), channel_id=1, source_target_pairs={{0,1},{1,0},{2,3},{3,2},{4,5},{5,4},{6,7},{7,6},{8,9},{9,8},{10,11... | collective-permute-start | bytes 2949128 | tf_op jit(solution)/shard_map/ppermute | solution.py:381
  283.6 42.3 %all-to-all-start.3 = ((bf16[8,40,1536]{2,1,0:T(8,128)(2,1)}), bf16[8,40,1536]{2,1,0:T(8,128)(2,1)}, u32[]{:S(2)}, u32[]{:S(2)}) async-start(bf16[8,40,1536]{2,1,0:T(8,128)(2,1)} %broadcast_in_dim.93), calls=%async_computation.3 | async-start | bytes 1966080 | tf_op jit(solution)/shard_map/all_to_all | solution.py:940
  296.2 5.8 collective-permute-start.27
  323.1 15.6 %collective-permute-start.28 = (bf16[512,1536]{1,0:T(8,128)(2,1)}, bf16[512,1536]{1,0:T(8,128)(2,1)}, u32[]{:S(2)}, u32[]{:S(2)}) collective-permute-start(bf16[512,1536]{1,0:T(8,128)(2,1)} %pad_maximum_fusion.13), channel_id=1, source_target_pairs={{0,1},{1,0},{2,3},{3,2},{4,5},{5,4},{6,7},{7,6},{8,9},{9,8},{10,11... | collective-permute-start | bytes 4718600 | tf_op jit(solution)/shard_map/ppermute | solution.py:399
  325.9 23.9 %collective-permute-start.30 = (bf16[320,1536]{1,0:T(8,128)(2,1)}, bf16[320,1536]{1,0:T(8,128)(2,1)S(1)}, u32[]{:S(2)}, u32[]{:S(2)}) collective-permute-start(bf16[320,1536]{1,0:T(8,128)(2,1)} %bitcast.18), channel_id=1, source_target_pairs={{0,2},{1,3},{2,0},{3,1},{4,6},{5,7},{6,4},{7,5},{8,10},{9,11},{10,... | collective-permute-start | bytes 2949128 | tf_op jit(solution)/shard_map/ppermute | solution.py:382
  327.1 22.8 %collective-permute-start.29 = (bf16[320,1536]{1,0:T(8,128)(2,1)}, bf16[320,1536]{1,0:T(8,128)(2,1)S(1)}, u32[]{:S(2)}, u32[]{:S(2)}) collective-permute-start(bf16[320,1536]{1,0:T(8,128)(2,1)} %bitcast.18), channel_id=1, source_target_pairs={{0,1},{1,0},{2,3},{3,2},{4,5},{5,4},{6,7},{7,6},{8,9},{9,8},{10,11... | collective-permute-start | bytes 2949128 | tf_op jit(solution)/shard_map/ppermute | solution.py:381
  349.9 2.6 collective-permute-start.32
  350.0 12.7 %collective-permute-start.22 = (bf16[512,1536]{1,0:T(8,128)(2,1)S(1)}, bf16[512,1536]{1,0:T(8,128)(2,1)S(1)}, u32[]{:S(2)}, u32[]{:S(2)}) collective-permute-start(bf16[512,1536]{1,0:T(8,128)(2,1)S(1)} %pad_maximum_fusion.12), channel_id=1, source_target_pairs={{0,1},{1,0},{2,3},{3,2},{4,5},{5,4},{6,7},{7,6},{8,9},{9,8},{10,11... | collective-permute-start | bytes 4718600 | tf_op jit(solution)/shard_map/ppermute | solution.py:399
  350.8 4.7 collective-permute-start.31
  361.6 13.5 %collective-permute-start.33 = (bf16[640,1536]{1,0:T(8,128)(2,1)S(1)}, bf16[640,1536]{1,0:T(8,128)(2,1)S(1)}, u32[]{:S(2)}, u32[]{:S(2)}) collective-permute-start(bf16[640,1536]{1,0:T(8,128)(2,1)S(1)} %pad_maximum_fusion.10), channel_id=1, source_target_pairs={{0,1},{1,0},{2,3},{3,2},{4,5},{5,4},{6,7},{7,6},{8,9},{9,8},{10,11... | collective-permute-start | bytes 5898248 | tf_op jit(solution)/shard_map/ppermute | solution.py:399
  374.0 85.3 %collective-permute-start.34 = (bf16[256,1536]{1,0:T(8,128)(2,1)}, bf16[256,1536]{1,0:T(8,128)(2,1)}, u32[]{:S(2)}, u32[]{:S(2)}) collective-permute-start(bf16[256,1536]{1,0:T(8,128)(2,1)} %add_convert_fusion.7), channel_id=1, source_target_pairs={{0,2},{1,3},{2,0},{3,1},{4,6},{5,7},{6,4},{7,5},{8,10},{9,11},{10,... | collective-permute-start | bytes 2359304 | tf_op jit(solution)/shard_map/ppermute | solution.py:1043
  376.7 82.6 %collective-permute-start.35 = (bf16[320,1536]{1,0:T(8,128)(2,1)}, bf16[320,1536]{1,0:T(8,128)(2,1)}, u32[]{:S(2)}, u32[]{:S(2)}) collective-permute-start(bf16[320,1536]{1,0:T(8,128)(2,1)} %add_convert_fusion.3), channel_id=1, source_target_pairs={{0,2},{1,3},{2,0},{3,1},{4,6},{5,7},{6,4},{7,5},{8,10},{9,11},{10,... | collective-permute-start | bytes 2949128 | tf_op jit(solution)/shard_map/ppermute | solution.py:1051
  380.9 87.8 %all-to-all-start.7 = ((bf16[8,192,192]{2,1,0:T(8,128)(2,1)}), bf16[8,192,192]{2,1,0:T(8,128)(2,1)S(1)}, u32[]{:S(2)}, u32[]{:S(2)}) async-start(bf16[8,192,192]{2,1,0:T(8,128)(2,1)} %bitcast.133), calls=%async_computation.7 | async-start | bytes 1572864 | tf_op jit(solution)/shard_map/all_to_all | solution.py:1102
  392.8 66.5 %copy-start.10 = (bf16[1024,1536]{1,0:T(8,128)(2,1)S(1)}, bf16[1024,1536]{1,0:T(8,128)(2,1)}, u32[]{:S(2)}) copy-start(bf16[1024,1536]{1,0:T(8,128)(2,1)} %copy-done.9) | copy-start | bytes 9437188
  392.8 66.5 %copy-start.75 = (f32[256]{0:T(256)S(1)}, f32[256]{0:T(256)}, u32[]{:S(2)}) copy-start(f32[256]{0:T(256)} %copy-done.74) | copy-start | bytes 3076
  392.8 66.5 %copy-start.80 = (f32[256]{0:T(256)S(1)}, f32[256]{0:T(256)}, u32[]{:S(2)}) copy-start(f32[256]{0:T(256)} %fusion.68) | copy-start | bytes 3076
  468.7 25.5 %all-to-all-start.5 = ((bf16[8,40,1536]{2,1,0:T(8,128)(2,1)}), bf16[8,40,1536]{2,1,0:T(8,128)(2,1)}, u32[]{:S(2)}, u32[]{:S(2)}) async-start(bf16[8,40,1536]{2,1,0:T(8,128)(2,1)} %bitcast.130), calls=%async_computation.5 | async-start | bytes 1966080 | tf_op jit(solution)/shard_map/all_to_all | solution.py:945
  476.6 19.2 %collective-permute-start.37 = (bf16[256,1536]{1,0:T(8,128)(2,1)}, bf16[256,1536]{1,0:T(8,128)(2,1)}, u32[]{:S(2)}, u32[]{:S(2)}) collective-permute-start(bf16[256,1536]{1,0:T(8,128)(2,1)} %multiply_convert_fusion.1), channel_id=1, source_target_pairs={{0,2},{1,3},{2,0},{3,1},{4,6},{5,7},{6,4},{7,5},{8,10},{9,11},{10,... | collective-permute-start | bytes 2359304 | tf_op jit(solution)/shard_map/ppermute | solution.py:382
  477.7 18.1 %collective-permute-start.36 = (bf16[256,1536]{1,0:T(8,128)(2,1)}, bf16[256,1536]{1,0:T(8,128)(2,1)}, u32[]{:S(2)}, u32[]{:S(2)}) collective-permute-start(bf16[256,1536]{1,0:T(8,128)(2,1)} %multiply_convert_fusion.1), channel_id=1, source_target_pairs={{0,1},{1,0},{2,3},{3,2},{4,5},{5,4},{6,7},{7,6},{8,9},{9,8},{10,11... | collective-permute-start | bytes 2359304 | tf_op jit(solution)/shard_map/ppermute | solution.py:381
  479.1 20.8 %collective-permute-start.43 = (bf16[640,1536]{1,0:T(8,128)(2,1)}, bf16[640,1536]{1,0:T(8,128)(2,1)}, u32[]{:S(2)}, u32[]{:S(2)}) collective-permute-start(bf16[640,1536]{1,0:T(8,128)(2,1)} %pad_maximum_fusion.11), channel_id=1, source_target_pairs={{0,1},{1,0},{2,3},{3,2},{4,5},{5,4},{6,7},{7,6},{8,9},{9,8},{10,11... | collective-permute-start | bytes 5898248 | tf_op jit(solution)/shard_map/ppermute | solution.py:399
  498.7 7.8 collective-permute-start.40
  502.3 97.6 %collective-permute-start.44 = (bf16[320,1536]{1,0:T(8,128)(2,1)}, bf16[320,1536]{1,0:T(8,128)(2,1)}, u32[]{:S(2)}, u32[]{:S(2)}) collective-permute-start(bf16[320,1536]{1,0:T(8,128)(2,1)} %add_convert_fusion.1), channel_id=1, source_target_pairs={{0,2},{1,3},{2,0},{3,1},{4,6},{5,7},{6,4},{7,5},{8,10},{9,11},{10,... | collective-permute-start | bytes 2949128 | tf_op jit(solution)/shard_map/ppermute | solution.py:1078
  504.4 6.1 collective-permute-start.39
  504.5 8.2 %collective-permute-start.38 = (bf16[256,1536]{1,0:T(8,128)(2,1)}, bf16[256,1536]{1,0:T(8,128)(2,1)S(1)}, u32[]{:S(2)}, u32[]{:S(2)}) collective-permute-start(bf16[256,1536]{1,0:T(8,128)(2,1)} %collective-permute-done.37), channel_id=1, source_target_pairs={{0,1},{1,0},{2,3},{3,2},{4,5},{5,4},{6,7},{7,6},{8,9},{9,8},{10,11... | collective-permute-start | bytes 2359304 | tf_op jit(solution)/shard_map/ppermute | solution.py:387
  506.5 4.0 collective-permute-start.41
  509.3 90.6 %collective-permute-start.42 = (bf16[256,1536]{1,0:T(8,128)(2,1)S(1)}, bf16[256,1536]{1,0:T(8,128)(2,1)}, u32[]{:S(2)}, u32[]{:S(2)}) collective-permute-start(bf16[256,1536]{1,0:T(8,128)(2,1)S(1)} %copy-done.41), channel_id=1, source_target_pairs={{0,2},{1,3},{2,0},{3,1},{4,6},{5,7},{6,4},{7,5},{8,10},{9,11},{10,... | collective-permute-start | bytes 2359304 | tf_op jit(solution)/shard_map/ppermute | solution.py:1076
  618.0 16.2 %collective-permute-start.46 = (bf16[128,1536]{1,0:T(8,128)(2,1)}, bf16[128,1536]{1,0:T(8,128)(2,1)}, u32[]{:S(2)}, u32[]{:S(2)}) collective-permute-start(bf16[128,1536]{1,0:T(8,128)(2,1)} %pad_maximum_fusion.31), channel_id=1, source_target_pairs={{0,1},{1,0},{2,3},{3,2},{4,5},{5,4},{6,7},{7,6},{8,9},{9,8},{10,11... | collective-permute-start | bytes 1179656 | tf_op jit(solution)/shard_map/ppermute | solution.py:399
  619.3 24.4 %collective-permute-start.45 = (bf16[512,1536]{1,0:T(8,128)(2,1)}, bf16[512,1536]{1,0:T(8,128)(2,1)}, u32[]{:S(2)}, u32[]{:S(2)}) collective-permute-start(bf16[512,1536]{1,0:T(8,128)(2,1)} %pad_maximum_fusion.14), channel_id=1, source_target_pairs={{0,1},{1,0},{2,3},{3,2},{4,5},{5,4},{6,7},{7,6},{8,9},{9,8},{10,11... | collective-permute-start | bytes 4718600 | tf_op jit(solution)/shard_map/ppermute | solution.py:399
  626.2 28.3 %all-to-all-start.6 = ((bf16[8,40,1536]{2,1,0:T(8,128)(2,1)}), bf16[8,40,1536]{2,1,0:T(8,128)(2,1)S(1)}, u32[]{:S(2)}, u32[]{:S(2)}) async-start(bf16[8,40,1536]{2,1,0:T(8,128)(2,1)} %bitcast.129), calls=%async_computation.6 | async-start | bytes 1966080 | tf_op jit(solution)/shard_map/all_to_all | solution.py:945
  629.9 143.6 %all-gather.4.cloned.1.call-start = ((), (), s32[]{:S(2)}) async-start(), calls=%async_computation.9 | async-start | bytes 1966080 | tf_op jit(solution)/shard_map/all_gather | solution.py:1153
  635.1 6.8 collective-permute-start.47
  749.3 17.1 %all-to-all-start.8 = ((f32[8,1,192]{2,1,0:T(1,128)}), f32[8,1,192]{2,1,0:T(1,128)S(1)}, u32[]{:S(2)}, u32[]{:S(2)}) async-start(f32[8,1,192]{2,1,0:T(1,128)} %copy.93), calls=%async_computation.8 | async-start | bytes 16384 | tf_op jit(solution)/shard_map/all_to_all | solution.py:1147
  (96 other events, 804.3 us)
Sparse Core Ops, SparseCore 0:
  734.6 18.1 all-gather.3

commit v4 on v3

--- a/solution.py
+++ b/solution.py
@@ -12,7 +12,7 @@
 LOW = jnp.bfloat16
 WIDE = jnp.float32
 TEXT_TILE = 64
-POOL_TILE = 8
+POOL_TILE = 16
 LANES = 128
 NT, NN, TN = ((1,), (1,)), ((1,), (0,)), ((0,), (0,))
 
@@ -286,93 +286,6 @@
     return held[: len(found)], held[len(found) :]
 
 
-def ring_to_dp(place, size):
-    return jnp.where(place < size // 2, 2 * place, 2 * (size - 1 - place) + 1)
-
-
-def dp_to_ring(index, size):
-    return jnp.where(index % 2 == 0, index // 2, size - 1 - index // 2)
-
-
-def ring_pairs(size, step):
-    order = list(range(0, size, 2)) + list(range(size - 1, 0, -2))
-    return [(order[p], order[(p + step) % size]) for p in range(size)]
-
-
-class GatherSteps:
-    def __init__(self, blocks, size):
-        self.size, self.step = size, 0
-        self.place = dp_to_ring(lax.axis_index("dp"), size)
-        if size != 8:
-            self.payload = ()
-            self.fulls = [lax.all_gather(block, "dp", axis=0, tiled=True) for block in blocks]
-            return
-        self.fulls = [
-            jnp.zeros((size * block.shape[0],) + block.shape[1:], block.dtype) for block in blocks
-        ]
-        self.payload = tuple(blocks) + tuple(blocks)
-        for i, block in enumerate(blocks):
-            self.put(i, block, self.place, 0)
-
-    def put(self, i, piece, at, offset):
-        rows = self.fulls[i].shape[0] // self.size
-        start = ring_to_dp(at % self.size, self.size) * rows + offset
-        self.fulls[i] = lax.dynamic_update_slice_in_dim(self.fulls[i], piece, start, 0)
-
-    def launch(self, payload):
-        self.step += 1
-        count = len(payload) // 2
-        if self.step == self.size // 2:
-            payload = [piece[: piece.shape[0] // 2] for piece in payload[:count]] + [
-                piece[piece.shape[0] // 2 :] for piece in payload[count:]
-            ]
-        return tuple(
-            lax.ppermute(piece, "dp", ring_pairs(self.size, 1 if i < count else -1))
-            for i, piece in enumerate(payload)
-        )
-
-    def land(self, got):
-        count = len(got) // 2
-        self.payload = got
-        for i, piece in enumerate(got):
-            direction = -1 if i < count else 1
-            half = self.step == self.size // 2 and i >= count
-            at = self.place + direction * self.step + self.size
-            self.put(i % count, piece, at, piece.shape[0] if half else 0)
-
-
-class Line:
-    def __init__(self):
-        self.jobs, self.flying, self.job = [], (), None
-
-    def add(self, job, steps):
-        if job.size == 8:
-            self.jobs += [job] * steps
-
-    def beat(self, *values):
-        count, flown = len(values), len(self.flying)
-        fresh = ()
-        if self.jobs and self.jobs[0] is not self.job:
-            fresh = tuple(self.jobs[0].payload)
-        held = tuple(values) + tuple(self.flying) + fresh
-        if held:
-            held = lax.optimization_barrier(held)
-        values = held[:count]
-        if flown:
-            self.job.land(held[count : count + flown])
-        self.flying = ()
-        if self.jobs:
-            job = self.jobs.pop(0)
-            self.flying = job.launch(job.payload if job is self.job else held[count + flown :])
-            self.job = job
-        return values[0] if count == 1 else values
-
-    def finish(self, job):
-        while job in self.jobs or (self.flying and self.job is job):
-            self.beat()
-        return job.fulls
-
-
 CORE = [(i, i ^ 1) for i in range(4)]
 CHIP = [(i, i ^ 2) for i in range(4)]
 
@@ -413,12 +326,13 @@
     return (index + 2) % 4 if hop == 2 else 3 - index
 
 
-def tail_kernel(columns, *refs):
-    here, there, text_first, scale, other, x_image, x_text, mid_image, mid_text = refs[:9]
-    grads, refs = refs[9:11], refs[11:]
-    image_grad, text_grad, mod_sum, mod_all, *sums = refs[:6]
-    far, terms, parts, low, slots, far_sem, part_sem, slot_sem = refs[6:14]
-    ring = ScatterRing(grads, sums, refs[14:])
+def tail_kernel(columns, count, *refs):
+    here, there, scale, other, x_image, x_text, mid_image, mid_text, text_out = refs[:9]
+    grads, refs = refs[9 : 9 + count], refs[9 + count :]
+    image_grad, mod_sum, mod_all, *wholes = refs[:5]
+    sums, refs = refs[5 : 5 + count], refs[5 + count :]
+    far, text_grad, terms, parts, low, slots, far_sem, part_sem, slot_sem, text_sem = refs[:10]
+    ring = ScatterRing(grads, sums, refs[10:])
     me, index = lax.axis_index("dp"), lax.axis_index("tensor")
     far_copy = pltpu.make_async_remote_copy(
         src_ref=there, dst_ref=far, send_sem=far_sem.at[0], recv_sem=far_sem.at[1],
@@ -440,6 +354,18 @@
             send_sem=slot_sem.at[0, hop - 1], recv_sem=slot_sem.at[1, hop - 1],
             device_id=((me + hop) % RING, index), device_id_type=MESH,
         )
+
+    def text_copy(i, hop):
+        source = (text_out, text_grad)[i]
+        return pltpu.make_async_remote_copy(
+            src_ref=source, dst_ref=wholes[i].at[index],
+            send_sem=text_sem.at[i, 0, hop], recv_sem=text_sem.at[i, 1, hop],
+            device_id=(me, tensor_peer(hop)), device_id_type=MESH,
+        )
+
+    def text_own(i):
+        source = (text_out, text_grad)[i]
+        return pltpu.make_async_copy(source, wholes[i].at[index], text_sem.at[i, 0, 0])
 
     def rows_back(first, x, middle, gain):
         x = x.astype(WIDE)
@@ -472,12 +398,18 @@
         return totals[0] + shift, totals[1] + gain
 
     zero = jnp.zeros((1, here.shape[1]), WIDE)
-    shift, gain = lax.fori_loop(0, here.shape[0] // chunk, image_chunk, (zero, zero))
+    image_rows = x_image.shape[0]
+    shift, gain = lax.fori_loop(0, image_rows // chunk, image_chunk, (zero, zero))
     terms[0:1] = shift
     terms[1:2] = gain
     ring.step(2)
-    out, shift, gain = rows_back(text_first[...], x_text[...], mid_text[...], scale[1:2])
+    text_first = here[image_rows:] + far[image_rows:].astype(WIDE)
+    out, shift, gain = rows_back(text_first, x_text[...], mid_text[...], scale[1:2])
     text_grad[...] = out
+    for i in range(2):
+        text_own(i).start()
+        for hop in (1, 2, 3):
+            text_copy(i, hop).start()
     terms[6:7] = shift
     terms[7:8] = gain
     for hop in (1, 2, 3):
@@ -498,26 +430,32 @@
         slot_copy(hop).wait()
     mod_all[...] = slots[...]
     ring.step(6)
+    for i in range(2):
+        text_own(i).wait()
+        for hop in (1, 2, 3):
+            text_copy(i, hop).wait()
     ring.step(7)
     ring.end()
 
 
-def tail_ring(here, there, text_first, scale, other, x, middle, grads, columns, ident):
+def tail_ring(here, there, scale, other, x, middle, text_out, grads, columns, ident):
     width, shapes = here.shape[1], [grad.shape for grad in grads]
-    rows, text_rows = here.shape[0], text_first.shape[0]
+    rows, text_rows = x[0].shape[0], x[1].shape[0]
     found = pl.pallas_call(
-        functools.partial(tail_kernel, columns),
+        functools.partial(tail_kernel, columns, len(grads)),
         out_shape=[
             jax.ShapeDtypeStruct((rows, width), WIDE),
-            jax.ShapeDtypeStruct((text_rows, width), WIDE),
             jax.ShapeDtypeStruct((16, columns), WIDE),
             jax.ShapeDtypeStruct((RING, 16, columns), LOW),
+            jax.ShapeDtypeStruct((4, text_rows, width), LOW),
+            jax.ShapeDtypeStruct((4, text_rows, width), WIDE),
             *[jax.ShapeDtypeStruct((r // RING, c), WIDE) for r, c in shapes],
         ],
         in_specs=[WHOLE] * 9 + [ANY] * len(grads),
-        out_specs=[WHOLE] * (4 + len(grads)),
+        out_specs=[WHOLE] * 3 + [ANY] * 2 + [WHOLE] * len(grads),
         scratch_shapes=[
-            pltpu.VMEM((rows, width), LOW),
+            pltpu.VMEM((rows + text_rows, width), LOW),
+            pltpu.VMEM((text_rows, width), WIDE),
             pltpu.VMEM((16, width), WIDE),
             pltpu.VMEM((3, 16, columns), WIDE),
             pltpu.VMEM((16, columns), LOW),
@@ -525,13 +463,14 @@
             pltpu.SemaphoreType.DMA((2,)),
             pltpu.SemaphoreType.DMA((2, 3)),
             pltpu.SemaphoreType.DMA((2, RING - 1)),
+            pltpu.SemaphoreType.DMA((2, 2, 4)),
             *ScatterRing.scratch(shapes),
         ],
         compiler_params=pltpu.CompilerParams(
             collective_id=ident, has_side_effects=True, vmem_limit_bytes=VMEM_LIMIT
         ),
         name="tail_ring",
-    )(here, there, text_first, scale, other, *x, *middle, *grads)
+    )(here, there, scale, other, *x, *middle, text_out, *grads)
     return found
 
 
@@ -563,6 +502,113 @@
     out_ref[...] = jnp.where(first, outs[0], outs[1]).astype(out_ref.dtype)
     flipped = jnp.where(first, totals[0], totals[1]).T
     lse_ref[0] = jnp.concatenate([flipped[:4], flipped[HEAD_DIM : HEAD_DIM + 4]], axis=0)
+
+
+def first_kernel(chunk, *refs):
+    x_image, x_text, cot_image, cot_text, mods, *blocks = refs[:7]
+    outs, fulls, refs = refs[7:10], refs[10:13], refs[13:]
+    mines, pooled, (row_sem, own_sem) = refs[:3], refs[3], refs[4:6]
+    ring = GatherRing([*blocks, pooled], fulls, refs[6:])
+    me = lax.axis_index("dp")
+
+    def row_copy(i, source, slot, hop, sem):
+        rows = mines[i].shape[0]
+        return pltpu.make_async_remote_copy(
+            src_ref=source, dst_ref=outs[i].at[pl.ds(slot * rows, rows)],
+            send_sem=row_sem.at[i, 0, sem], recv_sem=row_sem.at[i, 1, sem],
+            device_id=(me, tensor_peer(hop)), device_id_type=MESH,
+        )
+
+    def own(i):
+        rows = mines[i].shape[0]
+        return pltpu.make_async_copy(mines[i], outs[i].at[pl.ds(0, rows)], own_sem.at[i])
+
+    def to_far(i):
+        return row_copy(i, mines[i], 2, 2, 0)
+
+    def to_near(i):
+        return row_copy(i, mines[i], 1, 1, 1)
+
+    def forward(i):
+        rows = mines[i].shape[0]
+        return row_copy(i, outs[i].at[pl.ds(2 * rows, rows)], 3, 1, 2)
+
+    def send(i):
+        to_far(i).start()
+        to_near(i).start()
+        own(i).start()
+
+    def norm_rows(x, stream):
+        x = x.astype(WIDE)
+        centred = x - jnp.mean(x, axis=-1, keepdims=True)
+        spread = lax.rsqrt(jnp.mean(centred * centred, axis=-1, keepdims=True) + EPS)
+        gain, shift = mods[2 * stream : 2 * stream + 1], mods[2 * stream + 1 : 2 * stream + 2]
+        return (centred * spread * gain + shift).astype(LOW)
+
+    def over_chunks(body):
+        def step(i, _):
+            body(pl.ds(pl.multiple_of(i * chunk, chunk), chunk))
+            return 0
+
+        lax.fori_loop(0, x_image.shape[0] // chunk, step, 0)
+
+    meet([*ring.sides, *[(me, tensor_peer(hop)) for hop in (1, 2)]])
+    pooled[...] = (mods[5:6] * cot_text[: pooled.shape[0]].astype(WIDE)).astype(LOW)
+    ring.start()
+
+    def norm_chunk(some):
+        mines[0][some] = norm_rows(x_image[some], 0)
+
+    def grad_chunk(some):
+        mines[2][some] = (mods[4:5] * cot_image[some].astype(WIDE)).astype(LOW)
+
+    over_chunks(norm_chunk)
+    send(0)
+    mines[1][...] = norm_rows(x_text[...], 1)
+    send(1)
+    over_chunks(grad_chunk)
+    send(2)
+    ring.step(1)
+    for i in range(2):
+        to_far(i).wait()
+        forward(i).start()
+    ring.step(2)
+    to_far(2).wait()
+    forward(2).start()
+    ring.step(3)
+    for i in range(3):
+        own(i).wait()
+        to_near(i).wait()
+        forward(i).wait()
+    ring.step(4)
+    ring.end()
+
+
+def first_ring(x, cotangent, mods, blocks, pool_rows, ident):
+    width = mods.shape[1]
+    rows = [x[0].shape[0], x[1].shape[0], x[0].shape[0]]
+    fulls = [block.shape for block in blocks] + [(pool_rows, width)]
+    found = pl.pallas_call(
+        functools.partial(first_kernel, 64),
+        in_specs=[WHOLE] * 5 + [ANY] * 2,
+        out_specs=[ANY] * 6,
+        out_shape=[
+            *[jax.ShapeDtypeStruct((4 * n, width), LOW) for n in rows],
+            *[jax.ShapeDtypeStruct((RING * n, columns), LOW) for n, columns in fulls],
+        ],
+        scratch_shapes=[
+            *[pltpu.VMEM((n, width), LOW) for n in rows],
+            pltpu.VMEM((pool_rows, width), LOW),
+            pltpu.SemaphoreType.DMA((3, 2, 3)),
+            pltpu.SemaphoreType.DMA((3,)),
+            *GatherRing.scratch(3),
+        ],
+        compiler_params=pltpu.CompilerParams(
+            collective_id=ident, has_side_effects=True, vmem_limit_bytes=VMEM_LIMIT
+        ),
+        name="first_ring",
+    )(*x, *cotangent, mods, *blocks)
+    return found[:2], found[2], found[3:5], found[5]
 
 
 def exchange_sums(part, sent, got, sems, me):
@@ -747,6 +793,221 @@
         ),
         name="middle_ring",
     )(bias, joint, joint, joint, *x, mods, *out_blocks, *ffn_blocks)
+    return found
+
+
+def back_kernel(split, chunk, *refs):
+    bias_ref, q_ref, k_ref, v_ref, o_ref, lse_ref = refs[:6]
+    text_second, mid_image, mid_text, cot_image, cot_text, mods = refs[6:12]
+    partial, out_weights, grads, theirs, refs = refs[12], refs[13:15], refs[15:17], refs[17:19], refs[19:]
+    dq_ref, dk_ref, dv_ref, image_second, image_grad, text_grad = refs[:6]
+    image_rows, text_rows, *fars = refs[6:10]
+    sums, refs = refs[10:12], refs[12:]
+    dk_acc, dv_acc, weights, parts, got, far_sent, far_got, rows_in, mixed_grad = refs[:9]
+    part_sem, sems, row_sem, weight_sem, rows_sem, far_sem = refs[9:15]
+    ring = ScatterRing(grads, sums, refs[15:])
+    me = lax.axis_index("dp")
+    rows, texts = mid_image.shape[0], mid_text.shape[0]
+    block = q_ref.shape[0]
+    at = pl.program_id(0) * pl.num_programs(1) + pl.program_id(1)
+    last = pl.num_programs(0) * pl.num_programs(1) - 1
+
+    def part_of(b):
+        return partial.at[pl.ds(b * rows, rows)]
+
+    def keep(i):
+        return pltpu.make_async_copy(part_of(2 * i), parts.at[i], part_sem.at[i])
+
+    def near(i):
+        return pltpu.make_async_remote_copy(
+            src_ref=part_of(2 * i + 1), dst_ref=got.at[i],
+            send_sem=sems.at[0, i], recv_sem=sems.at[1, i],
+            device_id=(me, tensor_peer(1)), device_id_type=MESH,
+        )
+
+    def row_copy(source, slot, hop, sem):
+        return pltpu.make_async_remote_copy(
+            src_ref=source, dst_ref=rows_in.at[slot],
+            send_sem=row_sem.at[0, sem], recv_sem=row_sem.at[1, sem],
+            device_id=(me, tensor_peer(hop)), device_id_type=MESH,
+        )
+
+    def weight(s):
+        return pltpu.make_async_copy(out_weights[s], weights.at[s], weight_sem.at[s])
+
+    def save(b, s):
+        low, high, whole = ((0, rows, image_rows), (rows, texts, text_rows))[s]
+        return pltpu.make_async_copy(
+            rows_in.at[b, pl.ds(low, high)], whole.at[pl.ds(b * high, high)], rows_sem.at[s, b]
+        )
+
+    def rows_back(second, middle, cotangent, stream):
+        centred = middle - jnp.mean(middle, axis=-1, keepdims=True)
+        spread = lax.rsqrt(jnp.mean(centred * centred, axis=-1, keepdims=True) + EPS)
+        normed = centred * spread
+        wide = second * mods[2 * stream + 1 : 2 * stream + 2]
+        inner = jnp.mean(wide, axis=-1, keepdims=True)
+        cross = jnp.mean(wide * normed, axis=-1, keepdims=True)
+        grad = cotangent.astype(WIDE) + (wide - inner - normed * cross) * spread
+        return grad, (mods[2 * stream : 2 * stream + 1] * grad).astype(LOW)
+
+    @pl.when(at == 0)
+    def _():
+        for i in range(2):
+            keep(i).start()
+            weight(i).start()
+        ring.load_all()
+        meet([*ring.sides, *[(me, tensor_peer(hop)) for hop in (1, 2)]])
+        for i in range(2):
+            near(i).start()
+        ring.start()
+        for i in range(2):
+            keep(i).wait()
+            near(i).wait()
+        far_sent[...] = (parts[1].astype(WIDE) + got[1].astype(WIDE)).astype(LOW)
+        far = pltpu.make_async_remote_copy(
+            src_ref=far_sent, dst_ref=far_got, send_sem=sems.at[0, 2], recv_sem=sems.at[1, 2],
+            device_id=(me, tensor_peer(2)), device_id_type=MESH,
+        )
+        far.start()
+        grad, low = rows_back(text_second[...], mid_text[...], cot_text[...], 1)
+        text_grad[...] = grad
+        rows_in[0, rows:] = low
+        ring.step(1)
+        far.wait()
+
+        def image_chunk(i, _):
+            some = pl.ds(pl.multiple_of(i * chunk, chunk), chunk)
+            second = parts[0, some].astype(WIDE) + got[0, some].astype(WIDE)
+            second = second + far_got[some].astype(WIDE)
+            image_second[some] = second
+            grad, low = rows_back(second, mid_image[some], cot_image[some], 0)
+            image_grad[some] = grad
+            rows_in[0, some] = low
+            return 0
+
+        lax.fori_loop(0, rows // chunk, image_chunk, 0)
+        to_far = row_copy(rows_in.at[0], 2, 2, 0)
+        to_near = row_copy(rows_in.at[0], 1, 1, 1)
+        to_far.start()
+        to_near.start()
+        ring.step(2)
+        to_far.wait()
+        forward = row_copy(rows_in.at[2], 3, 1, 2)
+        forward.start()
+        for i in range(2):
+            weight(i).wait()
+        to_near.wait()
+
+        def through(b):
+            image = dot(rows_in[b, :rows], weights[0], NT).astype(LOW)
+            mixed_grad[b * rows : (b + 1) * rows] = image
+            text = dot(rows_in[b, rows:], weights[1], NT).astype(LOW)
+            mixed_grad[split + b * texts : split + (b + 1) * texts] = text
+
+        for b in range(3):
+            through(b)
+        ring.step(3)
+        forward.wait()
+        through(3)
+        for b in range(4):
+            for s in range(2):
+                save(b, s).start()
+
+    far_copies = [
+        pltpu.make_async_remote_copy(
+            src_ref=theirs[s], dst_ref=fars[s], send_sem=far_sem.at[0, s], recv_sem=far_sem.at[1, s],
+            device_id=(me, tensor_peer(2)), device_id_type=MESH,
+        )
+        for s in range(2)
+    ]
+
+    @pl.when(at == 1)
+    def _():
+        for copy in far_copies:
+            copy.start()
+
+    for step, when in ((4, 3), (5, 8), (6, 13)):
+
+        @pl.when(at == when)
+        def _():
+            ring.step(step)
+
+    place = (
+        pl.ds(pl.multiple_of(pl.program_id(1) * block, block), block),
+        pl.ds(pl.multiple_of(pl.program_id(0) * LANES, LANES), LANES),
+    )
+    attend_back_pair(
+        split,
+        (bias_ref, q_ref, k_ref, v_ref, o_ref, mixed_grad.at[place], lse_ref)
+        + (dq_ref, dk_ref, dv_ref, dk_acc, dv_acc),
+    )
+
+    @pl.when(at == last)
+    def _():
+        ring.step(7)
+        ring.end()
+        for copy in far_copies:
+            copy.wait()
+        for b in range(4):
+            for s in range(2):
+                save(b, s).wait()
+
+
+def back_ring(
+    joint, bias, mixed, lse, split, heads, text_second, middle, cotangent, mods, partial,
+    out_weights, grads, theirs, ident, block=256,
+):
+    rows, pairs = joint.shape[0], heads // 2
+    whole = lambda part: pl.BlockSpec((rows, LANES), lambda h, i: (0, part * pairs + h))
+    some = pl.BlockSpec((block, LANES), lambda h, i: (i, h))
+    image_rows, width = middle[0].shape
+    texts = middle[1].shape[0]
+    depth = heads * HEAD_DIM
+    found = pl.pallas_call(
+        functools.partial(back_kernel, split, 64),
+        grid=(pairs, rows // block),
+        in_specs=[
+            pl.BlockSpec((rows - split, 1), lambda h, i: (0, 0)),
+            some,
+            whole(1),
+            whole(2),
+            some,
+            pl.BlockSpec((1, 8, block), lambda h, i: (h, 0, i)),
+            *[WHOLE] * 6,
+            *[ANY] * 7,
+        ],
+        out_specs=[some, whole(0), whole(0), *[WHOLE] * 3, *[ANY] * 4, WHOLE, WHOLE],
+        out_shape=[
+            *[jax.ShapeDtypeStruct((rows, depth), LOW)] * 3,
+            *[jax.ShapeDtypeStruct((n, width), WIDE) for n in (image_rows, image_rows, texts)],
+            *[jax.ShapeDtypeStruct((4 * n, width), LOW) for n in (image_rows, texts)],
+            *[jax.ShapeDtypeStruct(t.shape, t.dtype) for t in theirs],
+            *[jax.ShapeDtypeStruct((g.shape[0] // RING, g.shape[1]), WIDE) for g in grads],
+        ],
+        scratch_shapes=[
+            *[pltpu.VMEM((rows, LANES), WIDE)] * 2,
+            pltpu.VMEM((2, depth, width), LOW),
+            *[pltpu.VMEM((2, image_rows, width), LOW)] * 2,
+            *[pltpu.VMEM((image_rows, width), LOW)] * 2,
+            pltpu.VMEM((4, image_rows + texts, width), LOW),
+            pltpu.VMEM((rows, depth), LOW),
+            pltpu.SemaphoreType.DMA((2,)),
+            pltpu.SemaphoreType.DMA((2, 3)),
+            pltpu.SemaphoreType.DMA((2, 3)),
+            pltpu.SemaphoreType.DMA((2,)),
+            pltpu.SemaphoreType.DMA((2, 4)),
+            pltpu.SemaphoreType.DMA((2, 2)),
+            *ScatterRing.scratch([g.shape for g in grads]),
+        ],
+        compiler_params=pltpu.CompilerParams(
+            collective_id=ident, has_side_effects=True, vmem_limit_bytes=VMEM_LIMIT
+        ),
+        name="back_ring",
+    )(
+        bias.T, joint, joint, joint, mixed, lse, text_second, *middle, *cotangent, mods,
+        partial, *out_weights, *grads, *theirs,
+    )
     return found
 
 
@@ -940,22 +1201,17 @@
         rows = lax.all_to_all(copies, "dp", split_axis=0, concat_axis=0, tiled=True)
         return rows.reshape(-1, width)
 
-    def unpool_end(part):
-        part = part.astype(LOW).reshape(size, pool_rows, width)
+    def unpool_end(here, far):
+        part = (here + far.astype(WIDE)).astype(LOW).reshape(size, pool_rows, width)
         part = lax.all_to_all(part, "dp", split_axis=0, concat_axis=0, tiled=True)
         total = jnp.sum(part.astype(WIDE), axis=0)
         return jnp.pad(total, ((0, text_rows - pool_rows), (0, 0)))
 
-    line = Line()
-    qkv_steps = GatherSteps(blocks_of(w_qkv), size)
-    line.add(qkv_steps, size // 2)
-    line.beat()
 
     cond_low = jax.nn.silu(cond).astype(LOW)
     cond_rows = lax.all_to_all(
         cond_low.reshape(seqs, ada_rows), "dp", split_axis=0, concat_axis=0, tiled=True
     )
-    cond_rows = line.beat(cond_rows)
     ada_low = w_ada.astype(LOW)
     mod_parts = jnp.einsum("nd,sdkf->nskf", cond_rows, ada_low, preferred_element_type=WIDE)
     mod_parts = lax.all_to_all(mod_parts, "dp", split_axis=0, concat_axis=0, tiled=True)
@@ -982,24 +1238,23 @@
         (normed_in[s] * (1.0 + mod_row(s, 1)) + mod_row(s, 0)).astype(LOW) for s in range(2)
     ]
     ffn_grad = [(mod_row(s, 5) * cotangent[s]).astype(LOW) for s in range(2)]
-    first_in = line.beat(*first_in)
-    moved = [gather_start(first_in[s]) for s in range(2)]
-    *image_moved, text_near, text_far = line.beat(*moved[0], *moved[1])
-    pooled_grad = pool_start(ffn_grad[1])
-    attn_rows = [
-        gather_end(first_in[0], *image_moved),
-        gather_end(first_in[1], text_near, text_far),
-    ]
-    qkv_full = line.finish(qkv_steps)
-    attn_rows = line.beat(*attn_rows)
+    cot_rows = [grad_image[0], own_text(grad_text[0])]
+    x_rows = [image[0], own_text(text[0])]
+    if size == RING:
+        mods = [1.0 + mod_row(0, 1), mod_row(0, 0), 1.0 + mod_row(1, 1), mod_row(1, 0)]
+        mods += [mod_row(0, 5), mod_row(1, 5), jnp.zeros((2, width), WIDE)]
+        attn_rows, ffn_rows, qkv_full, pooled_grad = first_ring(
+            x_rows, cot_rows, jnp.concatenate(mods, axis=0), blocks_of(w_qkv), pool_rows, 1
+        )
+    else:
+        attn_rows = [gather_rows(rows) for rows in first_in]
+        ffn_rows, pooled_grad = gather_rows(ffn_grad[0]), pool_start(ffn_grad[1])
+        qkv_full = gather_dp(blocks_of(w_qkv), size, 1)
     joint = jnp.concatenate(
         [dot(attn_rows[s], qkv_full[s], NN).astype(LOW) for s in range(2)], axis=0
     )
-    image_ffn_grad = ffn_grad[0]
-    ffn_moved = gather_start(image_ffn_grad)
     text_ffn_moved = gather_start(pooled_grad)
     ffn_blocks = [up_blocks[0], down_blocks[0]]
-    x_rows = [image[0], own_text(text[0])]
     if size == RING:
         mods = jnp.concatenate(
             [row for s in range(2) for row in (mod_row(s, 2), 1.0 + mod_row(s, 4), mod_row(s, 3))]
@@ -1025,83 +1280,97 @@
             for s in range(2)
         ]
         mlp_rows, text_in = gather_rows(second_in[0]), second_in[1]
-    mixed, *ffn_moved = lax.optimization_barrier((mixed, *ffn_moved, *text_ffn_moved))
+    mixed, *text_ffn_moved = lax.optimization_barrier((mixed, *text_ffn_moved))
+    text_ffn_rows = gather_end(pooled_grad, *text_ffn_moved)
     mixed_rows = [mixed[:split_at], mixed[split_at:]]
-    ffn_rows = gather_end(image_ffn_grad, *ffn_moved[:2])
-    text_ffn_rows = gather_end(pooled_grad, *ffn_moved[2:])
     normed_mid = [layer_norm(residual) for residual in middle]
-    pooled_in = pool_start(text_in)
-    text_moved = gather_start(pooled_in)
 
     def gelu_back(pre_act, hidden_grad):
         return jax.vjp(gelu_tanh, pre_act)[1](hidden_grad)[0].astype(LOW)
 
+    pooled_in = pool_start(text_in)
     pre_act = dot(mlp_rows, up_full, NN)
     hidden = gelu_tanh(pre_act).astype(LOW)
+    hidden, pre_act, pooled_in = lax.optimization_barrier((hidden, pre_act, pooled_in))
+    text_moved = gather_start(pooled_in)
     pre_grad = gelu_back(pre_act, dot(ffn_rows, down_full, NT))
-    here, there = scatter_start(dot(pre_grad, up_full, NT))
-    far = lax.ppermute(there, "tensor", CHIP)
+    second_part = dot(pre_grad, up_full, NT).astype(LOW)
     down_grad = dot(hidden, ffn_rows, TN).astype(LOW)
-    there, down_grad, *text_moved = lax.optimization_barrier((there, down_grad, *text_moved))
+    second_part, down_grad, *text_moved = lax.optimization_barrier(
+        (second_part, down_grad, *text_moved)
+    )
     text_mlp_rows = gather_end(pooled_in, *text_moved)
     text_pre_act = dot(text_mlp_rows, text_up, NN)
     text_hidden = gelu_tanh(text_pre_act).astype(LOW)
     text_pre_grad = gelu_back(text_pre_act, dot(text_ffn_rows, text_down, NT))
     text_here, text_there = scatter_start(dot(text_pre_grad, text_up, NT))
     text_far = lax.ppermute(text_there, "tensor", CHIP)
-    (down_sum,), (far, text_far) = beside(
-        scatter_dp, [down_grad], size, 4, [there, text_there], [far, text_far]
-    )
-    second_grad, ffn = [None, None], [None, None]
-    middle_grad, branch_grad = [None, None], [None, None]
-
-    def middle_back(s):
-        wide = second_grad[s] * (1.0 + mod_row(s, 4))
-        middle_grad[s] = cotangent[s] + jax.vjp(layer_norm, middle[s])[1](wide)[0]
-        branch_grad[s] = (mod_row(s, 2) * middle_grad[s]).astype(LOW)
-
-    second_grad[1] = unpool_end(text_here + text_far.astype(WIDE))
-    second_grad[0] = here + far.astype(WIDE)
-    middle_back(0)
-    moved = gather_start(branch_grad[0])
+    pre_grad, text_there = lax.optimization_barrier((pre_grad, text_there))
     up_grad = dot(mlp_rows, pre_grad, TN).astype(LOW)
     here, there = scatter_start(dot(hidden, down_full, NN))
-    up_grad, there, second_grad[1], *moved = lax.optimization_barrier(
-        (up_grad, there, second_grad[1], *moved)
-    )
-    middle_back(1)
-    text_moved = gather_start(branch_grad[1])
-    branch_rows = [gather_end(branch_grad[0], *moved), gather_end(branch_grad[1], *text_moved)]
-    out_grad = [dot(mixed_rows[s], branch_rows[s], TN).astype(LOW) for s in range(2)]
-    far = lax.ppermute(there, "tensor", CHIP)
+    up_grad, there, text_far = lax.optimization_barrier((up_grad, there, text_far))
+    second_grad, ffn = [None, None], [None, None]
+    second_grad[1] = unpool_end(text_here, text_far)
     text_here, text_there = scatter_start(dot(text_hidden, text_down, NN))
-    text_far = lax.ppermute(text_there, "tensor", CHIP)
-    mixed_grad = jnp.concatenate(
-        [dot(branch_rows[s], out_full[s], NT).astype(LOW) for s in range(2)], axis=0
+    text_down_grad = dot(text_hidden, text_ffn_rows, TN)
+    text_up_grad = dot(text_mlp_rows, text_pre_grad, TN)
+    second_part, second_grad[1], text_there, text_down_grad, text_up_grad = (
+        lax.optimization_barrier(
+            (second_part, second_grad[1], text_there, text_down_grad, text_up_grad)
+        )
     )
     if size == RING:
-        grads, (up_sum, *out_sum) = attend_back(
-            joint, bias, mixed, mixed_grad, log_total, split_at, heads_here,
-            [up_grad] + out_grad, 5, (2, 4),
-        )
+        mods = jnp.concatenate(
+            [row for s in range(2) for row in (mod_row(s, 2), 1.0 + mod_row(s, 4))]
+            + [jnp.zeros((4, width), WIDE)],
+            axis=0,
+        )
+        found = back_ring(
+            joint, bias, mixed, log_total, split_at, heads_here, second_grad[1], middle,
+            cot_rows, mods, second_part, out_full,
+            [down_grad, up_grad], [there, text_there], 5,
+        )
+        *grads, second_grad[0], image_middle, text_middle = found[:6]
+        middle_grad, branch_rows = [image_middle, text_middle], found[6:8]
+        far, text_far, down_sum, up_sum = found[8:]
     else:
-        grads, _ = attend_back(
+        second_grad[0] = scatter_rows(second_part)
+        middle_grad, branch_rows = [None, None], [None, None]
+        for s in range(2):
+            wide = second_grad[s] * (1.0 + mod_row(s, 4))
+            middle_grad[s] = cotangent[s] + jax.vjp(layer_norm, middle[s])[1](wide)[0]
+            branch_rows[s] = gather_rows((mod_row(s, 2) * middle_grad[s]).astype(LOW))
+        mixed_grad = jnp.concatenate(
+            [dot(branch_rows[s], out_full[s], NT).astype(LOW) for s in range(2)], axis=0
+        )
+        grads = attend_back(
             joint, bias, mixed, mixed_grad, log_total, split_at, heads_here, [], 0, ()
-        )
-        up_sum, *out_sum = scatter_dp([up_grad] + out_grad, size, 5)
+        )[0]
+        grads = list(grads)
+        down_sum, up_sum = scatter_dp([down_grad, up_grad], size, 5)
+        far = lax.ppermute(there, "tensor", CHIP)
+        text_far = lax.ppermute(text_there, "tensor", CHIP)
+    ffn[0], ffn[1] = here + far.astype(WIDE), unpool_end(text_here, text_far)
+    results = [(middle[s] + mod_row(s, 5) * ffn[s]).astype(LOW) for s in range(2)]
+    gate_terms = [jnp.sum(cotangent[s] * ffn[s], axis=0)[None] for s in range(2)]
+    out_grad = [dot(mixed_rows[s], branch_rows[s], TN).astype(LOW) for s in range(2)]
+    text_up_grad, grads[0] = lax.optimization_barrier((text_up_grad, grads[0]))
+    text_up_grad = lax.all_to_all(
+        text_up_grad.astype(LOW).reshape(size, -1, units),
+        "dp", split_axis=0, concat_axis=2, tiled=True,
+    )
     joint_grad = jnp.concatenate(grads, axis=1)
-    joint_grad, far, text_far = lax.optimization_barrier((joint_grad, far, text_far))
-    ffn[0] = here + far.astype(WIDE)
-    ffn[1] = unpool_end(text_here + text_far.astype(WIDE))
     joint_rows = [joint_grad[:split_at], joint_grad[split_at:]]
     qkv_grad = [dot(attn_rows[s], joint_rows[s], TN).astype(LOW) for s in range(2)]
-    here, there = scatter_start(dot(joint_rows[0], qkv_full[0], NT))
-    text_first = scatter_rows(dot(joint_rows[1], qkv_full[1], NT))
-    results = [(middle[s] + mod_row(s, 5) * ffn[s]).astype(LOW) for s in range(2)]
-    text_down_grad = dot(text_hidden, text_ffn_rows, TN)
-    text_up_grad = lax.all_to_all(
-        dot(text_mlp_rows, text_pre_grad, TN).astype(LOW).reshape(size, -1, units),
-        "dp", split_axis=0, concat_axis=2, tiled=True,
+    first_parts = [dot(joint_rows[s], qkv_full[s], NT).astype(LOW) for s in range(2)]
+    here, there = scatter_start(
+        jnp.concatenate(
+            [
+                part[b * (part.shape[0] // 4) : (b + 1) * (part.shape[0] // 4)]
+                for b in range(4)
+                for part in first_parts
+            ]
+        )
     )
     other = []
     for s in range(2):
@@ -1110,22 +1379,26 @@
             jnp.sum(middle_grad[s] * branches[s], axis=0)[None],
             jnp.sum(second_grad[s], axis=0)[None],
             jnp.sum(second_grad[s] * normed_mid[s], axis=0)[None],
-            jnp.sum(cotangent[s] * ffn[s], axis=0)[None],
+            gate_terms[s],
         ]
     other = jnp.concatenate(other + [jnp.zeros((4, width), WIDE)], axis=0)
     if size == RING:
         scale = jnp.concatenate([1.0 + mod_row(s, 1) for s in range(2)], axis=0)
-        *input_grad, mod_sum, mod_grad, qkv_image, qkv_text = tail_ring(
-            here, there, text_first, scale, other, x_rows, middle_grad, qkv_grad, width_here, 6
-        )
-        qkv_sums = [qkv_image, qkv_text]
+        image_input, mod_sum, mod_grad, text_out, text_grad, *found = tail_ring(
+            here, there, scale, other, x_rows, middle_grad, results[1], qkv_grad + out_grad,
+            width_here, 6,
+        )
+        qkv_image, qkv_text, out_image, out_text = found
+        qkv_sums, out_sum = [qkv_image, qkv_text], [out_image, out_text]
         mod_sum = mod_sum[:12].reshape(2, 6, width_here)
         mod_grad = mod_grad[:, :12].reshape(seqs, 2, 6, width_here)
         mod_grad, text_up_grad = lax.optimization_barrier((mod_grad, text_up_grad))
     else:
-        qkv_sums = scatter_dp(qkv_grad, size, 6)
+        *qkv_sums, out_image, out_text = scatter_dp(qkv_grad + out_grad, size, 6)
+        out_sum = [out_image, out_text]
         far = lax.ppermute(there, "tensor", CHIP)
-        first_grad = [here + far.astype(WIDE), text_first]
+        first_rows = here + far.astype(WIDE)
+        first_grad = [first_rows[:image_rows], first_rows[image_rows:]]
         input_grad, first_terms = [None, None], []
         for s in range(2):
             wide = first_grad[s] * (1.0 + mod_row(s, 1))
@@ -1133,6 +1406,9 @@
             shift = jnp.sum(first_grad[s], axis=0)
             gain = jnp.sum(first_grad[s] * normed_in[s], axis=0)
             first_terms.append(jnp.stack([shift, gain]))
+        image_input = input_grad[0]
+        text_out = lax.all_gather(results[1], "tensor", axis=0)
+        text_grad = lax.all_gather(input_grad[1], "tensor", axis=0)
         mod_terms = other[:12].reshape(2, 6, width).at[:, :2].set(jnp.stack(first_terms))
         mod_split = mod_terms.reshape(2, 6, 4, width_here).transpose(2, 0, 1, 3)
         mod_sum = jnp.sum(
@@ -1147,10 +1423,8 @@
     act_parts = lax.all_to_all(act_parts, "dp", split_axis=0, concat_axis=0, tiled=True)
     act_grad = lax.psum(act_parts.reshape(1, width), "tensor")
     cond_grad = jax.vjp(jax.nn.silu, cond)[1](act_grad)[0]
-    text_out, text_grad = results[1], input_grad[1]
-
-    def whole_text(rows):
-        blocks = lax.all_gather(rows, "tensor", axis=0)
+
+    def whole_text(blocks):
         return blocks[:, :text_own].reshape(4 * text_own, width)[:text_tokens][None]
 
     down_sum = jnp.stack([down_sum, text_down_grad])
@@ -1160,7 +1434,7 @@
     return (
         results[0][None],
         whole_text(text_out),
-        input_grad[0][None],
+        image_input[None],
         whole_text(text_grad),
         cond_grad,
         shift_grad[None],

time: 795 us -> 759 us (0.955)
  Pallas kernels: 346 us -> 423 us
  starting transfers between devices: 86.3 us -> 41.4 us
  other arithmetic: 74.9 us -> 48.7 us
  local copies, waits for them, and re-layouts: 81.3 us -> 62.1 us
  between operations: 16.1 us -> 1.99 us
  waiting for transfers between devices: 46.2 us -> 57.6 us
  blocking collectives: 20.2 us -> 11.7 us
    pallas_call x3, Pallas kernels: 221 us -> 301 us  [the longest x1 109 us: back_ring(): pl.pallas_call(functools.partial(back_kernel, split, 64), grid=(pairs, ro...]
    ppermute x19 -> x0, starting transfers between devices: 25.9 us -> none  [the longest x16 22.5 us: launch(): lax.ppermute(piece, 'dp', ring_pairs(self.size, 1 if i < count else -1))]
    dynamic_update_slice x17 -> x0, local copies, waits for them, and re-layouts: 24.8 us -> none  [put(): lax.dynamic_update_slice_in_dim(self.fulls[i], piece, start, 0)]
    ppermute x19 -> x0, waiting for transfers between devices: 20.3 us -> none  [the longest x16 15.4 us: launch(): lax.ppermute(piece, 'dp', ring_pairs(self.size, 1 if i < count else -1))]
    ppermute x2 -> x1, waiting for transfers between devices: 0.01 us -> 18.1 us  [local(): text_far = lax.ppermute(text_there, 'tensor', CHIP)]
    unnamed x211 -> x168, local copies, waits for them, and re-layouts: 10.7 us -> 26.6 us
    all_to_all x2, waiting for transfers between devices: 14.4 us -> 25 us  [unpool_end(): part = lax.all_to_all(part, 'dp', split_axis=0, concat_axis=0, tiled=True)]
    ppermute x7 -> x2, waiting for transfers between devices: 10.2 us -> 0.01 us  [gather_start(): far = lax.ppermute(own, 'tensor', CHIP)]
  transfers between devices with their start and end apart: 58 -> 19, of which waited for: 12 -> 7; matrix products, arithmetic and copies ran while one was open for 30% -> 23% of each run, Pallas kernels for 34% -> 28%
where the time goes in v4:
time: 759 us; the launch traced here: 754 us
  Pallas kernels  423 us (56%)
  matrix products  107 us (14%)
  local copies, waits for them, and re-layouts  62.1 us (8%)
  waiting for transfers between devices  57.6 us (8%)
  other arithmetic  48.7 us (6%)
  starting transfers between devices  41.4 us (5%)
  blocking collectives  11.7 us (2%)
    pallas_call x1, Pallas kernels, middle_ring(): pl.pallas_call(functools.partial(middle_kernel, split, 64), grid=(pairs,...  122 us
    pallas_call x1, Pallas kernels, back_ring(): pl.pallas_call(functools.partial(back_kernel, split, 64), grid=(pairs, ro...  109 us
    pallas_call x1, Pallas kernels, tail_ring(): pl.pallas_call(functools.partial(tail_kernel, columns, len(grads)), out_s...  105 us
    dot_general x20, matrix products, dot(): lax.dot_general(left, right, (dims, ((), ())), preferred_element_type=WIDE)  103 us
    pallas_call x1, Pallas kernels, first_ring(): pl.pallas_call(functools.partial(first_kernel, 64), in_specs=[WHOLE] * 5...  87.4 us
    unnamed x168, local copies, waits for them, and re-layouts  26.6 us
    all_to_all x2, waiting for transfers between devices, unpool_end(): part = lax.all_to_all(part, 'dp', split_axis=0, concat_axis=0, tiled=True)  25 us
    ppermute x1, waiting for transfers between devices, local(): text_far = lax.ppermute(text_there, 'tensor', CHIP)  18.1 us
  transfers between devices with their start and end apart: 19, of which 7 were waited for; matrix products, arithmetic and copies ran while one was open for 23% of the time, Pallas kernels for 28%

profile of v4, /device:TPU:0, one launch (start us, length us, event | category | flops | bytes accessed | tf_op | source)
XLA Modules:
  0.0 754.3 jit_solution(9365326954866768007)
XLA Ops:
  2.6 7.3 all-to-all-start
  9.9 1.9 convert.19
  18.4 2.5 convert.16
  22.0 6.0 all-to-all-start.1
  33.4 2.0 all-to-all-done.1
  35.4 4.0 all-to-all-start.3
  39.4 5.9 all_gather.3
  46.6 87.4 %first_ring.1 = (bf16[1024,1536]{1,0:T(8,128)(2,1)}, bf16[256,1536]{1,0:T(8,128)(2,1)}, bf16[1024,1536]{1,0:T(8,128)(2,1)}, bf16[1536,1152]{1,0:T(8,128)(2,1)}, ...) custom-call(bf16[256,1536]{1,0:T(8,128)(2,1)} %bitcast.132, bf16[64,1536]{1,0:T(8,128)(2,1)} %pad.24.refs_1_.refs_5_, ...), custom_call_target="tpu_custom_call" | custom-call | tf_op jit(solution)/shard_map/first_ring/pallas_call | solution.py:591
  134.1 1.6 collective-permute-start.2
  135.7 8.6 %convolution_convert_fusion.8 = bf16[1024,1152]{1,0:T(8,128)(2,1)} fusion(bf16[1024,1536]{1,0:T(8,128)(2,1)} %get-tuple-element.73, bf16[1536,1152]{1,0:T(8,128)(2,1)} %get-tuple-element.74), kind=kOutput, calls=%fused_computation.26 | convolution fusion | flops 3625058304 | bytes 9043968 | tf_op jit(solution)/shard_map/dot_general | solution.py:21
  145.0 3.3 convolution_convert_fusion.12
  148.4 1.9 pad_maximum_fusion.refs_1_.refs_2_.refs_3_
  150.3 122.1 %middle_ring.1 = (bf16[1280,384]{1,0:T(8,128)(2,1)}, f32[3,8,1280]{2,1,0:T(8,128)}, f32[256,1536]{1,0:T(8,128)}, f32[64,1536]{1,0:T(8,128)}, f32[256,1536]{1,0:T...) custom-call(f32[1,256]{1,0:T(1,128)} %and_select_fusion.refs_0_, ...), custom_call_target="tpu_custom_call" | custom-call | tf_op jit(solution)/shard_map/middle_ring/pallas_call | solution.py:748
  274.5 3.8 all-to-all-start.2
  279.4 11.1 %fusion.14 = (bf16[1024,1536]{1,0:T(8,128)(2,1)}, f32[1024,1536]{1,0:T(8,128)}) fusion(bf16[1024,1536]{1,0:T(8,128)(2,1)} %get-tuple-element.78, bf16[1536,1536]{1,0:T(8,128)(2,1)} %get-tuple-element.79), kind=kOutput, calls=%fused_computation.23 | convolution fusion | flops 4845993984 | bytes 17301504 | tf_op jit(solution)/shard_map/dot_general | solution.py:21
  291.7 2.4 constant_dynamic-update-slice_fusion.2
  294.1 2.4 constant_dynamic-update-slice_fusion.1
  296.5 8.4 %all-to-all-done.2 = bf16[8,48,1536]{2,1,0:T(8,128)(2,1)S(1)} async-done(((bf16[8,48,1536]{2,1,0:T(8,128)(2,1)}), bf16[8,48,1536]{2,1,0:T(8,128)(2,1)S(1)}, u32[]{:S(2)}, u32[]{:S(2)}) %all-to-all-start.2) | async-done | bytes 1179680 | tf_op jit(solution)/shard_map/all_to_all | solution.py:1201
  304.8 1.6 collective-permute-start.4
  306.4 11.6 %fusion.6 = bf16[1024,1536]{1,0:T(8,128)(2,1)S(1)} fusion(f32[1024,1536]{1,0:T(8,128)} %get-tuple-element.88, bf16[1024,1536]{1,0:T(8,128)(2,1)} %get-tuple-element.87, bf16[1536,1536]{1,0:T(8,128)(2,1)} %get-tuple-element.82), kind=kOutput, calls=%fused_computation.15 | convolution fusion | flops 4863295488 | bytes 17301504 | tf_op jit(solution)/shard_map/dot_general | solution.py:21
  318.0 1.7 copy-done.71
  319.7 9.0 %convolution_convert_fusion.6.refs_12_ = bf16[1024,1536]{1,0:T(8,128)(2,1)} fusion(bf16[1024,1536]{1,0:T(8,128)(2,1)S(1)} %fusion.6, bf16[1536,1536]{1,0:T(8,128)(2,1)} %get-tuple-element.79), kind=kOutput, calls=%fused_computation.24 | convolution fusion | flops 4833411072 | bytes 11010048 | tf_op jit(solution)/shard_map/dot_general | solution.py:21
  328.7 7.8 %convolution_convert_fusion.7 = bf16[1024,1536]{1,0:T(8,128)(2,1)S(1)} fusion(bf16[1024,1536]{1,0:T(8,128)(2,1)S(1)} %copy-done.70, bf16[1536,1536]{1,0:T(8,128)(2,1)} %get-tuple-element.82), kind=kOutput, calls=%fused_computation.25 | convolution fusion | flops 4833411072 | bytes 11010048 | tf_op jit(solution)/shard_map/dot_general | solution.py:21
  336.6 7.3 convolution_convert_fusion.2.refs_15_
  347.0 1.7 fusion.73
  349.5 2.1 fusion.25
  353.2 2.0 copy-done
  355.2 1.6 pad_maximum_fusion.1
  358.3 2.6 add_convert_fusion.6.refs_17_
  362.5 2.0 copy-done.9
  364.5 1.7 add_convert_fusion.3
  366.7 1.6 pad_maximum_fusion.2
  369.5 6.9 convolution_convert_fusion.1.refs_16_
  376.4 18.1 %collective-permute-done.8 = bf16[384,1536]{1,0:T(8,128)(2,1)S(1)} collective-permute-done((bf16[384,1536]{1,0:T(8,128)(2,1)S(1)}, bf16[384,1536]{1,0:T(8,128)(2,1)S(1)}, u32[]{:S(2)}, u32[]{:S(2)}) %collective-permute-start.8) | collective-permute-done | bytes 1179680 | tf_op jit(solution)/shard_map/ppermute | solution.py:1307
  394.5 2.7 add_convert_fusion.2
  397.2 4.1 all-to-all-start.4
  403.4 3.5 fusion.74
  407.0 4.5 fusion.65
  411.5 2.9 add_convert_fusion.1.refs_18_
  414.4 15.3 %all-to-all-done.4 = bf16[8,48,1536]{2,1,0:T(8,128)(2,1)S(1)} async-done(((bf16[8,48,1536]{2,1,0:T(8,128)(2,1)}), bf16[8,48,1536]{2,1,0:T(8,128)(2,1)S(1)}, u32[]{:S(2)}, u32[]{:S(2)}) %all-to-all-start.4) | async-done | bytes 1179680 | tf_op jit(solution)/shard_map/all_to_all | solution.py:1206
  430.6 109.3 %back_ring.1 = (bf16[1280,384]{1,0:T(8,128)(2,1)}, bf16[1280,384]{1,0:T(8,128)(2,1)}, bf16[1280,384]{1,0:T(8,128)(2,1)}, f32[256,1536]{1,0:T(8,128)}, f32[256,15...) custom-call(f32[256,1]{1,0:T(8,128)} %fusion.49.refs_0_, ...), custom_call_target="tpu_custom_call" | custom-call | tf_op jit(solution)/shard_map/back_ring/pallas_call | solution.py:967
  542.0 1.6 copy-done.63
  543.5 4.6 convolution_convert_fusion.9
  553.9 3.6 all-to-all-start.6
  557.6 3.3 pad_maximum_fusion.5
  562.8 3.2 multiply_reduce_fusion
  566.1 3.2 add_convert_fusion
  571.1 4.0 convolution_convert_fusion.3.refs_10_
  575.2 3.4 all-to-all-done.6
  578.5 3.9 all-to-all-start.5
  582.4 2.4 convolution_convert_fusion.10.refs_12_
  584.8 4.7 convolution_convert_fusion.11.refs_11_
  589.5 5.8 convolution_convert_fusion.refs_9_
  597.3 4.1 add_convert_fusion.4
  601.4 9.7 %all-to-all-done.5 = bf16[8,48,1536]{2,1,0:T(8,128)(2,1)S(1)} async-done(((bf16[8,48,1536]{2,1,0:T(8,128)(2,1)}), bf16[8,48,1536]{2,1,0:T(8,128)(2,1)S(1)}, u32[]{:S(2)}, u32[]{:S(2)}) %all-to-all-start.5) | async-done | bytes 1179680 | tf_op jit(solution)/shard_map/all_to_all | solution.py:1206
  613.6 104.7 %tail_ring.1 = (f32[256,1536]{1,0:T(8,128)}, f32[16,384]{1,0:T(8,128)}, bf16[8,16,384]{2,1,0:T(8,128)(2,1)}, bf16[4,64,1536]{2,1,0:T(8,128)(2,1)}, f32[4,64,1536...) custom-call(f32[320,1536]{1,0:T(8,128)} %get-tuple-element.211.refs_0_, ...), custom_call_target="tpu_custom_call" | custom-call | tf_op jit(solution)/shard_map/tail_ring/pallas_call | solution.py:444
  718.3 1.5 copy.90
  721.0 2.5 stack.34
  723.5 2.3 stack.35
  727.8 4.2 all-to-all-start.7
  735.7 2.9 pad_maximum_fusion.4
  739.5 2.5 convolution_bitcast_fusion
  743.8 1.9 copy.96
  746.4 5.8 psum.7
  (271 shorter events, 62.5 us)
Async XLA Ops:
  2.6 18.2 %all-to-all-start = ((bf16[8,1,192]{2,1,0:T(2,128)(2,1)}), bf16[8,1,192]{2,1,0:T(2,128)(2,1)S(1)}, u32[]{:S(2)}, u32[]{:S(2)}) async-start(bf16[8,1,192]{2,1,0:T(2,128)(2,1)} %all_to_all.66), calls=%async_computation | async-start | bytes 16384 | tf_op jit(solution)/shard_map/all_to_all | solution.py:1212
  9.9 3.8 copy-start.19
  15.7 5.1 copy-start.3
  20.9 8.3 %copy-start.51 = (bf16[8,1,192]{2,1,0:T(2,128)(2,1)}, bf16[8,1,192]{2,1,0:T(2,128)(2,1)S(1)}, u32[]{:S(2)}) copy-start(bf16[8,1,192]{2,1,0:T(2,128)(2,1)S(1)} %all-to-all-done) | copy-start | bytes 9220
  22.0 13.4 %all-to-all-start.1 = ((f32[8,2,6,384]{3,1,2,0:T(2,128)}), f32[8,2,6,384]{3,1,2,0:T(2,128)S(1)}, u32[]{:S(2)}, u32[]{:S(2)}) async-start(f32[8,2,6,384]{3,1,2,0:T(2,128)} %copy.85), calls=%async_computation.1 | async-start | bytes 294912 | tf_op jit(solution)/shard_map/all_to_all | solution.py:1217
  35.4 238.0 %all-to-all-start.3 = ((bf16[192,8,192]{0,2,1:T(8,128)(2,1)}), bf16[192,8,192]{0,2,1:T(8,128)(2,1)S(1)}, u32[]{:S(2)}, u32[]{:S(2)}) async-start(bf16[192,8,192]{0,2,1:T(8,128)(2,1)} %bitcast.23), calls=%async_computation.3 | async-start | bytes 1572864 | tf_op jit(solution)/shard_map/all_to_all | solution.py:1194
  45.9 98.4 %copy-start.42 = (f32[2,1536]{1,0:T(2,128)}, f32[2,1536]{1,0:T(2,128)S(1)}, u32[]{:S(2)}) copy-start(f32[2,1536]{1,0:T(2,128)S(1)} %broadcast.349) | copy-start | bytes 36868
  134.0 157.5 %collective-permute-start.1 = (bf16[384,1536]{1,0:T(8,128)(2,1)}, bf16[384,1536]{1,0:T(8,128)(2,1)}, u32[]{:S(2)}, u32[]{:S(2)}) collective-permute-start(bf16[384,1536]{1,0:T(8,128)(2,1)} %get-tuple-element.84), channel_id=1, source_target_pairs={{0,1},{1,0},{2,3},{3,2},{4,5},{5,4},{6,7},{7,6},{8,9},{9,8},{10,11... | collective-permute-start | bytes 3538952 | tf_op jit(solution)/shard_map/ppermute | solution.py:294
  134.1 157.5 %collective-permute-start.2 = (bf16[384,1536]{1,0:T(8,128)(2,1)}, bf16[384,1536]{1,0:T(8,128)(2,1)}, u32[]{:S(2)}, u32[]{:S(2)}) collective-permute-start(bf16[384,1536]{1,0:T(8,128)(2,1)} %get-tuple-element.84), channel_id=1, source_target_pairs={{0,2},{1,3},{2,0},{3,1},{4,6},{5,7},{6,4},{7,5},{8,10},{9,11},{10,... | collective-permute-start | bytes 3538952 | tf_op jit(solution)/shard_map/ppermute | solution.py:295
  135.7 9.3 %copy-start.17 = (bf16[256,1536]{1,0:T(8,128)(2,1)S(1)}, bf16[256,1536]{1,0:T(8,128)(2,1)}, u32[]{:S(2)}) copy-start(bf16[256,1536]{1,0:T(8,128)(2,1)} %get-tuple-element.75) | copy-start | bytes 2359300
  272.3 5.9 copy-start.29
  274.5 30.3 %all-to-all-start.2 = ((bf16[8,48,1536]{2,1,0:T(8,128)(2,1)}), bf16[8,48,1536]{2,1,0:T(8,128)(2,1)S(1)}, u32[]{:S(2)}, u32[]{:S(2)}) async-start(bf16[8,48,1536]{2,1,0:T(8,128)(2,1)} %broadcast_in_dim.61), calls=%async_computation.2 | async-start | bytes 2359296 | tf_op jit(solution)/shard_map/all_to_all | solution.py:1201
  291.6 54.3 %collective-permute-start.5 = (bf16[384,1536]{1,0:T(8,128)(2,1)}, bf16[384,1536]{1,0:T(8,128)(2,1)S(1)}, u32[]{:S(2)}, u32[]{:S(2)}) collective-permute-start(bf16[384,1536]{1,0:T(8,128)(2,1)} %collective-permute-done.2), channel_id=1, source_target_pairs={{0,1},{1,0},{2,3},{3,2},{4,5},{5,4},{6,7},{7,6},{8,9},{9,8},{10,11... | collective-permute-start | bytes 3538952 | tf_op jit(solution)/shard_map/ppermute | solution.py:300
  304.8 39.1 %collective-permute-start.3 = (bf16[384,1536]{1,0:T(8,128)(2,1)S(1)}, bf16[384,1536]{1,0:T(8,128)(2,1)S(1)}, u32[]{:S(2)}, u32[]{:S(2)}) collective-permute-start(bf16[384,1536]{1,0:T(8,128)(2,1)S(1)} %bitcast.137), channel_id=1, source_target_pairs={{0,1},{1,0},{2,3},{3,2},{4,5},{5,4},{6,7},{7,6},{8,9},{9,8},{10,11... | collective-permute-start | bytes 3538952 | tf_op jit(solution)/shard_map/ppermute | solution.py:294
  304.8 39.1 %collective-permute-start.4 = (bf16[384,1536]{1,0:T(8,128)(2,1)S(1)}, bf16[384,1536]{1,0:T(8,128)(2,1)S(1)}, u32[]{:S(2)}, u32[]{:S(2)}) collective-permute-start(bf16[384,1536]{1,0:T(8,128)(2,1)S(1)} %bitcast.138), channel_id=1, source_target_pairs={{0,2},{1,3},{2,0},{3,1},{4,6},{5,7},{6,4},{7,5},{8,10},{9,11},{10,... | collective-permute-start | bytes 3538952 | tf_op jit(solution)/shard_map/ppermute | solution.py:295
  319.7 9.0 %copy-start.70 = (bf16[1024,1536]{1,0:T(8,128)(2,1)S(1)}, bf16[1024,1536]{1,0:T(8,128)(2,1)}, u32[]{:S(2)}) copy-start(bf16[1024,1536]{1,0:T(8,128)(2,1)} %get-tuple-element.81) | copy-start | bytes 9437188
  328.7 7.8 %copy-start.66 = (bf16[1024,1536]{1,0:T(8,128)(2,1)S(1)}, bf16[1024,1536]{1,0:T(8,128)(2,1)}, u32[]{:S(2)}) copy-start(bf16[1024,1536]{1,0:T(8,128)(2,1)} %get-tuple-element.87) | copy-start | bytes 9437188
  328.7 17.1 %slice-start.2 = ((s8[4718592]{0:T(1024)(128)(4,1)}), s8[4194304]{0:T(1024)(128)(4,1)S(1)}, s32[]{:S(2)}) async-start(s8[4718592]{0:T(1024)(128)(4,1)} %bitcast.155), calls=%async_computation.10 | async-start | bytes 8388608
  336.5 7.3 copy-start.14
  336.6 9.3 %slice-start.3 = ((s8[4718592]{0:T(1024)(128)(4,1)}), s8[524288]{0:T(1024)(128)(4,1)S(1)}, s32[]{:S(2)}) async-start(s8[4718592]{0:T(1024)(128)(4,1)} %bitcast.155), calls=%async_computation.11 | async-start | bytes 1048576
  344.0 2.9 collective-permute-start.6
  345.5 12.8 %collective-permute-start = (bf16[512,1536]{1,0:T(8,128)(2,1)}, bf16[512,1536]{1,0:T(8,128)(2,1)}, u32[]{:S(2)}, u32[]{:S(2)}) collective-permute-start(bf16[512,1536]{1,0:T(8,128)(2,1)} %pad_maximum_fusion.7), channel_id=1, source_target_pairs={{0,1},{1,0},{2,3},{3,2},{4,5},{5,4},{6,7},{7,6},{8,9},{9,8},{10,11... | collective-permute-start | bytes 4718600 | tf_op jit(solution)/shard_map/ppermute | solution.py:312
  356.8 7.7 %collective-permute-start.7 = (bf16[768,1536]{1,0:T(8,128)(2,1)}, bf16[768,1536]{1,0:T(8,128)(2,1)}, u32[]{:S(2)}, u32[]{:S(2)}) collective-permute-start(bf16[768,1536]{1,0:T(8,128)(2,1)} %pad_maximum_fusion.1), channel_id=1, source_target_pairs={{0,1},{1,0},{2,3},{3,2},{4,5},{5,4},{6,7},{7,6},{8,9},{9,8},{10,11... | collective-permute-start | bytes 7077896 | tf_op jit(solution)/shard_map/ppermute | solution.py:312
  358.0 4.3 copy-start.59
  358.2 6.3 slice-start
  360.9 3.7 slice-start.1
  364.5 3.8 copy-start.72
  366.2 28.2 %collective-permute-start.8 = (bf16[384,1536]{1,0:T(8,128)(2,1)S(1)}, bf16[384,1536]{1,0:T(8,128)(2,1)S(1)}, u32[]{:S(2)}, u32[]{:S(2)}) collective-permute-start(bf16[384,1536]{1,0:T(8,128)(2,1)S(1)} %add_convert_fusion.3), channel_id=1, source_target_pairs={{0,2},{1,3},{2,0},{3,1},{4,6},{5,7},{6,4},{7,5},{8,10},{9,11},{10,... | collective-permute-start | bytes 3538952 | tf_op jit(solution)/shard_map/ppermute | solution.py:1307
  368.3 43.2 %collective-permute-start.9 = (bf16[768,1536]{1,0:T(8,128)(2,1)}, bf16[768,1536]{1,0:T(8,128)(2,1)}, u32[]{:S(2)}, u32[]{:S(2)}) collective-permute-start(bf16[768,1536]{1,0:T(8,128)(2,1)} %pad_maximum_fusion.2), channel_id=1, source_target_pairs={{0,1},{1,0},{2,3},{3,2},{4,5},{5,4},{6,7},{7,6},{8,9},{9,8},{10,11... | collective-permute-start | bytes 7077896 | tf_op jit(solution)/shard_map/ppermute | solution.py:312
  397.2 6.2 copy-start.28
  397.2 32.5 %all-to-all-start.4 = ((bf16[8,48,1536]{2,1,0:T(8,128)(2,1)}), bf16[8,48,1536]{2,1,0:T(8,128)(2,1)S(1)}, u32[]{:S(2)}, u32[]{:S(2)}) async-start(bf16[8,48,1536]{2,1,0:T(8,128)(2,1)} %bitcast.140), calls=%async_computation.4 | async-start | bytes 2359296 | tf_op jit(solution)/shard_map/all_to_all | solution.py:1206
  401.8 5.1 copy-start.48
  403.4 3.5 copy-start.69
  543.5 4.7 copy-start.35
  543.5 4.7 copy-start.62
  552.8 44.4 %collective-permute-start.10 = (bf16[640,1536]{1,0:T(8,128)(2,1)}, bf16[640,1536]{1,0:T(8,128)(2,1)}, u32[]{:S(2)}, u32[]{:S(2)}) collective-permute-start(bf16[640,1536]{1,0:T(8,128)(2,1)} %pad_maximum_fusion.6), channel_id=1, source_target_pairs={{0,1},{1,0},{2,3},{3,2},{4,5},{5,4},{6,7},{7,6},{8,9},{9,8},{10,11... | collective-permute-start | bytes 5898248 | tf_op jit(solution)/shard_map/ppermute | solution.py:312
  553.9 24.6 %all-to-all-start.6 = ((bf16[8,192,192]{2,1,0:T(8,128)(2,1)}), bf16[8,192,192]{2,1,0:T(8,128)(2,1)S(1)}, u32[]{:S(2)}, u32[]{:S(2)}) async-start(bf16[8,192,192]{2,1,0:T(8,128)(2,1)} %bitcast.33), calls=%async_computation.6 | async-start | bytes 1572864 | tf_op jit(solution)/shard_map/all_to_all | solution.py:1358
  557.6 3.4 copy-start.8
  557.6 3.4 copy-start.23
  557.6 3.7 copy-start.25
  566.0 5.1 copy-start.18
  575.1 7.2 copy-start.37
  578.5 32.6 %all-to-all-start.5 = ((bf16[8,48,1536]{2,1,0:T(8,128)(2,1)}), bf16[8,48,1536]{2,1,0:T(8,128)(2,1)S(1)}, u32[]{:S(2)}, u32[]{:S(2)}) async-start(bf16[8,48,1536]{2,1,0:T(8,128)(2,1)} %bitcast.28), calls=%async_computation.5 | async-start | bytes 2359296 | tf_op jit(solution)/shard_map/all_to_all | solution.py:1206
  584.8 4.7 copy-start.36
  584.8 4.7 copy-start.64
  597.2 14.0 %copy-start.32 = (bf16[39,1536]{1,0:T(8,128)(2,1)S(1)}, bf16[39,1536]{1,0:T(8,128)(2,1)}, u32[]{:S(2)}) copy-start(bf16[39,1536]{1,0:T(8,128)(2,1)} %copy-done.31) | copy-start | bytes 359428
  597.2 14.1 %copy-start.7 = (f32[64,1536]{1,0:T(8,128)S(1)}, f32[64,1536]{1,0:T(8,128)}, u32[]{:S(2)}) copy-start(f32[64,1536]{1,0:T(8,128)} %get-tuple-element.98.refs_8_) | copy-start | bytes 1179652
  597.2 14.1 %copy-start.13 = (f32[64,1536]{1,0:T(8,128)S(1)}, f32[64,1536]{1,0:T(8,128)}, u32[]{:S(2)}) copy-start(f32[64,1536]{1,0:T(8,128)} %pad.27.refs_6_) | copy-start | bytes 1179652
  597.2 14.1 %copy-start.50 = (f32[1536]{0:T(1024)S(1)}, f32[1536]{0:T(1024)}, u32[]{:S(2)}) copy-start(f32[1536]{0:T(1024)} %get-tuple-element.194) | copy-start | bytes 18436
  597.3 14.1 %copy-start.60 = (f32[64]{0:T(128)S(1)}, f32[64]{0:T(128)}, u32[]{:S(2)}) copy-start(f32[64]{0:T(128)} %copy-done.59) | copy-start | bytes 772
  597.3 14.1 %copy-start.61 = (f32[64]{0:T(128)S(1)}, f32[64]{0:T(128)}, u32[]{:S(2)}) copy-start(f32[64]{0:T(128)} %add_rsqrt_fusion.1) | copy-start | bytes 772
  601.4 10.8 %copy-start.43 = (f32[2,1536]{1,0:T(2,128)S(1)}, f32[2,1536]{1,0:T(2,128)}, u32[]{:S(2)}) copy-start(f32[2,1536]{1,0:T(2,128)} %copy-done.42) | copy-start | bytes 36868
  601.4 10.8 %copy-start.49 = (f32[4,1536]{1,0:T(4,128)S(1)}, f32[4,1536]{1,0:T(4,128)}, u32[]{:S(2)}) copy-start(f32[4,1536]{1,0:T(4,128)} %copy-done.48) | copy-start | bytes 73732
  601.4 10.8 %copy-start.53 = (f32[1,1536]{1,0:T(1,128)S(1)}, f32[1,1536]{1,0:T(1,128)}, u32[]{:S(2)}) copy-start(f32[1,1536]{1,0:T(1,128)} %broadcast_in_dim.66) | copy-start | bytes 18436
  601.4 10.8 %copy-start.54 = (f32[1,1536]{1,0:T(1,128)S(1)}, f32[1,1536]{1,0:T(1,128)}, u32[]{:S(2)}) copy-start(f32[1,1536]{1,0:T(1,128)} %broadcast_in_dim.67) | copy-start | bytes 18436
  601.4 10.8 %copy-start.55 = (f32[1,1536]{1,0:T(1,128)S(1)}, f32[1,1536]{1,0:T(1,128)}, u32[]{:S(2)}) copy-start(f32[1,1536]{1,0:T(1,128)} %broadcast_in_dim.68) | copy-start | bytes 18436
  613.6 106.3 %copy-start.20 = (bf16[1,192,1536]{2,1,0:T(8,128)(2,1)S(1)}, bf16[1,192,1536]{2,1,0:T(8,128)(2,1)}, u32[]{:S(2)}) copy-start(bf16[1,192,1536]{2,1,0:T(8,128)(2,1)} %all_to_all.63) | copy-start | bytes 1769476
  721.0 4.8 copy-start.4
  727.8 18.5 %all-to-all-start.7 = ((f32[8,1,192]{2,1,0:T(1,128)}), f32[8,1,192]{2,1,0:T(1,128)S(1)}, u32[]{:S(2)}, u32[]{:S(2)}) async-start(f32[8,1,192]{2,1,0:T(1,128)} %copy.95), calls=%async_computation.7 | async-start | bytes 16384 | tf_op jit(solution)/shard_map/all_to_all | solution.py:1423
  735.7 3.8 copy-start.39
  735.7 3.8 copy-start.52
  742.5 9.8 %copy-start.57 = (f32[1,1536]{1,0:T(1,128)S(1)}, f32[1,1536]{1,0:T(1,128)}, u32[]{:S(2)}) copy-start(f32[1,1536]{1,0:T(1,128)} %param.12) | copy-start | bytes 18436
  742.5 9.8 %copy-start.58 = (f32[1,1536]{1,0:T(1,128)S(1)}, f32[1,1536]{1,0:T(1,128)}, u32[]{:S(2)}) copy-start(f32[1,1536]{1,0:T(1,128)} %get-tuple-element.197) | copy-start | bytes 18436
  742.5 10.4 %copy-start.24 = (f32[256,1536]{1,0:T(8,128)S(1)}, f32[256,1536]{1,0:T(8,128)}, u32[]{:S(2)}) copy-start(f32[256,1536]{1,0:T(8,128)} %get-tuple-element.121) | copy-start | bytes 4718596
  (32 other events, 73.7 us)

commit v5 on v4

--- a/solution.py
+++ b/solution.py
@@ -505,11 +505,30 @@
 
 
 def first_kernel(chunk, *refs):
-    x_image, x_text, cot_image, cot_text, mods, *blocks = refs[:7]
-    outs, fulls, refs = refs[7:10], refs[10:13], refs[13:]
+    x_image, x_text, cot_image, cot_text, cond, ada, *blocks = refs[:8]
+    outs, fulls, pool, (mods, conds), refs = refs[8:11], refs[11:13], refs[13:14], refs[14:16], refs[16:]
     mines, pooled, (row_sem, own_sem) = refs[:3], refs[3], refs[4:6]
-    ring = GatherRing([*blocks, pooled], fulls, refs[6:])
-    me = lax.axis_index("dp")
+    cond_got, parts, got, cond_sem, part_sem, mod_sem = refs[6:12]
+    ring = GatherRing(blocks, fulls, refs[12:15])
+    text_ring = GatherRing([pooled], pool, refs[15:18])
+    me, index = lax.axis_index("dp"), lax.axis_index("tensor")
+    width, columns = mods.shape[1], ada.shape[2]
+
+    def dp_copy(hop, source, target, sem):
+        peer = (me + hop) % RING
+        return pltpu.make_async_remote_copy(
+            src_ref=source.at[peer], dst_ref=target.at[me],
+            send_sem=sem.at[0, hop - 1], recv_sem=sem.at[1, hop - 1],
+            device_id=(peer, index), device_id_type=MESH,
+        )
+
+    def mod_copy(hop):
+        here = mods.at[:, pl.ds(pl.multiple_of(index * columns, LANES), columns)]
+        return pltpu.make_async_remote_copy(
+            src_ref=here, dst_ref=here,
+            send_sem=mod_sem.at[0, hop - 1], recv_sem=mod_sem.at[1, hop - 1],
+            device_id=(me, tensor_peer(hop)), device_id_type=MESH,
+        )
 
     def row_copy(i, source, slot, hop, sem):
         rows = mines[i].shape[0]
@@ -542,7 +561,7 @@
         x = x.astype(WIDE)
         centred = x - jnp.mean(x, axis=-1, keepdims=True)
         spread = lax.rsqrt(jnp.mean(centred * centred, axis=-1, keepdims=True) + EPS)
-        gain, shift = mods[2 * stream : 2 * stream + 1], mods[2 * stream + 1 : 2 * stream + 2]
+        gain, shift = 1.0 + mods[6 * stream + 1 : 6 * stream + 2], mods[6 * stream : 6 * stream + 1]
         return (centred * spread * gain + shift).astype(LOW)
 
     def over_chunks(body):
@@ -552,15 +571,42 @@
 
         lax.fori_loop(0, x_image.shape[0] // chunk, step, 0)
 
-    meet([*ring.sides, *[(me, tensor_peer(hop)) for hop in (1, 2)]])
-    pooled[...] = (mods[5:6] * cot_text[: pooled.shape[0]].astype(WIDE)).astype(LOW)
+    meet(
+        [(me, tensor_peer(hop)) for hop in (1, 2, 3)]
+        + [((me + hop) % RING, index) for hop in range(1, RING)]
+    )
+    for hop in range(1, RING):
+        dp_copy(hop, cond, cond_got, cond_sem).start()
+    cond_got[pl.ds(me, 1)] = cond[pl.ds(me, 1)]
+    parts[...] = jnp.zeros_like(parts)
+    for hop in range(1, RING):
+        dp_copy(hop, cond, cond_got, cond_sem).wait()
+    rows = jnp.concatenate([cond_got[n, 0:1] for n in range(RING)], axis=0)
+    conds[...] = rows
+    rows = rows.astype(LOW)
+    for which in range(12):
+        part = dot(rows, ada[which], NN)
+        for n in range(RING):
+            parts[n, which : which + 1] = part[n : n + 1]
+    for hop in range(1, RING):
+        dp_copy(hop, parts, got, part_sem).start()
     ring.start()
+    got[pl.ds(me, 1)] = parts[pl.ds(me, 1)]
+    for hop in range(1, RING):
+        dp_copy(hop, parts, got, part_sem).wait()
+    mods[:, pl.ds(pl.multiple_of(index * columns, LANES), columns)] = jnp.sum(got[...], axis=0)
+    for hop in (1, 2, 3):
+        mod_copy(hop).start()
+    for hop in (1, 2, 3):
+        mod_copy(hop).wait()
+    pooled[...] = (mods[11:12] * cot_text[: pooled.shape[0]].astype(WIDE)).astype(LOW)
+    text_ring.start()
 
     def norm_chunk(some):
         mines[0][some] = norm_rows(x_image[some], 0)
 
     def grad_chunk(some):
-        mines[2][some] = (mods[4:5] * cot_image[some].astype(WIDE)).astype(LOW)
+        mines[2][some] = (mods[5:6] * cot_image[some].astype(WIDE)).astype(LOW)
 
     over_chunks(norm_chunk)
     send(0)
@@ -569,46 +615,59 @@
     over_chunks(grad_chunk)
     send(2)
     ring.step(1)
+    text_ring.step(1)
     for i in range(2):
         to_far(i).wait()
         forward(i).start()
     ring.step(2)
+    text_ring.step(2)
     to_far(2).wait()
     forward(2).start()
     ring.step(3)
+    text_ring.step(3)
     for i in range(3):
         own(i).wait()
         to_near(i).wait()
         forward(i).wait()
+    text_ring.step(4)
     ring.step(4)
+    text_ring.end()
     ring.end()
 
 
-def first_ring(x, cotangent, mods, blocks, pool_rows, ident):
-    width = mods.shape[1]
+def first_ring(x, cotangent, cond, ada, blocks, pool_rows, ident):
+    width, columns, depth = x[0].shape[1], ada.shape[2], ada.shape[1]
     rows = [x[0].shape[0], x[1].shape[0], x[0].shape[0]]
     fulls = [block.shape for block in blocks] + [(pool_rows, width)]
+    cond = jnp.broadcast_to(cond.astype(WIDE)[:, None], (RING, 8, depth))
     found = pl.pallas_call(
         functools.partial(first_kernel, 64),
-        in_specs=[WHOLE] * 5 + [ANY] * 2,
-        out_specs=[ANY] * 6,
+        in_specs=[WHOLE] * 6 + [ANY] * 2,
+        out_specs=[ANY] * 6 + [WHOLE] * 2,
         out_shape=[
             *[jax.ShapeDtypeStruct((4 * n, width), LOW) for n in rows],
-            *[jax.ShapeDtypeStruct((RING * n, columns), LOW) for n, columns in fulls],
+            *[jax.ShapeDtypeStruct((RING * n, wide), LOW) for n, wide in fulls],
+            jax.ShapeDtypeStruct((16, width), WIDE),
+            jax.ShapeDtypeStruct((RING, depth), WIDE),
         ],
         scratch_shapes=[
             *[pltpu.VMEM((n, width), LOW) for n in rows],
             pltpu.VMEM((pool_rows, width), LOW),
             pltpu.SemaphoreType.DMA((3, 2, 3)),
             pltpu.SemaphoreType.DMA((3,)),
-            *GatherRing.scratch(3),
+            pltpu.VMEM((RING, 8, depth), WIDE),
+            *[pltpu.VMEM((RING, 16, columns), WIDE)] * 2,
+            *[pltpu.SemaphoreType.DMA((2, RING - 1))] * 2,
+            pltpu.SemaphoreType.DMA((2, 3)),
+            *GatherRing.scratch(2),
+            *GatherRing.scratch(1),
         ],
         compiler_params=pltpu.CompilerParams(
             collective_id=ident, has_side_effects=True, vmem_limit_bytes=VMEM_LIMIT
         ),
         name="first_ring",
-    )(*x, *cotangent, mods, *blocks)
-    return found[:2], found[2], found[3:5], found[5]
+    )(*x, *cotangent, cond, ada, *blocks)
+    return found[:2], found[2], found[3:5], found[5], found[6][:12], found[7]
 
 
 def exchange_sums(part, sent, got, sems, me):
@@ -627,11 +686,12 @@
     out_blocks, ffn_blocks, refs = refs[7:9], refs[9:11], refs[11:]
     mixed, lse_ref, *wide_outs, text_in, image_in = refs[:8]
     branch_image, branch_text, mid_image, mid_text = wide_outs
-    out_fulls, ffn_fulls, refs = refs[8:10], refs[10:12], refs[12:]
+    pool, out_fulls, ffn_fulls, refs = refs[8:9], refs[9:11], refs[11:13], refs[13:]
     weights, sent, got, far_sent, far_got, here, mine = refs[:7]
     sems, weight_sem, row_sem, own_sem = refs[7:11]
     first = GatherRing(out_blocks, out_fulls, refs[11:14])
     second = GatherRing(ffn_blocks, ffn_fulls, refs[14:17])
+    third = GatherRing([text_in.at[pl.ds(0, pool[0].shape[0] // RING)]], pool, refs[17:20])
     me = lax.axis_index("dp")
     block = q_ref.shape[0]
     pair, at = pl.program_id(0), pl.program_id(0) * 2 + pl.program_id(1)
@@ -726,19 +786,25 @@
         middle, low = norm_rows(x_text[...], branch, 1)
         mid_text[...] = middle
         text_in[...] = low
+        third.start()
         second.step(2)
+        third.step(1)
         to_far.wait()
         last = row_copy(image_in.at[pl.ds(2 * rows, rows)], 3, 1, 2)
         last.start()
+        third.step(2)
         second.step(3)
+        third.step(3)
         own.wait()
         to_near.wait()
         last.wait()
+        third.step(4)
         second.step(4)
         second.end()
-
-
-def middle_ring(joint, bias, x, mods, split, heads, out_blocks, ffn_blocks, ident):
+        third.end()
+
+
+def middle_ring(joint, bias, x, mods, split, heads, out_blocks, ffn_blocks, pool_rows, ident):
     rows, pairs, block = joint.shape[0], heads // 2, joint.shape[0] // 2
     whole = lambda part: pl.BlockSpec((rows, LANES), lambda h, i: (0, part * pairs + h))
     image_rows, width = x[0].shape
@@ -760,7 +826,7 @@
             WHOLE,
             pl.BlockSpec((1, 8, block), lambda h, i: (h, 0, i)),
             *[WHOLE] * 5,
-            *[ANY] * 5,
+            *[ANY] * 6,
         ],
         out_shape=[
             jax.ShapeDtypeStruct((rows, depth), LOW),
@@ -768,6 +834,7 @@
             *[jax.ShapeDtypeStruct((n, width), WIDE) for n in (image_rows, text_rows) * 2],
             jax.ShapeDtypeStruct((text_rows, width), LOW),
             jax.ShapeDtypeStruct((4 * image_rows, width), LOW),
+            jax.ShapeDtypeStruct((RING * pool_rows, width), LOW),
             *[
                 jax.ShapeDtypeStruct((RING * b.shape[0], b.shape[1]), b.dtype)
                 for b in (*out_blocks, *ffn_blocks)
@@ -787,6 +854,7 @@
             pltpu.SemaphoreType.DMA((1,)),
             *GatherRing.scratch(2),
             *GatherRing.scratch(2),
+            *GatherRing.scratch(1),
         ],
         compiler_params=pltpu.CompilerParams(
             collective_id=ident, has_side_effects=True, vmem_limit_bytes=VMEM_LIMIT
@@ -798,14 +866,15 @@
 
 def back_kernel(split, chunk, *refs):
     bias_ref, q_ref, k_ref, v_ref, o_ref, lse_ref = refs[:6]
-    text_second, mid_image, mid_text, cot_image, cot_text, mods = refs[6:12]
+    mid_image, mid_text, cot_image, cot_text, mods, text_part = refs[6:12]
     partial, out_weights, grads, theirs, refs = refs[12], refs[13:15], refs[15:17], refs[17:19], refs[19:]
     dq_ref, dk_ref, dv_ref, image_second, image_grad, text_grad = refs[:6]
     image_rows, text_rows, *fars = refs[6:10]
-    sums, refs = refs[10:12], refs[12:]
+    sums, text_second, refs = refs[10:12], refs[12], refs[13:]
     dk_acc, dv_acc, weights, parts, got, far_sent, far_got, rows_in, mixed_grad = refs[:9]
-    part_sem, sems, row_sem, weight_sem, rows_sem, far_sem = refs[9:15]
-    ring = ScatterRing(grads, sums, refs[15:])
+    part_sem, sems, row_sem, weight_sem, rows_sem, far_sem, text_sum = refs[9:16]
+    ring = ScatterRing(grads, sums, refs[16:23])
+    text_ring = ScatterRing([text_part], [text_sum], refs[23:])
     me = lax.axis_index("dp")
     rows, texts = mid_image.shape[0], mid_text.shape[0]
     block = q_ref.shape[0]
@@ -856,10 +925,12 @@
         for i in range(2):
             keep(i).start()
             weight(i).start()
+        text_ring.load_all()
         ring.load_all()
         meet([*ring.sides, *[(me, tensor_peer(hop)) for hop in (1, 2)]])
         for i in range(2):
             near(i).start()
+        text_ring.start()
         ring.start()
         for i in range(2):
             keep(i).wait()
@@ -870,9 +941,8 @@
             device_id=(me, tensor_peer(2)), device_id_type=MESH,
         )
         far.start()
-        grad, low = rows_back(text_second[...], mid_text[...], cot_text[...], 1)
-        text_grad[...] = grad
-        rows_in[0, rows:] = low
+        for step in range(1, 4):
+            text_ring.step(step)
         ring.step(1)
         far.wait()
 
@@ -886,7 +956,16 @@
             rows_in[0, some] = low
             return 0
 
+        text_ring.step(4)
         lax.fori_loop(0, rows // chunk, image_chunk, 0)
+        for step in range(5, 8):
+            text_ring.step(step)
+        pooled = text_sum.shape[0]
+        text_second[...] = jnp.zeros_like(text_second)
+        text_second[:pooled] = text_sum[...]
+        grad, low = rows_back(text_second[...], mid_text[...], cot_text[...], 1)
+        text_grad[...] = grad
+        rows_in[0, rows:] = low
         to_far = row_copy(rows_in.at[0], 2, 2, 0)
         to_near = row_copy(rows_in.at[0], 1, 1, 1)
         to_far.start()
@@ -947,6 +1026,7 @@
     def _():
         ring.step(7)
         ring.end()
+        text_ring.end()
         for copy in far_copies:
             copy.wait()
         for b in range(4):
@@ -955,7 +1035,7 @@
 
 
 def back_ring(
-    joint, bias, mixed, lse, split, heads, text_second, middle, cotangent, mods, partial,
+    joint, bias, mixed, lse, split, heads, text_part, middle, cotangent, mods, partial,
     out_weights, grads, theirs, ident, block=256,
 ):
     rows, pairs = joint.shape[0], heads // 2
@@ -963,7 +1043,7 @@
     some = pl.BlockSpec((block, LANES), lambda h, i: (i, h))
     image_rows, width = middle[0].shape
     texts = middle[1].shape[0]
-    depth = heads * HEAD_DIM
+    depth, pooled = heads * HEAD_DIM, text_part.shape[0] // RING
     found = pl.pallas_call(
         functools.partial(back_kernel, split, 64),
         grid=(pairs, rows // block),
@@ -974,16 +1054,17 @@
             whole(2),
             some,
             pl.BlockSpec((1, 8, block), lambda h, i: (h, 0, i)),
-            *[WHOLE] * 6,
-            *[ANY] * 7,
-        ],
-        out_specs=[some, whole(0), whole(0), *[WHOLE] * 3, *[ANY] * 4, WHOLE, WHOLE],
+            *[WHOLE] * 5,
+            *[ANY] * 8,
+        ],
+        out_specs=[some, whole(0), whole(0), *[WHOLE] * 3, *[ANY] * 4, *[WHOLE] * 3],
         out_shape=[
             *[jax.ShapeDtypeStruct((rows, depth), LOW)] * 3,
             *[jax.ShapeDtypeStruct((n, width), WIDE) for n in (image_rows, image_rows, texts)],
             *[jax.ShapeDtypeStruct((4 * n, width), LOW) for n in (image_rows, texts)],
             *[jax.ShapeDtypeStruct(t.shape, t.dtype) for t in theirs],
             *[jax.ShapeDtypeStruct((g.shape[0] // RING, g.shape[1]), WIDE) for g in grads],
+            jax.ShapeDtypeStruct((texts, width), WIDE),
         ],
         scratch_shapes=[
             *[pltpu.VMEM((rows, LANES), WIDE)] * 2,
@@ -998,14 +1079,16 @@
             pltpu.SemaphoreType.DMA((2,)),
             pltpu.SemaphoreType.DMA((2, 4)),
             pltpu.SemaphoreType.DMA((2, 2)),
+            pltpu.VMEM((pooled, width), WIDE),
             *ScatterRing.scratch([g.shape for g in grads]),
+            *ScatterRing.scratch([text_part.shape]),
         ],
         compiler_params=pltpu.CompilerParams(
             collective_id=ident, has_side_effects=True, vmem_limit_bytes=VMEM_LIMIT
         ),
         name="back_ring",
     )(
-        bias.T, joint, joint, joint, mixed, lse, text_second, *middle, *cotangent, mods,
+        bias.T, joint, joint, joint, mixed, lse, *middle, *cotangent, mods, text_part,
         partial, *out_weights, *grads, *theirs,
     )
     return found
@@ -1202,28 +1285,40 @@
         return rows.reshape(-1, width)
 
     def unpool_end(here, far):
-        part = (here + far.astype(WIDE)).astype(LOW).reshape(size, pool_rows, width)
+        return own_pool((here + far.astype(WIDE)).astype(LOW))
+
+    def own_pool(part):
+        part = part.reshape(size, pool_rows, width)
         part = lax.all_to_all(part, "dp", split_axis=0, concat_axis=0, tiled=True)
         total = jnp.sum(part.astype(WIDE), axis=0)
         return jnp.pad(total, ((0, text_rows - pool_rows), (0, 0)))
 
 
     cond_low = jax.nn.silu(cond).astype(LOW)
-    cond_rows = lax.all_to_all(
-        cond_low.reshape(seqs, ada_rows), "dp", split_axis=0, concat_axis=0, tiled=True
-    )
+    cond_rows = cond_low.reshape(seqs, ada_rows)
     ada_low = w_ada.astype(LOW)
-    mod_parts = jnp.einsum("nd,sdkf->nskf", cond_rows, ada_low, preferred_element_type=WIDE)
-    mod_parts = lax.all_to_all(mod_parts, "dp", split_axis=0, concat_axis=0, tiled=True)
-    modulation = lax.all_gather(jnp.sum(mod_parts, axis=0), "tensor", axis=2, tiled=True)
-
-    def mod_row(stream, which):
-        return modulation[stream, which][None, :]
 
     def own_text(rows):
         padded = jnp.pad(rows, ((0, 4 * text_own - text_tokens), (0, 0)))
         own = lax.dynamic_slice_in_dim(padded, index * text_own, text_own, 0)
         return jnp.pad(own, ((0, text_rows - text_own), (0, 0)))
+
+    cot_rows = [grad_image[0], own_text(grad_text[0])]
+    x_rows = [image[0], own_text(text[0])]
+    if size == RING:
+        ada_rows_low = ada_low.transpose(0, 2, 1, 3).reshape(12, ada_rows, width_here)
+        attn_rows, ffn_rows, qkv_full, pooled_grad, modulation, cond_rows = first_ring(
+            x_rows, cot_rows, cond_rows, ada_rows_low, blocks_of(w_qkv), pool_rows, 1
+        )
+        modulation, cond_rows = modulation.reshape(2, 6, width), cond_rows.astype(LOW)
+    else:
+        cond_rows = lax.all_to_all(cond_rows, "dp", split_axis=0, concat_axis=0, tiled=True)
+        mod_parts = jnp.einsum("nd,sdkf->nskf", cond_rows, ada_low, preferred_element_type=WIDE)
+        mod_parts = lax.all_to_all(mod_parts, "dp", split_axis=0, concat_axis=0, tiled=True)
+        modulation = lax.all_gather(jnp.sum(mod_parts, axis=0), "tensor", axis=2, tiled=True)
+
+    def mod_row(stream, which):
+        return modulation[stream, which][None, :]
 
     split_at = 4 * image_rows
     places = jnp.arange(4 * text_rows)
@@ -1231,22 +1326,14 @@
     is_key = (places % text_rows < text_own) & (token < text_tokens)
     bias = jnp.where(is_key, 0.0, -1e30).astype(WIDE)[None, :]
 
-    streams = [image[0].astype(WIDE), own_text(text[0]).astype(WIDE)]
-    cotangent = [grad_image[0].astype(WIDE), own_text(grad_text[0]).astype(WIDE)]
+    streams = [rows.astype(WIDE) for rows in x_rows]
+    cotangent = [rows.astype(WIDE) for rows in cot_rows]
     normed_in = [layer_norm(residual) for residual in streams]
     first_in = [
         (normed_in[s] * (1.0 + mod_row(s, 1)) + mod_row(s, 0)).astype(LOW) for s in range(2)
     ]
     ffn_grad = [(mod_row(s, 5) * cotangent[s]).astype(LOW) for s in range(2)]
-    cot_rows = [grad_image[0], own_text(grad_text[0])]
-    x_rows = [image[0], own_text(text[0])]
-    if size == RING:
-        mods = [1.0 + mod_row(0, 1), mod_row(0, 0), 1.0 + mod_row(1, 1), mod_row(1, 0)]
-        mods += [mod_row(0, 5), mod_row(1, 5), jnp.zeros((2, width), WIDE)]
-        attn_rows, ffn_rows, qkv_full, pooled_grad = first_ring(
-            x_rows, cot_rows, jnp.concatenate(mods, axis=0), blocks_of(w_qkv), pool_rows, 1
-        )
-    else:
+    if size != RING:
         attn_rows = [gather_rows(rows) for rows in first_in]
         ffn_rows, pooled_grad = gather_rows(ffn_grad[0]), pool_start(ffn_grad[1])
         qkv_full = gather_dp(blocks_of(w_qkv), size, 1)
@@ -1262,11 +1349,12 @@
             axis=0,
         )
         found = middle_ring(
-            joint, bias, x_rows, mods, split_at, heads_here, blocks_of(w_out), ffn_blocks, 2
+            joint, bias, x_rows, mods, split_at, heads_here, blocks_of(w_out), ffn_blocks,
+            pool_rows, 2,
         )
         mixed, log_total, *found = found
-        branches, middle, text_in, mlp_rows = found[:2], found[2:4], found[4], found[5]
-        out_full, up_full, down_full = found[6:8], found[8], found[9]
+        branches, middle, mlp_rows, pooled_in = found[:2], found[2:4], found[5], found[6]
+        out_full, up_full, down_full = found[7:9], found[9], found[10]
     else:
         mixed, log_total, _ = attend(joint, bias, split_at, heads_here, [], 0, ())
         *out_full, up_full, down_full = gather_dp(blocks_of(w_out) + ffn_blocks, size, 2)
@@ -1279,7 +1367,7 @@
             (layer_norm(middle[s]) * (1.0 + mod_row(s, 4)) + mod_row(s, 3)).astype(LOW)
             for s in range(2)
         ]
-        mlp_rows, text_in = gather_rows(second_in[0]), second_in[1]
+        mlp_rows, pooled_in = gather_rows(second_in[0]), pool_start(second_in[1])
     mixed, *text_ffn_moved = lax.optimization_barrier((mixed, *text_ffn_moved))
     text_ffn_rows = gather_end(pooled_grad, *text_ffn_moved)
     mixed_rows = [mixed[:split_at], mixed[split_at:]]
@@ -1288,17 +1376,11 @@
     def gelu_back(pre_act, hidden_grad):
         return jax.vjp(gelu_tanh, pre_act)[1](hidden_grad)[0].astype(LOW)
 
-    pooled_in = pool_start(text_in)
+    text_moved = gather_start(pooled_in)
     pre_act = dot(mlp_rows, up_full, NN)
     hidden = gelu_tanh(pre_act).astype(LOW)
-    hidden, pre_act, pooled_in = lax.optimization_barrier((hidden, pre_act, pooled_in))
-    text_moved = gather_start(pooled_in)
     pre_grad = gelu_back(pre_act, dot(ffn_rows, down_full, NT))
-    second_part = dot(pre_grad, up_full, NT).astype(LOW)
-    down_grad = dot(hidden, ffn_rows, TN).astype(LOW)
-    second_part, down_grad, *text_moved = lax.optimization_barrier(
-        (second_part, down_grad, *text_moved)
-    )
+    pre_grad, *text_moved = lax.optimization_barrier((pre_grad, *text_moved))
     text_mlp_rows = gather_end(pooled_in, *text_moved)
     text_pre_act = dot(text_mlp_rows, text_up, NN)
     text_hidden = gelu_tanh(text_pre_act).astype(LOW)
@@ -1306,19 +1388,18 @@
     text_here, text_there = scatter_start(dot(text_pre_grad, text_up, NT))
     text_far = lax.ppermute(text_there, "tensor", CHIP)
     pre_grad, text_there = lax.optimization_barrier((pre_grad, text_there))
+    second_part = dot(pre_grad, up_full, NT).astype(LOW)
+    down_grad = dot(hidden, ffn_rows, TN).astype(LOW)
     up_grad = dot(mlp_rows, pre_grad, TN).astype(LOW)
     here, there = scatter_start(dot(hidden, down_full, NN))
-    up_grad, there, text_far = lax.optimization_barrier((up_grad, there, text_far))
+    up_grad, down_grad, second_part, there, text_far = lax.optimization_barrier(
+        (up_grad, down_grad, second_part, there, text_far)
+    )
     second_grad, ffn = [None, None], [None, None]
-    second_grad[1] = unpool_end(text_here, text_far)
+    text_second = (text_here + text_far.astype(WIDE)).astype(LOW)
     text_here, text_there = scatter_start(dot(text_hidden, text_down, NN))
     text_down_grad = dot(text_hidden, text_ffn_rows, TN)
     text_up_grad = dot(text_mlp_rows, text_pre_grad, TN)
-    second_part, second_grad[1], text_there, text_down_grad, text_up_grad = (
-        lax.optimization_barrier(
-            (second_part, second_grad[1], text_there, text_down_grad, text_up_grad)
-        )
-    )
     if size == RING:
         mods = jnp.concatenate(
             [row for s in range(2) for row in (mod_row(s, 2), 1.0 + mod_row(s, 4))]
@@ -1326,15 +1407,16 @@
             axis=0,
         )
         found = back_ring(
-            joint, bias, mixed, log_total, split_at, heads_here, second_grad[1], middle,
+            joint, bias, mixed, log_total, split_at, heads_here, text_second, middle,
             cot_rows, mods, second_part, out_full,
             [down_grad, up_grad], [there, text_there], 5,
         )
-        *grads, second_grad[0], image_middle, text_middle = found[:6]
+        *grads, image_second, image_middle, text_middle = found[:6]
         middle_grad, branch_rows = [image_middle, text_middle], found[6:8]
-        far, text_far, down_sum, up_sum = found[8:]
+        far, text_far, down_sum, up_sum, text_sum = found[8:]
+        second_grad = [image_second, text_sum]
     else:
-        second_grad[0] = scatter_rows(second_part)
+        second_grad = [scatter_rows(second_part), own_pool(text_second)]
         middle_grad, branch_rows = [None, None], [None, None]
         for s in range(2):
             wide = second_grad[s] * (1.0 + mod_row(s, 4))

time: 759 us -> 717 us (0.945)
  Pallas kernels: 423 us -> 461 us
  waiting for transfers between devices: 57.6 us -> 19.7 us
  starting transfers between devices: 41.4 us -> 23.5 us
  other arithmetic: 48.7 us -> 34.8 us
    all_to_all x5 -> x1, waiting for transfers between devices: 35.4 us -> 8.97 us  [own_pool(): part = lax.all_to_all(part, 'dp', split_axis=0, concat_axis=0, tiled=True)]
    all_to_all x5 -> x1, starting transfers between devices: 25 us -> 6.11 us  [own_pool(): part = lax.all_to_all(part, 'dp', split_axis=0, concat_axis=0, tiled=True)]
    pallas_call x1, Pallas kernels: 109 us -> 127 us  [back_ring(): pl.pallas_call(functools.partial(back_kernel, split, 64), grid=(pairs, ro...]
    pallas_call x1, Pallas kernels: 122 us -> 135 us  [middle_ring(): pl.pallas_call(functools.partial(middle_kernel, split, 64), grid=(pairs,...]
    pallas_call x1, Pallas kernels: 87.4 us -> 95.1 us  [first_ring(): pl.pallas_call(functools.partial(first_kernel, 64), in_specs=[WHOLE] * 6...]
    unnamed x168 -> x166, local copies, waits for them, and re-layouts: 26.6 us -> 33 us
  transfers between devices with their start and end apart: 19 -> 15, of which waited for: 7 -> 2; matrix products, arithmetic and copies ran while one was open for 23% -> 22% of each run, Pallas kernels for 28% -> 19%
where the time goes in v5:
time: 717 us; the launch traced here: 711 us
  Pallas kernels  461 us (64%)
  matrix products  102 us (14%)
  local copies, waits for them, and re-layouts  62.8 us (9%)
  other arithmetic  34.8 us (5%)
  starting transfers between devices  23.5 us (3%)
  waiting for transfers between devices  19.7 us (3%)
    pallas_call x1, Pallas kernels, middle_ring(): pl.pallas_call(functools.partial(middle_kernel, split, 64), grid=(pairs,...  135 us
    pallas_call x1, Pallas kernels, back_ring(): pl.pallas_call(functools.partial(back_kernel, split, 64), grid=(pairs, ro...  127 us
    pallas_call x1, Pallas kernels, tail_ring(): pl.pallas_call(functools.partial(tail_kernel, columns, len(grads)), out_s...  104 us
    dot_general x20, matrix products, dot(): lax.dot_general(left, right, (dims, ((), ())), preferred_element_type=WIDE)  98.3 us
    pallas_call x1, Pallas kernels, first_ring(): pl.pallas_call(functools.partial(first_kernel, 64), in_specs=[WHOLE] * 6...  95.1 us
    unnamed x166, local copies, waits for them, and re-layouts  33 us
  transfers between devices with their start and end apart: 15, of which 2 were waited for; matrix products, arithmetic and copies ran while one was open for 22% of the time, Pallas kernels for 19%

profile of v5, /device:TPU:0, one launch (start us, length us, event | category | flops | bytes accessed | tf_op | source)
XLA Modules:
  0.0 711.5 jit_solution(3509596220491128653)
XLA Ops:
  0.7 1.4 convert_reduce_fusion.1
  7.3 1.4 convert_element_type.212
  9.4 95.1 %first_ring.1 = (bf16[1024,1536]{1,0:T(8,128)(2,1)}, bf16[256,1536]{1,0:T(8,128)(2,1)}, bf16[1024,1536]{1,0:T(8,128)(2,1)}, bf16[1536,1152]{1,0:T(8,128)(2,1)}, ...) custom-call(bf16[256,1536]{1,0:T(8,128)(2,1)} %bitcast.121, ...), custom_call_target="tpu_custom_call" | custom-call | tf_op jit(solution)/shard_map/first_ring/pallas_call | solution.py:643
  110.7 3.3 convolution_convert_fusion.12
  114.0 6.1 convolution_convert_fusion.8
  120.2 1.8 pad_maximum_fusion.refs_1_.refs_2_.refs_3_
  122.7 134.6 %middle_ring.1 = (bf16[1280,384]{1,0:T(8,128)(2,1)}, f32[3,8,1280]{2,1,0:T(8,128)}, f32[256,1536]{1,0:T(8,128)}, f32[64,1536]{1,0:T(8,128)}, f32[256,1536]{1,0:T...) custom-call(f32[1,256]{1,0:T(1,128)} %and_select_fusion.refs_0_, ...), custom_call_target="tpu_custom_call" | custom-call | tf_op jit(solution)/shard_map/middle_ring/pallas_call | solution.py:814
  259.0 3.7 all-to-all-start
  262.8 8.1 %fusion.61 = f32[1024,1536]{1,0:T(8,128)S(1)} fusion(bf16[1024,1536]{1,0:T(8,128)(2,1)} %get-tuple-element.86, bf16[1536,1536]{1,0:T(8,128)(2,1)} %get-tuple-element.77), kind=kOutput, calls=%fused_computation.158 | convolution fusion | flops 4831838208 | bytes 14155776 | tf_op jit(solution)/shard_map/dot_general | solution.py:21
  270.9 11.0 %fusion.6 = (bf16[1024,1536]{1,0:T(8,128)(2,1)}, f32[1024,1536]{1,0:T(8,128)S(1)}) fusion(f32[1024,1536]{1,0:T(8,128)S(1)} %fusion.61, bf16[1024,1536]{1,0:T(8,128)(2,1)S(1)} %copy-done.68, bf16[1536,1536]{1,0:T(8,128)(2,1)} %get-tuple-element.76), kind=kOutput, calls=%fused_computation.14 | convolution fusion | flops 4863295488 | bytes 23592960 | tf_op jit(solution)/shard_map/dot_general | solution.py:21
  281.9 5.6 convolution_convert_fusion.7
  291.1 17.8 %convolution_convert_fusion.1.refs_15_ = bf16[1536,1536]{1,0:T(8,128)(2,1)} fusion(bf16[1024,1536]{1,0:T(8,128)(2,1)S(1)} %copy-done.70, f32[1024,1536]{1,0:T(8,128)S(1)} %get-tuple-element.195), kind=kOutput, calls=%fused_computation.3 | convolution fusion | flops 4848353280 | bytes 14155776 | tf_op jit(solution)/shard_map/dot_general | solution.py:21
  310.8 2.4 constant_dynamic-update-slice_fusion.3
  318.0 2.5 constant_dynamic-update-slice_fusion.2
  320.5 2.4 constant_dynamic-update-slice_fusion.1
  322.9 1.3 constant_dynamic-update-slice_fusion.6
  324.2 1.3 constant_dynamic-update-slice_fusion.5
  325.7 1.7 fusion.62
  328.4 2.0 fusion.17
  330.4 1.4 convolution_convert_fusion.5
  332.6 2.4 add_convert_fusion.6.refs_17_
  335.1 1.5 convolution_convert_fusion.4
  337.0 1.9 fusion.63
  339.0 2.2 convolution_bitcast_fusion
  341.5 1.6 collective-permute-start.8
  343.1 6.9 convolution_convert_fusion.2.refs_16_
  350.0 1.4 copy-done.19
  351.4 1.3 add_convert_fusion.1.refs_18_
  352.7 6.4 convolution_convert_fusion.6.refs_12_
  359.1 10.7 %collective-permute-done.8 = bf16[384,1536]{1,0:T(8,128)(2,1)S(1)} collective-permute-done((bf16[384,1536]{1,0:T(8,128)(2,1)S(1)}, bf16[384,1536]{1,0:T(8,128)(2,1)S(1)}, u32[]{:S(2)}, u32[]{:S(2)}) %collective-permute-start.8) | collective-permute-done | bytes 1179680 | tf_op jit(solution)/shard_map/ppermute | solution.py:1389
  369.8 1.4 add_convert_fusion.2.refs_11_
  371.2 126.9 %back_ring.1 = (bf16[1280,384]{1,0:T(8,128)(2,1)}, bf16[1280,384]{1,0:T(8,128)(2,1)}, bf16[1280,384]{1,0:T(8,128)(2,1)}, f32[256,1536]{1,0:T(8,128)}, f32[256,15...) custom-call(f32[256,1]{1,0:T(8,128)} %fusion.41.refs_0_, ...), custom_call_target="tpu_custom_call" | custom-call | tf_op jit(solution)/shard_map/back_ring/pallas_call | solution.py:1047
  498.2 1.4 constant_dynamic-update-slice_fusion.10
  500.1 1.6 copy-done.66
  501.7 2.1 convolution_convert_fusion.13
  505.0 4.5 convolution_convert_fusion.9
  509.5 2.2 copy.56
  511.7 4.4 all-to-all-start.2
  516.1 1.4 fusion.56
  518.3 1.5 pad_maximum_fusion.6
  521.8 1.6 pad_maximum_fusion.5
  524.9 3.3 multiply_reduce_fusion
  528.3 2.8 add_convert_fusion
  534.1 4.0 convolution_convert_fusion.3.refs_10_
  538.2 6.1 all-to-all-start.1
  544.3 1.5 convolution_convert_fusion.10.refs_12_
  545.8 4.5 convolution_convert_fusion.11.refs_11_
  550.3 5.8 convolution_convert_fusion.refs_9_
  556.1 1.7 copy.46
  557.7 1.5 all_to_all.40
  559.3 3.7 add_convert_fusion.4
  563.1 9.0 %all-to-all-done.1 = bf16[8,48,1536]{2,1,0:T(8,128)(2,1)S(1)} async-done(((bf16[8,48,1536]{2,1,0:T(8,128)(2,1)}), bf16[8,48,1536]{2,1,0:T(8,128)(2,1)S(1)}, u32[]{:S(2)}, u32[]{:S(2)}) %all-to-all-start.1) | async-done | bytes 1179680 | tf_op jit(solution)/shard_map/all_to_all | solution.py:1292
  572.3 1.7 multiply_reduce_fusion.4
  574.1 1.3 concatenate.60.refs_3_
  575.5 104.2 %tail_ring.1 = (f32[256,1536]{1,0:T(8,128)}, f32[16,384]{1,0:T(8,128)}, bf16[8,16,384]{2,1,0:T(8,128)(2,1)}, bf16[4,64,1536]{2,1,0:T(8,128)(2,1)}, f32[4,64,1536...) custom-call(f32[320,1536]{1,0:T(8,128)} %get-tuple-element.170.refs_0_, ...), custom_call_target="tpu_custom_call" | custom-call | tf_op jit(solution)/shard_map/tail_ring/pallas_call | solution.py:444
  683.2 4.5 all-to-all-start.3
  687.9 1.3 copy-done.43
  690.4 1.5 stack.34
  691.8 1.5 stack.35
  693.3 3.4 convolution_bitcast_fusion.1
  696.8 1.6 pad_maximum_fusion.4
  700.4 1.9 copy.50
  702.3 1.3 copy.52
  703.7 5.7 psum.7
  (255 shorter events, 45.4 us)
Async XLA Ops:
  0.6 4.0 copy-start.22
  4.9 2.4 copy-start.9
  9.4 96.7 %copy-start.44 = (f32[2,48,1536]{2,1,0:T(8,128)S(1)}, f32[2,48,1536]{2,1,0:T(8,128)}, u32[]{:S(2)}) copy-start(f32[2,48,1536]{2,1,0:T(8,128)} %param.15) | copy-start | bytes 1769476
  9.4 97.5 %copy-start.17 = (f32[2,192,1536]{2,1,0:T(8,128)S(1)}, f32[2,192,1536]{2,1,0:T(8,128)}, u32[]{:S(2)}) copy-start(f32[2,192,1536]{2,1,0:T(8,128)} %param.17) | copy-start | bytes 7077892
  104.5 213.3 %collective-permute-start.2 = (bf16[384,1536]{1,0:T(8,128)(2,1)}, bf16[384,1536]{1,0:T(8,128)(2,1)}, u32[]{:S(2)}, u32[]{:S(2)}) collective-permute-start(bf16[384,1536]{1,0:T(8,128)(2,1)} %get-tuple-element.79), channel_id=1, source_target_pairs={{0,2},{1,3},{2,0},{3,1},{4,6},{5,7},{6,4},{7,5},{8,10},{9,11},{10,... | collective-permute-start | bytes 3538952 | tf_op jit(solution)/shard_map/ppermute | solution.py:295
  105.5 212.2 %collective-permute-start.1 = (bf16[384,1536]{1,0:T(8,128)(2,1)}, bf16[384,1536]{1,0:T(8,128)(2,1)}, u32[]{:S(2)}, u32[]{:S(2)}) collective-permute-start(bf16[384,1536]{1,0:T(8,128)(2,1)} %get-tuple-element.79), channel_id=1, source_target_pairs={{0,1},{1,0},{2,3},{3,2},{4,5},{5,4},{6,7},{7,6},{8,9},{9,8},{10,11... | collective-permute-start | bytes 3538952 | tf_op jit(solution)/shard_map/ppermute | solution.py:294
  110.7 3.3 copy-start.64
  257.3 57.0 %collective-permute-start.5 = (bf16[384,1536]{1,0:T(8,128)(2,1)}, bf16[384,1536]{1,0:T(8,128)(2,1)}, u32[]{:S(2)}, u32[]{:S(2)}) collective-permute-start(bf16[384,1536]{1,0:T(8,128)(2,1)} %get-tuple-element.85), channel_id=1, source_target_pairs={{0,2},{1,3},{2,0},{3,1},{4,6},{5,7},{6,4},{7,5},{8,10},{9,11},{10,... | collective-permute-start | bytes 3538952 | tf_op jit(solution)/shard_map/ppermute | solution.py:295
  257.9 56.5 %collective-permute-start.4 = (bf16[384,1536]{1,0:T(8,128)(2,1)}, bf16[384,1536]{1,0:T(8,128)(2,1)}, u32[]{:S(2)}, u32[]{:S(2)}) collective-permute-start(bf16[384,1536]{1,0:T(8,128)(2,1)} %get-tuple-element.85), channel_id=1, source_target_pairs={{0,1},{1,0},{2,3},{3,2},{4,5},{5,4},{6,7},{7,6},{8,9},{9,8},{10,11... | collective-permute-start | bytes 3538952 | tf_op jit(solution)/shard_map/ppermute | solution.py:294
  259.0 57.6 %all-to-all-start = ((bf16[192,8,192]{0,2,1:T(8,128)(2,1)}), bf16[192,8,192]{0,2,1:T(8,128)(2,1)S(1)}, u32[]{:S(2)}, u32[]{:S(2)}) async-start(bf16[192,8,192]{0,2,1:T(8,128)(2,1)} %bitcast.17), calls=%async_computation | async-start | bytes 1572864 | tf_op jit(solution)/shard_map/all_to_all | solution.py:1277
  262.8 8.1 %copy-start.68 = (bf16[1024,1536]{1,0:T(8,128)(2,1)S(1)}, bf16[1024,1536]{1,0:T(8,128)(2,1)}, u32[]{:S(2)}) copy-start(bf16[1024,1536]{1,0:T(8,128)(2,1)} %get-tuple-element.75) | copy-start | bytes 9437188
  262.8 19.1 %slice-start.2 = ((s8[4718592]{0:T(1024)(128)(4,1)}), s8[4194304]{0:T(1024)(128)(4,1)S(1)}, s32[]{:S(2)}) async-start(s8[4718592]{0:T(1024)(128)(4,1)} %bitcast.146), calls=%async_computation.6 | async-start | bytes 8388608
  270.9 11.0 %slice-start.3 = ((s8[4718592]{0:T(1024)(128)(4,1)}), s8[524288]{0:T(1024)(128)(4,1)S(1)}, s32[]{:S(2)}) async-start(s8[4718592]{0:T(1024)(128)(4,1)} %bitcast.146), calls=%async_computation.7 | async-start | bytes 1048576
  287.5 2.4 copy-start.10
  287.6 3.5 copy-start.70
  289.8 19.0 %copy-start = (f32[256,1536]{1,0:T(8,128)S(1)}, f32[256,1536]{1,0:T(8,128)}, u32[]{:S(2)}) copy-start(f32[256,1536]{1,0:T(8,128)} %get-tuple-element.74.refs_6_) | copy-start | bytes 4718596
  289.8 42.8 %collective-permute-start = (bf16[512,1536]{1,0:T(8,128)(2,1)}, bf16[512,1536]{1,0:T(8,128)(2,1)}, u32[]{:S(2)}, u32[]{:S(2)}) collective-permute-start(bf16[512,1536]{1,0:T(8,128)(2,1)} %pad_maximum_fusion.7), channel_id=1, source_target_pairs={{0,1},{1,0},{2,3},{3,2},{4,5},{5,4},{6,7},{7,6},{8,9},{9,8},{10,11... | collective-permute-start | bytes 4718600 | tf_op jit(solution)/shard_map/ppermute | solution.py:312
  309.3 3.9 copy-start.28
  314.4 11.2 %collective-permute-start.6 = (bf16[384,1536]{1,0:T(8,128)(2,1)}, bf16[384,1536]{1,0:T(8,128)(2,1)S(1)}, u32[]{:S(2)}, u32[]{:S(2)}) collective-permute-start(bf16[384,1536]{1,0:T(8,128)(2,1)} %collective-permute-done.5), channel_id=1, source_target_pairs={{0,1},{1,0},{2,3},{3,2},{4,5},{5,4},{6,7},{7,6},{8,9},{9,8},{10,11... | collective-permute-start | bytes 3538952 | tf_op jit(solution)/shard_map/ppermute | solution.py:300
  317.7 5.1 copy-start.46
  317.7 9.6 %collective-permute-start.3 = (bf16[384,1536]{1,0:T(8,128)(2,1)}, bf16[384,1536]{1,0:T(8,128)(2,1)S(1)}, u32[]{:S(2)}, u32[]{:S(2)}) collective-permute-start(bf16[384,1536]{1,0:T(8,128)(2,1)} %collective-permute-done.2), channel_id=1, source_target_pairs={{0,1},{1,0},{2,3},{3,2},{4,5},{5,4},{6,7},{7,6},{8,9},{9,8},{10,11... | collective-permute-start | bytes 3538952 | tf_op jit(solution)/shard_map/ppermute | solution.py:300
  325.7 2.7 copy-start.14
  332.2 9.0 %collective-permute-start.7 = (bf16[768,1536]{1,0:T(8,128)(2,1)S(1)}, bf16[768,1536]{1,0:T(8,128)(2,1)S(1)}, u32[]{:S(2)}, u32[]{:S(2)}) collective-permute-start(bf16[768,1536]{1,0:T(8,128)(2,1)S(1)} %pad_maximum_fusion.1), channel_id=1, source_target_pairs={{0,1},{1,0},{2,3},{3,2},{4,5},{5,4},{6,7},{7,6},{8,9},{9,8},{10,11... | collective-permute-start | bytes 7077896 | tf_op jit(solution)/shard_map/ppermute | solution.py:312
  336.5 13.4 %copy-start.7 = (bf16[1536,1536]{1,0:T(8,128)(2,1)}, bf16[1536,1536]{1,0:T(8,128)(2,1)S(1)}, u32[]{:S(2)}) copy-start(bf16[1536,1536]{1,0:T(8,128)(2,1)S(1)} %convolution_convert_fusion.4) | copy-start | bytes 14155780
  336.9 13.1 %collective-permute-start.9 = (bf16[768,1536]{1,0:T(8,128)(2,1)S(1)}, bf16[768,1536]{1,0:T(8,128)(2,1)S(1)}, u32[]{:S(2)}, u32[]{:S(2)}) collective-permute-start(bf16[768,1536]{1,0:T(8,128)(2,1)S(1)} %pad_maximum_fusion.2), channel_id=1, source_target_pairs={{0,1},{1,0},{2,3},{3,2},{4,5},{5,4},{6,7},{7,6},{8,9},{9,8},{10,11... | collective-permute-start | bytes 7077896 | tf_op jit(solution)/shard_map/ppermute | solution.py:312
  339.0 4.1 copy-start.71
  341.2 11.5 %slice-start = ((s8[4718592]{0:T(1024)(128)(4,1)}), s8[4194304]{0:T(1024)(128)(4,1)S(1)}, s32[]{:S(2)}) async-start(s8[4718592]{0:T(1024)(128)(4,1)} %bitcast.144), calls=%async_computation.4 | async-start | bytes 8388608
  341.5 11.2 %slice-start.1 = ((s8[4718592]{0:T(1024)(128)(4,1)}), s8[524288]{0:T(1024)(128)(4,1)S(1)}, s32[]{:S(2)}) async-start(s8[4718592]{0:T(1024)(128)(4,1)} %bitcast.144), calls=%async_computation.5 | async-start | bytes 1048576
  341.5 28.3 %collective-permute-start.8 = (bf16[384,1536]{1,0:T(8,128)(2,1)S(1)}, bf16[384,1536]{1,0:T(8,128)(2,1)S(1)}, u32[]{:S(2)}, u32[]{:S(2)}) collective-permute-start(bf16[384,1536]{1,0:T(8,128)(2,1)S(1)} %add_convert_fusion.3), channel_id=1, source_target_pairs={{0,2},{1,3},{2,0},{3,1},{4,6},{5,7},{6,4},{7,5},{8,10},{9,11},{10,... | collective-permute-start | bytes 3538952 | tf_op jit(solution)/shard_map/ppermute | solution.py:1389
  501.7 3.3 copy-start.65
  511.7 26.4 %all-to-all-start.2 = ((bf16[8,192,192]{2,1,0:T(8,128)(2,1)}), bf16[8,192,192]{2,1,0:T(8,128)(2,1)}, u32[]{:S(2)}, u32[]{:S(2)}) async-start(bf16[8,192,192]{2,1,0:T(8,128)(2,1)} %bitcast.127), calls=%async_computation.2 | async-start | bytes 1572864 | tf_op jit(solution)/shard_map/all_to_all | solution.py:1440
  518.3 2.6 copy-start.23
  519.8 39.5 %collective-permute-start.10 = (bf16[640,1536]{1,0:T(8,128)(2,1)}, bf16[640,1536]{1,0:T(8,128)(2,1)}, u32[]{:S(2)}, u32[]{:S(2)}) collective-permute-start(bf16[640,1536]{1,0:T(8,128)(2,1)} %pad_maximum_fusion.6), channel_id=1, source_target_pairs={{0,1},{1,0},{2,3},{3,2},{4,5},{5,4},{6,7},{7,6},{8,9},{9,8},{10,11... | collective-permute-start | bytes 5898248 | tf_op jit(solution)/shard_map/ppermute | solution.py:312
  521.8 2.5 copy-start.3
  521.8 3.0 copy-start.25
  521.8 3.2 copy-start.41
  524.9 3.3 copy-start.20
  524.9 3.3 copy-start.31
  528.2 2.9 copy-start.26
  528.2 2.9 copy-start.45
  528.2 5.9 copy-start.16
  538.2 6.1 copy-start.27
  538.2 6.1 copy-start.39
  538.2 33.9 %all-to-all-start.1 = ((bf16[8,48,1536]{2,1,0:T(8,128)(2,1)}), bf16[8,48,1536]{2,1,0:T(8,128)(2,1)S(1)}, u32[]{:S(2)}, u32[]{:S(2)}) async-start(bf16[8,48,1536]{2,1,0:T(8,128)(2,1)} %bitcast.23), calls=%async_computation.1 | async-start | bytes 2359296 | tf_op jit(solution)/shard_map/all_to_all | solution.py:1292
  545.8 4.5 copy-start.38
  545.8 4.5 copy-start.67
  556.1 3.2 copy-start.11
  556.1 3.2 copy-start.12
  559.3 13.0 %copy-start.34 = (bf16[39,1536]{1,0:T(8,128)(2,1)S(1)}, bf16[39,1536]{1,0:T(8,128)(2,1)}, u32[]{:S(2)}) copy-start(bf16[39,1536]{1,0:T(8,128)(2,1)} %copy-done.33) | copy-start | bytes 359428
  559.3 13.0 %copy-start.5 = (f32[64,1536]{1,0:T(8,128)S(1)}, f32[64,1536]{1,0:T(8,128)}, u32[]{:S(2)}) copy-start(f32[64,1536]{1,0:T(8,128)} %get-tuple-element.82.refs_7_) | copy-start | bytes 1179652
  559.3 13.0 %copy-start.54 = (f32[1536]{0:T(1024)S(1)}, f32[1536]{0:T(1024)}, u32[]{:S(2)}) copy-start(f32[1536]{0:T(1024)} %get-tuple-element.187) | copy-start | bytes 18436
  559.3 13.0 %copy-start.63 = (f32[64]{0:T(128)S(1)}, f32[64]{0:T(128)}, u32[]{:S(2)}) copy-start(f32[64]{0:T(128)} %add_rsqrt_fusion.1) | copy-start | bytes 772
  563.1 11.0 %copy-start.51 = (f32[4,1536]{1,0:T(4,128)S(1)}, f32[4,1536]{1,0:T(4,128)}, u32[]{:S(2)}) copy-start(f32[4,1536]{1,0:T(4,128)} %copy-done.50) | copy-start | bytes 73732
  563.1 11.0 %copy-start.55 = (f32[1,1536]{1,0:T(1,128)S(1)}, f32[1,1536]{1,0:T(1,128)}, u32[]{:S(2)}) copy-start(f32[1,1536]{1,0:T(1,128)} %broadcast_in_dim.69) | copy-start | bytes 18436
  563.1 11.0 %copy-start.56 = (f32[1,1536]{1,0:T(1,128)S(1)}, f32[1,1536]{1,0:T(1,128)}, u32[]{:S(2)}) copy-start(f32[1,1536]{1,0:T(1,128)} %broadcast_in_dim.65) | copy-start | bytes 18436
  563.1 11.0 %copy-start.57 = (f32[1,1536]{1,0:T(1,128)S(1)}, f32[1,1536]{1,0:T(1,128)}, u32[]{:S(2)}) copy-start(f32[1,1536]{1,0:T(1,128)} %broadcast_in_dim.68) | copy-start | bytes 18436
  563.1 11.0 %copy-start.58 = (f32[1,1536]{1,0:T(1,128)S(1)}, f32[1,1536]{1,0:T(1,128)}, u32[]{:S(2)}) copy-start(f32[1,1536]{1,0:T(1,128)} %broadcast_in_dim.66) | copy-start | bytes 18436
  563.1 11.0 %copy-start.59 = (f32[1,1536]{1,0:T(1,128)S(1)}, f32[1,1536]{1,0:T(1,128)}, u32[]{:S(2)}) copy-start(f32[1,1536]{1,0:T(1,128)} %broadcast_in_dim.67) | copy-start | bytes 18436
  679.8 8.0 %copy-start.21 = (bf16[1,192,1536]{2,1,0:T(8,128)(2,1)S(1)}, bf16[1,192,1536]{2,1,0:T(8,128)(2,1)}, u32[]{:S(2)}) copy-start(bf16[1,192,1536]{2,1,0:T(8,128)(2,1)} %all_to_all.40) | copy-start | bytes 1769476
  683.2 20.4 %all-to-all-start.3 = ((f32[8,1,192]{2,1,0:T(1,128)}), f32[8,1,192]{2,1,0:T(1,128)S(1)}, u32[]{:S(2)}, u32[]{:S(2)}) async-start(f32[8,1,192]{2,1,0:T(1,128)} %copy.49), calls=%async_computation.3 | async-start | bytes 16384 | tf_op jit(solution)/shard_map/all_to_all | solution.py:1505
  693.3 3.4 copy-start.29
  702.3 7.2 %copy-start.61 = (f32[1,1536]{1,0:T(1,128)S(1)}, f32[1,1536]{1,0:T(1,128)}, u32[]{:S(2)}) copy-start(f32[1,1536]{1,0:T(1,128)} %param.12) | copy-start | bytes 18436
  702.3 7.2 %copy-start.62 = (f32[1,1536]{1,0:T(1,128)S(1)}, f32[1,1536]{1,0:T(1,128)}, u32[]{:S(2)}) copy-start(f32[1,1536]{1,0:T(1,128)} %get-tuple-element.156) | copy-start | bytes 18436
  702.3 7.8 %copy-start.24 = (f32[256,1536]{1,0:T(8,128)S(1)}, f32[256,1536]{1,0:T(8,128)}, u32[]{:S(2)}) copy-start(f32[256,1536]{1,0:T(8,128)} %get-tuple-element.113) | copy-start | bytes 4718596
  (27 other events, 44.4 us)

commit v6 on v5

--- a/solution.py
+++ b/solution.py
@@ -327,17 +327,49 @@
 
 
 def tail_kernel(columns, count, *refs):
-    here, there, scale, other, x_image, x_text, mid_image, mid_text, text_out = refs[:9]
-    grads, refs = refs[9 : 9 + count], refs[9 + count :]
-    image_grad, mod_sum, mod_all, *wholes = refs[:5]
-    sums, refs = refs[5 : 5 + count], refs[5 + count :]
+    d_parts, scale, other, x_image, x_text, mid_image, mid_text, text_out, ada = refs[:3], *refs[3:11]
+    qkv_weights, grads, refs = refs[11:13], refs[13 : 13 + count], refs[13 + count :]
+    image_grad, mod_sum, mod_all, cond_sum, *wholes = refs[:6]
+    sums, refs = refs[6 : 6 + count], refs[6 + count :]
     far, text_grad, terms, parts, low, slots, far_sem, part_sem, slot_sem, text_sem = refs[:10]
-    ring = ScatterRing(grads, sums, refs[10:])
+    weights, sent, got, far_sent, here, acts, act_got, act_rows, weight_sem, act_sem, act_row_sem = refs[10:21]
+    ring = ScatterRing(grads, sums, refs[21:])
     me, index = lax.axis_index("dp"), lax.axis_index("tensor")
     far_copy = pltpu.make_async_remote_copy(
-        src_ref=there, dst_ref=far, send_sem=far_sem.at[0], recv_sem=far_sem.at[1],
+        src_ref=far_sent, dst_ref=far, send_sem=far_sem.at[0, 1], recv_sem=far_sem.at[1, 1],
         device_id=(me, tensor_peer(2)), device_id_type=MESH,
     )
+    weight_copies = [
+        pltpu.make_async_copy(qkv_weights[s], weights.at[s], weight_sem.at[s]) for s in range(2)
+    ]
+
+    def first_part(b):
+        found = []
+        for s, rows in ((0, x_image.shape[0]), (1, x_text.shape[0])):
+            low_row = b * rows + (0 if s == 0 else 4 * x_image.shape[0])
+            total = None
+            for p in range(3):
+                wide = d_parts[p].shape[1]
+                weight = weights[s, :, p * wide : (p + 1) * wide]
+                part = dot(d_parts[p][low_row : low_row + rows], weight, NT)
+                total = part if total is None else total + part
+            found.append(total)
+        return jnp.concatenate(found, axis=0)
+
+    def act_copy(hop):
+        return pltpu.make_async_remote_copy(
+            src_ref=acts, dst_ref=act_got.at[hop - 1],
+            send_sem=act_sem.at[0, hop - 1], recv_sem=act_sem.at[1, hop - 1],
+            device_id=(me, tensor_peer(hop)), device_id_type=MESH,
+        )
+
+    def act_row_copy(hop):
+        peer = (me + hop) % RING
+        return pltpu.make_async_remote_copy(
+            src_ref=act_rows.at[peer], dst_ref=cond_sum.at[me],
+            send_sem=act_row_sem.at[0, hop - 1], recv_sem=act_row_sem.at[1, hop - 1],
+            device_id=(peer, index), device_id_type=MESH,
+        )
 
     def part_copy(hop):
         peer = tensor_peer(hop)
@@ -378,14 +410,25 @@
         sums = jnp.sum(first, axis=0, keepdims=True), jnp.sum(first * normed, axis=0, keepdims=True)
         return middle + (wide - inner - normed * cross) * spread, *sums
 
+    for copy in weight_copies:
+        copy.start()
     ring.load_all()
     meet(
         [(me, tensor_peer(hop)) for hop in (1, 2, 3)]
         + [((me + hop) % RING, index) for hop in range(1, RING)]
     )
+    ring.start()
+    for copy in weight_copies:
+        copy.wait()
+    near = exchange_sums(first_part, sent, got, far_sem, me)
+    ring.step(1)
+    here[...] = first_part(0)
+    far_sent[...] = first_part(2).astype(LOW)
+    near.wait()
+    far_sent[...] = (far_sent[...].astype(WIDE) + got[1].astype(WIDE)).astype(LOW)
     far_copy.start()
-    ring.start()
-    ring.step(1)
+    here[...] += got[0].astype(WIDE)
+    ring.step(2)
     far_copy.wait()
     terms[...] = other[...]
     chunk = 64
@@ -402,7 +445,7 @@
     shift, gain = lax.fori_loop(0, image_rows // chunk, image_chunk, (zero, zero))
     terms[0:1] = shift
     terms[1:2] = gain
-    ring.step(2)
+    ring.step(3)
     text_first = here[image_rows:] + far[image_rows:].astype(WIDE)
     out, shift, gain = rows_back(text_first, x_text[...], mid_text[...], scale[1:2])
     text_grad[...] = out
@@ -414,7 +457,7 @@
     terms[7:8] = gain
     for hop in (1, 2, 3):
         part_copy(hop).start()
-    ring.step(3)
+    ring.step(4)
     for hop in (1, 2, 3):
         part_copy(hop).wait()
     own = terms[:, pl.ds(pl.multiple_of(index * columns, LANES), columns)]
@@ -424,54 +467,83 @@
     slots[pl.ds(me, 1)] = total.astype(LOW)[None]
     for hop in range(1, RING):
         slot_copy(hop).start()
-    ring.step(4)
     ring.step(5)
     for hop in range(1, RING):
         slot_copy(hop).wait()
     mod_all[...] = slots[...]
-    ring.step(6)
+    wide = slots[...].astype(WIDE)
+    total = None
+    for which in range(12):
+        rows = jnp.concatenate([wide[n, which : which + 1] for n in range(RING)], axis=0)
+        part = dot(rows.astype(LOW), ada[which], NT)
+        total = part if total is None else total + part
+    acts[...] = total
+    for hop in (1, 2, 3):
+        act_copy(hop).start()
     for i in range(2):
         text_own(i).wait()
         for hop in (1, 2, 3):
             text_copy(i, hop).wait()
+    ring.step(6)
+    for hop in (1, 2, 3):
+        act_copy(hop).wait()
+    total = acts[...] + act_got[0] + act_got[1] + act_got[2]
+    for n in range(RING):
+        act_rows[n] = jnp.broadcast_to(total[n : n + 1], act_rows.shape[1:])
+    for hop in range(1, RING):
+        act_row_copy(hop).start()
+    cond_sum[pl.ds(me, 1)] = act_rows[pl.ds(me, 1)]
     ring.step(7)
+    for hop in range(1, RING):
+        act_row_copy(hop).wait()
     ring.end()
 
 
-def tail_ring(here, there, scale, other, x, middle, text_out, grads, columns, ident):
-    width, shapes = here.shape[1], [grad.shape for grad in grads]
+def tail_ring(d_parts, weights, scale, other, x, middle, text_out, ada, grads, ident):
+    width, shapes = scale.shape[1], [grad.shape for grad in grads]
     rows, text_rows = x[0].shape[0], x[1].shape[0]
-    found = pl.pallas_call(
+    both, (_, depth, columns) = rows + text_rows, ada.shape
+    return pl.pallas_call(
         functools.partial(tail_kernel, columns, len(grads)),
         out_shape=[
             jax.ShapeDtypeStruct((rows, width), WIDE),
             jax.ShapeDtypeStruct((16, columns), WIDE),
             jax.ShapeDtypeStruct((RING, 16, columns), LOW),
+            jax.ShapeDtypeStruct((RING, 8, depth), WIDE),
             jax.ShapeDtypeStruct((4, text_rows, width), LOW),
             jax.ShapeDtypeStruct((4, text_rows, width), WIDE),
             *[jax.ShapeDtypeStruct((r // RING, c), WIDE) for r, c in shapes],
         ],
-        in_specs=[WHOLE] * 9 + [ANY] * len(grads),
-        out_specs=[WHOLE] * 3 + [ANY] * 2 + [WHOLE] * len(grads),
+        in_specs=[WHOLE] * 11 + [ANY] * (2 + len(grads)),
+        out_specs=[WHOLE] * 4 + [ANY] * 2 + [WHOLE] * len(grads),
         scratch_shapes=[
-            pltpu.VMEM((rows + text_rows, width), LOW),
+            pltpu.VMEM((both, width), LOW),
             pltpu.VMEM((text_rows, width), WIDE),
             pltpu.VMEM((16, width), WIDE),
             pltpu.VMEM((3, 16, columns), WIDE),
             pltpu.VMEM((16, columns), LOW),
             pltpu.VMEM((RING, 16, columns), LOW),
+            pltpu.SemaphoreType.DMA((2, 2)),
+            pltpu.SemaphoreType.DMA((2, 3)),
+            pltpu.SemaphoreType.DMA((2, RING - 1)),
+            pltpu.SemaphoreType.DMA((2, 2, 4)),
+            pltpu.VMEM((2, *weights[0].shape), LOW),
+            *[pltpu.VMEM((2, both, width), LOW)] * 2,
+            pltpu.VMEM((both, width), LOW),
+            pltpu.VMEM((both, width), WIDE),
+            pltpu.VMEM((RING, depth), WIDE),
+            pltpu.VMEM((3, RING, depth), WIDE),
+            pltpu.VMEM((RING, 8, depth), WIDE),
             pltpu.SemaphoreType.DMA((2,)),
             pltpu.SemaphoreType.DMA((2, 3)),
             pltpu.SemaphoreType.DMA((2, RING - 1)),
-            pltpu.SemaphoreType.DMA((2, 2, 4)),
             *ScatterRing.scratch(shapes),
         ],
         compiler_params=pltpu.CompilerParams(
             collective_id=ident, has_side_effects=True, vmem_limit_bytes=VMEM_LIMIT
         ),
         name="tail_ring",
-    )(here, there, scale, other, *x, *middle, text_out, *grads)
-    return found
+    )(*d_parts, scale, other, *x, *middle, text_out, ada, *weights, *grads)
 
 
 def head_lanes(head):
@@ -867,15 +939,16 @@
 def back_kernel(split, chunk, *refs):
     bias_ref, q_ref, k_ref, v_ref, o_ref, lse_ref = refs[:6]
     mid_image, mid_text, cot_image, cot_text, mods, text_part = refs[6:12]
-    partial, out_weights, grads, theirs, refs = refs[12], refs[13:15], refs[15:17], refs[17:19], refs[19:]
+    partial, out_weights, grads, theirs = refs[12], refs[13:15], refs[15:17], refs[17:19]
+    units, refs = refs[19], refs[20:]
     dq_ref, dk_ref, dv_ref, image_second, image_grad, text_grad = refs[:6]
     image_rows, text_rows, *fars = refs[6:10]
-    sums, text_second, refs = refs[10:12], refs[12], refs[13:]
+    sums, text_second, units_got, refs = refs[10:12], refs[12], refs[13], refs[14:]
     dk_acc, dv_acc, weights, parts, got, far_sent, far_got, rows_in, mixed_grad = refs[:9]
-    part_sem, sems, row_sem, weight_sem, rows_sem, far_sem, text_sum = refs[9:16]
-    ring = ScatterRing(grads, sums, refs[16:23])
-    text_ring = ScatterRing([text_part], [text_sum], refs[23:])
-    me = lax.axis_index("dp")
+    part_sem, sems, row_sem, weight_sem, rows_sem, far_sem, text_sum, units_sem = refs[9:17]
+    ring = ScatterRing(grads, sums, refs[17:24])
+    text_ring = ScatterRing([text_part], [text_sum], refs[24:])
+    me, index = lax.axis_index("dp"), lax.axis_index("tensor")
     rows, texts = mid_image.shape[0], mid_text.shape[0]
     block = q_ref.shape[0]
     at = pl.program_id(0) * pl.num_programs(1) + pl.program_id(1)
@@ -894,12 +967,33 @@
             device_id=(me, tensor_peer(1)), device_id_type=MESH,
         )
 
-    def row_copy(source, slot, hop, sem):
+    def row_copy(source, slot, hop, sem, s):
+        some = (pl.ds(0, rows), pl.ds(rows, texts))[s]
         return pltpu.make_async_remote_copy(
-            src_ref=source, dst_ref=rows_in.at[slot],
-            send_sem=row_sem.at[0, sem], recv_sem=row_sem.at[1, sem],
+            src_ref=rows_in.at[source, some], dst_ref=rows_in.at[slot, some],
+            send_sem=row_sem.at[0, s, sem], recv_sem=row_sem.at[1, s, sem],
             device_id=(me, tensor_peer(hop)), device_id_type=MESH,
         )
+
+    def to_far(s):
+        return row_copy(0, 2, 2, 0, s)
+
+    def to_near(s):
+        return row_copy(0, 1, 1, 1, s)
+
+    def forward(s):
+        return row_copy(2, 3, 1, 2, s)
+
+    def units_copy(hop):
+        peer = (me + hop) % RING
+        return pltpu.make_async_remote_copy(
+            src_ref=units.at[peer], dst_ref=units_got.at[me],
+            send_sem=units_sem.at[0, hop - 1], recv_sem=units_sem.at[1, hop - 1],
+            device_id=(peer, index), device_id_type=MESH,
+        )
+
+    def units_own():
+        return pltpu.make_async_copy(units.at[me], units_got.at[me], units_sem.at[0, RING - 1])
 
     def weight(s):
         return pltpu.make_async_copy(out_weights[s], weights.at[s], weight_sem.at[s])
@@ -927,11 +1021,13 @@
             weight(i).start()
         text_ring.load_all()
         ring.load_all()
-        meet([*ring.sides, *[(me, tensor_peer(hop)) for hop in (1, 2)]])
+        meet(
+            [((me + hop) % RING, index) for hop in range(1, RING)]
+            + [(me, tensor_peer(hop)) for hop in (1, 2)]
+        )
         for i in range(2):
             near(i).start()
         text_ring.start()
-        ring.start()
         for i in range(2):
             keep(i).wait()
             near(i).wait()
@@ -941,9 +1037,9 @@
             device_id=(me, tensor_peer(2)), device_id_type=MESH,
         )
         far.start()
-        for step in range(1, 4):
+        for step in range(1, 6):
             text_ring.step(step)
-        ring.step(1)
+        ring.start()
         far.wait()
 
         def image_chunk(i, _):
@@ -956,9 +1052,10 @@
             rows_in[0, some] = low
             return 0
 
-        text_ring.step(4)
         lax.fori_loop(0, rows // chunk, image_chunk, 0)
-        for step in range(5, 8):
+        to_far(0).start()
+        to_near(0).start()
+        for step in (6, 7):
             text_ring.step(step)
         pooled = text_sum.shape[0]
         text_second[...] = jnp.zeros_like(text_second)
@@ -966,17 +1063,15 @@
         grad, low = rows_back(text_second[...], mid_text[...], cot_text[...], 1)
         text_grad[...] = grad
         rows_in[0, rows:] = low
-        to_far = row_copy(rows_in.at[0], 2, 2, 0)
-        to_near = row_copy(rows_in.at[0], 1, 1, 1)
-        to_far.start()
-        to_near.start()
-        ring.step(2)
-        to_far.wait()
-        forward = row_copy(rows_in.at[2], 3, 1, 2)
-        forward.start()
-        for i in range(2):
-            weight(i).wait()
-        to_near.wait()
+        to_far(1).start()
+        to_near(1).start()
+        ring.step(1)
+        for s in range(2):
+            to_far(s).wait()
+            forward(s).start()
+        for s in range(2):
+            weight(s).wait()
+            to_near(s).wait()
 
         def through(b):
             image = dot(rows_in[b, :rows], weights[0], NT).astype(LOW)
@@ -986,8 +1081,9 @@
 
         for b in range(3):
             through(b)
-        ring.step(3)
-        forward.wait()
+        ring.step(2)
+        for s in range(2):
+            forward(s).wait()
         through(3)
         for b in range(4):
             for s in range(2):
@@ -1005,8 +1101,11 @@
     def _():
         for copy in far_copies:
             copy.start()
-
-    for step, when in ((4, 3), (5, 8), (6, 13)):
+        units_own().start()
+        for hop in range(1, RING):
+            units_copy(hop).start()
+
+    for step, when in ((3, 1), (4, 6), (5, 11)):
 
         @pl.when(at == when)
         def _():
@@ -1024,11 +1123,15 @@
 
     @pl.when(at == last)
     def _():
+        ring.step(6)
         ring.step(7)
         ring.end()
         text_ring.end()
         for copy in far_copies:
             copy.wait()
+        units_own().wait()
+        for hop in range(1, RING):
+            units_copy(hop).wait()
         for b in range(4):
             for s in range(2):
                 save(b, s).wait()
@@ -1036,7 +1139,7 @@
 
 def back_ring(
     joint, bias, mixed, lse, split, heads, text_part, middle, cotangent, mods, partial,
-    out_weights, grads, theirs, ident, block=256,
+    out_weights, grads, theirs, units, ident, block=256,
 ):
     rows, pairs = joint.shape[0], heads // 2
     whole = lambda part: pl.BlockSpec((rows, LANES), lambda h, i: (0, part * pairs + h))
@@ -1055,9 +1158,9 @@
             some,
             pl.BlockSpec((1, 8, block), lambda h, i: (h, 0, i)),
             *[WHOLE] * 5,
-            *[ANY] * 8,
-        ],
-        out_specs=[some, whole(0), whole(0), *[WHOLE] * 3, *[ANY] * 4, *[WHOLE] * 3],
+            *[ANY] * 9,
+        ],
+        out_specs=[some, whole(0), whole(0), *[WHOLE] * 3, *[ANY] * 4, *[WHOLE] * 3, ANY],
         out_shape=[
             *[jax.ShapeDtypeStruct((rows, depth), LOW)] * 3,
             *[jax.ShapeDtypeStruct((n, width), WIDE) for n in (image_rows, image_rows, texts)],
@@ -1065,6 +1168,7 @@
             *[jax.ShapeDtypeStruct(t.shape, t.dtype) for t in theirs],
             *[jax.ShapeDtypeStruct((g.shape[0] // RING, g.shape[1]), WIDE) for g in grads],
             jax.ShapeDtypeStruct((texts, width), WIDE),
+            jax.ShapeDtypeStruct(units.shape, units.dtype),
         ],
         scratch_shapes=[
             *[pltpu.VMEM((rows, LANES), WIDE)] * 2,
@@ -1075,11 +1179,12 @@
             pltpu.VMEM((rows, depth), LOW),
             pltpu.SemaphoreType.DMA((2,)),
             pltpu.SemaphoreType.DMA((2, 3)),
-            pltpu.SemaphoreType.DMA((2, 3)),
+            pltpu.SemaphoreType.DMA((2, 2, 3)),
             pltpu.SemaphoreType.DMA((2,)),
             pltpu.SemaphoreType.DMA((2, 4)),
             pltpu.SemaphoreType.DMA((2, 2)),
             pltpu.VMEM((pooled, width), WIDE),
+            pltpu.SemaphoreType.DMA((2, RING)),
             *ScatterRing.scratch([g.shape for g in grads]),
             *ScatterRing.scratch([text_part.shape]),
         ],
@@ -1089,7 +1194,7 @@
         name="back_ring",
     )(
         bias.T, joint, joint, joint, mixed, lse, *middle, *cotangent, mods, text_part,
-        partial, *out_weights, *grads, *theirs,
+        partial, *out_weights, *grads, *theirs, units,
     )
     return found
 
@@ -1284,9 +1389,6 @@
         rows = lax.all_to_all(copies, "dp", split_axis=0, concat_axis=0, tiled=True)
         return rows.reshape(-1, width)
 
-    def unpool_end(here, far):
-        return own_pool((here + far.astype(WIDE)).astype(LOW))
-
     def own_pool(part):
         part = part.reshape(size, pool_rows, width)
         part = lax.all_to_all(part, "dp", split_axis=0, concat_axis=0, tiled=True)
@@ -1399,7 +1501,7 @@
     text_second = (text_here + text_far.astype(WIDE)).astype(LOW)
     text_here, text_there = scatter_start(dot(text_hidden, text_down, NN))
     text_down_grad = dot(text_hidden, text_ffn_rows, TN)
-    text_up_grad = dot(text_mlp_rows, text_pre_grad, TN)
+    text_up_grad = dot(text_mlp_rows, text_pre_grad, TN).astype(LOW).reshape(size, -1, units)
     if size == RING:
         mods = jnp.concatenate(
             [row for s in range(2) for row in (mod_row(s, 2), 1.0 + mod_row(s, 4))]
@@ -1409,11 +1511,12 @@
         found = back_ring(
             joint, bias, mixed, log_total, split_at, heads_here, text_second, middle,
             cot_rows, mods, second_part, out_full,
-            [down_grad, up_grad], [there, text_there], 5,
+            [down_grad, up_grad], [there, text_there], text_up_grad, 5,
         )
         *grads, image_second, image_middle, text_middle = found[:6]
         middle_grad, branch_rows = [image_middle, text_middle], found[6:8]
-        far, text_far, down_sum, up_sum, text_sum = found[8:]
+        far, text_far, down_sum, up_sum, text_sum, text_up_grad = found[8:]
+        text_up_grad = text_up_grad.transpose(1, 0, 2)
         second_grad = [image_second, text_sum]
     else:
         second_grad = [scatter_rows(second_part), own_pool(text_second)]
@@ -1432,28 +1535,18 @@
         down_sum, up_sum = scatter_dp([down_grad, up_grad], size, 5)
         far = lax.ppermute(there, "tensor", CHIP)
         text_far = lax.ppermute(text_there, "tensor", CHIP)
-    ffn[0], ffn[1] = here + far.astype(WIDE), unpool_end(text_here, text_far)
+        text_up_grad = lax.all_to_all(
+            text_up_grad, "dp", split_axis=0, concat_axis=2, tiled=True
+        )
+    text_ffn = (text_here + text_far.astype(WIDE)).astype(LOW)
+    text_ffn, *grads = lax.optimization_barrier((text_ffn, *grads))
+    ffn[0], ffn[1] = here + far.astype(WIDE), own_pool(text_ffn)
     results = [(middle[s] + mod_row(s, 5) * ffn[s]).astype(LOW) for s in range(2)]
     gate_terms = [jnp.sum(cotangent[s] * ffn[s], axis=0)[None] for s in range(2)]
     out_grad = [dot(mixed_rows[s], branch_rows[s], TN).astype(LOW) for s in range(2)]
-    text_up_grad, grads[0] = lax.optimization_barrier((text_up_grad, grads[0]))
-    text_up_grad = lax.all_to_all(
-        text_up_grad.astype(LOW).reshape(size, -1, units),
-        "dp", split_axis=0, concat_axis=2, tiled=True,
-    )
     joint_grad = jnp.concatenate(grads, axis=1)
     joint_rows = [joint_grad[:split_at], joint_grad[split_at:]]
     qkv_grad = [dot(attn_rows[s], joint_rows[s], TN).astype(LOW) for s in range(2)]
-    first_parts = [dot(joint_rows[s], qkv_full[s], NT).astype(LOW) for s in range(2)]
-    here, there = scatter_start(
-        jnp.concatenate(
-            [
-                part[b * (part.shape[0] // 4) : (b + 1) * (part.shape[0] // 4)]
-                for b in range(4)
-                for part in first_parts
-            ]
-        )
-    )
     other = []
     for s in range(2):
         other += [
@@ -1466,10 +1559,11 @@
     other = jnp.concatenate(other + [jnp.zeros((4, width), WIDE)], axis=0)
     if size == RING:
         scale = jnp.concatenate([1.0 + mod_row(s, 1) for s in range(2)], axis=0)
-        image_input, mod_sum, mod_grad, text_out, text_grad, *found = tail_ring(
-            here, there, scale, other, x_rows, middle_grad, results[1], qkv_grad + out_grad,
-            width_here, 6,
-        )
+        image_input, mod_sum, mod_grad, act_grad, text_out, text_grad, *found = tail_ring(
+            grads, qkv_full, scale, other, x_rows, middle_grad, results[1], ada_rows_low,
+            qkv_grad + out_grad, 6,
+        )
+        act_grad = act_grad[:, 0].reshape(1, width)
         qkv_image, qkv_text, out_image, out_text = found
         qkv_sums, out_sum = [qkv_image, qkv_text], [out_image, out_text]
         mod_sum = mod_sum[:12].reshape(2, 6, width_here)
@@ -1478,6 +1572,16 @@
     else:
         *qkv_sums, out_image, out_text = scatter_dp(qkv_grad + out_grad, size, 6)
         out_sum = [out_image, out_text]
+        first_parts = [dot(joint_rows[s], qkv_full[s], NT).astype(LOW) for s in range(2)]
+        here, there = scatter_start(
+            jnp.concatenate(
+                [
+                    part[b * (part.shape[0] // 4) : (b + 1) * (part.shape[0] // 4)]
+                    for b in range(4)
+                    for part in first_parts
+                ]
+            )
+        )
         far = lax.ppermute(there, "tensor", CHIP)
         first_rows = here + far.astype(WIDE)
         first_grad = [first_rows[:image_rows], first_rows[image_rows:]]
@@ -1498,12 +1602,12 @@
         )
         mod_low = jnp.broadcast_to(mod_sum.astype(LOW)[None], (seqs,) + mod_sum.shape)
         mod_grad = lax.all_to_all(mod_low, "dp", split_axis=0, concat_axis=0, tiled=True)
+        act_parts = jnp.einsum("nskf,sdkf->nd", mod_grad, ada_low, preferred_element_type=WIDE)
+        act_parts = lax.all_to_all(act_parts, "dp", split_axis=0, concat_axis=0, tiled=True)
+        act_grad = lax.psum(act_parts.reshape(1, width), "tensor")
     shift_grad = mod_sum[:, 3]
     text_up_grad = text_up_grad.reshape(-1, size * units).astype(WIDE)
     ada_grad = jnp.einsum("nd,nskf->sdkf", cond_rows, mod_grad, preferred_element_type=WIDE)
-    act_parts = jnp.einsum("nskf,sdkf->nd", mod_grad, ada_low, preferred_element_type=WIDE)
-    act_parts = lax.all_to_all(act_parts, "dp", split_axis=0, concat_axis=0, tiled=True)
-    act_grad = lax.psum(act_parts.reshape(1, width), "tensor")
     cond_grad = jax.vjp(jax.nn.silu, cond)[1](act_grad)[0]
 
     def whole_text(blocks):

time: 717 us -> 699 us (0.975)
  Pallas kernels: 461 us -> 480 us
  matrix products: 102 us -> 83.6 us
  local copies, waits for them, and re-layouts: 62.8 us -> 50 us
  starting transfers between devices: 23.5 us -> 12.3 us
    dot_general x20 -> x18, matrix products: 98.3 us -> 81.1 us  [dot(): lax.dot_general(left, right, (dims, ((), ())), preferred_element_type=WIDE)]
    pallas_call x1, Pallas kernels: 127 us -> 142 us  [back_ring(): pl.pallas_call(functools.partial(back_kernel, split, 64), grid=(pairs, ro...]
    all_to_all x2 -> x0, starting transfers between devices: 8.85 us -> none  [the longest x1 4.47 us: local(): lax.all_to_all(act_parts, 'dp', split_axis=0, concat_axis=0, tiled=True)]
    unnamed x166 -> x154, local copies, waits for them, and re-layouts: 33 us -> 29.5 us
  transfers between devices with their start and end apart: 15 -> 12, of which waited for: 2 -> 2; matrix products, arithmetic and copies ran while one was open for 22% -> 18% of each run, Pallas kernels for 19% -> 20%
where the time goes in v6:
time: 699 us; the launch traced here: 688 us
  Pallas kernels  480 us (69%)
  matrix products  83.6 us (12%)
  local copies, waits for them, and re-layouts  50 us (7%)
  other arithmetic  40.8 us (6%)
  waiting for transfers between devices  19.3 us (3%)
  starting transfers between devices  12.3 us (2%)
    pallas_call x1, Pallas kernels, back_ring(): pl.pallas_call(functools.partial(back_kernel, split, 64), grid=(pairs, ro...  142 us
    pallas_call x1, Pallas kernels, middle_ring(): pl.pallas_call(functools.partial(middle_kernel, split, 64), grid=(pairs,...  135 us
    pallas_call x1, Pallas kernels, tail_ring(): pl.pallas_call(functools.partial(tail_kernel, columns, len(grads)), out_s...  109 us
    pallas_call x1, Pallas kernels, first_ring(): pl.pallas_call(functools.partial(first_kernel, 64), in_specs=[WHOLE] * 6...  95.1 us
    dot_general x18, matrix products, dot(): lax.dot_general(left, right, (dims, ((), ())), preferred_element_type=WIDE)  81.1 us
    unnamed x154, local copies, waits for them, and re-layouts  29.5 us
  transfers between devices with their start and end apart: 12, of which 2 were waited for; matrix products, arithmetic and copies ran while one was open for 18% of the time, Pallas kernels for 20%

profile of v6, /device:TPU:0, one launch (start us, length us, event | category | flops | bytes accessed | tf_op | source)
XLA Modules:
  0.0 688.3 jit_solution(17632837701908422457)
XLA Ops:
  0.7 1.4 convert_reduce_fusion.1
  2.2 1.1 pad_dynamic-slice_fusion
  7.3 1.4 convert_element_type.200
  9.4 95.1 %first_ring.1 = (bf16[1024,1536]{1,0:T(8,128)(2,1)}, bf16[256,1536]{1,0:T(8,128)(2,1)}, bf16[1024,1536]{1,0:T(8,128)(2,1)}, bf16[1536,1152]{1,0:T(8,128)(2,1)}, ...) custom-call(bf16[256,1536]{1,0:T(8,128)(2,1)} %bitcast.112, ...), custom_call_target="tpu_custom_call" | custom-call | tf_op jit(solution)/shard_map/first_ring/pallas_call | solution.py:715
  109.1 1.1 fusion.49
  110.2 1.8 reshape.313
  112.0 2.3 fusion.38
  114.3 2.5 convolution_convert_fusion.11
  116.8 6.1 convolution_convert_fusion.8
  123.0 1.8 pad_maximum_fusion.refs_1_.refs_2_.refs_3_
  125.6 134.6 %middle_ring.1 = (bf16[1280,384]{1,0:T(8,128)(2,1)}, f32[3,8,1280]{2,1,0:T(8,128)}, f32[256,1536]{1,0:T(8,128)}, f32[64,1536]{1,0:T(8,128)}, f32[256,1536]{1,0:T...) custom-call(f32[1,256]{1,0:T(1,128)} %and_select_fusion.refs_0_, ...), custom_call_target="tpu_custom_call" | custom-call | tf_op jit(solution)/shard_map/middle_ring/pallas_call | solution.py:886
  260.7 1.2 copy.48
  261.9 3.7 all-to-all-start
  265.6 8.1 %fusion.51 = f32[1024,1536]{1,0:T(8,128)S(1)} fusion(bf16[1024,1536]{1,0:T(8,128)(2,1)} %get-tuple-element.90, bf16[1536,1536]{1,0:T(8,128)(2,1)} %get-tuple-element.81), kind=kOutput, calls=%fused_computation.147 | convolution fusion | flops 4831838208 | bytes 14155776 | tf_op jit(solution)/shard_map/dot_general | solution.py:21
  273.7 11.0 %fusion.6 = (bf16[1024,1536]{1,0:T(8,128)(2,1)}, f32[1024,1536]{1,0:T(8,128)S(1)}) fusion(f32[1024,1536]{1,0:T(8,128)S(1)} %fusion.51, bf16[1024,1536]{1,0:T(8,128)(2,1)S(1)} %copy-done.58, bf16[1536,1536]{1,0:T(8,128)(2,1)} %get-tuple-element.80), kind=kOutput, calls=%fused_computation.14 | convolution fusion | flops 4863295488 | bytes 23592960 | tf_op jit(solution)/shard_map/dot_general | solution.py:21
  284.8 5.6 convolution_convert_fusion.7
  290.5 1.2 pad_maximum_fusion.6
  294.0 7.4 %convolution_convert_fusion.1.refs_15_ = bf16[1536,1536]{1,0:T(8,128)(2,1)} fusion(bf16[1024,1536]{1,0:T(8,128)(2,1)S(1)} %copy-done.60, f32[1024,1536]{1,0:T(8,128)S(1)} %get-tuple-element.193), kind=kOutput, calls=%fused_computation.3 | convolution fusion | flops 4848353280 | bytes 14155776 | tf_op jit(solution)/shard_map/dot_general | solution.py:21
  303.4 2.4 constant_dynamic-update-slice_fusion.3
  305.8 1.1 constant_dynamic-update-slice_fusion.7
  310.0 2.5 constant_dynamic-update-slice_fusion.2
  312.5 2.4 constant_dynamic-update-slice_fusion.1
  314.9 1.3 constant_dynamic-update-slice_fusion.6
  316.2 1.3 constant_dynamic-update-slice_fusion.5
  317.7 1.7 fusion.52
  320.1 2.1 copy-done.40
  322.3 2.0 fusion.14
  324.3 1.4 convolution_convert_fusion.5
  325.9 2.0 copy-done
  327.9 1.6 pad_maximum_fusion.1
  329.8 2.4 add_convert_fusion.5.refs_17_
  332.2 1.5 convolution_convert_fusion.4
  333.9 2.1 copy-done.6
  336.0 1.6 pad_maximum_fusion.2
  337.7 1.1 convolution_convert_fusion.12
  338.7 1.2 copy.41
  339.9 5.1 convolution_bitcast_fusion
  345.0 1.7 add_convert_fusion.3
  346.7 1.5 collective-permute-start.8
  348.3 7.4 %convolution_convert_fusion.2.refs_16_ = bf16[1536,1536]{1,0:T(8,128)(2,1)} fusion(bf16[1024,1536]{1,0:T(8,128)(2,1)S(1)} %copy-done.59, bf16[1024,1536]{1,0:T(8,128)(2,1)S(1)} %copy-done.63), kind=kOutput, calls=%fused_computation.4 | convolution fusion | flops 4834197504 | bytes 11010048 | tf_op jit(solution)/shard_map/dot_general | solution.py:21
  355.6 2.6 add_convert_fusion.1.refs_18_
  358.2 6.4 convolution_convert_fusion.6.refs_12_
  364.6 10.4 %collective-permute-done.8 = bf16[384,1536]{1,0:T(8,128)(2,1)S(1)} collective-permute-done((bf16[384,1536]{1,0:T(8,128)(2,1)S(1)}, bf16[384,1536]{1,0:T(8,128)(2,1)S(1)}, u32[]{:S(2)}, u32[]{:S(2)}) %collective-permute-start.8) | collective-permute-done | bytes 1179680 | tf_op jit(solution)/shard_map/ppermute | solution.py:1491
  375.0 2.7 add_convert_fusion.2.refs_11_
  377.7 141.6 %back_ring.1 = (bf16[1280,384]{1,0:T(8,128)(2,1)}, bf16[1280,384]{1,0:T(8,128)(2,1)}, bf16[1280,384]{1,0:T(8,128)(2,1)}, f32[256,1536]{1,0:T(8,128)}, f32[256,15...) custom-call(f32[256,1]{1,0:T(8,128)} %fusion.34.refs_0_, ...), custom_call_target="tpu_custom_call" | custom-call | tf_op jit(solution)/shard_map/back_ring/pallas_call | solution.py:1150
  519.4 1.2 multiply_reduce_fusion.6
  520.7 1.6 multiply_reduce_fusion.3
  522.4 3.5 multiply_reduce_fusion
  525.8 2.7 add_convert_fusion
  528.6 4.0 all-to-all-start.1
  532.6 2.7 convolution_convert_fusion.9.refs_16_
  537.3 1.6 pad_maximum_fusion.5
  538.9 3.0 convolution_convert_fusion.3.refs_14_
  541.8 2.4 convolution_convert_fusion.10.refs_15_
  544.3 5.8 convolution_convert_fusion.refs_13_
  550.1 8.9 %all-to-all-done.1 = bf16[8,48,1536]{2,1,0:T(8,128)(2,1)S(1)} async-done(((bf16[8,48,1536]{2,1,0:T(8,128)(2,1)}), bf16[8,48,1536]{2,1,0:T(8,128)(2,1)S(1)}, u32[]{:S(2)}, u32[]{:S(2)}) %all-to-all-start.1) | async-done | bytes 1179680 | tf_op jit(solution)/shard_map/all_to_all | solution.py:1394
  560.0 1.3 concatenate.43.refs_4_
  561.4 109.1 %tail_ring.1 = (f32[256,1536]{1,0:T(8,128)}, f32[16,384]{1,0:T(8,128)}, bf16[8,16,384]{2,1,0:T(8,128)(2,1)}, f32[8,8,192]{2,1,0:T(8,128)}, bf16[4,64,1536]{2,1,0...) custom-call(bf16[1280,384]{1,0:T(8,128)(2,1)} %get-tuple-element.107, ...), custom_call_target="tpu_custom_call" | custom-call | tf_op jit(solution)/shard_map/tail_ring/pallas_call | solution.py:506
  670.6 1.2 slice.200
  674.6 1.9 copy.44
  677.8 1.3 copy.46
  681.6 2.8 pad_maximum_fusion.4
  684.5 2.5 convolution_bitcast_fusion.1
  686.9 1.1 copy.60
  (228 shorter events, 29.2 us)
Async XLA Ops:
  0.6 4.0 copy-start.20
  4.9 2.4 copy-start.12
  9.4 96.7 %copy-start.35 = (f32[2,48,1536]{2,1,0:T(8,128)S(1)}, f32[2,48,1536]{2,1,0:T(8,128)}, u32[]{:S(2)}) copy-start(f32[2,48,1536]{2,1,0:T(8,128)} %param.15) | copy-start | bytes 1769476
  9.4 97.5 %copy-start.17 = (f32[2,192,1536]{2,1,0:T(8,128)S(1)}, f32[2,192,1536]{2,1,0:T(8,128)}, u32[]{:S(2)}) copy-start(f32[2,192,1536]{2,1,0:T(8,128)} %param.17) | copy-start | bytes 7077892
  104.5 205.2 %collective-permute-start.2 = (bf16[384,1536]{1,0:T(8,128)(2,1)}, bf16[384,1536]{1,0:T(8,128)(2,1)}, u32[]{:S(2)}, u32[]{:S(2)}) collective-permute-start(bf16[384,1536]{1,0:T(8,128)(2,1)} %get-tuple-element.83), channel_id=1, source_target_pairs={{0,2},{1,3},{2,0},{3,1},{4,6},{5,7},{6,4},{7,5},{8,10},{9,11},{10,... | collective-permute-start | bytes 3538952 | tf_op jit(solution)/shard_map/ppermute | solution.py:295
  105.5 204.2 %collective-permute-start.1 = (bf16[384,1536]{1,0:T(8,128)(2,1)}, bf16[384,1536]{1,0:T(8,128)(2,1)}, u32[]{:S(2)}, u32[]{:S(2)}) collective-permute-start(bf16[384,1536]{1,0:T(8,128)(2,1)} %get-tuple-element.83), channel_id=1, source_target_pairs={{0,1},{1,0},{2,3},{3,2},{4,5},{5,4},{6,7},{7,6},{8,9},{9,8},{10,11... | collective-permute-start | bytes 3538952 | tf_op jit(solution)/shard_map/ppermute | solution.py:294
  106.9 2.1 copy-start.18
  109.0 5.4 copy-start.11
  114.3 2.5 copy-start.10
  125.6 135.1 %copy-start.19 = (bf16[1,192,1536]{2,1,0:T(8,128)(2,1)S(1)}, bf16[1,192,1536]{2,1,0:T(8,128)(2,1)}, u32[]{:S(2)}) copy-start(bf16[1,192,1536]{2,1,0:T(8,128)(2,1)} %get-tuple-element.175) | copy-start | bytes 1769476
  260.1 46.7 %collective-permute-start.5 = (bf16[384,1536]{1,0:T(8,128)(2,1)}, bf16[384,1536]{1,0:T(8,128)(2,1)}, u32[]{:S(2)}, u32[]{:S(2)}) collective-permute-start(bf16[384,1536]{1,0:T(8,128)(2,1)} %get-tuple-element.89), channel_id=1, source_target_pairs={{0,2},{1,3},{2,0},{3,1},{4,6},{5,7},{6,4},{7,5},{8,10},{9,11},{10,... | collective-permute-start | bytes 3538952 | tf_op jit(solution)/shard_map/ppermute | solution.py:295
  260.7 46.2 %collective-permute-start.4 = (bf16[384,1536]{1,0:T(8,128)(2,1)}, bf16[384,1536]{1,0:T(8,128)(2,1)}, u32[]{:S(2)}, u32[]{:S(2)}) collective-permute-start(bf16[384,1536]{1,0:T(8,128)(2,1)} %get-tuple-element.89), channel_id=1, source_target_pairs={{0,1},{1,0},{2,3},{3,2},{4,5},{5,4},{6,7},{7,6},{8,9},{9,8},{10,11... | collective-permute-start | bytes 3538952 | tf_op jit(solution)/shard_map/ppermute | solution.py:294
  261.9 46.7 %all-to-all-start = ((bf16[192,8,192]{0,2,1:T(8,128)(2,1)}), bf16[192,8,192]{0,2,1:T(8,128)(2,1)S(1)}, u32[]{:S(2)}, u32[]{:S(2)}) async-start(bf16[192,8,192]{0,2,1:T(8,128)(2,1)} %bitcast.17), calls=%async_computation | async-start | bytes 1572864 | tf_op jit(solution)/shard_map/all_to_all | solution.py:1382
  265.6 8.1 %copy-start.58 = (bf16[1024,1536]{1,0:T(8,128)(2,1)S(1)}, bf16[1024,1536]{1,0:T(8,128)(2,1)}, u32[]{:S(2)}) copy-start(bf16[1024,1536]{1,0:T(8,128)(2,1)} %get-tuple-element.79) | copy-start | bytes 9437188
  265.6 19.1 %slice-start.4 = ((s8[4718592]{0:T(1024)(128)(4,1)}), s8[4194304]{0:T(1024)(128)(4,1)S(1)}, s32[]{:S(2)}) async-start(s8[4718592]{0:T(1024)(128)(4,1)} %bitcast.137), calls=%async_computation.6 | async-start | bytes 8388608
  273.7 11.1 %slice-start.5 = ((s8[4718592]{0:T(1024)(128)(4,1)}), s8[524288]{0:T(1024)(128)(4,1)S(1)}, s32[]{:S(2)}) async-start(s8[4718592]{0:T(1024)(128)(4,1)} %bitcast.137), calls=%async_computation.7 | async-start | bytes 1048576
  290.4 2.4 copy-start.13
  290.5 3.5 copy-start.60
  292.7 8.7 %copy-start.1 = (f32[256,1536]{1,0:T(8,128)S(1)}, f32[256,1536]{1,0:T(8,128)}, u32[]{:S(2)}) copy-start(f32[256,1536]{1,0:T(8,128)} %get-tuple-element.78.refs_6_) | copy-start | bytes 4718596
  292.7 37.1 %collective-permute-start = (bf16[512,1536]{1,0:T(8,128)(2,1)}, bf16[512,1536]{1,0:T(8,128)(2,1)}, u32[]{:S(2)}, u32[]{:S(2)}) collective-permute-start(bf16[512,1536]{1,0:T(8,128)(2,1)} %pad_maximum_fusion.6), channel_id=1, source_target_pairs={{0,1},{1,0},{2,3},{3,2},{4,5},{5,4},{6,7},{7,6},{8,9},{9,8},{10,11... | collective-permute-start | bytes 4718600 | tf_op jit(solution)/shard_map/ppermute | solution.py:312
  301.8 3.9 copy-start.25
  306.9 10.7 %collective-permute-start.6 = (bf16[384,1536]{1,0:T(8,128)(2,1)}, bf16[384,1536]{1,0:T(8,128)(2,1)S(1)}, u32[]{:S(2)}, u32[]{:S(2)}) collective-permute-start(bf16[384,1536]{1,0:T(8,128)(2,1)} %collective-permute-done.5), channel_id=1, source_target_pairs={{0,1},{1,0},{2,3},{3,2},{4,5},{5,4},{6,7},{7,6},{8,9},{9,8},{10,11... | collective-permute-start | bytes 3538952 | tf_op jit(solution)/shard_map/ppermute | solution.py:300
  309.7 5.2 copy-start.38
  309.7 9.7 %collective-permute-start.3 = (bf16[384,1536]{1,0:T(8,128)(2,1)}, bf16[384,1536]{1,0:T(8,128)(2,1)S(1)}, u32[]{:S(2)}, u32[]{:S(2)}) collective-permute-start(bf16[384,1536]{1,0:T(8,128)(2,1)} %collective-permute-done.2), channel_id=1, source_target_pairs={{0,1},{1,0},{2,3},{3,2},{4,5},{5,4},{6,7},{7,6},{8,9},{9,8},{10,11... | collective-permute-start | bytes 3538952 | tf_op jit(solution)/shard_map/ppermute | solution.py:300
  317.7 2.3 copy-start.39
  317.7 4.6 copy-start.15
  319.4 12.9 %copy-start.62 = (f32[1536,192]{0,1:T(8,128)}, f32[1536,192]{0,1:T(8,128)S(1)}, u32[]{:S(2)}) copy-start(f32[1536,192]{0,1:T(8,128)S(1)} %fusion.52) | copy-start | bytes 3538948
  320.1 2.2 copy-start.40
  325.7 2.1 copy-start
  329.4 15.5 %collective-permute-start.7 = (bf16[768,1536]{1,0:T(8,128)(2,1)}, bf16[768,1536]{1,0:T(8,128)(2,1)}, u32[]{:S(2)}, u32[]{:S(2)}) collective-permute-start(bf16[768,1536]{1,0:T(8,128)(2,1)} %pad_maximum_fusion.1), channel_id=1, source_target_pairs={{0,1},{1,0},{2,3},{3,2},{4,5},{5,4},{6,7},{7,6},{8,9},{9,8},{10,11... | collective-permute-start | bytes 7077896 | tf_op jit(solution)/shard_map/ppermute | solution.py:312
  333.7 2.2 copy-start.6
  337.5 18.1 %collective-permute-start.9 = (bf16[768,1536]{1,0:T(8,128)(2,1)}, bf16[768,1536]{1,0:T(8,128)(2,1)S(1)}, u32[]{:S(2)}, u32[]{:S(2)}) collective-permute-start(bf16[768,1536]{1,0:T(8,128)(2,1)} %pad_maximum_fusion.2), channel_id=1, source_target_pairs={{0,1},{1,0},{2,3},{3,2},{4,5},{5,4},{6,7},{7,6},{8,9},{9,8},{10,11... | collective-permute-start | bytes 7077896 | tf_op jit(solution)/shard_map/ppermute | solution.py:312
  338.7 6.2 slice-start
  339.9 5.1 slice-start.1
  339.9 8.4 %copy-start.63 = (bf16[1024,1536]{1,0:T(8,128)(2,1)S(1)}, bf16[1024,1536]{1,0:T(8,128)(2,1)}, u32[]{:S(2)}) copy-start(bf16[1024,1536]{1,0:T(8,128)(2,1)} %get-tuple-element.94) | copy-start | bytes 9437188
  345.0 3.3 copy-start.59
  345.0 13.2 %slice-start.2 = ((s8[4718592]{0:T(1024)(128)(4,1)}), s8[4194304]{0:T(1024)(128)(4,1)S(1)}, s32[]{:S(2)}) async-start(s8[4718592]{0:T(1024)(128)(4,1)} %bitcast.135), calls=%async_computation.4 | async-start | bytes 8388608
  346.7 11.5 %slice-start.3 = ((s8[4718592]{0:T(1024)(128)(4,1)}), s8[524288]{0:T(1024)(128)(4,1)S(1)}, s32[]{:S(2)}) async-start(s8[4718592]{0:T(1024)(128)(4,1)} %bitcast.135), calls=%async_computation.5 | async-start | bytes 1048576
  346.7 28.3 %collective-permute-start.8 = (bf16[384,1536]{1,0:T(8,128)(2,1)S(1)}, bf16[384,1536]{1,0:T(8,128)(2,1)S(1)}, u32[]{:S(2)}, u32[]{:S(2)}) collective-permute-start(bf16[384,1536]{1,0:T(8,128)(2,1)S(1)} %add_convert_fusion.3), channel_id=1, source_target_pairs={{0,2},{1,3},{2,0},{3,1},{4,6},{5,7},{6,4},{7,5},{8,10},{9,11},{10,... | collective-permute-start | bytes 3538952 | tf_op jit(solution)/shard_map/ppermute | solution.py:1491
  377.7 141.7 %copy-start.36 = (f32[64,1536]{1,0:T(8,128)S(1)}, f32[64,1536]{1,0:T(8,128)}, u32[]{:S(2)}) copy-start(f32[64,1536]{1,0:T(8,128)} %get-tuple-element.114) | copy-start | bytes 1179652
  377.7 142.9 %copy-start.21 = (f32[256,1536]{1,0:T(8,128)S(1)}, f32[256,1536]{1,0:T(8,128)}, u32[]{:S(2)}) copy-start(f32[256,1536]{1,0:T(8,128)} %get-tuple-element.111) | copy-start | bytes 4718596
  519.4 2.9 copy-start.2
  519.4 2.9 copy-start.3
  519.4 2.9 copy-start.23
  519.4 2.9 copy-start.47
  519.4 2.9 copy-start.56
  522.3 3.5 copy-start.28
  528.6 4.0 copy-start.24
  528.6 6.8 copy-start.7
  528.6 30.4 %all-to-all-start.1 = ((bf16[8,48,1536]{2,1,0:T(8,128)(2,1)}), bf16[8,48,1536]{2,1,0:T(8,128)(2,1)S(1)}, u32[]{:S(2)}, u32[]{:S(2)}) async-start(bf16[8,48,1536]{2,1,0:T(8,128)(2,1)} %bitcast.24), calls=%async_computation.1 | async-start | bytes 2359296 | tf_op jit(solution)/shard_map/all_to_all | solution.py:1394
  532.6 2.9 copy-start.8
  538.9 3.0 copy-start.61
  541.8 2.4 copy-start.57
  544.3 14.9 %copy-start.30 = (bf16[39,1536]{1,0:T(8,128)(2,1)S(1)}, bf16[39,1536]{1,0:T(8,128)(2,1)}, u32[]{:S(2)}) copy-start(bf16[39,1536]{1,0:T(8,128)(2,1)} %copy-done.29) | copy-start | bytes 359428
  544.3 14.9 %copy-start.5 = (f32[64,1536]{1,0:T(8,128)S(1)}, f32[64,1536]{1,0:T(8,128)}, u32[]{:S(2)}) copy-start(f32[64,1536]{1,0:T(8,128)} %get-tuple-element.86.refs_7_) | copy-start | bytes 1179652
  544.3 14.9 %copy-start.37 = (f32[64,1536]{1,0:T(8,128)S(1)}, f32[64,1536]{1,0:T(8,128)}, u32[]{:S(2)}) copy-start(f32[64,1536]{1,0:T(8,128)} %get-tuple-element.115) | copy-start | bytes 1179652
  544.3 15.0 %copy-start.46 = (f32[1536]{0:T(1024)S(1)}, f32[1536]{0:T(1024)}, u32[]{:S(2)}) copy-start(f32[1536]{0:T(1024)} %get-tuple-element.185) | copy-start | bytes 18436
  670.5 3.1 copy-start.52
  670.5 3.7 copy-start.43
  670.5 3.7 copy-start.34
  674.6 1.9 copy-start.32
  674.6 2.3 copy-start.31
  681.6 2.8 copy-start.55
  684.5 2.5 copy-start.22
  (18 other events, 25.5 us)

commit v7 on v6

--- a/solution.py
+++ b/solution.py
@@ -779,6 +779,8 @@
         @pl.when(at == step)
         def _():
             first.step(step)
+            if step == 3:
+                second.start()
 
     weight_copies = [
         pltpu.make_async_copy(out_fulls[s], weights.at[s], weight_sem.at[s]) for s in range(2)
@@ -787,7 +789,6 @@
     @pl.when(at == 4)
     def _():
         first.end()
-        second.start()
         for copy in weight_copies:
             copy.start()
 
@@ -1028,6 +1029,9 @@
         for i in range(2):
             near(i).start()
         text_ring.start()
+        units_own().start()
+        for hop in range(1, RING):
+            units_copy(hop).start()
         for i in range(2):
             keep(i).wait()
             near(i).wait()
@@ -1101,9 +1105,6 @@
     def _():
         for copy in far_copies:
             copy.start()
-        units_own().start()
-        for hop in range(1, RING):
-            units_copy(hop).start()
 
     for step, when in ((3, 1), (4, 6), (5, 11)):
 
@@ -1539,7 +1540,10 @@
             text_up_grad, "dp", split_axis=0, concat_axis=2, tiled=True
         )
     text_ffn = (text_here + text_far.astype(WIDE)).astype(LOW)
-    text_ffn, *grads = lax.optimization_barrier((text_ffn, *grads))
+    text_ffn, *held = lax.optimization_barrier(
+        (text_ffn, *grads, *second_grad, *middle_grad, *branch_rows)
+    )
+    grads, second_grad, middle_grad, branch_rows = held[:3], held[3:5], held[5:7], held[7:]
     ffn[0], ffn[1] = here + far.astype(WIDE), own_pool(text_ffn)
     results = [(middle[s] + mod_row(s, 5) * ffn[s]).astype(LOW) for s in range(2)]
     gate_terms = [jnp.sum(cotangent[s] * ffn[s], axis=0)[None] for s in range(2)]

time: 699 us -> 687 us (0.983)
  Pallas kernels: 480 us -> 470 us
    pallas_call x1, Pallas kernels: 142 us -> 133 us  [back_ring(): pl.pallas_call(functools.partial(back_kernel, split, 64), grid=(pairs, ro...]
    unnamed x154 -> x158, local copies, waits for them, and re-layouts: 29.5 us -> 31.1 us
where the time goes in v7:
time: 687 us; the launch traced here: 677 us
  Pallas kernels  470 us (68%)
  matrix products  83.5 us (12%)
  local copies, waits for them, and re-layouts  51.6 us (8%)
  other arithmetic  38.5 us (6%)
  waiting for transfers between devices  18 us (3%)
  starting transfers between devices  13.2 us (2%)
    pallas_call x1, Pallas kernels, back_ring(): pl.pallas_call(functools.partial(back_kernel, split, 64), grid=(pairs, ro...  133 us
    pallas_call x1, Pallas kernels, middle_ring(): pl.pallas_call(functools.partial(middle_kernel, split, 64), grid=(pairs,...  133 us
    pallas_call x1, Pallas kernels, tail_ring(): pl.pallas_call(functools.partial(tail_kernel, columns, len(grads)), out_s...  109 us
    pallas_call x1, Pallas kernels, first_ring(): pl.pallas_call(functools.partial(first_kernel, 64), in_specs=[WHOLE] * 6...  95.1 us
    dot_general x18, matrix products, dot(): lax.dot_general(left, right, (dims, ((), ())), preferred_element_type=WIDE)  81.1 us
    unnamed x158, local copies, waits for them, and re-layouts  31.1 us
  transfers between devices with their start and end apart: 12, of which 2 were waited for; matrix products, arithmetic and copies ran while one was open for 18% of the time, Pallas kernels for 20%

profile of v7, /device:TPU:0, one launch (start us, length us, event | category | flops | bytes accessed | tf_op | source)
XLA Modules:
  0.0 677.1 jit_solution(2137665022821848831)
XLA Ops:
  0.7 1.4 convert_reduce_fusion.1
  2.2 1.1 pad_dynamic-slice_fusion
  7.3 1.4 convert_element_type.200
  9.4 95.1 %first_ring.1 = (bf16[1024,1536]{1,0:T(8,128)(2,1)}, bf16[256,1536]{1,0:T(8,128)(2,1)}, bf16[1024,1536]{1,0:T(8,128)(2,1)}, bf16[1536,1152]{1,0:T(8,128)(2,1)}, ...) custom-call(bf16[256,1536]{1,0:T(8,128)(2,1)} %bitcast.112, ...), custom_call_target="tpu_custom_call" | custom-call | tf_op jit(solution)/shard_map/first_ring/pallas_call | solution.py:715
  104.5 1.1 collective-permute-start.2
  107.0 1.0 copy-done.15
  109.1 1.1 fusion.49
  110.2 1.8 reshape.313
  112.0 2.3 fusion.38
  114.3 2.5 convolution_convert_fusion.11
  116.8 6.1 convolution_convert_fusion.8
  123.0 1.8 pad_maximum_fusion.refs_1_.refs_2_.refs_3_
  125.6 133.2 %middle_ring.1 = (bf16[1280,384]{1,0:T(8,128)(2,1)}, f32[3,8,1280]{2,1,0:T(8,128)}, f32[256,1536]{1,0:T(8,128)}, f32[64,1536]{1,0:T(8,128)}, f32[256,1536]{1,0:T...) custom-call(f32[1,256]{1,0:T(1,128)} %and_select_fusion.refs_0_, ...), custom_call_target="tpu_custom_call" | custom-call | tf_op jit(solution)/shard_map/middle_ring/pallas_call | solution.py:887
  259.4 1.2 copy.48
  260.5 3.7 all-to-all-start
  264.3 8.1 %fusion.51 = f32[1024,1536]{1,0:T(8,128)S(1)} fusion(bf16[1024,1536]{1,0:T(8,128)(2,1)} %get-tuple-element.96, bf16[1536,1536]{1,0:T(8,128)(2,1)} %get-tuple-element.87), kind=kOutput, calls=%fused_computation.147 | convolution fusion | flops 4831838208 | bytes 14155776 | tf_op jit(solution)/shard_map/dot_general | solution.py:21
  272.3 11.0 %fusion.6 = (bf16[1024,1536]{1,0:T(8,128)(2,1)}, f32[1024,1536]{1,0:T(8,128)S(1)}) fusion(f32[1024,1536]{1,0:T(8,128)S(1)} %fusion.51, bf16[1024,1536]{1,0:T(8,128)(2,1)S(1)} %copy-done.60, bf16[1536,1536]{1,0:T(8,128)(2,1)} %get-tuple-element.86), kind=kOutput, calls=%fused_computation.14 | convolution fusion | flops 4863295488 | bytes 23592960 | tf_op jit(solution)/shard_map/dot_general | solution.py:21
  283.4 5.6 convolution_convert_fusion.7
  289.1 1.2 pad_maximum_fusion.6
  292.6 7.6 %convolution_convert_fusion.1.refs_15_ = bf16[1536,1536]{1,0:T(8,128)(2,1)} fusion(bf16[1024,1536]{1,0:T(8,128)(2,1)S(1)} %copy-done.62, f32[1024,1536]{1,0:T(8,128)S(1)} %get-tuple-element.205), kind=kOutput, calls=%fused_computation.3 | convolution fusion | flops 4848353280 | bytes 14155776 | tf_op jit(solution)/shard_map/dot_general | solution.py:21
  302.2 2.4 constant_dynamic-update-slice_fusion.3
  304.6 1.1 constant_dynamic-update-slice_fusion.7
  308.8 2.5 constant_dynamic-update-slice_fusion.2
  311.4 2.4 constant_dynamic-update-slice_fusion.1
  313.7 1.3 constant_dynamic-update-slice_fusion.6
  315.1 1.3 constant_dynamic-update-slice_fusion.5
  316.6 1.7 fusion.52
  319.0 2.1 copy-done.42
  321.1 2.0 fusion.14
  323.1 1.4 convolution_convert_fusion.5
  324.8 2.0 copy-done
  326.7 1.6 pad_maximum_fusion.1
  328.7 2.4 add_convert_fusion.5.refs_17_
  331.2 1.5 convolution_convert_fusion.4
  332.8 2.1 copy-done.7
  334.9 1.6 pad_maximum_fusion.2
  336.5 1.1 convolution_convert_fusion.12
  337.6 1.2 copy.41
  338.7 5.1 convolution_bitcast_fusion
  343.8 1.7 add_convert_fusion.3
  345.6 1.5 collective-permute-start.8
  347.1 7.1 %convolution_convert_fusion.2.refs_16_ = bf16[1536,1536]{1,0:T(8,128)(2,1)} fusion(bf16[1024,1536]{1,0:T(8,128)(2,1)S(1)} %copy-done.61, bf16[1024,1536]{1,0:T(8,128)(2,1)S(1)} %copy-done.65), kind=kOutput, calls=%fused_computation.4 | convolution fusion | flops 4834197504 | bytes 11010048 | tf_op jit(solution)/shard_map/dot_general | solution.py:21
  354.1 2.6 add_convert_fusion.1.refs_18_
  356.7 6.4 convolution_convert_fusion.6.refs_12_
  363.1 10.8 %collective-permute-done.8 = bf16[384,1536]{1,0:T(8,128)(2,1)S(1)} collective-permute-done((bf16[384,1536]{1,0:T(8,128)(2,1)S(1)}, bf16[384,1536]{1,0:T(8,128)(2,1)S(1)}, u32[]{:S(2)}, u32[]{:S(2)}) %collective-permute-start.8) | collective-permute-done | bytes 1179680 | tf_op jit(solution)/shard_map/ppermute | solution.py:1492
  374.0 2.7 add_convert_fusion.2.refs_11_
  376.7 133.2 %back_ring.1 = (bf16[1280,384]{1,0:T(8,128)(2,1)}, bf16[1280,384]{1,0:T(8,128)(2,1)}, bf16[1280,384]{1,0:T(8,128)(2,1)}, f32[256,1536]{1,0:T(8,128)}, f32[256,15...) custom-call(f32[256,1]{1,0:T(8,128)} %fusion.34.refs_0_, ...), custom_call_target="tpu_custom_call" | custom-call | tf_op jit(solution)/shard_map/back_ring/pallas_call | solution.py:1151
  510.0 3.2 add_convert_fusion
  515.3 3.1 multiply_reduce_fusion
  518.5 4.8 all-to-all-start.1
  523.3 2.7 convolution_convert_fusion.9.refs_16_
  528.0 1.6 pad_maximum_fusion.5
  529.6 3.0 convolution_convert_fusion.3.refs_14_
  532.6 2.4 convolution_convert_fusion.10.refs_15_
  535.1 5.8 convolution_convert_fusion.refs_13_
  540.8 7.2 %all-to-all-done.1 = bf16[8,48,1536]{2,1,0:T(8,128)(2,1)S(1)} async-done(((bf16[8,48,1536]{2,1,0:T(8,128)(2,1)}), bf16[8,48,1536]{2,1,0:T(8,128)(2,1)S(1)}, u32[]{:S(2)}, u32[]{:S(2)}) %all-to-all-start.1) | async-done | bytes 1179680 | tf_op jit(solution)/shard_map/all_to_all | solution.py:1395
  549.0 1.3 concatenate.43.refs_4_
  550.4 109.0 %tail_ring.1 = (f32[256,1536]{1,0:T(8,128)}, f32[16,384]{1,0:T(8,128)}, bf16[8,16,384]{2,1,0:T(8,128)(2,1)}, f32[8,8,192]{2,1,0:T(8,128)}, bf16[4,64,1536]{2,1,0...) custom-call(bf16[1280,384]{1,0:T(8,128)(2,1)} %get-tuple-element.119, ...), custom_call_target="tpu_custom_call" | custom-call | tf_op jit(solution)/shard_map/tail_ring/pallas_call | solution.py:506
  659.4 1.2 slice.200
  663.4 1.9 copy.44
  666.6 1.3 copy.46
  670.4 2.8 pad_maximum_fusion.4
  673.3 2.5 convolution_bitcast_fusion.1
  675.7 1.1 copy.60
  (232 shorter events, 29.2 us)
Async XLA Ops:
  0.6 4.0 copy-start.21
  4.9 2.4 copy-start.13
  9.4 96.7 %copy-start.37 = (f32[2,48,1536]{2,1,0:T(8,128)S(1)}, f32[2,48,1536]{2,1,0:T(8,128)}, u32[]{:S(2)}) copy-start(f32[2,48,1536]{2,1,0:T(8,128)} %param.15) | copy-start | bytes 1769476
  9.4 97.5 %copy-start.18 = (f32[2,192,1536]{2,1,0:T(8,128)S(1)}, f32[2,192,1536]{2,1,0:T(8,128)}, u32[]{:S(2)}) copy-start(f32[2,192,1536]{2,1,0:T(8,128)} %param.17) | copy-start | bytes 7077892
  104.5 204.1 %collective-permute-start.2 = (bf16[384,1536]{1,0:T(8,128)(2,1)}, bf16[384,1536]{1,0:T(8,128)(2,1)}, u32[]{:S(2)}, u32[]{:S(2)}) collective-permute-start(bf16[384,1536]{1,0:T(8,128)(2,1)} %get-tuple-element.89), channel_id=1, source_target_pairs={{0,2},{1,3},{2,0},{3,1},{4,6},{5,7},{6,4},{7,5},{8,10},{9,11},{10,... | collective-permute-start | bytes 3538952 | tf_op jit(solution)/shard_map/ppermute | solution.py:295
  105.5 203.1 %collective-permute-start.1 = (bf16[384,1536]{1,0:T(8,128)(2,1)}, bf16[384,1536]{1,0:T(8,128)(2,1)}, u32[]{:S(2)}, u32[]{:S(2)}) collective-permute-start(bf16[384,1536]{1,0:T(8,128)(2,1)} %get-tuple-element.89), channel_id=1, source_target_pairs={{0,1},{1,0},{2,3},{3,2},{4,5},{5,4},{6,7},{7,6},{8,9},{9,8},{10,11... | collective-permute-start | bytes 3538952 | tf_op jit(solution)/shard_map/ppermute | solution.py:294
  106.9 2.1 copy-start.19
  109.0 5.4 copy-start.12
  114.3 2.5 copy-start.11
  125.6 133.8 %copy-start.20 = (bf16[1,192,1536]{2,1,0:T(8,128)(2,1)S(1)}, bf16[1,192,1536]{2,1,0:T(8,128)(2,1)}, u32[]{:S(2)}) copy-start(bf16[1,192,1536]{2,1,0:T(8,128)(2,1)} %get-tuple-element.187) | copy-start | bytes 1769476
  258.8 47.0 %collective-permute-start.5 = (bf16[384,1536]{1,0:T(8,128)(2,1)}, bf16[384,1536]{1,0:T(8,128)(2,1)}, u32[]{:S(2)}, u32[]{:S(2)}) collective-permute-start(bf16[384,1536]{1,0:T(8,128)(2,1)} %get-tuple-element.95), channel_id=1, source_target_pairs={{0,2},{1,3},{2,0},{3,1},{4,6},{5,7},{6,4},{7,5},{8,10},{9,11},{10,... | collective-permute-start | bytes 3538952 | tf_op jit(solution)/shard_map/ppermute | solution.py:295
  259.4 46.3 %collective-permute-start.4 = (bf16[384,1536]{1,0:T(8,128)(2,1)}, bf16[384,1536]{1,0:T(8,128)(2,1)}, u32[]{:S(2)}, u32[]{:S(2)}) collective-permute-start(bf16[384,1536]{1,0:T(8,128)(2,1)} %get-tuple-element.95), channel_id=1, source_target_pairs={{0,1},{1,0},{2,3},{3,2},{4,5},{5,4},{6,7},{7,6},{8,9},{9,8},{10,11... | collective-permute-start | bytes 3538952 | tf_op jit(solution)/shard_map/ppermute | solution.py:294
  260.5 46.9 %all-to-all-start = ((bf16[192,8,192]{0,2,1:T(8,128)(2,1)}), bf16[192,8,192]{0,2,1:T(8,128)(2,1)S(1)}, u32[]{:S(2)}, u32[]{:S(2)}) async-start(bf16[192,8,192]{0,2,1:T(8,128)(2,1)} %bitcast.17), calls=%async_computation | async-start | bytes 1572864 | tf_op jit(solution)/shard_map/all_to_all | solution.py:1383
  264.2 8.1 %copy-start.60 = (bf16[1024,1536]{1,0:T(8,128)(2,1)S(1)}, bf16[1024,1536]{1,0:T(8,128)(2,1)}, u32[]{:S(2)}) copy-start(bf16[1024,1536]{1,0:T(8,128)(2,1)} %get-tuple-element.85) | copy-start | bytes 9437188
  264.3 19.1 %slice-start.4 = ((s8[4718592]{0:T(1024)(128)(4,1)}), s8[4194304]{0:T(1024)(128)(4,1)S(1)}, s32[]{:S(2)}) async-start(s8[4718592]{0:T(1024)(128)(4,1)} %bitcast.137), calls=%async_computation.6 | async-start | bytes 8388608
  272.3 11.1 %slice-start.5 = ((s8[4718592]{0:T(1024)(128)(4,1)}), s8[524288]{0:T(1024)(128)(4,1)S(1)}, s32[]{:S(2)}) async-start(s8[4718592]{0:T(1024)(128)(4,1)} %bitcast.137), calls=%async_computation.7 | async-start | bytes 1048576
  289.0 2.4 copy-start.14
  289.1 3.5 copy-start.62
  291.3 8.9 %copy-start.1 = (f32[256,1536]{1,0:T(8,128)S(1)}, f32[256,1536]{1,0:T(8,128)}, u32[]{:S(2)}) copy-start(f32[256,1536]{1,0:T(8,128)} %get-tuple-element.84.refs_6_) | copy-start | bytes 4718596
  291.3 37.4 %collective-permute-start = (bf16[512,1536]{1,0:T(8,128)(2,1)}, bf16[512,1536]{1,0:T(8,128)(2,1)}, u32[]{:S(2)}, u32[]{:S(2)}) collective-permute-start(bf16[512,1536]{1,0:T(8,128)(2,1)} %pad_maximum_fusion.6), channel_id=1, source_target_pairs={{0,1},{1,0},{2,3},{3,2},{4,5},{5,4},{6,7},{7,6},{8,9},{9,8},{10,11... | collective-permute-start | bytes 4718600 | tf_op jit(solution)/shard_map/ppermute | solution.py:312
  300.7 3.9 copy-start.27
  305.7 10.7 %collective-permute-start.6 = (bf16[384,1536]{1,0:T(8,128)(2,1)}, bf16[384,1536]{1,0:T(8,128)(2,1)S(1)}, u32[]{:S(2)}, u32[]{:S(2)}) collective-permute-start(bf16[384,1536]{1,0:T(8,128)(2,1)} %collective-permute-done.5), channel_id=1, source_target_pairs={{0,1},{1,0},{2,3},{3,2},{4,5},{5,4},{6,7},{7,6},{8,9},{9,8},{10,11... | collective-permute-start | bytes 3538952 | tf_op jit(solution)/shard_map/ppermute | solution.py:300
  308.6 5.1 copy-start.40
  308.6 9.6 %collective-permute-start.3 = (bf16[384,1536]{1,0:T(8,128)(2,1)}, bf16[384,1536]{1,0:T(8,128)(2,1)S(1)}, u32[]{:S(2)}, u32[]{:S(2)}) collective-permute-start(bf16[384,1536]{1,0:T(8,128)(2,1)} %collective-permute-done.2), channel_id=1, source_target_pairs={{0,1},{1,0},{2,3},{3,2},{4,5},{5,4},{6,7},{7,6},{8,9},{9,8},{10,11... | collective-permute-start | bytes 3538952 | tf_op jit(solution)/shard_map/ppermute | solution.py:300
  316.5 2.3 copy-start.41
  316.5 4.6 copy-start.16
  318.2 12.9 %copy-start.64 = (f32[1536,192]{0,1:T(8,128)}, f32[1536,192]{0,1:T(8,128)S(1)}, u32[]{:S(2)}) copy-start(f32[1536,192]{0,1:T(8,128)S(1)} %fusion.52) | copy-start | bytes 3538948
  319.0 2.1 copy-start.42
  324.6 2.1 copy-start
  328.3 15.5 %collective-permute-start.7 = (bf16[768,1536]{1,0:T(8,128)(2,1)}, bf16[768,1536]{1,0:T(8,128)(2,1)}, u32[]{:S(2)}, u32[]{:S(2)}) collective-permute-start(bf16[768,1536]{1,0:T(8,128)(2,1)} %pad_maximum_fusion.1), channel_id=1, source_target_pairs={{0,1},{1,0},{2,3},{3,2},{4,5},{5,4},{6,7},{7,6},{8,9},{9,8},{10,11... | collective-permute-start | bytes 7077896 | tf_op jit(solution)/shard_map/ppermute | solution.py:312
  332.6 2.2 copy-start.7
  336.4 17.7 %collective-permute-start.9 = (bf16[768,1536]{1,0:T(8,128)(2,1)}, bf16[768,1536]{1,0:T(8,128)(2,1)S(1)}, u32[]{:S(2)}, u32[]{:S(2)}) collective-permute-start(bf16[768,1536]{1,0:T(8,128)(2,1)} %pad_maximum_fusion.2), channel_id=1, source_target_pairs={{0,1},{1,0},{2,3},{3,2},{4,5},{5,4},{6,7},{7,6},{8,9},{9,8},{10,11... | collective-permute-start | bytes 7077896 | tf_op jit(solution)/shard_map/ppermute | solution.py:312
  337.6 6.2 slice-start
  338.7 5.1 slice-start.1
  338.7 8.3 %copy-start.65 = (bf16[1024,1536]{1,0:T(8,128)(2,1)S(1)}, bf16[1024,1536]{1,0:T(8,128)(2,1)}, u32[]{:S(2)}) copy-start(bf16[1024,1536]{1,0:T(8,128)(2,1)} %get-tuple-element.100) | copy-start | bytes 9437188
  343.8 3.3 copy-start.61
  343.8 12.9 %slice-start.2 = ((s8[4718592]{0:T(1024)(128)(4,1)}), s8[4194304]{0:T(1024)(128)(4,1)S(1)}, s32[]{:S(2)}) async-start(s8[4718592]{0:T(1024)(128)(4,1)} %bitcast.135), calls=%async_computation.4 | async-start | bytes 8388608
  345.5 11.1 %slice-start.3 = ((s8[4718592]{0:T(1024)(128)(4,1)}), s8[524288]{0:T(1024)(128)(4,1)S(1)}, s32[]{:S(2)}) async-start(s8[4718592]{0:T(1024)(128)(4,1)} %bitcast.135), calls=%async_computation.5 | async-start | bytes 1048576
  345.6 28.4 %collective-permute-start.8 = (bf16[384,1536]{1,0:T(8,128)(2,1)S(1)}, bf16[384,1536]{1,0:T(8,128)(2,1)S(1)}, u32[]{:S(2)}, u32[]{:S(2)}) collective-permute-start(bf16[384,1536]{1,0:T(8,128)(2,1)S(1)} %add_convert_fusion.3), channel_id=1, source_target_pairs={{0,2},{1,3},{2,0},{3,1},{4,6},{5,7},{6,4},{7,5},{8,10},{9,11},{10,... | collective-permute-start | bytes 3538952 | tf_op jit(solution)/shard_map/ppermute | solution.py:1492
  509.9 3.3 copy-start.25
  509.9 3.3 copy-start.38
  509.9 3.4 copy-start.4
  509.9 3.4 copy-start.22
  509.9 3.7 copy-start.35
  513.2 2.1 copy-start.24
  513.2 2.1 copy-start.49
  513.2 2.1 copy-start.58
  518.4 4.9 copy-start.26
  518.4 7.6 %copy-start.8 = (bf16[1280,384]{1,0:T(8,128)(2,1)S(1)}, bf16[1280,384]{1,0:T(8,128)(2,1)}, u32[]{:S(2)}) copy-start(bf16[1280,384]{1,0:T(8,128)(2,1)} %get-tuple-element.119.refs_0_) | copy-start | bytes 2949124
  518.5 29.5 %all-to-all-start.1 = ((bf16[8,48,1536]{2,1,0:T(8,128)(2,1)}), bf16[8,48,1536]{2,1,0:T(8,128)(2,1)S(1)}, u32[]{:S(2)}, u32[]{:S(2)}) async-start(bf16[8,48,1536]{2,1,0:T(8,128)(2,1)} %bitcast.24), calls=%async_computation.1 | async-start | bytes 2359296 | tf_op jit(solution)/shard_map/all_to_all | solution.py:1395
  523.3 2.9 copy-start.9
  529.6 3.0 copy-start.63
  532.6 2.4 copy-start.59
  535.0 13.1 %copy-start.31 = (bf16[39,1536]{1,0:T(8,128)(2,1)S(1)}, bf16[39,1536]{1,0:T(8,128)(2,1)}, u32[]{:S(2)}) copy-start(bf16[39,1536]{1,0:T(8,128)(2,1)} %copy-done.30) | copy-start | bytes 359428
  535.0 13.2 %copy-start.6 = (f32[64,1536]{1,0:T(8,128)S(1)}, f32[64,1536]{1,0:T(8,128)}, u32[]{:S(2)}) copy-start(f32[64,1536]{1,0:T(8,128)} %get-tuple-element.92.refs_7_) | copy-start | bytes 1179652
  535.0 13.2 %copy-start.39 = (f32[64,1536]{1,0:T(8,128)S(1)}, f32[64,1536]{1,0:T(8,128)}, u32[]{:S(2)}) copy-start(f32[64,1536]{1,0:T(8,128)} %get-tuple-element.127) | copy-start | bytes 1179652
  535.0 13.2 %copy-start.48 = (f32[1536]{0:T(1024)S(1)}, f32[1536]{0:T(1024)}, u32[]{:S(2)}) copy-start(f32[1536]{0:T(1024)} %get-tuple-element.197) | copy-start | bytes 18436
  659.3 3.1 copy-start.54
  659.4 3.7 copy-start.45
  659.4 3.7 copy-start.36
  663.4 1.9 copy-start.33
  663.4 2.3 copy-start.32
  670.4 2.8 copy-start.57
  673.3 2.5 copy-start.23
  (20 other events, 28.5 us)
